TPU v7x, 32 devices: a whole 2x2x4 slice. The times are simulated.
32 devices in a mesh: groups: 2 (over y), gs: 4 (over x, core), tile: 4 (over z).
Axes of the slice: x: 2, y: 2, z: 4, core: 2. Of those that a mesh axis runs over, the one named last changes fastest.
Arguments:
- params: float32 [59, 8192], P(None, ('groups', 'gs')), parts along dimension 1, as said below
- adam_m: float32 [59, 8192], P(None, ('groups', 'gs')), parts along dimension 1, may hold values from -0.6 to 0.6
- adam_v: float32 [59, 8192], P(None, ('groups', 'gs')), parts along dimension 1, may hold values from 0.0001 to 0.01
- cameras: float32 [8, 12], P('groups'), parts along dimension 0, as said below
- target: float32 [3, 16384], P(None, ('groups', 'gs', 'tile')), parts along dimension 1, may hold values from -2 to 2
- tile_ids: int32 [64], P(('groups', 'gs', 'tile')), parts along dimension 0, may hold values from 0 to 32639, as said below
- hit_shard: int32 [64, 256, 1], P(('groups', 'gs', 'tile')), parts along dimension 0, may hold values from 0 to 3, as said below
- hit_local: int32 [64, 256], P(('groups', 'gs', 'tile')), parts along dimension 0, may hold values from 0 to 1023, as said below
Outputs:
- rendered: float32 [3, 16384], P(None, ('groups', 'gs', 'tile')), parts along dimension 1
- new_params: float32 [59, 8192], P(None, ('groups', 'gs')), parts along dimension 1
- new_m: float32 [59, 8192], P(None, ('groups', 'gs')), parts along dimension 1
- new_v: float32 [59, 8192], P(None, ('groups', 'gs')), parts along dimension 1
There are 2 independent parts, one for each index of `groups`. A program takes and returns all parts, laid end to end along the dimension named above; each array names one. Nothing has to cross between parts.
Inputs may be any that keep to these rules, and one draw needn't show every extreme that they name: `hit_shard`: among the entries of the 2 tiles of one device no shard is named more than 256 times; one shard, the same for all of that device's tiles, is named exactly 2 * 256 / 4 times in each of them. `hit_local`: no Gaussian stands twice in one list; the lists of tile slots 8 * q to 8 * q + 7 name only local indices q * 256 to (q + 1) * 256 - 1; along each list the Gaussians' third camera coordinate in the tile's view increases, and each listed Gaussian's mean projects in that view within 4 pixels of the block of eight tiles. `tile_ids`: distinct tiles of the window; tile v * 120 * 68 + r * 120 + c is column c of tile row r of view v; slots 8 * q to 8 * q + 7 hold a block of 4 by 2 tiles of one view, row by row, whose first tile has an even row and a column divisible by 4. `cameras`: orthonormal rotations; every Gaussian lies at least 50 units in front of every camera. `params`: each quaternion's first component is 0.5 or more.
All inputs are finite; a program needn't handle non-finite values.
Results may differ from a plain program's by a relative error of at most 0.0003.
Values sent between devices are 32-bit elements; how exact they have to be, the bound alone decides.
No kernel may reach another device: no remote copies, remote signals or barrier semaphores. Data moves between devices by JAX's collectives and lax.ppermute only.
A program may use at most 128 MiB of HBM per device.

v0:
```python
import jax
import jax.numpy as jnp
from jax import lax
from jax.sharding import PartitionSpec as P

TILES_X = 120
TILES_Y = 68
TILE_SIDE = 16


focal_length = 1000.0
center_x = 960.0
center_y = 540.0
dilation = 0.3
beta_one = 0.9
beta_two = 0.999
learn_rate = 0.01
adam_eps = 1e-08
adam_steps = 100.0
sh_const = (
    0.28209479177387814,
    0.4886025119029199,
    1.0925484305920792,
    0.31539156525252005,
    0.5462742152960396,
    0.5900435899266435,
    2.890611442640554,
    0.4570457994644658,
    0.3731763325901154,
    1.445305721320277,
)


def sh_basis(unit_x, unit_y, unit_z):
    sq_x = unit_x * unit_x
    sq_y = unit_y * unit_y
    sq_z = unit_z * unit_z
    terms = [
        sh_const[0] + 0.0 * unit_x,
        -sh_const[1] * unit_y,
        sh_const[1] * unit_z,
        -sh_const[1] * unit_x,
        sh_const[2] * unit_x * unit_y,
        -sh_const[2] * unit_y * unit_z,
        sh_const[3] * (2.0 * sq_z - sq_x - sq_y),
        -sh_const[2] * unit_x * unit_z,
        sh_const[4] * (sq_x - sq_y),
        -sh_const[5] * unit_y * (3.0 * sq_x - sq_y),
        sh_const[6] * unit_x * unit_y * unit_z,
        -sh_const[7] * unit_y * (4.0 * sq_z - sq_x - sq_y),
        sh_const[8] * unit_z * (2.0 * sq_z - 3.0 * sq_x - 3.0 * sq_y),
        -sh_const[7] * unit_x * (4.0 * sq_z - sq_x - sq_y),
        sh_const[9] * unit_z * (sq_x - sq_y),
        -sh_const[5] * unit_x * (sq_x - 3.0 * sq_y),
    ]
    return jnp.stack(terms)


def project(params, camera):
    rotate = [[camera[3 * row_i + col_i] for col_i in range(3)] for row_i in range(3)]
    offset = [params[axis_i] - camera[9 + axis_i] for axis_i in range(3)]
    in_camera = [
        rotate[row_i][0] * offset[0] + rotate[row_i][1] * offset[1] + rotate[row_i][2] * offset[2]
        for row_i in range(3)
    ]
    inverse = 1.0 / in_camera[2]
    mean_x = focal_length * in_camera[0] * inverse + center_x
    mean_y = focal_length * in_camera[1] * inverse + center_y
    squared = jnp.exp(2.0 * params[3:6])
    rotor = params[6:10] * lax.rsqrt(jnp.sum(params[6:10] * params[6:10], axis=0))[None, :]
    real_w, imag_x, imag_y, imag_z = (rotor[0], rotor[1], rotor[2], rotor[3])
    turn = [
        [
            1.0 - 2.0 * (imag_y * imag_y + imag_z * imag_z),
            2.0 * (imag_x * imag_y - real_w * imag_z),
            2.0 * (imag_x * imag_z + real_w * imag_y),
        ],
        [
            2.0 * (imag_x * imag_y + real_w * imag_z),
            1.0 - 2.0 * (imag_x * imag_x + imag_z * imag_z),
            2.0 * (imag_y * imag_z - real_w * imag_x),
        ],
        [
            2.0 * (imag_x * imag_z - real_w * imag_y),
            2.0 * (imag_y * imag_z + real_w * imag_x),
            1.0 - 2.0 * (imag_x * imag_x + imag_y * imag_y),
        ],
    ]
    spread = [
        [
            sum((turn[row_i][inner] * turn[col_i][inner] * squared[inner] for inner in range(3)))
            for col_i in range(3)
        ]
        for row_i in range(3)
    ]
    nought = jnp.zeros_like(inverse)
    jacobian = [
        [focal_length * inverse, nought, -focal_length * in_camera[0] * inverse * inverse],
        [nought, focal_length * inverse, -focal_length * in_camera[1] * inverse * inverse],
    ]
    screen = [
        [
            sum((jacobian[row_i][inner] * rotate[inner][col_i] for inner in range(3)))
            for col_i in range(3)
        ]
        for row_i in range(2)
    ]

    def covariance(first, second):
        return sum(
            (
                screen[first][row_i] * spread[row_i][col_i] * screen[second][col_i]
                for row_i in range(3)
                for col_i in range(3)
            )
        )

    cov_xx = covariance(0, 0) + dilation
    cov_xy = covariance(0, 1)
    cov_yy = covariance(1, 1) + dilation
    determinant = cov_xx * cov_yy - cov_xy * cov_xy
    conic_a = cov_yy / determinant
    conic_b = -cov_xy / determinant
    conic_c = cov_xx / determinant
    opacity = jax.nn.sigmoid(params[10])
    length = jnp.sqrt(offset[0] * offset[0] + offset[1] * offset[1] + offset[2] * offset[2])
    basis = sh_basis(offset[0] / length, offset[1] / length, offset[2] / length)
    coeffs = params[11:59].reshape(3, 16, -1)
    colour = 0.5 + jnp.sum(coeffs * basis[None], axis=1)
    return jnp.stack(
        [mean_x, mean_y, conic_a, conic_b, conic_c, opacity, colour[0], colour[1], colour[2]]
    )


def pixel_grid(tile_id, pixel_count):
    within = tile_id % (TILES_X * TILES_Y)
    tile_row = within // TILES_X
    tile_col = within % TILES_X
    pixel = jnp.arange(pixel_count, dtype=jnp.int32)
    pixel_x = (tile_col * TILE_SIDE + pixel % TILE_SIDE).astype(jnp.float32) + 0.5
    pixel_y = (tile_row * TILE_SIDE + pixel // TILE_SIDE).astype(jnp.float32) + 0.5
    return (pixel_x, pixel_y)


def composite(entry_rows, pixel_x, pixel_y):
    delta_x = pixel_x[:, None] - entry_rows[0][None, :]
    delta_y = pixel_y[:, None] - entry_rows[1][None, :]
    power = (
        -0.5
        * (entry_rows[2][None, :] * delta_x * delta_x + entry_rows[4][None, :] * delta_y * delta_y)
        - entry_rows[3][None, :] * delta_x * delta_y
    )
    alpha = entry_rows[5][None, :] * jnp.exp(power)
    order = jnp.arange(entry_rows.shape[1], dtype=jnp.int32)
    earlier = (order[:, None] < order[None, :]).astype(jnp.float32)
    before = jnp.dot(jnp.log1p(-alpha), earlier, precision=lax.Precision.HIGHEST)
    weight = alpha * jnp.exp(before)
    return jnp.einsum("cj,pj->cp", entry_rows[6:9], weight, precision=lax.Precision.HIGHEST)


def adam_update(params, moment, second, grad):
    new_m = beta_one * moment + (1.0 - beta_one) * grad
    new_v = beta_two * second + (1.0 - beta_two) * grad * grad
    m_hat = new_m / (1.0 - beta_one**adam_steps)
    v_hat = new_v / (1.0 - beta_two**adam_steps)
    return (params - learn_rate * m_hat / (jnp.sqrt(v_hat) + adam_eps), new_m, new_v)


def local(params, adam_m, adam_v, cameras, target, tile_ids, hit_shard, hit_local):
    g_local = params.shape[1]
    view_count = cameras.shape[0]
    tile_count, listed = hit_local.shape
    pixel_count = target.shape[1] // tile_count
    shards = lax.axis_size("gs")
    span = view_count * g_local

    def project_all(values):
        return jnp.concatenate(
            [project(values, cameras[view_index]) for view_index in range(view_count)], axis=1
        )

    projected, pull_proj = jax.vjp(project_all, params)
    shard_of = hit_shard[:, :, 0].reshape(-1)
    local_of = hit_local.reshape(-1)
    view_of = jnp.repeat(tile_ids // (TILES_X * TILES_Y), listed)
    row_id = view_of * g_local + local_of
    whole = lax.all_gather(projected, "gs", axis=1, tiled=True)
    entries = jnp.take(whole, shard_of * span + row_id, axis=1)
    tile_rows = jnp.moveaxis(entries.reshape(9, tile_count, listed), 1, 0)
    goals = jnp.moveaxis(target.reshape(3, tile_count, pixel_count), 1, 0)

    def one_tile(inputs):
        entry_rows, tile_id, goal = inputs
        pixel_x, pixel_y = pixel_grid(tile_id, pixel_count)
        colour, pull_tile = jax.vjp(lambda values: composite(values, pixel_x, pixel_y), entry_rows)
        return (colour, pull_tile(colour - goal)[0])

    colours, row_grads = lax.map(one_tile, (tile_rows, tile_ids, goals))
    rendered = jnp.moveaxis(colours, 0, 1).reshape(3, -1)
    entry_grads = jnp.moveaxis(row_grads, 0, 1).reshape(9, -1)
    whole_ids = shard_of * span + row_id
    partial_rows = jax.vmap(lambda column: jax.ops.segment_sum(column, whole_ids, shards * span))(
        entry_grads
    )
    proj_grads = lax.psum_scatter(partial_rows, "gs", scatter_dimension=1, tiled=True)
    grad = pull_proj(proj_grads)[0]
    total = lax.psum(grad, "tile")
    new_params, new_m, new_v = adam_update(params, adam_m, adam_v, total)
    return (rendered, new_params, new_m, new_v)


def solution(mesh):
    return jax.shard_map(
        local,
        mesh=mesh,
        in_specs=(
            P(None, ("groups", "gs")),
            P(None, ("groups", "gs")),
            P(None, ("groups", "gs")),
            P("groups", None),
            P(None, ("groups", "gs", "tile")),
            P(("groups", "gs", "tile")),
            P(("groups", "gs", "tile"), None, None),
            P(("groups", "gs", "tile"), None),
        ),
        out_specs=(
            P(None, ("groups", "gs", "tile")),
            P(None, ("groups", "gs")),
            P(None, ("groups", "gs")),
            P(None, ("groups", "gs")),
        ),
        check_vma=False,
    )
```

profile of v0, /device:TPU:0, one launch (start us, length us, event | category | flops | bytes accessed | tf_op | source)
XLA Modules:
  0.0 329.8 jit_solution(10411629151889725884)
XLA Ops:
  7.2 2.1 fusion.297
  9.3 2.1 fusion.296
  11.4 1.7 fusion.298
  16.9 1.0 slice.575
  17.8 0.9 multiply_reduce_fusion.13
  22.6 0.8 multiply_exponential_fusion
  47.8 1.3 compare_and_fusion
  49.2 6.4 %multiply_multiply_fusion.39 = (f32[1,1024]{1,0:T(1,128)S(1)}, f32[1,1024]{1,0:T(1,128)S(1)}, f32[1,1024]{1,0:T(1,128)S(1)}, f32[1,1024]{1,0:T(1,128)S(1)}, f32[...) fusion(f32[]{:T(128)} %bitcast.32, ...), kind=kLoop, calls=%fused_computation.744 | loop fusion | flops 49152 | bytes 61476 | tf_op jit(solution)/shard_map/jvp()/mul | solution.py:54
  55.6 4.6 %multiply_multiply_fusion.40 = (f32[1,1024]{1,0:T(1,128)S(1)}, f32[1,1024]{1,0:T(1,128)S(1)}, f32[1,1024]{1,0:T(1,128)S(1)}, f32[1,1024]{1,0:T(1,128)S(1)}, f32[...) fusion(f32[1,1024]{1,0:T(1,128)S(1)} %get-tuple-element.467, ...), kind=kLoop, calls=%fused_computation.745 | loop fusion | flops 36864 | bytes 73752 | tf_op jit(solution)/shard_map/jvp()/mul | solution.py:53
  60.2 2.7 multiply_multiply_fusion.29
  63.0 2.8 multiply_multiply_fusion.18
  65.9 2.7 multiply_multiply_fusion.51
  69.3 0.9 broadcast_multiply_fusion.12
  70.2 9.3 %fusion.289 = (f32[1,1024]{1,0:T(1,128)S(1)}, f32[1,1024]{1,0:T(1,128)S(1)}, f32[1,1024]{1,0:T(1,128)}, f32[1,1024]{1,0:T(1,128)S(1)}, f32[1,1024]{1,0:T(1,128)}...) fusion(f32[]{:T(128)} %bitcast.24, ...), kind=kLoop, calls=%fused_computation.884 | loop fusion | flops 206848 | bytes 266336 | tf_op jit(solution)/shard_map/jvp()/div | solution.py:124
  79.7 9.1 %fusion.290 = (f32[1,1024]{1,0:T(1,128)S(1)}, f32[1,1024]{1,0:T(1,128)S(1)}, f32[1,1024]{1,0:T(1,128)}, f32[1,1024]{1,0:T(1,128)S(1)}, f32[1,1024]{1,0:T(1,128)}...) fusion(f32[1,1024]{1,0:T(1,128)S(1)} %get-tuple-element.379, ...), kind=kLoop, calls=%fused_computation.885 | loop fusion | flops 126976 | bytes 163936 | tf_op jit(solution)/shard_map/jvp()/div | solution.py:124
  89.3 9.1 %fusion.291 = (f32[1,1024]{1,0:T(1,128)S(1)}, f32[1,1024]{1,0:T(1,128)S(1)}, f32[1,1024]{1,0:T(1,128)}, f32[1,1024]{1,0:T(1,128)S(1)}, f32[1,1024]{1,0:T(1,128)}...) fusion(f32[1,1024]{1,0:T(1,128)S(1)} %get-tuple-element.379, ...), kind=kLoop, calls=%fused_computation.886 | loop fusion | flops 126976 | bytes 163936 | tf_op jit(solution)/shard_map/jvp()/div | solution.py:124
  99.1 9.2 %fusion.292 = (f32[1,1024]{1,0:T(1,128)S(1)}, f32[1,1024]{1,0:T(1,128)S(1)}, f32[1,1024]{1,0:T(1,128)}, f32[1,1024]{1,0:T(1,128)S(1)}, f32[1,1024]{1,0:T(1,128)}...) fusion(f32[1,1024]{1,0:T(1,128)S(1)} %get-tuple-element.379, ...), kind=kLoop, calls=%fused_computation.887 | loop fusion | flops 126976 | bytes 163936 | tf_op jit(solution)/shard_map/jvp()/div | solution.py:124
  109.7 51.9 %all_gather.3 = f32[9,16384]{0,1:T(8,128)} all-gather(f32[9,4096]{0,1:T(8,128)S(1)} %copy.793), channel_id=1, replica_groups=mesh['groups'=2,'gs'=4,'tile'=4] {'gs'}, dimensions={1}, use_global_device_ids=true | all-gather | bytes 737280 | tf_op jit(solution)/shard_map/all_gather | solution.py:187
  161.6 4.4 %gather_fusion = f32[512,9]{1,0:T(8,128)S(1)} fusion(f32[9,16384]{0,1:T(8,128)} %all_gather.3, s32[1024]{0:T(1024)S(1)} %pad_clamp_fusion), kind=kCustom, calls=%fused_computation | custom fusion | bytes 38912 | tf_op jit(solution)/shard_map/jit(_take)/gather | solution.py:188
  166.2 8.1 %while.15 = (s32[]{:T(128)}, f32[2,3,256]{2,1,0:T(4,128)S(1)}, f32[2,9,256]{2,1,0:T(8,128)S(1)}, f32[2,9,256]{2,1,0:T(8,128)S(1)}, s32[2]{0:T(128)S(1)}, /*index...) while((s32[]{:T(128)}, f32[2,3,256]{2,1,0:T(4,128)S(1)}, ...), condition=%wide.region_12.13_spmd, body=%wide.region_5.12_spmd.sunk | while | flops 416303648 | bytes 1695222 | solution.py:198
  169.5 0.8 fusion.307
  173.5 0.8 fusion.307
  175.1 6.1 %scatter_custom_fusion = f32[9,16384]{0,1:T(8,128)} fusion(s32[512]{0:T(512)S(1)} %bitcast.251, f32[512,9]{1,0:T(8,128)S(1)} %copy.797, f32[]{:T(128)} %constant.193.clone.1), kind=kCustom, calls=%fused_computation.76 | custom fusion | flops 4608 | bytes 589828 | tf_op jit(solution)/shard_map/vmap()/scatter-add | solution.py:202
  181.4 6.1 %copy.798 = f32[9,16384]{1,0:T(8,128)} copy(f32[9,16384]{0,1:T(8,128)} %scatter_custom_fusion) | data formatting | bytes 1179648 | tf_op jit(solution)/shard_map/vmap()/scatter-add | solution.py:202
  187.8 25.7 %reduce-scatter.2.cloned.1.call-done = f32[9,4096]{1,0:T(8,128)} async-done(((f32[9,16384]{1,0:T(8,128)}), f32[9,4096]{1,0:T(8,128)}) %reduce-scatter.2.cloned.1.call-update) | async-done | bytes 147472 | tf_op jit(solution)/shard_map/reduce_scatter | solution.py:205
  213.5 1.1 slice_multiply_fusion.23
  214.6 1.2 add_add_fusion.12
  216.0 1.1 negate_add_fusion.2
  217.1 1.1 multiply_multiply_fusion.63
  218.2 1.2 add_add_fusion.29
  219.6 0.8 fusion.260
  220.4 0.9 multiply_multiply_fusion.75
  221.6 0.9 multiply_multiply_fusion.64
  222.5 0.8 fusion.253
  223.3 0.8 multiply_multiply_fusion.76
  224.7 0.8 fusion.293
  226.6 0.8 fusion.294
  228.2 8.8 %multiply_add_fusion.105 = (f32[1,1024]{1,0:T(1,128)S(1)}, f32[1,1024]{1,0:T(1,128)S(1)}, f32[1,1024]{1,0:T(1,128)S(1)}, f32[1,1024]{1,0:T(1,128)S(1)}, f32[1,10...) fusion(f32[]{:T(128)} %bitcast.66, f32[]{:T(128)} %bitcast.63, f32[]{:T(128)} %bitcast.59, ...), kind=kLoop, calls=%fused_computation.529 | loop fusion | flops 280576 | bytes 303152 | tf_op jit(solution)/shard_map/transpose(jvp())/add_any | solution.py:63
  236.9 5.1 %multiply_add_fusion.104 = (f32[1,1024]{1,0:T(1,128)S(1)}, f32[1,1024]{1,0:T(1,128)S(1)}) fusion(f32[1,1024]{1,0:T(1,128)S(1)} %get-tuple-element.208, f32[1,1024]{1,0:T(1,128)S(1)} %get-tuple-element.207, f32[1,1024]{1,0:T(1,128)S(1)} %get-tuple-element.206, f32[1,1024]{1,0:T(1,128)S(1)} %get-tuple-element.203, f32[1,1024]{1,0:T(1,128)S(1)} %get-tuple-element.204, ...), kind=kLoop, calls=%fused_computation.528 | loop fusion | flops 22528 | bytes 45088 | tf_op jit(solution)/shard_map/transpose(jvp())/add_any | solution.py:63
  242.8 8.7 %multiply_add_fusion.79 = (f32[1,1024]{1,0:T(1,128)S(1)}, f32[1,1024]{1,0:T(1,128)S(1)}, f32[1,1024]{1,0:T(1,128)S(1)}, f32[1,1024]{1,0:T(1,128)S(1)}, f32[1,102...) fusion(f32[]{:T(128)} %bitcast.54, f32[]{:T(128)} %bitcast.51, f32[]{:T(128)} %bitcast.47, ...), kind=kLoop, calls=%fused_computation.496 | loop fusion | flops 280576 | bytes 303152 | tf_op jit(solution)/shard_map/transpose(jvp())/add_any | solution.py:63
  251.5 4.9 %multiply_add_fusion.78 = (f32[1,1024]{1,0:T(1,128)S(1)}, f32[1,1024]{1,0:T(1,128)S(1)}) fusion(f32[1,1024]{1,0:T(1,128)S(1)} %get-tuple-element.245, f32[1,1024]{1,0:T(1,128)S(1)} %get-tuple-element.244, f32[1,1024]{1,0:T(1,128)S(1)} %get-tuple-element.243, f32[1,1024]{1,0:T(1,128)S(1)} %get-tuple-element.240, f32[1,1024]{1,0:T(1,128)S(1)} %get-tuple-element.241, ...), kind=kLoop, calls=%fused_computation.495 | loop fusion | flops 22528 | bytes 45088 | tf_op jit(solution)/shard_map/transpose(jvp())/add_any | solution.py:63
  256.7 8.6 %multiply_add_fusion.53 = (f32[1,1024]{1,0:T(1,128)S(1)}, f32[1,1024]{1,0:T(1,128)S(1)}, f32[1,1024]{1,0:T(1,128)S(1)}, f32[1,1024]{1,0:T(1,128)S(1)}, f32[1,102...) fusion(f32[]{:T(128)} %bitcast.42, f32[]{:T(128)} %bitcast.39, f32[]{:T(128)} %bitcast.35, ...), kind=kLoop, calls=%fused_computation.463 | loop fusion | flops 263168 | bytes 278576 | tf_op jit(solution)/shard_map/transpose(jvp())/add_any | solution.py:63
  265.3 4.9 %multiply_add_fusion.52 = (f32[1,1024]{1,0:T(1,128)S(1)}, f32[1,1024]{1,0:T(1,128)S(1)}) fusion(f32[1,1024]{1,0:T(1,128)S(1)} %get-tuple-element.306, f32[1,1024]{1,0:T(1,128)S(1)} %get-tuple-element.305, f32[1,1024]{1,0:T(1,128)S(1)} %get-tuple-element.304, f32[1,1024]{1,0:T(1,128)S(1)} %get-tuple-element.301, f32[1,1024]{1,0:T(1,128)S(1)} %get-tuple-element.302, ...), kind=kLoop, calls=%fused_computation.462 | loop fusion | flops 22528 | bytes 45088 | tf_op jit(solution)/shard_map/transpose(jvp())/add_any | solution.py:63
  270.3 8.7 %multiply_add_fusion.27 = (f32[1,1024]{1,0:T(1,128)S(1)}, f32[1,1024]{1,0:T(1,128)S(1)}, f32[1,1024]{1,0:T(1,128)S(1)}, f32[1,1024]{1,0:T(1,128)S(1)}, f32[1,102...) fusion(f32[]{:T(128)} %bitcast.29, f32[]{:T(128)} %bitcast.26, f32[]{:T(128)} %bitcast.22, ...), kind=kLoop, calls=%fused_computation.430 | loop fusion | flops 244736 | bytes 254000 | tf_op jit(solution)/shard_map/transpose(jvp())/add_any | solution.py:63
  279.0 5.0 %multiply_add_fusion.26 = (f32[1,1024]{1,0:T(1,128)S(1)}, f32[1,1024]{1,0:T(1,128)S(1)}) fusion(f32[1,1024]{1,0:T(1,128)S(1)} %get-tuple-element.345, f32[1,1024]{1,0:T(1,128)S(1)} %get-tuple-element.344, f32[1,1024]{1,0:T(1,128)S(1)} %get-tuple-element.343, f32[1,1024]{1,0:T(1,128)S(1)} %get-tuple-element.340, f32[1,1024]{1,0:T(1,128)S(1)} %get-tuple-element.341, ...), kind=kLoop, calls=%fused_computation.429 | loop fusion | flops 22528 | bytes 45088 | tf_op jit(solution)/shard_map/transpose(jvp())/add_any | solution.py:63
  284.5 1.0 fusion.68
  285.6 35.5 %all-reduce.177.cloned.1.call-done = f32[59,1024]{1,0:T(8,128)} async-done(((f32[59,1024]{1,0:T(8,128)}), f32[59,1024]{1,0:T(8,128)}) %all-reduce.177.cloned.1.call-update) | async-done | bytes 241680 | tf_op jit(solution)/shard_map/psum | solution.py:207
  321.1 1.9 divide_subtract_fusion
  (224 shorter events, 15.8 us)
Async XLA Ops:
  7.2 206.3 %reduce-scatter.2.cloned.1.call-start = ((), (), s32[]{:S(2)}) async-start(), calls=%async_computation.1 | async-start | bytes 1310720 | tf_op jit(solution)/shard_map/reduce_scatter | solution.py:205
  68.7 97.4 %copy-start.60 = (pred[2,256]{1,0:T(4,128)(4,1)S(1)}, pred[2,256]{1,0:T(4,128)(4,1)}, u32[]{:S(2)}) copy-start(pred[2,256]{1,0:T(4,128)(4,1)} %compare_and_fusion) | copy-start | bytes 1540
  68.7 97.4 %copy-start.11 = (f32[3,512]{1,0:T(4,128)S(1)}, f32[3,512]{1,0:T(4,128)}, u32[]{:S(2)}) copy-start(f32[3,512]{1,0:T(4,128)} %param.14) | copy-start | bytes 18436
  68.7 97.4 %copy-start.61 = (s32[2]{0:T(128)S(1)}, s32[2]{0:T(128)}, u32[]{:S(2)}) copy-start(s32[2]{0:T(128)} %param.15) | copy-start | bytes 28
  68.8 97.4 %copy-start.62 = (f32[2,3,256]{2,1,0:T(4,128)S(1)}, f32[2,3,256]{2,1,0:T(4,128)}, u32[]{:S(2)}) copy-start(f32[2,3,256]{2,1,0:T(4,128)} %custom-call.2) | copy-start | bytes 18436
  98.5 67.7 %copy-start.51 = (f32[1,1024]{1,0:T(1,128)}, f32[1,1024]{1,0:T(1,128)S(1)}, u32[]{:S(2)}) copy-start(f32[1,1024]{1,0:T(1,128)S(1)} %get-tuple-element.462) | copy-start | bytes 12292
  98.5 67.7 %copy-start.52 = (f32[1,1024]{1,0:T(1,128)}, f32[1,1024]{1,0:T(1,128)S(1)}, u32[]{:S(2)}) copy-start(f32[1,1024]{1,0:T(1,128)S(1)} %get-tuple-element.463) | copy-start | bytes 12292
  108.2 58.0 %copy-start.53 = (f32[1,1024]{1,0:T(1,128)}, f32[1,1024]{1,0:T(1,128)S(1)}, u32[]{:S(2)}) copy-start(f32[1,1024]{1,0:T(1,128)S(1)} %get-tuple-element.516) | copy-start | bytes 12292
  108.3 58.0 %copy-start.54 = (f32[1,1024]{1,0:T(1,128)}, f32[1,1024]{1,0:T(1,128)S(1)}, u32[]{:S(2)}) copy-start(f32[1,1024]{1,0:T(1,128)S(1)} %get-tuple-element.517) | copy-start | bytes 12292
  108.3 58.0 %copy-start.55 = (f32[1,1024]{1,0:T(1,128)}, f32[1,1024]{1,0:T(1,128)S(1)}, u32[]{:S(2)}) copy-start(f32[1,1024]{1,0:T(1,128)S(1)} %get-tuple-element.518) | copy-start | bytes 12292
  175.0 41.0 %copy-start.6 = (f32[1,1024]{1,0:T(1,128)S(1)}, f32[1,1024]{1,0:T(1,128)}, u32[]{:S(2)}) copy-start(f32[1,1024]{1,0:T(1,128)} %copy-done.5) | copy-start | bytes 12292
  175.0 41.0 %copy-start.8 = (f32[1,1024]{1,0:T(1,128)S(1)}, f32[1,1024]{1,0:T(1,128)}, u32[]{:S(2)}) copy-start(f32[1,1024]{1,0:T(1,128)} %copy-done.7) | copy-start | bytes 12292
  175.0 41.0 %copy-start.10 = (f32[1,1024]{1,0:T(1,128)S(1)}, f32[1,1024]{1,0:T(1,128)}, u32[]{:S(2)}) copy-start(f32[1,1024]{1,0:T(1,128)} %copy-done.9) | copy-start | bytes 12292
  175.0 43.2 %copy-start.24 = (f32[1,1024]{1,0:T(1,128)S(1)}, f32[1,1024]{1,0:T(1,128)}, u32[]{:S(2)}) copy-start(f32[1,1024]{1,0:T(1,128)} %get-tuple-element.426) | copy-start | bytes 12292
  175.0 43.2 %copy-start.25 = (f32[1,1024]{1,0:T(1,128)S(1)}, f32[1,1024]{1,0:T(1,128)}, u32[]{:S(2)}) copy-start(f32[1,1024]{1,0:T(1,128)} %get-tuple-element.429) | copy-start | bytes 12292
  175.0 44.5 %copy-start.3 = (f32[1,1024]{1,0:T(1,128)S(1)}, f32[1,1024]{1,0:T(1,128)}, u32[]{:S(2)}) copy-start(f32[1,1024]{1,0:T(1,128)} %get-tuple-element.385) | copy-start | bytes 12292
  175.0 44.5 %copy-start.4 = (f32[1,1024]{1,0:T(1,128)S(1)}, f32[1,1024]{1,0:T(1,128)}, u32[]{:S(2)}) copy-start(f32[1,1024]{1,0:T(1,128)} %get-tuple-element.387) | copy-start | bytes 12292
  175.1 45.4 %copy-start.29 = (f32[1,1024]{1,0:T(1,128)S(1)}, f32[1,1024]{1,0:T(1,128)}, u32[]{:S(2)}) copy-start(f32[1,1024]{1,0:T(1,128)} %get-tuple-element.381) | copy-start | bytes 12292
  175.1 45.4 %copy-start.30 = (f32[1,1024]{1,0:T(1,128)S(1)}, f32[1,1024]{1,0:T(1,128)}, u32[]{:S(2)}) copy-start(f32[1,1024]{1,0:T(1,128)} %get-tuple-element.382) | copy-start | bytes 12292
  181.1 43.3 %copy-start = (f32[59,1024]{1,0:T(8,128)S(1)}, f32[59,1024]{1,0:T(8,128)}, u32[]{:S(2)}) copy-start(f32[59,1024]{1,0:T(8,128)} %param.10) | copy-start | bytes 724996
  181.1 44.6 %copy-start.12 = (f32[1,1024]{1,0:T(1,128)S(1)}, f32[1,1024]{1,0:T(1,128)}, u32[]{:S(2)}) copy-start(f32[1,1024]{1,0:T(1,128)} %get-tuple-element.353) | copy-start | bytes 12292
  181.1 44.6 %copy-start.14 = (f32[1,1024]{1,0:T(1,128)S(1)}, f32[1,1024]{1,0:T(1,128)}, u32[]{:S(2)}) copy-start(f32[1,1024]{1,0:T(1,128)} %get-tuple-element.357) | copy-start | bytes 12292
  181.2 44.7 %copy-start.16 = (f32[1,1024]{1,0:T(1,128)S(1)}, f32[1,1024]{1,0:T(1,128)}, u32[]{:S(2)}) copy-start(f32[1,1024]{1,0:T(1,128)} %get-tuple-element.361) | copy-start | bytes 12292
  181.2 44.7 %copy-start.13 = (f32[1,1024]{1,0:T(1,128)S(1)}, f32[1,1024]{1,0:T(1,128)}, u32[]{:S(2)}) copy-start(f32[1,1024]{1,0:T(1,128)} %get-tuple-element.354) | copy-start | bytes 12292
  181.2 44.7 %copy-start.15 = (f32[1,1024]{1,0:T(1,128)S(1)}, f32[1,1024]{1,0:T(1,128)}, u32[]{:S(2)}) copy-start(f32[1,1024]{1,0:T(1,128)} %get-tuple-element.358) | copy-start | bytes 12292
  181.2 44.7 %copy-start.17 = (f32[1,1024]{1,0:T(1,128)S(1)}, f32[1,1024]{1,0:T(1,128)}, u32[]{:S(2)}) copy-start(f32[1,1024]{1,0:T(1,128)} %get-tuple-element.362) | copy-start | bytes 12292
  181.2 60.9 %copy-start.46 = (f32[1,1024]{1,0:T(1,128)S(1)}, f32[1,1024]{1,0:T(1,128)}, u32[]{:S(2)}) copy-start(f32[1,1024]{1,0:T(1,128)} %get-tuple-element.438) | copy-start | bytes 12292
  181.2 60.9 %copy-start.47 = (f32[1,1024]{1,0:T(1,128)S(1)}, f32[1,1024]{1,0:T(1,128)}, u32[]{:S(2)}) copy-start(f32[1,1024]{1,0:T(1,128)} %get-tuple-element.440) | copy-start | bytes 12292
  181.2 60.9 %copy-start.48 = (f32[1,1024]{1,0:T(1,128)S(1)}, f32[1,1024]{1,0:T(1,128)}, u32[]{:S(2)}) copy-start(f32[1,1024]{1,0:T(1,128)} %get-tuple-element.442) | copy-start | bytes 12292
  181.2 60.9 %copy-start.49 = (f32[1,1024]{1,0:T(1,128)S(1)}, f32[1,1024]{1,0:T(1,128)}, u32[]{:S(2)}) copy-start(f32[1,1024]{1,0:T(1,128)} %get-tuple-element.444) | copy-start | bytes 12292
  181.2 75.3 %copy-start.32 = (f32[1,1024]{1,0:T(1,128)S(1)}, f32[1,1024]{1,0:T(1,128)}, u32[]{:S(2)}) copy-start(f32[1,1024]{1,0:T(1,128)} %get-tuple-element.408) | copy-start | bytes 12292
  181.2 75.3 %copy-start.35 = (f32[1,1024]{1,0:T(1,128)S(1)}, f32[1,1024]{1,0:T(1,128)}, u32[]{:S(2)}) copy-start(f32[1,1024]{1,0:T(1,128)} %get-tuple-element.412) | copy-start | bytes 12292
  181.2 75.3 %copy-start.38 = (f32[1,1024]{1,0:T(1,128)S(1)}, f32[1,1024]{1,0:T(1,128)}, u32[]{:S(2)}) copy-start(f32[1,1024]{1,0:T(1,128)} %get-tuple-element.416) | copy-start | bytes 12292
  181.3 75.3 %copy-start.31 = (f32[1,1024]{1,0:T(1,128)S(1)}, f32[1,1024]{1,0:T(1,128)}, u32[]{:S(2)}) copy-start(f32[1,1024]{1,0:T(1,128)} %get-tuple-element.407) | copy-start | bytes 12292
  181.3 75.3 %copy-start.33 = (f32[1,1024]{1,0:T(1,128)S(1)}, f32[1,1024]{1,0:T(1,128)}, u32[]{:S(2)}) copy-start(f32[1,1024]{1,0:T(1,128)} %get-tuple-element.409) | copy-start | bytes 12292
  181.3 75.3 %copy-start.34 = (f32[1,1024]{1,0:T(1,128)S(1)}, f32[1,1024]{1,0:T(1,128)}, u32[]{:S(2)}) copy-start(f32[1,1024]{1,0:T(1,128)} %get-tuple-element.411) | copy-start | bytes 12292
  181.3 75.3 %copy-start.36 = (f32[1,1024]{1,0:T(1,128)S(1)}, f32[1,1024]{1,0:T(1,128)}, u32[]{:S(2)}) copy-start(f32[1,1024]{1,0:T(1,128)} %get-tuple-element.413) | copy-start | bytes 12292
  181.3 75.3 %copy-start.37 = (f32[1,1024]{1,0:T(1,128)S(1)}, f32[1,1024]{1,0:T(1,128)}, u32[]{:S(2)}) copy-start(f32[1,1024]{1,0:T(1,128)} %get-tuple-element.415) | copy-start | bytes 12292
  181.3 75.3 %copy-start.39 = (f32[1,1024]{1,0:T(1,128)S(1)}, f32[1,1024]{1,0:T(1,128)}, u32[]{:S(2)}) copy-start(f32[1,1024]{1,0:T(1,128)} %get-tuple-element.417) | copy-start | bytes 12292
  181.3 75.4 %copy-start.41 = (f32[1,1024]{1,0:T(1,128)S(1)}, f32[1,1024]{1,0:T(1,128)}, u32[]{:S(2)}) copy-start(f32[1,1024]{1,0:T(1,128)} %copy-done.40) | copy-start | bytes 12292
  181.3 75.4 %copy-start.43 = (f32[1,1024]{1,0:T(1,128)S(1)}, f32[1,1024]{1,0:T(1,128)}, u32[]{:S(2)}) copy-start(f32[1,1024]{1,0:T(1,128)} %copy-done.42) | copy-start | bytes 12292
  181.3 75.4 %copy-start.45 = (f32[1,1024]{1,0:T(1,128)S(1)}, f32[1,1024]{1,0:T(1,128)}, u32[]{:S(2)}) copy-start(f32[1,1024]{1,0:T(1,128)} %copy-done.44) | copy-start | bytes 12292
  181.3 88.9 %copy-start.19 = (f32[1,1024]{1,0:T(1,128)S(1)}, f32[1,1024]{1,0:T(1,128)}, u32[]{:S(2)}) copy-start(f32[1,1024]{1,0:T(1,128)} %copy-done.18) | copy-start | bytes 12292
  181.4 88.9 %copy-start.21 = (f32[1,1024]{1,0:T(1,128)S(1)}, f32[1,1024]{1,0:T(1,128)}, u32[]{:S(2)}) copy-start(f32[1,1024]{1,0:T(1,128)} %copy-done.20) | copy-start | bytes 12292
  181.4 88.9 %copy-start.23 = (f32[1,1024]{1,0:T(1,128)S(1)}, f32[1,1024]{1,0:T(1,128)}, u32[]{:S(2)}) copy-start(f32[1,1024]{1,0:T(1,128)} %copy-done.22) | copy-start | bytes 12292
  181.4 139.7 %copy-start.1 = (f32[59,1024]{1,0:T(8,128)S(1)}, f32[59,1024]{1,0:T(8,128)}, u32[]{:S(2)}) copy-start(f32[59,1024]{1,0:T(8,128)} %param.11) | copy-start | bytes 724996
  181.4 139.7 %copy-start.2 = (f32[59,1024]{1,0:T(8,128)S(1)}, f32[59,1024]{1,0:T(8,128)}, u32[]{:S(2)}) copy-start(f32[59,1024]{1,0:T(8,128)} %param.12) | copy-start | bytes 724996
  187.6 133.5 %all-reduce.177.cloned.1.call-start = ((), (), s32[]{:S(2)}) async-start(), calls=%async_computation.2 | async-start | bytes 524288 | tf_op jit(solution)/shard_map/psum | solution.py:207
  (18 other events, 176.3 us)
Sparse Core Ops, SparseCore 0:
  187.7 25.7 reduce-scatter.1
  285.7 35.3 all-reduce.176
where the time goes:
time: 334 us; the launch traced here: 330 us
  other arithmetic  142 us (43%)
  waiting for transfers between devices  61.2 us (18%)
  blocking collectives  51.9 us (16%)
  between operations  45.3 us (14%)
  local copies, waits for them, and re-layouts  22.4 us (7%)
  matrix products  5.3 us (2%)
    all_gather x1, blocking collectives, local(): whole = lax.all_gather(projected, 'gs', axis=1, tiled=True)  51.9 us
    div x4, other arithmetic, project(): conic_c = cov_xx / determinant  36.7 us
    psum x1, waiting for transfers between devices, local(): total = lax.psum(grad, 'tile')  35.5 us
    add_any x4, other arithmetic, project(): rotate[row_i][2] * offset[2]  34.8 us
    reduce_scatter x1, waiting for transfers between devices, local(): lax.psum_scatter(partial_rows, 'gs', scatter_dimension=1, tiled=True)  25.7 us
    add_any x4, other arithmetic, project(): rotate[row_i][1] * offset[1]  20 us
    mul x4, other arithmetic, sh_basis(): sh_const[9] * unit_z * (sq_x - sq_y)  12.7 us
    mul x11, other arithmetic, project(): turn[row_i][inner] * turn[col_i][inner] * squared[inner]  7.09 us
  transfers between devices with their start and end apart: 2, of which 2 were waited for; matrix products, arithmetic and copies ran while one was open for 0% of the time, Pallas kernels for 0%

commit v1 on v0

v1 whole, which is shorter than its diff:
```python
import functools

import jax
import jax.numpy as jnp
from jax import lax
from jax.experimental import pallas as pl
from jax.experimental.pallas import tpu as pltpu
from jax.sharding import PartitionSpec as P

TILES_X = 120
TILES_Y = 68
TILE_SIDE = 16
BLOCK_TILES = 8
LANES = 128
ROWS = 16
F32 = jnp.float32
BF16 = jnp.bfloat16

focal_length = 1000.0
center_x = 960.0
center_y = 540.0
dilation = 0.3
beta_one = 0.9
beta_two = 0.999
learn_rate = 0.01
adam_eps = 1e-08
adam_steps = 100.0
sh_const = (
    0.28209479177387814,
    0.4886025119029199,
    1.0925484305920792,
    0.31539156525252005,
    0.5462742152960396,
    0.5900435899266435,
    2.890611442640554,
    0.4570457994644658,
    0.3731763325901154,
    1.445305721320277,
)


def sh_basis(x, y, z):
    s = sh_const
    xx, yy, zz = x * x, y * y, z * z
    return [
        None,
        -s[1] * y,
        s[1] * z,
        -s[1] * x,
        s[2] * (x * y),
        -s[2] * (y * z),
        s[3] * (2.0 * zz - xx - yy),
        -s[2] * (x * z),
        s[4] * (xx - yy),
        -s[5] * y * (3.0 * xx - yy),
        s[6] * (x * y) * z,
        -s[7] * y * (4.0 * zz - xx - yy),
        s[8] * z * (2.0 * zz - 3.0 * xx - 3.0 * yy),
        -s[7] * x * (4.0 * zz - xx - yy),
        s[9] * z * (xx - yy),
        -s[5] * x * (xx - 3.0 * yy),
    ]


def sh_pull(h, x, y, z):
    s = sh_const
    xx, yy, zz = x * x, y * y, z * z
    xy, xz, yz = x * y, x * z, y * z
    diff = xx - yy
    ring = 4.0 * zz - xx - yy
    g_x = (
        -s[1] * h[3]
        + s[2] * (h[4] * y - h[7] * z)
        - (2.0 * s[3]) * h[6] * x
        + (2.0 * s[4]) * h[8] * x
        - (6.0 * s[5]) * h[9] * xy
        + s[6] * h[10] * yz
        + (2.0 * s[7]) * h[11] * xy
        - (6.0 * s[8]) * h[12] * xz
        - s[7] * h[13] * (ring - 2.0 * xx)
        + (2.0 * s[9]) * h[14] * xz
        - (3.0 * s[5]) * h[15] * diff
    )
    g_y = (
        -s[1] * h[1]
        + s[2] * (h[4] * x - h[5] * z)
        - (2.0 * s[3]) * h[6] * y
        - (2.0 * s[4]) * h[8] * y
        - (3.0 * s[5]) * h[9] * diff
        + s[6] * h[10] * xz
        - s[7] * h[11] * (ring - 2.0 * yy)
        - (6.0 * s[8]) * h[12] * yz
        + (2.0 * s[7]) * h[13] * xy
        - (2.0 * s[9]) * h[14] * yz
        + (6.0 * s[5]) * h[15] * xy
    )
    g_z = (
        s[1] * h[2]
        - s[2] * (h[5] * y + h[7] * x)
        + (4.0 * s[3]) * h[6] * z
        + s[6] * h[10] * xy
        - (8.0 * s[7]) * (h[11] * yz + h[13] * xz)
        + s[8] * h[12] * (6.0 * zz - 3.0 * xx - 3.0 * yy)
        + s[9] * h[14] * diff
    )
    return g_x, g_y, g_z


def project_parts(feat, cam):
    rot = [[cam[3 * r + c] for c in range(3)] for r in range(3)]
    off = [feat(a) - cam[9 + a] for a in range(3)]
    in_cam = [rot[r][0] * off[0] + rot[r][1] * off[1] + rot[r][2] * off[2] for r in range(3)]
    inv = 1.0 / in_cam[2]
    u = in_cam[0] * inv
    v = in_cam[1] * inv
    finv = focal_length * inv
    scale = [jnp.exp(2.0 * feat(3 + a)) for a in range(3)]
    quat = [feat(6 + a) for a in range(4)]
    rnorm = lax.rsqrt(quat[0] * quat[0] + quat[1] * quat[1] + quat[2] * quat[2] + quat[3] * quat[3])
    w, x, y, z = [q * rnorm for q in quat]
    turn = [
        [1.0 - 2.0 * (y * y + z * z), 2.0 * (x * y - w * z), 2.0 * (x * z + w * y)],
        [2.0 * (x * y + w * z), 1.0 - 2.0 * (x * x + z * z), 2.0 * (y * z - w * x)],
        [2.0 * (x * z - w * y), 2.0 * (y * z + w * x), 1.0 - 2.0 * (x * x + y * y)],
    ]
    screen = [
        [finv * (rot[0][c] - u * rot[2][c]) for c in range(3)],
        [finv * (rot[1][c] - v * rot[2][c]) for c in range(3)],
    ]
    axes = [
        [sum(screen[r][c] * turn[c][k] for c in range(3)) for k in range(3)] for r in range(2)
    ]
    wide = [[axes[r][k] * scale[k] for k in range(3)] for r in range(2)]
    cov_xx = sum(wide[0][k] * axes[0][k] for k in range(3)) + dilation
    cov_xy = sum(wide[0][k] * axes[1][k] for k in range(3))
    cov_yy = sum(wide[1][k] * axes[1][k] for k in range(3)) + dilation
    rdet = 1.0 / (cov_xx * cov_yy - cov_xy * cov_xy)
    conic = (cov_yy * rdet, -cov_xy * rdet, cov_xx * rdet)
    opacity = 1.0 / (1.0 + jnp.exp(-feat(10)))
    rlen = lax.rsqrt(off[0] * off[0] + off[1] * off[1] + off[2] * off[2])
    way = [off[a] * rlen for a in range(3)]
    return dict(
        rot=rot, inv=inv, u=u, v=v, finv=finv, scale=scale, rnorm=rnorm, rotor=(w, x, y, z), turn=turn,
        screen=screen, axes=axes, wide=wide, conic=conic, opacity=opacity, rlen=rlen, way=way,
    )


def project_rows(feat, cam):
    part = project_parts(feat, cam)
    basis = sh_basis(*part["way"])
    colours = []
    for k in range(3):
        total = 0.5 + sh_const[0] * feat(11 + 16 * k)
        for b in range(1, 16):
            total = total + feat(11 + 16 * k + b) * basis[b]
        colours.append(total)
    mean_x = focal_length * part["u"] + center_x
    mean_y = focal_length * part["v"] + center_y
    return [mean_x, mean_y, *part["conic"], part["opacity"], *colours]


def project_pull(feat, cam, grads, put):
    part = project_parts(feat, cam)
    g_mx, g_my, g_a, g_b, g_c, g_o = grads[:6]
    g_col = grads[6:9]
    way, rlen = part["way"], part["rlen"]
    basis = sh_basis(*way)
    pulled = [None]
    for k in range(3):
        put(11 + 16 * k, sh_const[0] * g_col[k])
    for b in range(1, 16):
        total = 0.0
        for k in range(3):
            put(11 + 16 * k + b, g_col[k] * basis[b])
            total = total + g_col[k] * feat(11 + 16 * k + b)
        pulled.append(total)
    g_way = sh_pull(pulled, *way)
    along = way[0] * g_way[0] + way[1] * g_way[1] + way[2] * g_way[2]
    g_off = [(g_way[a] - way[a] * along) * rlen for a in range(3)]
    put(10, g_o * part["opacity"] * (1.0 - part["opacity"]))
    a, b, c = part["conic"]
    g_xx = -(a * a * g_a + a * b * g_b + b * b * g_c)
    g_xy = -(2.0 * a * b * g_a + (a * c + b * b) * g_b + 2.0 * b * c * g_c)
    g_yy = -(b * b * g_a + b * c * g_b + c * c * g_c)
    axes, wide, turn, screen = part["axes"], part["wide"], part["turn"], part["screen"]
    for k in range(3):
        g_scale = (
            g_xx * axes[0][k] * wide[0][k]
            + g_xy * axes[0][k] * wide[1][k]
            + g_yy * axes[1][k] * wide[1][k]
        )
        put(3 + k, 2.0 * g_scale)
    g_axes = [
        [2.0 * g_xx * wide[0][k] + g_xy * wide[1][k] for k in range(3)],
        [2.0 * g_yy * wide[1][k] + g_xy * wide[0][k] for k in range(3)],
    ]
    g_screen = [
        [sum(g_axes[r][k] * turn[c][k] for k in range(3)) for c in range(3)] for r in range(2)
    ]
    gm = [
        [g_axes[0][k] * screen[0][c] + g_axes[1][k] * screen[1][c] for k in range(3)]
        for c in range(3)
    ]
    w, x, y, z = part["rotor"]
    up_xy, up_xz, up_yz = gm[0][1] + gm[1][0], gm[0][2] + gm[2][0], gm[1][2] + gm[2][1]
    un_xy, un_xz, un_yz = gm[1][0] - gm[0][1], gm[0][2] - gm[2][0], gm[2][1] - gm[1][2]
    g_rotor = [
        2.0 * (z * un_xy + y * un_xz + x * un_yz),
        2.0 * (y * up_xy + z * up_xz + w * un_yz - 2.0 * x * (gm[1][1] + gm[2][2])),
        2.0 * (x * up_xy + z * up_yz + w * un_xz - 2.0 * y * (gm[0][0] + gm[2][2])),
        2.0 * (x * up_xz + y * up_yz + w * un_xy - 2.0 * z * (gm[0][0] + gm[1][1])),
    ]
    rotor = (w, x, y, z)
    along = sum(rotor[i] * g_rotor[i] for i in range(4))
    for i in range(4):
        put(6 + i, (g_rotor[i] - rotor[i] * along) * part["rnorm"])
    rot, inv, finv, u, v = part["rot"], part["inv"], part["finv"], part["u"], part["v"]
    g_u = focal_length * g_mx - finv * sum(g_screen[0][c] * rot[2][c] for c in range(3))
    g_v = focal_length * g_my - finv * sum(g_screen[1][c] * rot[2][c] for c in range(3))
    g_f = sum(g_screen[r][c] * screen[r][c] for r in range(2) for c in range(3))
    g_in = [g_u * inv, g_v * inv, -(g_f + g_u * u + g_v * v) * inv]
    for axis in range(3):
        put(
            axis,
            g_off[axis] + rot[0][axis] * g_in[0] + rot[1][axis] * g_in[1] + rot[2][axis] * g_in[2],
        )


def split(value):
    high = value.astype(BF16)
    return high, (value - high.astype(F32)).astype(BF16)


def matmul(a, b, dims=((1,), (0,))):
    return lax.dot_general(a, b, (dims, ((), ())), preferred_element_type=F32)


def spread_features(parts, scratch, count):
    tiles = sum(part.shape[1] for part in parts) // LANES
    at = 0
    for part in parts:
        for first in range(0, part.shape[1], LANES):
            for row in range(0, count, 8):
                rows = min(8, count - row)
                scratch[pl.ds(row * tiles + at, rows, stride=tiles), :] = part[
                    row : row + rows, first : first + LANES
                ]
            at += 1
    return tiles


def render_kernel(blocks, pieces, *refs):
    tile_ids, cams = refs[0], refs[1]
    parts = refs[2 : 2 + pieces]
    place, inverse, target, rendered, packet = refs[2 + pieces : 7 + pieces]
    feats, rows, e_s, t_s, d_s, hi_s, lo_s, acc_s = refs[7 + pieces :]
    tile_count, listed = place.shape
    pixels = target.shape[1] // tile_count
    side = TILE_SIDE
    view = tile_ids[0] // (TILES_X * TILES_Y)
    cam = [cams[view, i] for i in range(12)]
    slabs = spread_features(parts, feats, parts[0].shape[0])
    projected = project_rows(lambda f: feats[f * slabs : (f + 1) * slabs, :], cam)
    for f, value in enumerate(projected):
        rows[pl.ds(f, slabs, stride=ROWS), :] = value
    zero_row = jnp.zeros((slabs, LANES), F32)
    for f in range(len(projected), ROWS):
        rows[pl.ds(f, slabs, stride=ROWS), :] = zero_row

    lists = []
    for t in range(tile_count):
        halves = []
        for first in range(0, listed, LANES):
            at = jnp.broadcast_to(place[t : t + 1, first : first + LANES], (ROWS, LANES))
            lane, slab = at & (LANES - 1), at >> 7
            found = jnp.zeros((ROWS, LANES), F32)
            for s in range(slabs):
                here = jnp.take_along_axis(
                    rows[s * ROWS : (s + 1) * ROWS, :], lane, axis=1, mode="promise_in_bounds"
                )
                found = jnp.where(slab == s, here, found)
            halves.append(found)
        lists.append(jnp.concatenate(halves, axis=1))

    row_i = lax.broadcasted_iota(jnp.int32, (listed, listed), 0)
    col_i = lax.broadcasted_iota(jnp.int32, (listed, listed), 1)
    earlier = jnp.where(row_i < col_i, 1.0, 0.0).astype(BF16)
    later = jnp.where(row_i > col_i, 1.0, 0.0).astype(BF16)
    step = lax.broadcasted_iota(jnp.int32, (side, listed), 0).astype(F32)

    setup = []
    for t in range(tile_count):
        entry = lists[t]
        within = tile_ids[t] % (TILES_X * TILES_Y)
        x_0 = ((within % TILES_X) * side).astype(F32) + 0.5
        y_0 = ((within // TILES_X) * side).astype(F32) + 0.5
        quad_a, quad_b, quad_c = -0.5 * entry[2:3], -entry[3:4], -0.5 * entry[4:5]
        opacity = entry[5:6]
        dx = (step + x_0) - entry[0:1]
        dy = (step + y_0) - entry[1:2]
        adx2 = quad_a * dx * dx
        bdy = quad_b * dy
        cdy2 = quad_c * dy * dy
        setup.append((entry, quad_a, quad_b, quad_c, opacity, dx, dy, adx2, bdy, cdy2))
        for row in range(side):
            at = slice(row * side, (row + 1) * side)
            power = adx2 + dx * bdy[row : row + 1] + cdy2[row : row + 1]
            bell = jnp.exp(power)
            e_s[t, at, :] = bell
            hi_s[t, at, :], lo_s[t, at, :] = split(jnp.log(1.0 - opacity * bell))

    for t in range(tile_count):
        t_s[t] = matmul(hi_s[t], earlier) + matmul(lo_s[t], earlier)

    errors = []
    for t in range(tile_count):
        entry, opacity = setup[t][0], setup[t][4]
        for row in range(side):
            at = slice(row * side, (row + 1) * side)
            passed = jnp.exp(t_s[t, at, :])
            t_s[t, at, :] = passed
            hi_s[t, at, :], lo_s[t, at, :] = split(opacity * e_s[t, at, :] * passed)
        colours = entry[6:9]
        c_hi, c_lo = split(colours)
        both = (((1,), (1,)))
        image = (
            matmul(c_hi, hi_s[t], both) + matmul(c_lo, hi_s[t], both) + matmul(c_hi, lo_s[t], both)
        )
        here = slice(t * pixels, (t + 1) * pixels)
        rendered[:, here] = image
        error = image - target[:, here]
        g_hi, g_lo = split(error)
        errors.append((g_hi, g_lo))
        first = ((0,), (0,))
        d_s[t] = matmul(g_hi, c_hi, first) + matmul(g_lo, c_hi, first) + matmul(g_hi, c_lo, first)
        g_colours = matmul(g_hi, hi_s[t]) + matmul(g_lo, hi_s[t]) + matmul(g_hi, lo_s[t])
        acc_s[t, 6:9, :] = g_colours

    for t in range(tile_count):
        opacity = setup[t][4]
        for row in range(side):
            at = slice(row * side, (row + 1) * side)
            pushed = t_s[t, at, :] * d_s[t, at, :]
            t_s[t, at, :] = pushed
            hi_s[t, at, :], lo_s[t, at, :] = split(opacity * e_s[t, at, :] * pushed)
        d_s[t] = matmul(hi_s[t], later) + matmul(lo_s[t], later)

    for t in range(tile_count):
        entry, quad_a, quad_b, quad_c, opacity, dx, dy, adx2, bdy, cdy2 = setup[t]
        r_0 = r_1 = r_2 = None
        for row in range(side):
            at = slice(row * side, (row + 1) * side)
            bell = e_s[t, at, :]
            flow = bell * (t_s[t, at, :] - d_s[t, at, :] / (1.0 - opacity * bell))
            one = flow * dy[row : row + 1]
            two = one * dy[row : row + 1]
            r_0 = flow if r_0 is None else r_0 + flow
            r_1 = one if r_1 is None else r_1 + one
            r_2 = two if r_2 is None else r_2 + two
        rdx = r_0 * dx
        m_00 = jnp.sum(r_0, axis=0, keepdims=True)
        m_10 = jnp.sum(rdx, axis=0, keepdims=True)
        m_20 = jnp.sum(rdx * dx, axis=0, keepdims=True)
        m_01 = jnp.sum(r_1, axis=0, keepdims=True)
        m_11 = jnp.sum(r_1 * dx, axis=0, keepdims=True)
        m_02 = jnp.sum(r_2, axis=0, keepdims=True)
        acc_s[t, 0:1, :] = -opacity * (2.0 * quad_a * m_10 + quad_b * m_01)
        acc_s[t, 1:2, :] = -opacity * (2.0 * quad_c * m_01 + quad_b * m_10)
        acc_s[t, 2:3, :] = -0.5 * opacity * m_20
        acc_s[t, 3:4, :] = -opacity * m_11
        acc_s[t, 4:5, :] = -0.5 * opacity * m_02
        acc_s[t, 5:6, :] = m_00
        acc_s[t, 9:16, :] = jnp.zeros((7, listed), F32)

    share = view.astype(F32) * (tile_count / BLOCK_TILES)
    row_of = lax.broadcasted_iota(jnp.int32, (ROWS, LANES), 0)
    chunk = packet.shape[2]
    for s in range(slabs):
        total = jnp.zeros((ROWS, LANES), F32)
        for t in range(tile_count):
            at = jnp.broadcast_to(inverse[t : t + 1, s * LANES : (s + 1) * LANES], (ROWS, LANES))
            lane, half = at & (LANES - 1), at >> 7
            for h in range(listed // LANES):
                here = jnp.take_along_axis(
                    acc_s[t, :, h * LANES : (h + 1) * LANES], lane, axis=1, mode="promise_in_bounds"
                )
                total = total + jnp.where(half == h, here, 0.0)
        mine = jnp.broadcast_to(
            jnp.where(inverse[tile_count : tile_count + 1, s * LANES : (s + 1) * LANES] > 0, share, 0.0),
            (ROWS, LANES),
        )
        total = jnp.where(row_of == 9, mine, total)
        packet[s * LANES // chunk, :, s * LANES % chunk : s * LANES % chunk + LANES] = total


def update_kernel(cams, params, adam_m, adam_v, packet, new_params, new_m, new_v, feats, rows, grads):
    features, width = params.shape
    slabs = spread_features([params], feats, features)
    chunk = packet.shape[2]
    for s in range(slabs):
        rows[pl.ds(s, ROWS, stride=slabs), :] = packet[
            s * LANES // chunk, :, s * LANES % chunk : s * LANES % chunk + LANES
        ]
    pulled = [rows[f * slabs : (f + 1) * slabs, :] for f in range(10)]
    view = pulled[9]
    cam = []
    for i in range(12):
        value = jnp.full((slabs, LANES), cams[0, i], F32)
        for v in range(1, cams.shape[0]):
            value = jnp.where(view == float(v), cams[v, i], value)
        cam.append(value)

    def put(f, value):
        grads[f * slabs : (f + 1) * slabs, :] = value

    project_pull(lambda f: feats[f * slabs : (f + 1) * slabs, :], cam, pulled[:9], put)
    rate = learn_rate / (1.0 - beta_one**adam_steps)
    unbias = 1.0 / (1.0 - beta_two**adam_steps)
    for s in range(slabs):
        for row in range(0, features, 8):
            count = min(8, features - row)
            at = (slice(row, row + count), slice(s * LANES, (s + 1) * LANES))
            grad = grads[pl.ds(row * slabs + s, count, stride=slabs), :]
            moment = beta_one * adam_m[at] + (1.0 - beta_one) * grad
            second = beta_two * adam_v[at] + (1.0 - beta_two) * grad * grad
            new_m[at] = moment
            new_v[at] = second
            new_params[at] = params[at] - rate * moment / (jnp.sqrt(second * unbias) + adam_eps)


def vmem():
    return pl.BlockSpec(memory_space=pltpu.VMEM)


def smem():
    return pl.BlockSpec(memory_space=pltpu.SMEM)


def render(tile_ids, cameras, parts, place, inverse, target, chunks):
    width = sum(part.shape[1] for part in parts)
    features = parts[0].shape[0]
    slabs = width // LANES
    tile_count, listed = place.shape
    pixels = target.shape[1] // tile_count
    square = (tile_count, pixels, listed)
    return pl.pallas_call(
        functools.partial(render_kernel, 1, len(parts)),
        out_shape=(
            jax.ShapeDtypeStruct(target.shape, F32),
            jax.ShapeDtypeStruct((chunks, ROWS, width // chunks), F32),
        ),
        in_specs=[smem(), smem()] + [vmem()] * (len(parts) + 3),
        out_specs=(vmem(), vmem()),
        scratch_shapes=[
            pltpu.VMEM((features * slabs, LANES), F32),
            pltpu.VMEM((ROWS * slabs, LANES), F32),
            pltpu.VMEM(square, F32),
            pltpu.VMEM(square, F32),
            pltpu.VMEM(square, F32),
            pltpu.VMEM(square, BF16),
            pltpu.VMEM(square, BF16),
            pltpu.VMEM((tile_count, ROWS, listed), F32),
        ],
        compiler_params=pltpu.CompilerParams(vmem_limit_bytes=32 * 1024 * 1024),
        name="render",
    )(tile_ids, cameras, *parts, place, inverse, target)


def update(cameras, params, adam_m, adam_v, packet):
    features, width = params.shape
    slabs = width // LANES
    shape = jax.ShapeDtypeStruct(params.shape, F32)
    return pl.pallas_call(
        update_kernel,
        out_shape=(shape, shape, shape),
        in_specs=[smem()] + [vmem()] * 4,
        out_specs=(vmem(), vmem(), vmem()),
        scratch_shapes=[
            pltpu.VMEM((features * slabs, LANES), F32),
            pltpu.VMEM((ROWS * slabs, LANES), F32),
            pltpu.VMEM((features * slabs, LANES), F32),
        ],
        compiler_params=pltpu.CompilerParams(vmem_limit_bytes=32 * 1024 * 1024),
        name="update",
    )(cameras, params, adam_m, adam_v, packet)


def local(params, adam_m, adam_v, cameras, target, tile_ids, hit_shard, hit_local):
    width = params.shape[1]
    tile_count, listed = hit_local.shape
    shards = lax.axis_size("gs")
    along = lax.axis_size("tile")
    chunk = width // shards
    group = lax.axis_index("gs")
    aligned = chunk % LANES == 0

    place = (hit_shard[:, :, 0] ^ group) * chunk + (hit_local - group * chunk)
    column = jnp.arange(width, dtype=jnp.int32)
    order = jnp.arange(listed, dtype=jnp.int32)
    named = place[:, :, None] == column[None, None, :]
    inverse = jnp.max(jnp.where(named, order[None, :, None], -1), axis=1)
    blocks = along * tile_count // BLOCK_TILES
    my_block = lax.axis_index("tile") * tile_count // BLOCK_TILES
    mine = (column % chunk) // (chunk // blocks) == my_block
    inverse = jnp.concatenate([inverse, mine.astype(jnp.int32)[None]], axis=0)

    parts = []
    for d in range(shards):
        piece = lax.dynamic_slice_in_dim(params, (group ^ d) * chunk, chunk, axis=1)
        if d > 0:
            piece = lax.ppermute(piece, "gs", [(k, k ^ d) for k in range(shards)])
        parts.append(piece)
    if not aligned:
        parts = [jnp.concatenate(parts, axis=1)]
    rendered, packet = render(
        tile_ids, cameras, parts, place, inverse, target, shards if aligned else 1
    )
    if not aligned:
        packet = packet.reshape(ROWS, shards, chunk).transpose(1, 0, 2)
    packet = packet[jnp.arange(shards) ^ group]
    packet = lax.all_to_all(packet, "gs", 0, 0)
    packet = lax.psum(packet, "tile")
    if not aligned:
        packet = packet.transpose(1, 0, 2).reshape(1, ROWS, width)
    new_params, new_m, new_v = update(cameras, params, adam_m, adam_v, packet)
    return (rendered, new_params, new_m, new_v)


def solution(mesh):
    return jax.shard_map(
        local,
        mesh=mesh,
        in_specs=(
            P(None, ("groups", "gs")),
            P(None, ("groups", "gs")),
            P(None, ("groups", "gs")),
            P("groups", None),
            P(None, ("groups", "gs", "tile")),
            P(("groups", "gs", "tile")),
            P(("groups", "gs", "tile"), None, None),
            P(("groups", "gs", "tile"), None),
        ),
        out_specs=(
            P(None, ("groups", "gs", "tile")),
            P(None, ("groups", "gs")),
            P(None, ("groups", "gs")),
            P(None, ("groups", "gs")),
        ),
        check_vma=False,
    )
```

time: 334 us -> 70.2 us (0.21); the launches traced: 330 us -> 70 us
  other arithmetic: 142 us -> 0.41 us
  blocking collectives: 51.9 us -> 7.16 us
  between operations: 45.3 us -> 14.2 us
  waiting for transfers between devices: 61.2 us -> 38.2 us
  local copies, waits for them, and re-layouts: 22.4 us -> 2.44 us
  matrix products: 5.3 us -> 0 us
  Pallas kernels: 0 us -> 4.45 us
    add_any x28 -> x0, other arithmetic: 62.5 us -> none  [the longest x4 34.8 us: project(): rotate[row_i][2] * offset[2]]
    all_gather x1 -> x0, blocking collectives: 51.9 us -> none  [local(): whole = lax.all_gather(projected, 'gs', axis=1, tiled=True)]
    div x8 -> x0, other arithmetic: 36.8 us -> none  [the longest x4 36.7 us: project(): conic_c = cov_xx / determinant]
    mul x31 -> x0, other arithmetic: 29.7 us -> none  [the longest x4 12.7 us: sh_basis(): sh_const[9] * unit_z * (sq_x - sq_y)]
    reduce_scatter x1 -> x0, waiting for transfers between devices: 25.7 us -> none  [local(): lax.psum_scatter(partial_rows, 'gs', scatter_dimension=1, tiled=True)]
    all_to_all x0 -> x1, blocking collectives: none -> 7.16 us  [local(): packet = lax.all_to_all(packet, 'gs', 0, 0)]
    slice x6 -> x0, local copies, waits for them, and re-layouts: 6.96 us -> none  [the longest x3 5.94 us: project(): camera[3 * row_i + col_i]]
    scatter-add x1 -> x0, local copies, waits for them, and re-layouts: 6.15 us -> none  [local(): jax.ops.segment_sum(column, whole_ids, shards * span)]
  transfers between devices with their start and end apart: 2 -> 4, of which waited for: 2 -> 3; matrix products, arithmetic and copies ran while one was open for 0% -> 1% of each run, Pallas kernels for 0% -> 0%
where the time goes in v1:
time: 70.2 us; the launch traced here: 70 us
  waiting for transfers between devices  38.2 us (54%)
  between operations  14.2 us (20%)
  blocking collectives  7.16 us (10%)
  Pallas kernels  4.45 us (6%)
  starting transfers between devices  3.16 us (5%)
  local copies, waits for them, and re-layouts  2.44 us (3%)
    psum x1, waiting for transfers between devices, local(): packet = lax.psum(packet, 'tile')  34.7 us
    all_to_all x1, blocking collectives, local(): packet = lax.all_to_all(packet, 'gs', 0, 0)  7.16 us
    ppermute x3, waiting for transfers between devices, local(): piece = lax.ppermute(piece, 'gs', [(k, k ^ d) for k in range(shards)])  3.53 us
    ppermute x3, starting transfers between devices, local(): piece = lax.ppermute(piece, 'gs', [(k, k ^ d) for k in range(shards)])  3.12 us
    pallas_call x1, Pallas kernels, render(): pl.pallas_call(functools.partial(render_kernel, 1, len(parts)), out_shape...  2.71 us
    pallas_call x1, Pallas kernels, update(): pl.pallas_call(update_kernel, out_shape=(shape, shape, shape), in_specs=[...  1.75 us
  transfers between devices with their start and end apart: 4, of which 3 were waited for; matrix products, arithmetic and copies ran while one was open for 1% of the time, Pallas kernels for 0%

profile of v1, /device:TPU:0, one launch (start us, length us, event | category | flops | bytes accessed | tf_op | source)
XLA Modules:
  0.0 70.0 jit_solution(2130010119821694278)
XLA Ops:
  7.2 0.0 all-reduce.2.cloned.1.call-start
  7.2 0.0 copy-start.7
  7.2 0.0 copy-start.8
  7.3 0.0 copy-start.4
  7.3 0.0 copy-start.5
  7.3 0.0 copy-start.6
  7.3 0.0 copy-start.2
  7.3 1.0 %constant_dynamic-slice_fusion = (f32[59,256]{1,0:T(8,128)S(1)}, f32[59,256]{1,0:T(8,128)S(1)}, f32[59,256]{1,0:T(8,128)S(1)}, f32[59,256]{1,0:T(8,128)S(1)}) fusion(f32[59,1024]{1,0:T(8,128)} %params.1, s32[]{:T(128)S(6)} %select_n.59, s32[]{:T(128)S(6)} %select_n.58, s32[]{:T(128)S(6)} %select_n.57, s32[]{:T(128)S(6)} %select_n.56), kind=kLoop, calls=%fused_computation.15 | loop fusion | bytes 483344 | tf_op jit(solution)/shard_map/dynamic_slice | solution.py:509
  8.3 2.4 %collective-permute-start.2 = (f32[59,256]{1,0:T(8,128)S(1)}, f32[59,256]{1,0:T(8,128)S(1)}, u32[]{:S(2)}, u32[]{:S(2)}) collective-permute-start(f32[59,256]{1,0:T(8,128)S(1)} %get-tuple-element.14), channel_id=1, source_target_pairs={{0,12},{4,8},{8,4},{12,0},{1,13},{5,9},{9,5},{13,1},{2,14},{6,10},... | collective-permute-start | bytes 181256 | tf_op jit(solution)/shard_map/ppermute | solution.py:511
  10.8 0.6 collective-permute-start.1
  11.4 0.0 collective-permute-start
  11.5 0.0 copy-done.7
  11.5 0.0 copy-done.8
  11.5 0.4 select_reduce_fusion
  11.9 1.3 %collective-permute-done.2.refs_5_ = f32[59,256]{1,0:T(8,128)S(1)} collective-permute-done((f32[59,256]{1,0:T(8,128)S(1)}, f32[59,256]{1,0:T(8,128)S(1)}, u32[]{:S(2)}, u32[]{:S(2)}) %collective-permute-start.2) | collective-permute-done | bytes 60448 | tf_op jit(solution)/shard_map/ppermute | solution.py:511
  13.2 2.2 %collective-permute-done.1.refs_4_ = f32[59,256]{1,0:T(8,128)S(1)} collective-permute-done((f32[59,256]{1,0:T(8,128)S(1)}, f32[59,256]{1,0:T(8,128)S(1)}, u32[]{:S(2)}, u32[]{:S(2)}) %collective-permute-start.1) | collective-permute-done | bytes 60448 | tf_op jit(solution)/shard_map/ppermute | solution.py:511
  15.4 0.0 collective-permute-done.refs_3_
  15.4 0.0 copy-done.4
  15.4 0.0 copy-done.5
  15.4 0.0 copy-done.6
  15.4 0.0 copy-start
  15.5 0.0 copy-start.1
  15.5 2.7 %render.1 = (f32[3,512]{1,0:T(4,128)}, f32[4,16,256]{2,1,0:T(8,128)S(1)}) custom-call(s32[2]{0:T(128)S(1)} %copy-done.6, f32[4,12]{1,0:T(4,128)S(1)} %copy-done.4, f32[59,256]{1,0:T(8,128)S(1)} %get-tuple-element.17.refs_2_, f32[59,256]{1,0:T(8,128)S(1)} %collective-permute-done.refs_3_, f32[59,256]{1,0:T(8,128)S(1)} %collective-permute-done.1.refs_4_, ...), custom_call_target="tpu_custom_call" | custom-call | tf_op jit(solution)/shard_map/render/pallas_call | solution.py:446
  18.2 0.6 gather_fusion
  18.7 7.2 %all_to_all.5 = f32[4,16,256]{2,1,0:T(8,128)} all-to-all(f32[4,16,256]{2,1,0:T(8,128)S(1)} %gather_fusion), channel_id=1, replica_groups=mesh['groups'=2,'gs'=4,'tile'=4] {'gs'}, dimensions={0} | all-to-all | bytes 131072 | tf_op jit(solution)/shard_map/all_to_all | solution.py:521
  25.9 0.0 all-reduce.2.cloned.1.call-update
  25.9 34.7 %all-reduce.2.cloned.1.call-done.packet = f32[4,16,256]{2,1,0:T(8,128)} async-done(((f32[4,16,256]{2,1,0:T(8,128)}), f32[4,16,256]{2,1,0:T(8,128)}) %all-reduce.2.cloned.1.call-update) | async-done | bytes 65552 | tf_op jit(solution)/shard_map/psum | solution.py:522
  60.6 0.0 copy-done.2
  60.6 0.0 copy-done
  60.6 0.0 copy-done.1
  60.6 0.0 copy-start.3
  60.6 0.8 %copy-done.3 = f32[4,16,256]{2,1,0:T(8,128)S(1)} copy-done((f32[4,16,256]{2,1,0:T(8,128)S(1)}, f32[4,16,256]{2,1,0:T(8,128)}, u32[]{:S(2)}) %copy-start.3) | copy-done | bytes 65560
  61.4 1.7 %update.1 = (f32[59,1024]{1,0:T(8,128)}, f32[59,1024]{1,0:T(8,128)}, f32[59,1024]{1,0:T(8,128)}) custom-call(f32[4,12]{1,0:T(4,128)S(1)} %copy-done.4, f32[59,1024]{1,0:T(8,128)S(1)} %copy-done, f32[59,1024]{1,0:T(8,128)S(1)} %copy-done.1, f32[59,1024]{1,0:T(8,128)S(1)} %copy-done.2, f32[4,16,256]{2,1,0:T(8,128)S(1)} %copy-done.3), custom_call_target="tpu_custom_call" | custom-call | tf_op jit(solution)/shard_map/update/pallas_call | solution.py:473
  (5 shorter events, 0.0 us)
Async XLA Ops:
  7.2 53.4 %all-reduce.2.cloned.1.call-start = ((), (), s32[]{:S(2)}) async-start(), calls=%async_computation.1 | async-start | bytes 131072 | tf_op jit(solution)/shard_map/psum | solution.py:522
  7.2 4.2 %copy-start.7 = (s32[2,256,1]{1,2,0:T(1,128)S(1)}, s32[2,256,1]{1,2,0:T(1,128)}, u32[]{:S(2)}) copy-start(s32[2,256,1]{1,2,0:T(1,128)} %param.14) | copy-start | bytes 6148
  7.2 4.2 %copy-start.8 = (s32[2,256]{1,0:T(2,128)S(1)}, s32[2,256]{1,0:T(2,128)}, u32[]{:S(2)}) copy-start(s32[2,256]{1,0:T(2,128)} %param.15) | copy-start | bytes 6148
  7.3 8.2 %copy-start.4 = (f32[4,12]{1,0:T(4,128)S(1)}, f32[4,12]{1,0:T(4,128)}, u32[]{:S(2)}) copy-start(f32[4,12]{1,0:T(4,128)} %cams.1) | copy-start | bytes 580
  7.3 8.2 %copy-start.5 = (f32[3,512]{1,0:T(4,128)S(1)}, f32[3,512]{1,0:T(4,128)}, u32[]{:S(2)}) copy-start(f32[3,512]{1,0:T(4,128)} %refs_8_.1) | copy-start | bytes 18436
  7.3 8.2 %copy-start.6 = (s32[2]{0:T(128)S(1)}, s32[2]{0:T(128)}, u32[]{:S(2)}) copy-start(s32[2]{0:T(128)} %refs_0_.1) | copy-start | bytes 28
  7.3 53.3 %copy-start.2 = (f32[59,1024]{1,0:T(8,128)S(1)}, f32[59,1024]{1,0:T(8,128)}, u32[]{:S(2)}) copy-start(f32[59,1024]{1,0:T(8,128)} %adam_v.1) | copy-start | bytes 724996
  8.3 4.9 %collective-permute-start.2 = (f32[59,256]{1,0:T(8,128)S(1)}, f32[59,256]{1,0:T(8,128)S(1)}, u32[]{:S(2)}, u32[]{:S(2)}) collective-permute-start(f32[59,256]{1,0:T(8,128)S(1)} %get-tuple-element.14), channel_id=1, source_target_pairs={{0,12},{4,8},{8,4},{12,0},{1,13},{5,9},{9,5},{13,1},{2,14},{6,10},... | collective-permute-start | bytes 181256 | tf_op jit(solution)/shard_map/ppermute | solution.py:511
  10.8 4.7 %collective-permute-start.1 = (f32[59,256]{1,0:T(8,128)S(1)}, f32[59,256]{1,0:T(8,128)S(1)}, u32[]{:S(2)}, u32[]{:S(2)}) collective-permute-start(f32[59,256]{1,0:T(8,128)S(1)} %get-tuple-element.15), channel_id=1, source_target_pairs={{0,8},{4,12},{8,0},{12,4},{1,9},{5,13},{9,1},{13,5},{2,10},{6,14},... | collective-permute-start | bytes 181256 | tf_op jit(solution)/shard_map/ppermute | solution.py:511
  11.4 4.0 %collective-permute-start = (f32[59,256]{1,0:T(8,128)S(1)}, f32[59,256]{1,0:T(8,128)S(1)}, u32[]{:S(2)}, u32[]{:S(2)}) collective-permute-start(f32[59,256]{1,0:T(8,128)S(1)} %get-tuple-element.16), channel_id=1, source_target_pairs={{0,4},{4,0},{8,12},{12,8},{1,5},{5,1},{9,13},{13,9},{2,6},{6,2},{1... | collective-permute-start | bytes 181256 | tf_op jit(solution)/shard_map/ppermute | solution.py:511
  15.4 45.1 %copy-start = (f32[59,1024]{1,0:T(8,128)S(1)}, f32[59,1024]{1,0:T(8,128)}, u32[]{:S(2)}) copy-start(f32[59,1024]{1,0:T(8,128)} %params.1) | copy-start | bytes 724996
  15.5 45.1 %copy-start.1 = (f32[59,1024]{1,0:T(8,128)S(1)}, f32[59,1024]{1,0:T(8,128)}, u32[]{:S(2)}) copy-start(f32[59,1024]{1,0:T(8,128)} %adam_m.1) | copy-start | bytes 724996
  60.6 0.8 %copy-start.3 = (f32[4,16,256]{2,1,0:T(8,128)S(1)}, f32[4,16,256]{2,1,0:T(8,128)}, u32[]{:S(2)}) copy-start(f32[4,16,256]{2,1,0:T(8,128)} %all-reduce.2.cloned.1.call-done.packet) | copy-start | bytes 196612
Sparse Core Ops, SparseCore 0:
  26.1 34.4 all-reduce.1

commit v2 on v1

--- a/solution.py
+++ b/solution.py
@@ -249,13 +249,16 @@
     return tiles
 
 
-def render_kernel(blocks, pieces, *refs):
-    tile_ids, cams = refs[0], refs[1]
-    parts = refs[2 : 2 + pieces]
-    place, inverse, target, rendered, packet = refs[2 + pieces : 7 + pieces]
-    feats, rows, e_s, t_s, d_s, hi_s, lo_s, acc_s = refs[7 + pieces :]
-    tile_count, listed = place.shape
-    pixels = target.shape[1] // tile_count
+def render_kernel(pieces, groups, blocks, *refs):
+    tile_ids, cams, where = refs[:3]
+    parts = refs[3 : 3 + pieces]
+    infos = refs[3 + pieces : 3 + pieces + groups]
+    inverse, rendered = refs[3 + pieces + groups : 5 + pieces + groups]
+    rest = refs[5 + pieces + groups :]
+    packets = rest[: len(rest) - 9]
+    feats, rows, e_s, t_s, d_s, hi_s, lo_s, acc_s, info_s = rest[len(rest) - 9 :]
+    tile_count, listed = e_s.shape[0], e_s.shape[2]
+    pixels = e_s.shape[1]
     side = TILE_SIDE
     view = tile_ids[0] // (TILES_X * TILES_Y)
     cam = [cams[view, i] for i in range(12)]
@@ -266,141 +269,171 @@
     zero_row = jnp.zeros((slabs, LANES), F32)
     for f in range(len(projected), ROWS):
         rows[pl.ds(f, slabs, stride=ROWS), :] = zero_row
-
-    lists = []
-    for t in range(tile_count):
-        halves = []
-        for first in range(0, listed, LANES):
-            at = jnp.broadcast_to(place[t : t + 1, first : first + LANES], (ROWS, LANES))
-            lane, slab = at & (LANES - 1), at >> 7
-            found = jnp.zeros((ROWS, LANES), F32)
-            for s in range(slabs):
-                here = jnp.take_along_axis(
-                    rows[s * ROWS : (s + 1) * ROWS, :], lane, axis=1, mode="promise_in_bounds"
-                )
-                found = jnp.where(slab == s, here, found)
-            halves.append(found)
-        lists.append(jnp.concatenate(halves, axis=1))
+    for g in range(groups):
+        info_s[g] = infos[g][...]
 
     row_i = lax.broadcasted_iota(jnp.int32, (listed, listed), 0)
     col_i = lax.broadcasted_iota(jnp.int32, (listed, listed), 1)
     earlier = jnp.where(row_i < col_i, 1.0, 0.0).astype(BF16)
     later = jnp.where(row_i > col_i, 1.0, 0.0).astype(BF16)
     step = lax.broadcasted_iota(jnp.int32, (side, listed), 0).astype(F32)
-
-    setup = []
-    for t in range(tile_count):
-        entry = lists[t]
-        within = tile_ids[t] % (TILES_X * TILES_Y)
-        x_0 = ((within % TILES_X) * side).astype(F32) + 0.5
-        y_0 = ((within // TILES_X) * side).astype(F32) + 0.5
-        quad_a, quad_b, quad_c = -0.5 * entry[2:3], -entry[3:4], -0.5 * entry[4:5]
-        opacity = entry[5:6]
-        dx = (step + x_0) - entry[0:1]
-        dy = (step + y_0) - entry[1:2]
-        adx2 = quad_a * dx * dx
-        bdy = quad_b * dy
-        cdy2 = quad_c * dy * dy
-        setup.append((entry, quad_a, quad_b, quad_c, opacity, dx, dy, adx2, bdy, cdy2))
-        for row in range(side):
-            at = slice(row * side, (row + 1) * side)
-            power = adx2 + dx * bdy[row : row + 1] + cdy2[row : row + 1]
-            bell = jnp.exp(power)
-            e_s[t, at, :] = bell
-            hi_s[t, at, :], lo_s[t, at, :] = split(jnp.log(1.0 - opacity * bell))
-
-    for t in range(tile_count):
-        t_s[t] = matmul(hi_s[t], earlier) + matmul(lo_s[t], earlier)
-
-    errors = []
-    for t in range(tile_count):
-        entry, opacity = setup[t][0], setup[t][4]
-        for row in range(side):
-            at = slice(row * side, (row + 1) * side)
-            passed = jnp.exp(t_s[t, at, :])
-            t_s[t, at, :] = passed
-            hi_s[t, at, :], lo_s[t, at, :] = split(opacity * e_s[t, at, :] * passed)
-        colours = entry[6:9]
-        c_hi, c_lo = split(colours)
-        both = (((1,), (1,)))
-        image = (
-            matmul(c_hi, hi_s[t], both) + matmul(c_lo, hi_s[t], both) + matmul(c_hi, lo_s[t], both)
-        )
-        here = slice(t * pixels, (t + 1) * pixels)
-        rendered[:, here] = image
-        error = image - target[:, here]
-        g_hi, g_lo = split(error)
-        errors.append((g_hi, g_lo))
-        first = ((0,), (0,))
-        d_s[t] = matmul(g_hi, c_hi, first) + matmul(g_lo, c_hi, first) + matmul(g_hi, c_lo, first)
-        g_colours = matmul(g_hi, hi_s[t]) + matmul(g_lo, hi_s[t]) + matmul(g_hi, lo_s[t])
-        acc_s[t, 6:9, :] = g_colours
-
-    for t in range(tile_count):
-        opacity = setup[t][4]
-        for row in range(side):
-            at = slice(row * side, (row + 1) * side)
-            pushed = t_s[t, at, :] * d_s[t, at, :]
-            t_s[t, at, :] = pushed
-            hi_s[t, at, :], lo_s[t, at, :] = split(opacity * e_s[t, at, :] * pushed)
-        d_s[t] = matmul(hi_s[t], later) + matmul(lo_s[t], later)
-
-    for t in range(tile_count):
-        entry, quad_a, quad_b, quad_c, opacity, dx, dy, adx2, bdy, cdy2 = setup[t]
-        r_0 = r_1 = r_2 = None
-        for row in range(side):
-            at = slice(row * side, (row + 1) * side)
-            bell = e_s[t, at, :]
-            flow = bell * (t_s[t, at, :] - d_s[t, at, :] / (1.0 - opacity * bell))
-            one = flow * dy[row : row + 1]
-            two = one * dy[row : row + 1]
-            r_0 = flow if r_0 is None else r_0 + flow
-            r_1 = one if r_1 is None else r_1 + one
-            r_2 = two if r_2 is None else r_2 + two
-        rdx = r_0 * dx
-        m_00 = jnp.sum(r_0, axis=0, keepdims=True)
-        m_10 = jnp.sum(rdx, axis=0, keepdims=True)
-        m_20 = jnp.sum(rdx * dx, axis=0, keepdims=True)
-        m_01 = jnp.sum(r_1, axis=0, keepdims=True)
-        m_11 = jnp.sum(r_1 * dx, axis=0, keepdims=True)
-        m_02 = jnp.sum(r_2, axis=0, keepdims=True)
-        acc_s[t, 0:1, :] = -opacity * (2.0 * quad_a * m_10 + quad_b * m_01)
-        acc_s[t, 1:2, :] = -opacity * (2.0 * quad_c * m_01 + quad_b * m_10)
-        acc_s[t, 2:3, :] = -0.5 * opacity * m_20
-        acc_s[t, 3:4, :] = -opacity * m_11
-        acc_s[t, 4:5, :] = -0.5 * opacity * m_02
-        acc_s[t, 5:6, :] = m_00
-        acc_s[t, 9:16, :] = jnp.zeros((7, listed), F32)
-
-    share = view.astype(F32) * (tile_count / BLOCK_TILES)
+    within = tile_ids[0] % (TILES_X * TILES_Y)
+    first_row = (within // TILES_X) // 2 * 2
+    first_col = (within % TILES_X) // 4 * 4
+    me = where[0]
+
+    def one_group(g, carry):
+        lists = []
+        for t in range(tile_count):
+            halves = []
+            for first in range(t * listed, (t + 1) * listed, LANES):
+                at = info_s[g, 3:4, first : first + LANES].astype(jnp.int32)
+                at = jnp.broadcast_to(at, (ROWS, LANES))
+                lane, slab = at & (LANES - 1), at >> 7
+                found = jnp.zeros((ROWS, LANES), F32)
+                for s in range(slabs):
+                    here = jnp.take_along_axis(
+                        rows[s * ROWS : (s + 1) * ROWS, :], lane, axis=1, mode="promise_in_bounds"
+                    )
+                    found = jnp.where(slab == s, here, found)
+                halves.append(found)
+            lists.append(jnp.concatenate(halves, axis=1))
+
+        setup = []
+        for t in range(tile_count):
+            entry = lists[t]
+            slot = (me ^ g) * tile_count + t
+            x_0 = ((first_col + slot % 4) * side).astype(F32) + 0.5
+            y_0 = ((first_row + slot // 4) * side).astype(F32) + 0.5
+            quad_a, quad_b, quad_c = -0.5 * entry[2:3], -entry[3:4], -0.5 * entry[4:5]
+            opacity = entry[5:6]
+            dx = (step + x_0) - entry[0:1]
+            dy = (step + y_0) - entry[1:2]
+            adx2 = quad_a * dx * dx
+            bdy = quad_b * dy
+            cdy2 = quad_c * dy * dy
+            setup.append((entry, quad_a, quad_b, quad_c, opacity, dx, dy))
+            for row in range(side):
+                at = slice(row * side, (row + 1) * side)
+                power = adx2 + dx * bdy[row : row + 1] + cdy2[row : row + 1]
+                bell = jnp.exp(power)
+                e_s[t, at, :] = bell
+                hi_s[t, at, :], lo_s[t, at, :] = split(jnp.log(1.0 - opacity * bell))
+
+        for t in range(tile_count):
+            t_s[t] = matmul(hi_s[t], earlier) + matmul(lo_s[t], earlier)
+
+        for t in range(tile_count):
+            entry, opacity = setup[t][0], setup[t][4]
+            for row in range(side):
+                at = slice(row * side, (row + 1) * side)
+                passed = jnp.exp(t_s[t, at, :])
+                t_s[t, at, :] = passed
+                hi_s[t, at, :], lo_s[t, at, :] = split(opacity * e_s[t, at, :] * passed)
+            c_hi, c_lo = split(entry[6:9])
+            both = ((1,), (1,))
+            image = (
+                matmul(c_hi, hi_s[t], both)
+                + matmul(c_lo, hi_s[t], both)
+                + matmul(c_hi, lo_s[t], both)
+            )
+            here = slice(t * pixels, (t + 1) * pixels)
+
+            @pl.when(g == 0)
+            def _():
+                rendered[:, here] = image
+
+            error = image - info_s[g, 0:3, here]
+            g_hi, g_lo = split(error)
+            first = ((0,), (0,))
+            d_s[t] = (
+                matmul(g_hi, c_hi, first) + matmul(g_lo, c_hi, first) + matmul(g_hi, c_lo, first)
+            )
+            g_colours = matmul(g_hi, hi_s[t]) + matmul(g_lo, hi_s[t]) + matmul(g_hi, lo_s[t])
+            acc_s[g, t, 6:9, :] = g_colours
+
+        for t in range(tile_count):
+            opacity = setup[t][4]
+            for row in range(side):
+                at = slice(row * side, (row + 1) * side)
+                pushed = t_s[t, at, :] * d_s[t, at, :]
+                t_s[t, at, :] = pushed
+                hi_s[t, at, :], lo_s[t, at, :] = split(opacity * e_s[t, at, :] * pushed)
+            d_s[t] = matmul(hi_s[t], later) + matmul(lo_s[t], later)
+
+        for t in range(tile_count):
+            entry, quad_a, quad_b, quad_c, opacity, dx, dy = setup[t]
+            r_0 = r_1 = r_2 = None
+            for row in range(side):
+                at = slice(row * side, (row + 1) * side)
+                bell = e_s[t, at, :]
+                flow = bell * (t_s[t, at, :] - d_s[t, at, :] / (1.0 - opacity * bell))
+                one = flow * dy[row : row + 1]
+                two = one * dy[row : row + 1]
+                r_0 = flow if r_0 is None else r_0 + flow
+                r_1 = one if r_1 is None else r_1 + one
+                r_2 = two if r_2 is None else r_2 + two
+            rdx = r_0 * dx
+            m_00 = jnp.sum(r_0, axis=0, keepdims=True)
+            m_10 = jnp.sum(rdx, axis=0, keepdims=True)
+            m_20 = jnp.sum(rdx * dx, axis=0, keepdims=True)
+            m_01 = jnp.sum(r_1, axis=0, keepdims=True)
+            m_11 = jnp.sum(r_1 * dx, axis=0, keepdims=True)
+            m_02 = jnp.sum(r_2, axis=0, keepdims=True)
+            acc_s[g, t, 0:1, :] = -opacity * (2.0 * quad_a * m_10 + quad_b * m_01)
+            acc_s[g, t, 1:2, :] = -opacity * (2.0 * quad_c * m_01 + quad_b * m_10)
+            acc_s[g, t, 2:3, :] = -0.5 * opacity * m_20
+            acc_s[g, t, 3:4, :] = -opacity * m_11
+            acc_s[g, t, 4:5, :] = -0.5 * opacity * m_02
+            acc_s[g, t, 5:6, :] = m_00
+            acc_s[g, t, 9:16, :] = jnp.zeros((7, listed), F32)
+        return carry
+
+    lax.fori_loop(0, groups, one_group, 0)
+
+    share = view.astype(F32)
     row_of = lax.broadcasted_iota(jnp.int32, (ROWS, LANES), 0)
-    chunk = packet.shape[2]
+    lane_of = lax.broadcasted_iota(jnp.int32, (ROWS, LANES), 1)
+    chunk = packets[0].shape[1]
     for s in range(slabs):
-        total = jnp.zeros((ROWS, LANES), F32)
-        for t in range(tile_count):
-            at = jnp.broadcast_to(inverse[t : t + 1, s * LANES : (s + 1) * LANES], (ROWS, LANES))
-            lane, half = at & (LANES - 1), at >> 7
-            for h in range(listed // LANES):
-                here = jnp.take_along_axis(
-                    acc_s[t, :, h * LANES : (h + 1) * LANES], lane, axis=1, mode="promise_in_bounds"
-                )
-                total = total + jnp.where(half == h, here, 0.0)
-        mine = jnp.broadcast_to(
-            jnp.where(inverse[tile_count : tile_count + 1, s * LANES : (s + 1) * LANES] > 0, share, 0.0),
-            (ROWS, LANES),
-        )
+        totals = []
+        for g in range(groups):
+            total = jnp.zeros((ROWS, LANES), F32)
+            for t in range(tile_count):
+                at = inverse[g * tile_count + t : g * tile_count + t + 1, s * LANES : (s + 1) * LANES]
+                at = jnp.broadcast_to(at, (ROWS, LANES))
+                lane, half = at & (LANES - 1), at >> 7
+                for h in range(listed // LANES):
+                    here = jnp.take_along_axis(
+                        acc_s[g, t, :, h * LANES : (h + 1) * LANES],
+                        lane,
+                        axis=1,
+                        mode="promise_in_bounds",
+                    )
+                    total = total + jnp.where(half == h, here, 0.0)
+            totals.append(total)
+        while len(totals) > 1:
+            totals = [totals[k] + totals[k + 1] for k in range(0, len(totals), 2)]
+        total = totals[0]
+        if blocks == 1:
+            mine = share
+        else:
+            column = s * LANES + lane_of
+            mine = jnp.where(column % where[2] // (where[2] // blocks) == where[1], share, 0.0)
         total = jnp.where(row_of == 9, mine, total)
-        packet[s * LANES // chunk, :, s * LANES % chunk : s * LANES % chunk + LANES] = total
-
-
-def update_kernel(cams, params, adam_m, adam_v, packet, new_params, new_m, new_v, feats, rows, grads):
+        packets[s * LANES // chunk][:, s * LANES % chunk : s * LANES % chunk + LANES] = total
+
+
+def update_kernel(pieces, where, cams, params, adam_m, adam_v, *refs):
+    packets = refs[:pieces]
+    new_params, new_m, new_v, feats, rows, grads = refs[pieces:]
     features, width = params.shape
     slabs = spread_features([params], feats, features)
-    chunk = packet.shape[2]
-    for s in range(slabs):
-        rows[pl.ds(s, ROWS, stride=slabs), :] = packet[
-            s * LANES // chunk, :, s * LANES % chunk : s * LANES % chunk + LANES
-        ]
+    chunk = packets[0].shape[1]
+    for d in range(pieces):
+        for h in range(chunk // LANES):
+            slab = (where[0] ^ d) * (chunk // LANES) + h
+            rows[pl.ds(slab, ROWS, stride=slabs), :] = packets[d][:, h * LANES : (h + 1) * LANES]
     pulled = [rows[f * slabs : (f + 1) * slabs, :] for f in range(10)]
     view = pulled[9]
     cam = []
@@ -436,21 +469,19 @@
     return pl.BlockSpec(memory_space=pltpu.SMEM)
 
 
-def render(tile_ids, cameras, parts, place, inverse, target, chunks):
+def render(tile_ids, cameras, where, parts, infos, inverse, tile_count, blocks):
     width = sum(part.shape[1] for part in parts)
     features = parts[0].shape[0]
     slabs = width // LANES
-    tile_count, listed = place.shape
-    pixels = target.shape[1] // tile_count
+    pixels = listed = infos[0].shape[1] // tile_count
     square = (tile_count, pixels, listed)
-    return pl.pallas_call(
-        functools.partial(render_kernel, 1, len(parts)),
-        out_shape=(
-            jax.ShapeDtypeStruct(target.shape, F32),
-            jax.ShapeDtypeStruct((chunks, ROWS, width // chunks), F32),
-        ),
-        in_specs=[smem(), smem()] + [vmem()] * (len(parts) + 3),
-        out_specs=(vmem(), vmem()),
+    groups = len(infos)
+    packet = jax.ShapeDtypeStruct((ROWS, parts[0].shape[1]), F32)
+    out = pl.pallas_call(
+        functools.partial(render_kernel, len(parts), groups, blocks),
+        out_shape=(jax.ShapeDtypeStruct((3, tile_count * pixels), F32),) + (packet,) * len(parts),
+        in_specs=[smem()] * 3 + [vmem()] * (len(parts) + groups + 1),
+        out_specs=(vmem(),) * (1 + len(parts)),
         scratch_shapes=[
             pltpu.VMEM((features * slabs, LANES), F32),
             pltpu.VMEM((ROWS * slabs, LANES), F32),
@@ -459,21 +490,23 @@
             pltpu.VMEM(square, F32),
             pltpu.VMEM(square, BF16),
             pltpu.VMEM(square, BF16),
-            pltpu.VMEM((tile_count, ROWS, listed), F32),
+            pltpu.VMEM((groups, tile_count, ROWS, listed), F32),
+            pltpu.VMEM((groups,) + infos[0].shape, F32),
         ],
         compiler_params=pltpu.CompilerParams(vmem_limit_bytes=32 * 1024 * 1024),
         name="render",
-    )(tile_ids, cameras, *parts, place, inverse, target)
-
-
-def update(cameras, params, adam_m, adam_v, packet):
+    )(tile_ids, cameras, where, *parts, *infos, inverse)
+    return out[0], list(out[1:])
+
+
+def update(where, cameras, params, adam_m, adam_v, packets):
     features, width = params.shape
     slabs = width // LANES
     shape = jax.ShapeDtypeStruct(params.shape, F32)
     return pl.pallas_call(
-        update_kernel,
+        functools.partial(update_kernel, len(packets)),
         out_shape=(shape, shape, shape),
-        in_specs=[smem()] + [vmem()] * 4,
+        in_specs=[smem()] * 2 + [vmem()] * (3 + len(packets)),
         out_specs=(vmem(), vmem(), vmem()),
         scratch_shapes=[
             pltpu.VMEM((features * slabs, LANES), F32),
@@ -482,7 +515,13 @@
         ],
         compiler_params=pltpu.CompilerParams(vmem_limit_bytes=32 * 1024 * 1024),
         name="update",
-    )(cameras, params, adam_m, adam_v, packet)
+    )(where, cameras, params, adam_m, adam_v, *packets)
+
+
+def swap(value, axis, d):
+    if d == 0:
+        return value
+    return lax.ppermute(value, axis, [(k, k ^ d) for k in range(lax.axis_size(axis))])
 
 
 def local(params, adam_m, adam_v, cameras, target, tile_ids, hit_shard, hit_local):
@@ -492,38 +531,52 @@
     along = lax.axis_size("tile")
     chunk = width // shards
     group = lax.axis_index("gs")
+    seat = lax.axis_index("tile")
     aligned = chunk % LANES == 0
+    team = BLOCK_TILES // tile_count
+    blocks = along // team
 
     place = (hit_shard[:, :, 0] ^ group) * chunk + (hit_local - group * chunk)
-    column = jnp.arange(width, dtype=jnp.int32)
+    info = jnp.concatenate([target, place.reshape(1, -1).astype(F32)], axis=0)
+    infos = [swap(info, "tile", d) for d in range(team)]
+    parts = [
+        swap(lax.dynamic_slice_in_dim(params, (group ^ d) * chunk, chunk, axis=1), "gs", d)
+        for d in range(shards)
+    ]
+    column = jnp.arange(width, dtype=jnp.int32).astype(F32)
     order = jnp.arange(listed, dtype=jnp.int32)
-    named = place[:, :, None] == column[None, None, :]
+    places = jnp.concatenate([each[3].reshape(tile_count, listed) for each in infos], axis=0)
+    named = places[:, :, None] == column[None, None, :]
     inverse = jnp.max(jnp.where(named, order[None, :, None], -1), axis=1)
-    blocks = along * tile_count // BLOCK_TILES
-    my_block = lax.axis_index("tile") * tile_count // BLOCK_TILES
-    mine = (column % chunk) // (chunk // blocks) == my_block
-    inverse = jnp.concatenate([inverse, mine.astype(jnp.int32)[None]], axis=0)
-
-    parts = []
-    for d in range(shards):
-        piece = lax.dynamic_slice_in_dim(params, (group ^ d) * chunk, chunk, axis=1)
-        if d > 0:
-            piece = lax.ppermute(piece, "gs", [(k, k ^ d) for k in range(shards)])
-        parts.append(piece)
+
     if not aligned:
         parts = [jnp.concatenate(parts, axis=1)]
-    rendered, packet = render(
-        tile_ids, cameras, parts, place, inverse, target, shards if aligned else 1
+    where = jnp.stack([seat % team, seat // team, jnp.int32(chunk)]).astype(jnp.int32)
+    rendered, packets = render(
+        tile_ids, cameras, where, parts, infos, inverse, tile_count, blocks
     )
     if not aligned:
-        packet = packet.reshape(ROWS, shards, chunk).transpose(1, 0, 2)
-    packet = packet[jnp.arange(shards) ^ group]
-    packet = lax.all_to_all(packet, "gs", 0, 0)
-    packet = lax.psum(packet, "tile")
-    if not aligned:
-        packet = packet.transpose(1, 0, 2).reshape(1, ROWS, width)
-    new_params, new_m, new_v = update(cameras, params, adam_m, adam_v, packet)
+        packets = [packets[0][:, d * chunk : (d + 1) * chunk] for d in range(shards)]
+    packets = [swap(packets[d], "gs", d) for d in range(shards)]
+    if blocks > 1:
+        packets = [block_sum(packet, along, team) for packet in packets]
+    if aligned:
+        own = group
+    else:
+        packets = [jnp.stack(packets)[jnp.arange(shards) ^ group].transpose(1, 0, 2).reshape(ROWS, -1)]
+        own = jnp.int32(0)
+    new_params, new_m, new_v = update(
+        own.reshape(1), cameras, params, adam_m, adam_v, packets
+    )
     return (rendered, new_params, new_m, new_v)
+
+
+def block_sum(packet, along, team):
+    step = team
+    while step < along:
+        packet = packet + swap(packet, "tile", step)
+        step *= 2
+    return packet
 
 
 def solution(mesh):

time: 70.2 us -> 30.2 us (0.43)
  waiting for transfers between devices: 38.2 us -> 3.7 us
  between operations: 14.2 us -> 0.7 us
  blocking collectives: 7.16 us -> 0 us
  Pallas kernels: 4.45 us -> 10.9 us
  starting transfers between devices: 3.16 us -> 9.57 us
  other arithmetic: 0.41 us -> 3.97 us
  local copies, waits for them, and re-layouts: 2.44 us -> 1.15 us
    psum x1 -> x0, waiting for transfers between devices: 34.7 us -> none  [local(): packet = lax.psum(packet, 'tile')]
    all_to_all x1 -> x0, blocking collectives: 7.16 us -> none  [local(): packet = lax.all_to_all(packet, 'gs', 0, 0)]
    ppermute x3 -> x9, starting transfers between devices: 3.12 us -> 9.57 us  [swap(): lax.ppermute(value, axis, [(k, k ^ d) for k in range(lax.axis_size(axis))])]
    pallas_call x2, Pallas kernels: 4.45 us -> 10.9 us  [the longest x1 9.1 us: render(): pl.pallas_call(functools.partial(render_kernel, len(parts), groups, block...]
    reduce_max x1, other arithmetic: 0.37 us -> 2.47 us  [local(): inverse = jnp.max(jnp.where(named, order[None, :, None], -1), axis=1)]
    unnamed x18 -> x11, local copies, waits for them, and re-layouts: 0.88 us -> 0.03 us
    concatenate x1 -> x2, other arithmetic: 0.01 us -> 0.72 us  [the longest x1 0.71 us: local(): info = jnp.concatenate([target, place.reshape(1, -1).astype(F32)], axis=0)]
    ppermute x3 -> x9, waiting for transfers between devices: 3.53 us -> 3.7 us  [swap(): lax.ppermute(value, axis, [(k, k ^ d) for k in range(lax.axis_size(axis))])]
  transfers between devices with their start and end apart: 4 -> 9, of which waited for: 3 -> 4; matrix products, arithmetic and copies ran while one was open for 1% -> 12% of each run, Pallas kernels for 0% -> 0%
where the time goes in v2:
time: 30.2 us; the launch traced here: 30 us
  Pallas kernels  10.9 us (36%)
  starting transfers between devices  9.57 us (32%)
  other arithmetic  3.97 us (13%)
  waiting for transfers between devices  3.7 us (12%)
  local copies, waits for them, and re-layouts  1.15 us (4%)
  between operations  0.7 us (2%)
    ppermute x9, starting transfers between devices, swap(): lax.ppermute(value, axis, [(k, k ^ d) for k in range(lax.axis_size(axis))])  9.57 us
    pallas_call x1, Pallas kernels, render(): pl.pallas_call(functools.partial(render_kernel, len(parts), groups, block...  9.1 us
    ppermute x9, waiting for transfers between devices, swap(): lax.ppermute(value, axis, [(k, k ^ d) for k in range(lax.axis_size(axis))])  3.7 us
    reduce_max x1, other arithmetic, local(): inverse = jnp.max(jnp.where(named, order[None, :, None], -1), axis=1)  2.47 us
    pallas_call x1, Pallas kernels, update(): pl.pallas_call(functools.partial(update_kernel, len(packets)), out_shape=...  1.76 us
    dynamic_slice x1, local copies, waits for them, and re-layouts, local(): lax.dynamic_slice_in_dim(params, (group ^ d) * chunk, chunk, axis=1)  1.03 us
    concatenate x1, other arithmetic, local(): info = jnp.concatenate([target, place.reshape(1, -1).astype(F32)], axis=0)  0.71 us
    convert_element_type x1, other arithmetic, local(): info = jnp.concatenate([target, place.reshape(1, -1).astype(F32)], axis=0)  0.71 us
  transfers between devices with their start and end apart: 9, of which 4 were waited for; matrix products, arithmetic and copies ran while one was open for 12% of the time, Pallas kernels for 0%

profile of v2, /device:TPU:0, one launch (start us, length us, event | category | flops | bytes accessed | tf_op | source)
XLA Modules:
  0.0 30.0 jit_solution(15580368772133601155)
XLA Ops:
  0.6 0.7 %fusion = f32[2,256]{1,0:T(2,128)S(1)} fusion(s32[2,256,1]{1,2,0:T(1,128)} %param.14, s32[2,256]{1,0:T(2,128)} %param.15, s32[]{:T(128)S(6)} %mul.22, s32[]{:T(128)} %axis_index.25), kind=kLoop, calls=%fused_computation.8 | loop fusion | flops 2560 | bytes 6152 | tf_op jit(solution)/shard_map/convert_element_type | solution.py:540
  1.3 0.7 %pad_maximum_fusion.refs_7_ = f32[4,512]{1,0:T(4,128)S(1)} fusion(f32[1,512]{1,0:T(1,128)S(1)} %bitcast.11, f32[3,512]{1,0:T(4,128)} %param.12), kind=kLoop, calls=%fused_computation.1 | loop fusion | flops 2048 | bytes 16384 | tf_op jit(solution)/shard_map/concatenate | solution.py:540
  2.1 5.0 %collective-permute-start.5 = (f32[4,512]{1,0:T(4,128)S(1)}, f32[4,512]{1,0:T(4,128)S(1)}, u32[]{:S(2)}, u32[]{:S(2)}) collective-permute-start(f32[4,512]{1,0:T(4,128)S(1)} %pad_maximum_fusion.refs_7_), channel_id=1, source_target_pairs={{0,3},{1,2},{2,1},{3,0},{4,7},{5,6},{6,5},{7,4},{8,11},{9,10},{10,... | collective-permute-start | bytes 24584 | tf_op jit(solution)/shard_map/ppermute | solution.py:524
  7.1 0.0 collective-permute-start.4
  7.1 0.6 %collective-permute-start.3 = (f32[4,512]{1,0:T(4,128)S(1)}, f32[4,512]{1,0:T(4,128)S(1)}, u32[]{:S(2)}, u32[]{:S(2)}) collective-permute-start(f32[4,512]{1,0:T(4,128)S(1)} %pad_maximum_fusion.refs_7_), channel_id=1, source_target_pairs={{0,1},{1,0},{2,3},{3,2},{4,5},{5,4},{6,7},{7,6},{8,9},{9,8},{10,11... | collective-permute-start | bytes 24584 | tf_op jit(solution)/shard_map/ppermute | solution.py:524
  7.7 0.0 copy-start.3
  7.7 0.0 copy-start.4
  7.7 0.0 copy-start.1
  7.8 0.0 copy-start.2
  7.8 1.0 %constant_dynamic-slice_fusion = (f32[59,256]{1,0:T(8,128)S(1)}, f32[59,256]{1,0:T(8,128)S(1)}, f32[59,256]{1,0:T(8,128)S(1)}, f32[59,256]{1,0:T(8,128)S(1)}) fusion(f32[59,1024]{1,0:T(8,128)} %params.1, s32[]{:T(128)S(6)} %select_n.32, s32[]{:T(128)S(6)} %select_n.31, s32[]{:T(128)S(6)} %select_n.30, s32[]{:T(128)S(6)} %select_n.29), kind=kLoop, calls=%fused_computation.11 | loop fusion | bytes 483344 | tf_op jit(solution)/shard_map/dynamic_slice | solution.py:543
  8.8 0.0 copy-start
  8.8 0.4 %collective-permute-start.2 = (f32[59,256]{1,0:T(8,128)S(1)}, f32[59,256]{1,0:T(8,128)S(1)}, u32[]{:S(2)}, u32[]{:S(2)}) collective-permute-start(f32[59,256]{1,0:T(8,128)S(1)} %get-tuple-element.20), channel_id=1, source_target_pairs={{0,12},{4,8},{8,4},{12,0},{1,13},{5,9},{9,5},{13,1},{2,14},{6,10},... | collective-permute-start | bytes 181256 | tf_op jit(solution)/shard_map/ppermute | solution.py:524
  9.2 1.3 %collective-permute-start.1 = (f32[59,256]{1,0:T(8,128)S(1)}, f32[59,256]{1,0:T(8,128)S(1)}, u32[]{:S(2)}, u32[]{:S(2)}) collective-permute-start(f32[59,256]{1,0:T(8,128)S(1)} %get-tuple-element.21), channel_id=1, source_target_pairs={{0,8},{4,12},{8,0},{12,4},{1,9},{5,13},{9,1},{13,5},{2,10},{6,14},... | collective-permute-start | bytes 181256 | tf_op jit(solution)/shard_map/ppermute | solution.py:524
  10.6 0.1 pad_add_fusion.refs_2_
  10.7 0.0 collective-permute-done.5.refs_10_
  10.7 0.2 collective-permute-start
  10.9 0.8 %collective-permute-done.4.refs_9_ = f32[4,512]{1,0:T(4,128)S(1)} collective-permute-done((f32[4,512]{1,0:T(4,128)S(1)}, f32[4,512]{1,0:T(4,128)S(1)}, u32[]{:S(2)}, u32[]{:S(2)}) %collective-permute-start.4) | collective-permute-done | bytes 8224 | tf_op jit(solution)/shard_map/ppermute | solution.py:524
  11.7 0.0 collective-permute-done.3.refs_8_
  11.8 2.5 %select_reduce_fusion.refs_11_ = s32[8,1024]{1,0:T(8,128)S(1)} fusion(f32[1024]{0:T(1024)S(1)} %iota_convert_fusion, f32[8,256]{1,0:T(8,128)S(1)} %pad_maximum_fusion.1), kind=kLoop, calls=%fused_computation | loop fusion | flops 6283264 | bytes 45056 | tf_op jit(solution)/shard_map/reduce_max | solution.py:550
  14.2 0.0 collective-permute-done.2.refs_6_
  14.3 0.4 %collective-permute-done.1.refs_5_ = f32[59,256]{1,0:T(8,128)S(1)} collective-permute-done((f32[59,256]{1,0:T(8,128)S(1)}, f32[59,256]{1,0:T(8,128)S(1)}, u32[]{:S(2)}, u32[]{:S(2)}) %collective-permute-start.1) | collective-permute-done | bytes 60448 | tf_op jit(solution)/shard_map/ppermute | solution.py:524
  14.7 0.0 collective-permute-done.refs_4_
  14.7 0.0 copy-done.3
  14.7 0.0 copy-done.4
  14.7 9.1 %render.1 = (f32[3,512]{1,0:T(4,128)}, f32[16,256]{1,0:T(8,128)S(1)}, f32[16,256]{1,0:T(8,128)S(1)}, f32[16,256]{1,0:T(8,128)S(1)}, f32[16,256]{1,0:T(8,128)S(1)}) custom-call(s32[2]{0:T(128)S(1)} %copy-done.4, f32[4,12]{1,0:T(4,128)S(1)} %copy-done.3, s32[3]{0:T(128)S(1)} %pad_add_fusion.refs_2_, f32[59,256]{1,0:T(8,128)S(1)} %get-tuple-element.23.refs_3_, ...), custom_call_target="tpu_custom_call" | custom-call | tf_op jit(solution)/shard_map/render/pallas_call | solution.py:480
  23.8 0.2 collective-permute-start.6
  23.9 1.1 %collective-permute-start.7 = (f32[16,256]{1,0:T(8,128)S(1)}, f32[16,256]{1,0:T(8,128)S(1)}, u32[]{:S(2)}, u32[]{:S(2)}) collective-permute-start(f32[16,256]{1,0:T(8,128)S(1)} %get-tuple-element.15), channel_id=1, source_target_pairs={{0,8},{4,12},{8,0},{12,4},{1,9},{5,13},{9,1},{13,5},{2,10},{6,14},... | collective-permute-start | bytes 49160 | tf_op jit(solution)/shard_map/ppermute | solution.py:524
  25.0 0.7 %collective-permute-start.8 = (f32[16,256]{1,0:T(8,128)S(1)}, f32[16,256]{1,0:T(8,128)S(1)}, u32[]{:S(2)}, u32[]{:S(2)}) collective-permute-start(f32[16,256]{1,0:T(8,128)S(1)} %get-tuple-element.16), channel_id=1, source_target_pairs={{0,12},{4,8},{8,4},{12,0},{1,13},{5,9},{9,5},{13,1},{2,14},{6,10},... | collective-permute-start | bytes 49160 | tf_op jit(solution)/shard_map/ppermute | solution.py:524
  25.7 0.0 collective-permute-done.6.refs_1_
  25.7 1.9 %collective-permute-done.7.refs_2_ = f32[16,256]{1,0:T(8,128)S(1)} collective-permute-done((f32[16,256]{1,0:T(8,128)S(1)}, f32[16,256]{1,0:T(8,128)S(1)}, u32[]{:S(2)}, u32[]{:S(2)}) %collective-permute-start.7) | collective-permute-done | bytes 16416 | tf_op jit(solution)/shard_map/ppermute | solution.py:524
  27.7 0.5 %collective-permute-done.8.refs_3_ = f32[16,256]{1,0:T(8,128)S(1)} collective-permute-done((f32[16,256]{1,0:T(8,128)S(1)}, f32[16,256]{1,0:T(8,128)S(1)}, u32[]{:S(2)}, u32[]{:S(2)}) %collective-permute-start.8) | collective-permute-done | bytes 16416 | tf_op jit(solution)/shard_map/ppermute | solution.py:524
  28.2 0.0 copy-done.1
  28.2 0.0 copy-done.2
  28.2 0.0 copy-done
  28.2 1.8 %update.1 = (f32[59,1024]{1,0:T(8,128)}, f32[59,1024]{1,0:T(8,128)}, f32[59,1024]{1,0:T(8,128)}) custom-call(s32[1]{0:T(128)} %bitcast.3.where, f32[4,12]{1,0:T(4,128)S(1)} %copy-done.3, f32[59,1024]{1,0:T(8,128)S(1)} %copy-done, f32[59,1024]{1,0:T(8,128)S(1)} %copy-done.1, f32[59,1024]{1,0:T(8,128)S(1)} %copy-done.2, ...), custom_call_target="tpu_custom_call" | custom-call | tf_op jit(solution)/shard_map/update/pallas_call | solution.py:506
  (9 shorter events, 0.1 us)
Async XLA Ops:
  2.1 8.6 %collective-permute-start.5 = (f32[4,512]{1,0:T(4,128)S(1)}, f32[4,512]{1,0:T(4,128)S(1)}, u32[]{:S(2)}, u32[]{:S(2)}) collective-permute-start(f32[4,512]{1,0:T(4,128)S(1)} %pad_maximum_fusion.refs_7_), channel_id=1, source_target_pairs={{0,3},{1,2},{2,1},{3,0},{4,7},{5,6},{6,5},{7,4},{8,11},{9,10},{10,... | collective-permute-start | bytes 24584 | tf_op jit(solution)/shard_map/ppermute | solution.py:524
  7.1 4.5 %collective-permute-start.4 = (f32[4,512]{1,0:T(4,128)S(1)}, f32[4,512]{1,0:T(4,128)S(1)}, u32[]{:S(2)}, u32[]{:S(2)}) collective-permute-start(f32[4,512]{1,0:T(4,128)S(1)} %pad_maximum_fusion.refs_7_), channel_id=1, source_target_pairs={{0,2},{1,3},{2,0},{3,1},{4,6},{5,7},{6,4},{7,5},{8,10},{9,11},{10,... | collective-permute-start | bytes 24584 | tf_op jit(solution)/shard_map/ppermute | solution.py:524
  7.1 4.6 %collective-permute-start.3 = (f32[4,512]{1,0:T(4,128)S(1)}, f32[4,512]{1,0:T(4,128)S(1)}, u32[]{:S(2)}, u32[]{:S(2)}) collective-permute-start(f32[4,512]{1,0:T(4,128)S(1)} %pad_maximum_fusion.refs_7_), channel_id=1, source_target_pairs={{0,1},{1,0},{2,3},{3,2},{4,5},{5,4},{6,7},{7,6},{8,9},{9,8},{10,11... | collective-permute-start | bytes 24584 | tf_op jit(solution)/shard_map/ppermute | solution.py:524
  7.7 6.9 %copy-start.3 = (f32[4,12]{1,0:T(4,128)S(1)}, f32[4,12]{1,0:T(4,128)}, u32[]{:S(2)}) copy-start(f32[4,12]{1,0:T(4,128)} %cams.1) | copy-start | bytes 580
  7.7 6.9 %copy-start.4 = (s32[2]{0:T(128)S(1)}, s32[2]{0:T(128)}, u32[]{:S(2)}) copy-start(s32[2]{0:T(128)} %refs_0_.1) | copy-start | bytes 28
  7.7 20.4 %copy-start.1 = (f32[59,1024]{1,0:T(8,128)S(1)}, f32[59,1024]{1,0:T(8,128)}, u32[]{:S(2)}) copy-start(f32[59,1024]{1,0:T(8,128)} %adam_m.1) | copy-start | bytes 724996
  7.8 20.4 %copy-start.2 = (f32[59,1024]{1,0:T(8,128)S(1)}, f32[59,1024]{1,0:T(8,128)}, u32[]{:S(2)}) copy-start(f32[59,1024]{1,0:T(8,128)} %adam_v.1) | copy-start | bytes 724996
  8.8 19.4 %copy-start = (f32[59,1024]{1,0:T(8,128)S(1)}, f32[59,1024]{1,0:T(8,128)}, u32[]{:S(2)}) copy-start(f32[59,1024]{1,0:T(8,128)} %params.1) | copy-start | bytes 724996
  8.8 5.4 %collective-permute-start.2 = (f32[59,256]{1,0:T(8,128)S(1)}, f32[59,256]{1,0:T(8,128)S(1)}, u32[]{:S(2)}, u32[]{:S(2)}) collective-permute-start(f32[59,256]{1,0:T(8,128)S(1)} %get-tuple-element.20), channel_id=1, source_target_pairs={{0,12},{4,8},{8,4},{12,0},{1,13},{5,9},{9,5},{13,1},{2,14},{6,10},... | collective-permute-start | bytes 181256 | tf_op jit(solution)/shard_map/ppermute | solution.py:524
  9.2 5.4 %collective-permute-start.1 = (f32[59,256]{1,0:T(8,128)S(1)}, f32[59,256]{1,0:T(8,128)S(1)}, u32[]{:S(2)}, u32[]{:S(2)}) collective-permute-start(f32[59,256]{1,0:T(8,128)S(1)} %get-tuple-element.21), channel_id=1, source_target_pairs={{0,8},{4,12},{8,0},{12,4},{1,9},{5,13},{9,1},{13,5},{2,10},{6,14},... | collective-permute-start | bytes 181256 | tf_op jit(solution)/shard_map/ppermute | solution.py:524
  10.7 4.0 %collective-permute-start = (f32[59,256]{1,0:T(8,128)S(1)}, f32[59,256]{1,0:T(8,128)S(1)}, u32[]{:S(2)}, u32[]{:S(2)}) collective-permute-start(f32[59,256]{1,0:T(8,128)S(1)} %get-tuple-element.22), channel_id=1, source_target_pairs={{0,4},{4,0},{8,12},{12,8},{1,5},{5,1},{9,13},{13,9},{2,6},{6,2},{1... | collective-permute-start | bytes 181256 | tf_op jit(solution)/shard_map/ppermute | solution.py:524
  23.8 1.9 %collective-permute-start.6 = (f32[16,256]{1,0:T(8,128)S(1)}, f32[16,256]{1,0:T(8,128)S(1)}, u32[]{:S(2)}, u32[]{:S(2)}) collective-permute-start(f32[16,256]{1,0:T(8,128)S(1)} %get-tuple-element.14), channel_id=1, source_target_pairs={{0,4},{4,0},{8,12},{12,8},{1,5},{5,1},{9,13},{13,9},{2,6},{6,2},{1... | collective-permute-start | bytes 49160 | tf_op jit(solution)/shard_map/ppermute | solution.py:524
  23.9 3.7 %collective-permute-start.7 = (f32[16,256]{1,0:T(8,128)S(1)}, f32[16,256]{1,0:T(8,128)S(1)}, u32[]{:S(2)}, u32[]{:S(2)}) collective-permute-start(f32[16,256]{1,0:T(8,128)S(1)} %get-tuple-element.15), channel_id=1, source_target_pairs={{0,8},{4,12},{8,0},{12,4},{1,9},{5,13},{9,1},{13,5},{2,10},{6,14},... | collective-permute-start | bytes 49160 | tf_op jit(solution)/shard_map/ppermute | solution.py:524
  25.0 3.2 %collective-permute-start.8 = (f32[16,256]{1,0:T(8,128)S(1)}, f32[16,256]{1,0:T(8,128)S(1)}, u32[]{:S(2)}, u32[]{:S(2)}) collective-permute-start(f32[16,256]{1,0:T(8,128)S(1)} %get-tuple-element.16), channel_id=1, source_target_pairs={{0,12},{4,8},{8,4},{12,0},{1,13},{5,9},{9,5},{13,1},{2,14},{6,10},... | collective-permute-start | bytes 49160 | tf_op jit(solution)/shard_map/ppermute | solution.py:524

commit v3 on v2

--- a/solution.py
+++ b/solution.py
@@ -249,12 +249,88 @@
     return tiles
 
 
+def cut_kernel(shards, where, params, *refs):
+    pieces, sems = refs[:shards], refs[shards]
+    chunk = params.shape[1] // shards
+    copies = []
+    for d in range(shards):
+        first = pl.multiple_of((where[0] ^ d) * chunk, LANES)
+        copies.append(
+            pltpu.make_async_copy(params.at[:, pl.ds(first, chunk)], pieces[d], sems.at[d])
+        )
+    for copy in copies:
+        copy.start()
+    for copy in copies:
+        copy.wait()
+
+
+def cut(group, params, shards):
+    features, columns = params.shape
+    piece = jax.ShapeDtypeStruct((features, columns // shards), F32)
+    return pl.pallas_call(
+        functools.partial(cut_kernel, shards),
+        out_shape=(piece,) * shards,
+        in_specs=[smem(), pl.BlockSpec(memory_space=pl.ANY)],
+        out_specs=(vmem(),) * shards,
+        scratch_shapes=[pltpu.SemaphoreType.DMA((shards,))],
+        compiler_params=pltpu.CompilerParams(vmem_limit_bytes=32 * 1024 * 1024),
+        name="cut",
+    )(group.reshape(1), params)
+
+
+def pack_kernel(shards, where, shard_of, local_of, target, _, info, place_s):
+    group = where[0]
+    width = info.shape[1]
+    tile_count, listed = local_of.shape
+    rows_each = (info.shape[0] - 4) // tile_count
+    columns = rows_each * width
+    chunk = columns // shards
+    info[0:3, :] = target[...]
+    for t in range(tile_count):
+        place = (shard_of[t] ^ group) * chunk + (local_of[t : t + 1, :] - group * chunk)
+        info[3:4, t * listed : (t + 1) * listed] = place.astype(F32)
+        row_i = lax.broadcasted_iota(jnp.int32, (LANES, LANES), 0)
+        col_i = lax.broadcasted_iota(jnp.int32, (LANES, LANES), 1)
+        for first in range(0, listed, LANES):
+            spread = jnp.broadcast_to(place[:, first : first + LANES].astype(F32), (LANES, LANES))
+            place_s[first : first + LANES, :] = jnp.broadcast_to(
+                jnp.sum(jnp.where(row_i == col_i, spread, 0.0), axis=1, keepdims=True), (LANES, LANES)
+            )
+        lane_of = lax.broadcasted_iota(jnp.int32, (8, LANES), 1).astype(F32)
+        row_of = lax.broadcasted_iota(jnp.int32, (8, LANES), 0).astype(F32)
+        for s in range(columns // LANES):
+            best = jnp.full((8, LANES), -1.0, F32)
+            column = lane_of + float(s * LANES)
+            for first in range(0, listed, 8):
+                best = jnp.where(
+                    place_s[first : first + 8, :] == column, row_of + float(first), best
+                )
+            best = jnp.max(best, axis=0, keepdims=True)
+            row, at = 4 + t * rows_each + s * LANES // width, s * LANES % width
+            info[row : row + 1, at : at + LANES] = best
+
+
+def pack(group, columns, target, hit_shard, hit_local, shards, after):
+    tile_count, listed = hit_local.shape
+    width = target.shape[1]
+    rows = 4 + tile_count * (columns // width)
+    return pl.pallas_call(
+        functools.partial(pack_kernel, shards),
+        out_shape=jax.ShapeDtypeStruct((rows, width), F32),
+        in_specs=[smem()] + [vmem()] * 3 + [pl.BlockSpec(memory_space=pl.ANY)],
+        out_specs=vmem(),
+        scratch_shapes=[pltpu.VMEM((listed, LANES), F32)],
+        compiler_params=pltpu.CompilerParams(vmem_limit_bytes=32 * 1024 * 1024),
+        name="pack",
+    )(group.reshape(1), hit_shard.reshape(tile_count, 1, listed), hit_local, target, after)
+
+
 def render_kernel(pieces, groups, blocks, *refs):
     tile_ids, cams, where = refs[:3]
     parts = refs[3 : 3 + pieces]
     infos = refs[3 + pieces : 3 + pieces + groups]
-    inverse, rendered = refs[3 + pieces + groups : 5 + pieces + groups]
-    rest = refs[5 + pieces + groups :]
+    rendered = refs[3 + pieces + groups]
+    rest = refs[4 + pieces + groups :]
     packets = rest[: len(rest) - 9]
     feats, rows, e_s, t_s, d_s, hi_s, lo_s, acc_s, info_s = rest[len(rest) - 9 :]
     tile_count, listed = e_s.shape[0], e_s.shape[2]
@@ -395,12 +471,15 @@
     row_of = lax.broadcasted_iota(jnp.int32, (ROWS, LANES), 0)
     lane_of = lax.broadcasted_iota(jnp.int32, (ROWS, LANES), 1)
     chunk = packets[0].shape[1]
+    width = info_s.shape[2]
+    rows_each = slabs * LANES // width
     for s in range(slabs):
         totals = []
         for g in range(groups):
             total = jnp.zeros((ROWS, LANES), F32)
             for t in range(tile_count):
-                at = inverse[g * tile_count + t : g * tile_count + t + 1, s * LANES : (s + 1) * LANES]
+                row, first = 4 + t * rows_each + s * LANES // width, s * LANES % width
+                at = info_s[g, row : row + 1, first : first + LANES].astype(jnp.int32)
                 at = jnp.broadcast_to(at, (ROWS, LANES))
                 lane, half = at & (LANES - 1), at >> 7
                 for h in range(listed // LANES):
@@ -469,7 +548,7 @@
     return pl.BlockSpec(memory_space=pltpu.SMEM)
 
 
-def render(tile_ids, cameras, where, parts, infos, inverse, tile_count, blocks):
+def render(tile_ids, cameras, where, parts, infos, tile_count, blocks):
     width = sum(part.shape[1] for part in parts)
     features = parts[0].shape[0]
     slabs = width // LANES
@@ -480,7 +559,7 @@
     out = pl.pallas_call(
         functools.partial(render_kernel, len(parts), groups, blocks),
         out_shape=(jax.ShapeDtypeStruct((3, tile_count * pixels), F32),) + (packet,) * len(parts),
-        in_specs=[smem()] * 3 + [vmem()] * (len(parts) + groups + 1),
+        in_specs=[smem()] * 3 + [vmem()] * (len(parts) + groups),
         out_specs=(vmem(),) * (1 + len(parts)),
         scratch_shapes=[
             pltpu.VMEM((features * slabs, LANES), F32),
@@ -495,7 +574,7 @@
         ],
         compiler_params=pltpu.CompilerParams(vmem_limit_bytes=32 * 1024 * 1024),
         name="render",
-    )(tile_ids, cameras, where, *parts, *infos, inverse)
+    )(tile_ids, cameras, where, *parts, *infos)
     return out[0], list(out[1:])
 
 
@@ -536,25 +615,21 @@
     team = BLOCK_TILES // tile_count
     blocks = along // team
 
-    place = (hit_shard[:, :, 0] ^ group) * chunk + (hit_local - group * chunk)
-    info = jnp.concatenate([target, place.reshape(1, -1).astype(F32)], axis=0)
+    if aligned:
+        parts = cut(group, params, shards)
+    else:
+        parts = [
+            lax.dynamic_slice_in_dim(params, (group ^ d) * chunk, chunk, axis=1)
+            for d in range(shards)
+        ]
+    info = pack(group, width, target, hit_shard, hit_local, shards, parts[0])
+    parts = [swap(parts[d], "gs", d) for d in range(shards)]
+    info, parts[1] = lax.optimization_barrier((info, parts[1]))
     infos = [swap(info, "tile", d) for d in range(team)]
-    parts = [
-        swap(lax.dynamic_slice_in_dim(params, (group ^ d) * chunk, chunk, axis=1), "gs", d)
-        for d in range(shards)
-    ]
-    column = jnp.arange(width, dtype=jnp.int32).astype(F32)
-    order = jnp.arange(listed, dtype=jnp.int32)
-    places = jnp.concatenate([each[3].reshape(tile_count, listed) for each in infos], axis=0)
-    named = places[:, :, None] == column[None, None, :]
-    inverse = jnp.max(jnp.where(named, order[None, :, None], -1), axis=1)
-
     if not aligned:
         parts = [jnp.concatenate(parts, axis=1)]
     where = jnp.stack([seat % team, seat // team, jnp.int32(chunk)]).astype(jnp.int32)
-    rendered, packets = render(
-        tile_ids, cameras, where, parts, infos, inverse, tile_count, blocks
-    )
+    rendered, packets = render(tile_ids, cameras, where, parts, infos, tile_count, blocks)
     if not aligned:
         packets = [packets[0][:, d * chunk : (d + 1) * chunk] for d in range(shards)]
     packets = [swap(packets[d], "gs", d) for d in range(shards)]

time: 30.2 us -> 30.5 us (level)
  other arithmetic: 3.97 us -> 0.08 us
  waiting for transfers between devices: 3.7 us -> 6.72 us
  local copies, waits for them, and re-layouts: 1.15 us -> 1.93 us
  Pallas kernels: 10.9 us -> 11.4 us
    ppermute x9, waiting for transfers between devices: 3.7 us -> 6.72 us  [swap(): lax.ppermute(value, axis, [(k, k ^ d) for k in range(lax.axis_size(axis))])]
    reduce_max x1 -> x0, other arithmetic: 2.47 us -> none  [local(): inverse = jnp.max(jnp.where(named, order[None, :, None], -1), axis=1)]
    unnamed x11 -> x18, local copies, waits for them, and re-layouts: 0.03 us -> 1.93 us
    dynamic_slice x1 -> x0, local copies, waits for them, and re-layouts: 1.03 us -> none  [local(): lax.dynamic_slice_in_dim(params, (group ^ d) * chunk, chunk, axis=1)]
    concatenate x2 -> x0, other arithmetic: 0.72 us -> none  [the longest x1 0.71 us: local(): info = jnp.concatenate([target, place.reshape(1, -1).astype(F32)], axis=0)]
    convert_element_type x2 -> x0, other arithmetic: 0.71 us -> none  [the longest x1 0.71 us: local(): info = jnp.concatenate([target, place.reshape(1, -1).astype(F32)], axis=0)]
    pallas_call x0 -> x2, Pallas kernels: none -> 0.34 us  [the longest x1 0.24 us: pack(): pl.pallas_call(functools.partial(pack_kernel, shards), out_shape=jax.Shap...]
  transfers between devices with their start and end apart: 9 -> 9, of which waited for: 4 -> 4; matrix products, arithmetic and copies ran while one was open for 12% -> 0% of each run, Pallas kernels for 0% -> 1%
where the time goes in v3:
time: 30.5 us; the launch traced here: 30.4 us
  Pallas kernels  11.4 us (37%)
  starting transfers between devices  9.56 us (31%)
  waiting for transfers between devices  6.72 us (22%)
  local copies, waits for them, and re-layouts  1.93 us (6%)
  between operations  0.72 us (2%)
    ppermute x9, starting transfers between devices, swap(): lax.ppermute(value, axis, [(k, k ^ d) for k in range(lax.axis_size(axis))])  9.56 us
    pallas_call x1, Pallas kernels, render(): pl.pallas_call(functools.partial(render_kernel, len(parts), groups, block...  9.26 us
    ppermute x9, waiting for transfers between devices, swap(): lax.ppermute(value, axis, [(k, k ^ d) for k in range(lax.axis_size(axis))])  6.72 us
    unnamed x18, local copies, waits for them, and re-layouts  1.93 us
    pallas_call x1, Pallas kernels, update(): pl.pallas_call(functools.partial(update_kernel, len(packets)), out_shape=...  1.75 us
  transfers between devices with their start and end apart: 9, of which 4 were waited for; matrix products, arithmetic and copies ran while one was open for 0% of the time, Pallas kernels for 1%

profile of v3, /device:TPU:0, one launch (start us, length us, event | category | flops | bytes accessed | tf_op | source)
XLA Modules:
  0.0 30.4 jit_solution(3212574000899767877)
XLA Ops:
  0.6 0.0 copy-start
  0.7 0.9 %copy-done = f32[59,1024]{1,0:T(8,128)S(1)} copy-done((f32[59,1024]{1,0:T(8,128)S(1)}, f32[59,1024]{1,0:T(8,128)}, u32[]{:S(2)}) %copy-start) | copy-done | bytes 241688
  1.6 0.0 copy-start.5
  1.6 0.0 copy-start.6
  1.6 0.0 copy-start.7
  1.6 0.0 copy-start.4
  1.6 0.0 copy-start.8
  1.6 0.0 copy-start.2
  1.6 0.1 cut.1
  1.7 0.0 copy-start.1
  1.7 0.5 %collective-permute-start = (f32[59,256]{1,0:T(8,128)S(1)}, f32[59,256]{1,0:T(8,128)S(1)}, u32[]{:S(2)}, u32[]{:S(2)}) collective-permute-start(f32[59,256]{1,0:T(8,128)S(1)} %get-tuple-element.19), channel_id=1, source_target_pairs={{0,4},{4,0},{8,12},{12,8},{1,5},{5,1},{9,13},{13,9},{2,6},{6,2},{1... | collective-permute-start | bytes 181256 | tf_op jit(solution)/shard_map/ppermute | solution.py:603
  2.3 2.6 %collective-permute-start.1 = (f32[59,256]{1,0:T(8,128)S(1)}, f32[59,256]{1,0:T(8,128)S(1)}, u32[]{:S(2)}, u32[]{:S(2)}) collective-permute-start(f32[59,256]{1,0:T(8,128)S(1)} %get-tuple-element.21), channel_id=1, source_target_pairs={{0,8},{4,12},{8,0},{12,4},{1,9},{5,13},{9,1},{13,5},{2,10},{6,14},... | collective-permute-start | bytes 181256 | tf_op jit(solution)/shard_map/ppermute | solution.py:603
  4.8 0.1 collective-permute-start.2
  4.9 0.0 copy-done.5
  4.9 0.0 copy-done.6
  4.9 0.0 copy-done.7
  4.9 0.2 pack.1.refs_7_
  5.2 0.0 collective-permute-done.refs_4_
  5.2 3.9 %collective-permute-start.5 = (f32[8,512]{1,0:T(8,128)S(1)}, f32[8,512]{1,0:T(8,128)S(1)}, u32[]{:S(2)}, u32[]{:S(2)}) collective-permute-start(f32[8,512]{1,0:T(8,128)S(1)} %pack.1.refs_7_), channel_id=1, source_target_pairs={{0,3},{1,2},{2,1},{3,0},{4,7},{5,6},{6,5},{7,4},{8,11},{9,10},{10,... | collective-permute-start | bytes 49160 | tf_op jit(solution)/shard_map/ppermute | solution.py:603
  9.1 0.0 collective-permute-start.4
  9.1 0.6 %collective-permute-start.3 = (f32[8,512]{1,0:T(8,128)S(1)}, f32[8,512]{1,0:T(8,128)S(1)}, u32[]{:S(2)}, u32[]{:S(2)}) collective-permute-start(f32[8,512]{1,0:T(8,128)S(1)} %pack.1.refs_7_), channel_id=1, source_target_pairs={{0,1},{1,0},{2,3},{3,2},{4,5},{5,4},{6,7},{7,6},{8,9},{9,8},{10,11... | collective-permute-start | bytes 49160 | tf_op jit(solution)/shard_map/ppermute | solution.py:603
  9.7 0.1 pad_add_fusion.refs_2_
  9.8 0.0 collective-permute-done.1.refs_5_
  9.8 0.0 collective-permute-done.2.refs_6_
  9.8 1.0 %collective-permute-done.5.refs_10_ = f32[8,512]{1,0:T(8,128)S(1)} collective-permute-done((f32[8,512]{1,0:T(8,128)S(1)}, f32[8,512]{1,0:T(8,128)S(1)}, u32[]{:S(2)}, u32[]{:S(2)}) %collective-permute-start.5) | collective-permute-done | bytes 16416 | tf_op jit(solution)/shard_map/ppermute | solution.py:603
  10.8 2.9 %collective-permute-done.4.refs_9_ = f32[8,512]{1,0:T(8,128)S(1)} collective-permute-done((f32[8,512]{1,0:T(8,128)S(1)}, f32[8,512]{1,0:T(8,128)S(1)}, u32[]{:S(2)}, u32[]{:S(2)}) %collective-permute-start.4) | collective-permute-done | bytes 16416 | tf_op jit(solution)/shard_map/ppermute | solution.py:603
  13.7 0.0 collective-permute-done.3.refs_8_
  13.7 0.0 copy-done.4
  13.7 0.0 copy-done.8
  13.7 9.3 %render.1 = (f32[3,512]{1,0:T(4,128)}, f32[16,256]{1,0:T(8,128)S(1)}, f32[16,256]{1,0:T(8,128)S(1)}, f32[16,256]{1,0:T(8,128)S(1)}, f32[16,256]{1,0:T(8,128)S(1)}) custom-call(s32[2]{0:T(128)S(1)} %copy-done.8, f32[4,12]{1,0:T(4,128)S(1)} %copy-done.4, s32[3]{0:T(128)S(1)} %pad_add_fusion.refs_2_, f32[59,256]{1,0:T(8,128)S(1)} %get-tuple-element.18._.refs_3_, ...), custom_call_target="tpu_custom_call" | custom-call | tf_op jit(solution)/shard_map/render/pallas_call | solution.py:559
  23.0 0.0 collective-permute-start.6
  23.0 1.5 %collective-permute-start.7 = (f32[16,256]{1,0:T(8,128)S(1)}, f32[16,256]{1,0:T(8,128)S(1)}, u32[]{:S(2)}, u32[]{:S(2)}) collective-permute-start(f32[16,256]{1,0:T(8,128)S(1)} %get-tuple-element.27), channel_id=1, source_target_pairs={{0,8},{4,12},{8,0},{12,4},{1,9},{5,13},{9,1},{13,5},{2,10},{6,14},... | collective-permute-start | bytes 49160 | tf_op jit(solution)/shard_map/ppermute | solution.py:603
  24.5 0.4 %collective-permute-start.8 = (f32[16,256]{1,0:T(8,128)S(1)}, f32[16,256]{1,0:T(8,128)S(1)}, u32[]{:S(2)}, u32[]{:S(2)}) collective-permute-start(f32[16,256]{1,0:T(8,128)S(1)} %get-tuple-element.28), channel_id=1, source_target_pairs={{0,12},{4,8},{8,4},{12,0},{1,13},{5,9},{9,5},{13,1},{2,14},{6,10},... | collective-permute-start | bytes 49160 | tf_op jit(solution)/shard_map/ppermute | solution.py:603
  24.8 0.0 collective-permute-done.6.refs_1_
  24.8 1.9 %collective-permute-done.7.refs_2_ = f32[16,256]{1,0:T(8,128)S(1)} collective-permute-done((f32[16,256]{1,0:T(8,128)S(1)}, f32[16,256]{1,0:T(8,128)S(1)}, u32[]{:S(2)}, u32[]{:S(2)}) %collective-permute-start.7) | collective-permute-done | bytes 16416 | tf_op jit(solution)/shard_map/ppermute | solution.py:603
  26.7 0.9 %collective-permute-done.8.refs_3_ = f32[16,256]{1,0:T(8,128)S(1)} collective-permute-done((f32[16,256]{1,0:T(8,128)S(1)}, f32[16,256]{1,0:T(8,128)S(1)}, u32[]{:S(2)}, u32[]{:S(2)}) %collective-permute-start.8) | collective-permute-done | bytes 16416 | tf_op jit(solution)/shard_map/ppermute | solution.py:603
  27.6 0.0 copy-done.2
  27.6 0.0 copy-done.1
  27.6 0.0 copy-start.3
  27.6 0.9 %copy-done.3 = f32[59,1024]{1,0:T(8,128)S(1)} copy-done((f32[59,1024]{1,0:T(8,128)S(1)}, f32[59,1024]{1,0:T(8,128)}, u32[]{:S(2)}) %copy-start.3) | copy-done | bytes 241688
  28.6 1.8 %update.1 = (f32[59,1024]{1,0:T(8,128)}, f32[59,1024]{1,0:T(8,128)}, f32[59,1024]{1,0:T(8,128)}) custom-call(s32[1]{0:T(128)} %bitcast.2.where, f32[4,12]{1,0:T(4,128)S(1)} %copy-done.4, f32[59,1024]{1,0:T(8,128)S(1)} %copy-done.1, f32[59,1024]{1,0:T(8,128)S(1)} %copy-done.2, f32[59,1024]{1,0:T(8,128)S(1)} %copy-done.3, ...), custom_call_target="tpu_custom_call" | custom-call | tf_op jit(solution)/shard_map/update/pallas_call | solution.py:585
Async XLA Ops:
  0.6 1.0 %copy-start = (f32[59,1024]{1,0:T(8,128)S(1)}, f32[59,1024]{1,0:T(8,128)}, u32[]{:S(2)}) copy-start(f32[59,1024]{1,0:T(8,128)} %params.3) | copy-start | bytes 724996
  1.6 3.3 %copy-start.5 = (f32[3,512]{1,0:T(4,128)S(1)}, f32[3,512]{1,0:T(4,128)}, u32[]{:S(2)}) copy-start(f32[3,512]{1,0:T(4,128)} %target.1) | copy-start | bytes 18436
  1.6 3.3 %copy-start.6 = (s32[2,256,1]{1,2,0:T(1,128)S(1)}, s32[2,256,1]{1,2,0:T(1,128)}, u32[]{:S(2)}) copy-start(s32[2,256,1]{1,2,0:T(1,128)} %param.14) | copy-start | bytes 6148
  1.6 3.3 %copy-start.7 = (s32[2,256]{1,0:T(2,128)S(1)}, s32[2,256]{1,0:T(2,128)}, u32[]{:S(2)}) copy-start(s32[2,256]{1,0:T(2,128)} %local_of.1) | copy-start | bytes 6148
  1.6 12.1 %copy-start.4 = (f32[4,12]{1,0:T(4,128)S(1)}, f32[4,12]{1,0:T(4,128)}, u32[]{:S(2)}) copy-start(f32[4,12]{1,0:T(4,128)} %cams.1) | copy-start | bytes 580
  1.6 12.1 %copy-start.8 = (s32[2]{0:T(128)S(1)}, s32[2]{0:T(128)}, u32[]{:S(2)}) copy-start(s32[2]{0:T(128)} %refs_0_.1) | copy-start | bytes 28
  1.6 26.0 %copy-start.2 = (f32[59,1024]{1,0:T(8,128)S(1)}, f32[59,1024]{1,0:T(8,128)}, u32[]{:S(2)}) copy-start(f32[59,1024]{1,0:T(8,128)} %adam_m.1) | copy-start | bytes 724996
  1.7 25.9 %copy-start.1 = (f32[59,1024]{1,0:T(8,128)S(1)}, f32[59,1024]{1,0:T(8,128)}, u32[]{:S(2)}) copy-start(f32[59,1024]{1,0:T(8,128)} %params.3) | copy-start | bytes 724996
  1.7 3.4 %collective-permute-start = (f32[59,256]{1,0:T(8,128)S(1)}, f32[59,256]{1,0:T(8,128)S(1)}, u32[]{:S(2)}, u32[]{:S(2)}) collective-permute-start(f32[59,256]{1,0:T(8,128)S(1)} %get-tuple-element.19), channel_id=1, source_target_pairs={{0,4},{4,0},{8,12},{12,8},{1,5},{5,1},{9,13},{13,9},{2,6},{6,2},{1... | collective-permute-start | bytes 181256 | tf_op jit(solution)/shard_map/ppermute | solution.py:603
  2.3 7.5 %collective-permute-start.1 = (f32[59,256]{1,0:T(8,128)S(1)}, f32[59,256]{1,0:T(8,128)S(1)}, u32[]{:S(2)}, u32[]{:S(2)}) collective-permute-start(f32[59,256]{1,0:T(8,128)S(1)} %get-tuple-element.21), channel_id=1, source_target_pairs={{0,8},{4,12},{8,0},{12,4},{1,9},{5,13},{9,1},{13,5},{2,10},{6,14},... | collective-permute-start | bytes 181256 | tf_op jit(solution)/shard_map/ppermute | solution.py:603
  4.8 5.0 %collective-permute-start.2 = (f32[59,256]{1,0:T(8,128)S(1)}, f32[59,256]{1,0:T(8,128)S(1)}, u32[]{:S(2)}, u32[]{:S(2)}) collective-permute-start(f32[59,256]{1,0:T(8,128)S(1)} %get-tuple-element.22), channel_id=1, source_target_pairs={{0,12},{4,8},{8,4},{12,0},{1,13},{5,9},{9,5},{13,1},{2,14},{6,10},... | collective-permute-start | bytes 181256 | tf_op jit(solution)/shard_map/ppermute | solution.py:603
  5.2 5.6 %collective-permute-start.5 = (f32[8,512]{1,0:T(8,128)S(1)}, f32[8,512]{1,0:T(8,128)S(1)}, u32[]{:S(2)}, u32[]{:S(2)}) collective-permute-start(f32[8,512]{1,0:T(8,128)S(1)} %pack.1.refs_7_), channel_id=1, source_target_pairs={{0,3},{1,2},{2,1},{3,0},{4,7},{5,6},{6,5},{7,4},{8,11},{9,10},{10,... | collective-permute-start | bytes 49160 | tf_op jit(solution)/shard_map/ppermute | solution.py:603
  9.1 4.6 %collective-permute-start.4 = (f32[8,512]{1,0:T(8,128)S(1)}, f32[8,512]{1,0:T(8,128)S(1)}, u32[]{:S(2)}, u32[]{:S(2)}) collective-permute-start(f32[8,512]{1,0:T(8,128)S(1)} %pack.1.refs_7_), channel_id=1, source_target_pairs={{0,2},{1,3},{2,0},{3,1},{4,6},{5,7},{6,4},{7,5},{8,10},{9,11},{10,... | collective-permute-start | bytes 49160 | tf_op jit(solution)/shard_map/ppermute | solution.py:603
  9.1 4.6 %collective-permute-start.3 = (f32[8,512]{1,0:T(8,128)S(1)}, f32[8,512]{1,0:T(8,128)S(1)}, u32[]{:S(2)}, u32[]{:S(2)}) collective-permute-start(f32[8,512]{1,0:T(8,128)S(1)} %pack.1.refs_7_), channel_id=1, source_target_pairs={{0,1},{1,0},{2,3},{3,2},{4,5},{5,4},{6,7},{7,6},{8,9},{9,8},{10,11... | collective-permute-start | bytes 49160 | tf_op jit(solution)/shard_map/ppermute | solution.py:603
  23.0 1.9 %collective-permute-start.6 = (f32[16,256]{1,0:T(8,128)S(1)}, f32[16,256]{1,0:T(8,128)S(1)}, u32[]{:S(2)}, u32[]{:S(2)}) collective-permute-start(f32[16,256]{1,0:T(8,128)S(1)} %get-tuple-element.26), channel_id=1, source_target_pairs={{0,4},{4,0},{8,12},{12,8},{1,5},{5,1},{9,13},{13,9},{2,6},{6,2},{1... | collective-permute-start | bytes 49160 | tf_op jit(solution)/shard_map/ppermute | solution.py:603
  23.0 3.7 %collective-permute-start.7 = (f32[16,256]{1,0:T(8,128)S(1)}, f32[16,256]{1,0:T(8,128)S(1)}, u32[]{:S(2)}, u32[]{:S(2)}) collective-permute-start(f32[16,256]{1,0:T(8,128)S(1)} %get-tuple-element.27), channel_id=1, source_target_pairs={{0,8},{4,12},{8,0},{12,4},{1,9},{5,13},{9,1},{13,5},{2,10},{6,14},... | collective-permute-start | bytes 49160 | tf_op jit(solution)/shard_map/ppermute | solution.py:603
  24.5 3.2 %collective-permute-start.8 = (f32[16,256]{1,0:T(8,128)S(1)}, f32[16,256]{1,0:T(8,128)S(1)}, u32[]{:S(2)}, u32[]{:S(2)}) collective-permute-start(f32[16,256]{1,0:T(8,128)S(1)} %get-tuple-element.28), channel_id=1, source_target_pairs={{0,12},{4,8},{8,4},{12,0},{1,13},{5,9},{9,5},{13,1},{2,14},{6,10},... | collective-permute-start | bytes 49160 | tf_op jit(solution)/shard_map/ppermute | solution.py:603
  27.6 1.0 %copy-start.3 = (f32[59,1024]{1,0:T(8,128)S(1)}, f32[59,1024]{1,0:T(8,128)}, u32[]{:S(2)}) copy-start(f32[59,1024]{1,0:T(8,128)} %adam_v.1) | copy-start | bytes 724996

commit v4 on v3

--- a/solution.py
+++ b/solution.py
@@ -249,43 +249,31 @@
     return tiles
 
 
-def cut_kernel(shards, where, params, *refs):
-    pieces, sems = refs[:shards], refs[shards]
-    chunk = params.shape[1] // shards
-    copies = []
-    for d in range(shards):
-        first = pl.multiple_of((where[0] ^ d) * chunk, LANES)
-        copies.append(
-            pltpu.make_async_copy(params.at[:, pl.ds(first, chunk)], pieces[d], sems.at[d])
+def pack_kernel(shards, pieces, where, *refs):
+    sources, refs = refs[: 3 + (pieces > 0)], refs[3 + (pieces > 0) :]
+    info, parts, refs = refs[0], refs[1 : 1 + pieces], refs[1 + pieces :]
+    shard_of, local_of, goal, place_s, sems, cut_sems = refs
+    group = where[0]
+    loads = [
+        pltpu.make_async_copy(source, held, sems.at[k])
+        for k, (source, held) in enumerate(zip(sources, (shard_of, local_of, goal)))
+    ]
+    for d in range(pieces):
+        chunk = parts[d].shape[1]
+        first = pl.multiple_of((group ^ d) * chunk, LANES)
+        loads.append(
+            pltpu.make_async_copy(sources[3].at[:, pl.ds(first, chunk)], parts[d], cut_sems.at[d])
         )
-    for copy in copies:
-        copy.start()
-    for copy in copies:
-        copy.wait()
-
-
-def cut(group, params, shards):
-    features, columns = params.shape
-    piece = jax.ShapeDtypeStruct((features, columns // shards), F32)
-    return pl.pallas_call(
-        functools.partial(cut_kernel, shards),
-        out_shape=(piece,) * shards,
-        in_specs=[smem(), pl.BlockSpec(memory_space=pl.ANY)],
-        out_specs=(vmem(),) * shards,
-        scratch_shapes=[pltpu.SemaphoreType.DMA((shards,))],
-        compiler_params=pltpu.CompilerParams(vmem_limit_bytes=32 * 1024 * 1024),
-        name="cut",
-    )(group.reshape(1), params)
-
-
-def pack_kernel(shards, where, shard_of, local_of, target, _, info, place_s):
-    group = where[0]
+    for load in loads:
+        load.start()
+    for load in loads[:3]:
+        load.wait()
     width = info.shape[1]
     tile_count, listed = local_of.shape
     rows_each = (info.shape[0] - 4) // tile_count
     columns = rows_each * width
     chunk = columns // shards
-    info[0:3, :] = target[...]
+    info[0:3, :] = goal[...]
     for t in range(tile_count):
         place = (shard_of[t] ^ group) * chunk + (local_of[t : t + 1, :] - group * chunk)
         info[3:4, t * listed : (t + 1) * listed] = place.astype(F32)
@@ -308,55 +296,47 @@
             best = jnp.max(best, axis=0, keepdims=True)
             row, at = 4 + t * rows_each + s * LANES // width, s * LANES % width
             info[row : row + 1, at : at + LANES] = best
-
-
-def pack(group, columns, target, hit_shard, hit_local, shards, after):
+    for load in loads[3:]:
+        load.wait()
+
+
+def pack(group, params, target, hit_shard, hit_local, shards, aligned):
+    features, columns = params.shape
     tile_count, listed = hit_local.shape
     width = target.shape[1]
     rows = 4 + tile_count * (columns // width)
-    return pl.pallas_call(
-        functools.partial(pack_kernel, shards),
-        out_shape=jax.ShapeDtypeStruct((rows, width), F32),
-        in_specs=[smem()] + [vmem()] * 3 + [pl.BlockSpec(memory_space=pl.ANY)],
-        out_specs=vmem(),
-        scratch_shapes=[pltpu.VMEM((listed, LANES), F32)],
-        compiler_params=pltpu.CompilerParams(vmem_limit_bytes=32 * 1024 * 1024),
-        name="pack",
-    )(group.reshape(1), hit_shard.reshape(tile_count, 1, listed), hit_local, target, after)
-
-
-def render_kernel(pieces, groups, blocks, *refs):
-    tile_ids, cams, where = refs[:3]
-    parts = refs[3 : 3 + pieces]
-    infos = refs[3 + pieces : 3 + pieces + groups]
-    rendered = refs[3 + pieces + groups]
-    rest = refs[4 + pieces + groups :]
-    packets = rest[: len(rest) - 9]
-    feats, rows, e_s, t_s, d_s, hi_s, lo_s, acc_s, info_s = rest[len(rest) - 9 :]
-    tile_count, listed = e_s.shape[0], e_s.shape[2]
-    pixels = e_s.shape[1]
+    pieces = shards if aligned else 0
+    piece = jax.ShapeDtypeStruct((features, columns // shards), F32)
+    args = (hit_shard.reshape(tile_count, 1, listed), hit_local, target) + (params,) * aligned
+    out = call(
+        functools.partial(pack_kernel, shards, pieces),
+        "pack",
+        (jax.ShapeDtypeStruct((rows, width), F32),) + (piece,) * pieces,
+        [smem()] + [pl.BlockSpec(memory_space=pltpu.HBM)] * len(args),
+        [
+            pltpu.VMEM((tile_count, 1, listed), jnp.int32),
+            pltpu.VMEM((tile_count, listed), jnp.int32),
+            pltpu.VMEM(target.shape, F32),
+            pltpu.VMEM((listed, LANES), F32),
+            pltpu.SemaphoreType.DMA((3,)),
+            pltpu.SemaphoreType.DMA((shards,)),
+        ],
+        (group.reshape(1),) + args,
+    )
+    return out[0], list(out[1:])
+
+
+def composite(tiles, first_group, me, rows, info_s, rendered, work):
+    e_s, t_s, d_s, hi_s, lo_s, acc_s = work
+    tile_count, pixels, listed = e_s.shape
+    slabs = rows.shape[0] // ROWS
     side = TILE_SIDE
-    view = tile_ids[0] // (TILES_X * TILES_Y)
-    cam = [cams[view, i] for i in range(12)]
-    slabs = spread_features(parts, feats, parts[0].shape[0])
-    projected = project_rows(lambda f: feats[f * slabs : (f + 1) * slabs, :], cam)
-    for f, value in enumerate(projected):
-        rows[pl.ds(f, slabs, stride=ROWS), :] = value
-    zero_row = jnp.zeros((slabs, LANES), F32)
-    for f in range(len(projected), ROWS):
-        rows[pl.ds(f, slabs, stride=ROWS), :] = zero_row
-    for g in range(groups):
-        info_s[g] = infos[g][...]
-
+    first_col, first_row = tiles
     row_i = lax.broadcasted_iota(jnp.int32, (listed, listed), 0)
     col_i = lax.broadcasted_iota(jnp.int32, (listed, listed), 1)
     earlier = jnp.where(row_i < col_i, 1.0, 0.0).astype(BF16)
     later = jnp.where(row_i > col_i, 1.0, 0.0).astype(BF16)
     step = lax.broadcasted_iota(jnp.int32, (side, listed), 0).astype(F32)
-    within = tile_ids[0] % (TILES_X * TILES_Y)
-    first_row = (within // TILES_X) // 2 * 2
-    first_col = (within % TILES_X) // 4 * 4
-    me = where[0]
 
     def one_group(g, carry):
         lists = []
@@ -378,7 +358,7 @@
         setup = []
         for t in range(tile_count):
             entry = lists[t]
-            slot = (me ^ g) * tile_count + t
+            slot = (me ^ (first_group + g)) * tile_count + t
             x_0 = ((first_col + slot % 4) * side).astype(F32) + 0.5
             y_0 = ((first_row + slot // 4) * side).astype(F32) + 0.5
             quad_a, quad_b, quad_c = -0.5 * entry[2:3], -entry[3:4], -0.5 * entry[4:5]
@@ -414,10 +394,11 @@
                 + matmul(c_hi, lo_s[t], both)
             )
             here = slice(t * pixels, (t + 1) * pixels)
-
-            @pl.when(g == 0)
-            def _():
-                rendered[:, here] = image
+            if rendered is not None:
+
+                @pl.when(g == 0)
+                def _():
+                    rendered[:, here] = image
 
             error = image - info_s[g, 0:3, here]
             g_hi, g_lo = split(error)
@@ -465,35 +446,70 @@
             acc_s[g, t, 9:16, :] = jnp.zeros((7, listed), F32)
         return carry
 
-    lax.fori_loop(0, groups, one_group, 0)
-
-    share = view.astype(F32)
+    lax.fori_loop(0, acc_s.shape[0], one_group, 0)
+
+
+def pool_sum(slab, info_s, acc_s):
+    _, tile_count, _, listed = acc_s.shape
+    width = info_s.shape[2]
+    rows_each = (info_s.shape[1] - 4) // tile_count
+    totals = []
+    for g in range(2):
+        total = jnp.zeros((ROWS, LANES), F32)
+        for t in range(tile_count):
+            row, first = 4 + t * rows_each + slab * LANES // width, slab * LANES % width
+            at = info_s[g, row : row + 1, first : first + LANES].astype(jnp.int32)
+            at = jnp.broadcast_to(at, (ROWS, LANES))
+            lane, half = at & (LANES - 1), at >> 7
+            for h in range(listed // LANES):
+                here = jnp.take_along_axis(
+                    acc_s[g, t, :, h * LANES : (h + 1) * LANES],
+                    lane,
+                    axis=1,
+                    mode="promise_in_bounds",
+                )
+                total = total + jnp.where(half == h, here, 0.0)
+        totals.append(total)
+    return totals[0] + totals[1]
+
+
+def block_start(tile_id):
+    within = tile_id % (TILES_X * TILES_Y)
+    return (within % TILES_X) // 4 * 4, (within // TILES_X) // 2 * 2
+
+
+def near_kernel(pieces, tile_ids, cams, where, own, other, *refs):
+    parts = refs[:pieces]
+    rendered, rows, partial, feats, info_s, *work = refs[pieces:]
+    view = tile_ids[0] // (TILES_X * TILES_Y)
+    cam = [cams[view, i] for i in range(12)]
+    slabs = spread_features(parts, feats, parts[0].shape[0])
+    projected = project_rows(lambda f: feats[f * slabs : (f + 1) * slabs, :], cam)
+    for f, value in enumerate(projected):
+        rows[pl.ds(f, slabs, stride=ROWS), :] = value
+    zero_row = jnp.zeros((slabs, LANES), F32)
+    for f in range(len(projected), ROWS):
+        rows[pl.ds(f, slabs, stride=ROWS), :] = zero_row
+    info_s[0] = own[...]
+    info_s[1] = other[...]
+    composite(block_start(tile_ids[0]), 0, where[0], rows, info_s, rendered, work)
+    for s in range(slabs):
+        partial[:, s * LANES : (s + 1) * LANES] = pool_sum(s, info_s, work[-1])
+
+
+def far_kernel(blocks, tile_ids, where, rows, partial, infos, *refs):
+    *packets, info_s = refs[: len(refs) - 6]
+    work = refs[len(refs) - 6 :]
+    half = infos.shape[0] // 2
+    info_s[0] = infos[:half, :]
+    info_s[1] = infos[half:, :]
+    composite(block_start(tile_ids[0]), 2, where[0], rows, info_s, None, work)
+    share = (tile_ids[0] // (TILES_X * TILES_Y)).astype(F32)
     row_of = lax.broadcasted_iota(jnp.int32, (ROWS, LANES), 0)
     lane_of = lax.broadcasted_iota(jnp.int32, (ROWS, LANES), 1)
     chunk = packets[0].shape[1]
-    width = info_s.shape[2]
-    rows_each = slabs * LANES // width
-    for s in range(slabs):
-        totals = []
-        for g in range(groups):
-            total = jnp.zeros((ROWS, LANES), F32)
-            for t in range(tile_count):
-                row, first = 4 + t * rows_each + s * LANES // width, s * LANES % width
-                at = info_s[g, row : row + 1, first : first + LANES].astype(jnp.int32)
-                at = jnp.broadcast_to(at, (ROWS, LANES))
-                lane, half = at & (LANES - 1), at >> 7
-                for h in range(listed // LANES):
-                    here = jnp.take_along_axis(
-                        acc_s[g, t, :, h * LANES : (h + 1) * LANES],
-                        lane,
-                        axis=1,
-                        mode="promise_in_bounds",
-                    )
-                    total = total + jnp.where(half == h, here, 0.0)
-            totals.append(total)
-        while len(totals) > 1:
-            totals = [totals[k] + totals[k + 1] for k in range(0, len(totals), 2)]
-        total = totals[0]
+    for s in range(rows.shape[0] // ROWS):
+        total = partial[:, s * LANES : (s + 1) * LANES] + pool_sum(s, info_s, work[-1])
         if blocks == 1:
             mine = share
         else:
@@ -503,12 +519,23 @@
         packets[s * LANES // chunk][:, s * LANES % chunk : s * LANES % chunk + LANES] = total
 
 
-def update_kernel(pieces, where, cams, params, adam_m, adam_v, *refs):
+def join_kernel(first, second, out):
+    half = first.shape[0]
+    out[:half, :] = first[...]
+    out[half:, :] = second[...]
+
+
+def update_kernel(pieces, where, cams, *refs):
     packets = refs[:pieces]
-    new_params, new_m, new_v, feats, rows, grads = refs[pieces:]
+    sources, sinks = refs[pieces : pieces + 3], refs[pieces + 3 : pieces + 6]
+    feats, rows, grads, held, made, in_sems, out_sems = refs[pieces + 6 :]
+    params, adam_m, adam_v = held.at[0], held.at[1], held.at[2]
     features, width = params.shape
-    slabs = spread_features([params], feats, features)
+    loads = [pltpu.make_async_copy(sources[k], held.at[k], in_sems.at[k]) for k in range(3)]
+    for load in loads:
+        load.start()
     chunk = packets[0].shape[1]
+    slabs = width // LANES
     for d in range(pieces):
         for h in range(chunk // LANES):
             slab = (where[0] ^ d) * (chunk // LANES) + h
@@ -525,19 +552,35 @@
     def put(f, value):
         grads[f * slabs : (f + 1) * slabs, :] = value
 
+    loads[0].wait()
+    spread_features([params], feats, features)
     project_pull(lambda f: feats[f * slabs : (f + 1) * slabs, :], cam, pulled[:9], put)
     rate = learn_rate / (1.0 - beta_one**adam_steps)
     unbias = 1.0 / (1.0 - beta_two**adam_steps)
-    for s in range(slabs):
-        for row in range(0, features, 8):
-            count = min(8, features - row)
+    loads[1].wait()
+    loads[2].wait()
+    stores = []
+    for row in range(0, features, 8):
+        count = min(8, features - row)
+        for s in range(slabs):
             at = (slice(row, row + count), slice(s * LANES, (s + 1) * LANES))
             grad = grads[pl.ds(row * slabs + s, count, stride=slabs), :]
             moment = beta_one * adam_m[at] + (1.0 - beta_one) * grad
             second = beta_two * adam_v[at] + (1.0 - beta_two) * grad * grad
-            new_m[at] = moment
-            new_v[at] = second
-            new_params[at] = params[at] - rate * moment / (jnp.sqrt(second * unbias) + adam_eps)
+            made.at[1][at] = moment
+            made.at[2][at] = second
+            made.at[0][at] = params[at] - rate * moment / (jnp.sqrt(second * unbias) + adam_eps)
+        if row % 16 == 8 or row + count == features:
+            first = row // 16 * 16
+            span = pl.ds(first, row + count - first)
+            for k in range(3):
+                store = pltpu.make_async_copy(
+                    made.at[k, span], sinks[k].at[span], out_sems.at[k, first // 16]
+                )
+                store.start()
+                stores.append(store)
+    for store in stores:
+        store.wait()
 
 
 def vmem():
@@ -548,53 +591,96 @@
     return pl.BlockSpec(memory_space=pltpu.SMEM)
 
 
-def render(tile_ids, cameras, where, parts, infos, tile_count, blocks):
+def any_space():
+    return pl.BlockSpec(memory_space=pl.ANY)
+
+
+def call(kernel, name, out_shape, in_specs, scratch, args, out_specs=None):
+    return pl.pallas_call(
+        kernel,
+        out_shape=out_shape,
+        in_specs=in_specs,
+        out_specs=out_specs or tuple(vmem() for _ in out_shape),
+        scratch_shapes=scratch,
+        compiler_params=pltpu.CompilerParams(vmem_limit_bytes=32 * 1024 * 1024),
+        name=name,
+    )(*args)
+
+
+def work_shapes(tile_count, pixels, listed):
+    square = (tile_count, pixels, listed)
+    return [
+        pltpu.VMEM(square, F32),
+        pltpu.VMEM(square, F32),
+        pltpu.VMEM(square, F32),
+        pltpu.VMEM(square, BF16),
+        pltpu.VMEM(square, BF16),
+        pltpu.VMEM((2, tile_count, ROWS, listed), F32),
+    ]
+
+
+def near(tile_ids, cameras, where, own, other, parts, tile_count):
     width = sum(part.shape[1] for part in parts)
     features = parts[0].shape[0]
     slabs = width // LANES
-    pixels = listed = infos[0].shape[1] // tile_count
-    square = (tile_count, pixels, listed)
-    groups = len(infos)
-    packet = jax.ShapeDtypeStruct((ROWS, parts[0].shape[1]), F32)
-    out = pl.pallas_call(
-        functools.partial(render_kernel, len(parts), groups, blocks),
-        out_shape=(jax.ShapeDtypeStruct((3, tile_count * pixels), F32),) + (packet,) * len(parts),
-        in_specs=[smem()] * 3 + [vmem()] * (len(parts) + groups),
-        out_specs=(vmem(),) * (1 + len(parts)),
-        scratch_shapes=[
-            pltpu.VMEM((features * slabs, LANES), F32),
-            pltpu.VMEM((ROWS * slabs, LANES), F32),
-            pltpu.VMEM(square, F32),
-            pltpu.VMEM(square, F32),
-            pltpu.VMEM(square, F32),
-            pltpu.VMEM(square, BF16),
-            pltpu.VMEM(square, BF16),
-            pltpu.VMEM((groups, tile_count, ROWS, listed), F32),
-            pltpu.VMEM((groups,) + infos[0].shape, F32),
-        ],
-        compiler_params=pltpu.CompilerParams(vmem_limit_bytes=32 * 1024 * 1024),
-        name="render",
-    )(tile_ids, cameras, where, *parts, *infos)
-    return out[0], list(out[1:])
+    pixels = listed = own.shape[1] // tile_count
+    return call(
+        functools.partial(near_kernel, len(parts)),
+        "near",
+        (
+            jax.ShapeDtypeStruct((3, own.shape[1]), F32),
+            jax.ShapeDtypeStruct((ROWS * slabs, LANES), F32),
+            jax.ShapeDtypeStruct((ROWS, width), F32),
+        ),
+        [smem()] * 3 + [vmem()] * (2 + len(parts)),
+        [pltpu.VMEM((features * slabs, LANES), F32), pltpu.VMEM((2,) + own.shape, F32)]
+        + work_shapes(tile_count, pixels, listed),
+        (tile_ids, cameras, where, own, other, *parts),
+    )
+
+
+def far(tile_ids, where, rows, partial, infos, pieces, tile_count, blocks):
+    width = partial.shape[1]
+    pixels = listed = infos.shape[1] // tile_count
+    info = (infos.shape[0] // 2, infos.shape[1])
+    return call(
+        functools.partial(far_kernel, blocks),
+        "far",
+        (jax.ShapeDtypeStruct((ROWS, width // pieces), F32),) * pieces,
+        [smem()] * 2 + [vmem()] * 3,
+        [pltpu.VMEM((2,) + info, F32)] + work_shapes(tile_count, pixels, listed),
+        (tile_ids, where, rows, partial, infos),
+    )
+
+
+def join(first, second):
+    shape = (2 * first.shape[0], first.shape[1])
+    return call(
+        join_kernel, "join", (jax.ShapeDtypeStruct(shape, F32),), [vmem()] * 2, [], (first, second)
+    )[0]
 
 
 def update(where, cameras, params, adam_m, adam_v, packets):
     features, width = params.shape
     slabs = width // LANES
     shape = jax.ShapeDtypeStruct(params.shape, F32)
-    return pl.pallas_call(
+    return call(
         functools.partial(update_kernel, len(packets)),
-        out_shape=(shape, shape, shape),
-        in_specs=[smem()] * 2 + [vmem()] * (3 + len(packets)),
-        out_specs=(vmem(), vmem(), vmem()),
-        scratch_shapes=[
+        "update",
+        (shape, shape, shape),
+        [smem()] * 2 + [vmem()] * len(packets) + [any_space()] * 3,
+        [
             pltpu.VMEM((features * slabs, LANES), F32),
             pltpu.VMEM((ROWS * slabs, LANES), F32),
             pltpu.VMEM((features * slabs, LANES), F32),
+            pltpu.VMEM((3,) + params.shape, F32),
+            pltpu.VMEM((3,) + params.shape, F32),
+            pltpu.SemaphoreType.DMA((3,)),
+            pltpu.SemaphoreType.DMA((3, (features + 15) // 16)),
         ],
-        compiler_params=pltpu.CompilerParams(vmem_limit_bytes=32 * 1024 * 1024),
-        name="update",
-    )(where, cameras, params, adam_m, adam_v, *packets)
+        (where, cameras, *packets, params, adam_m, adam_v),
+        (any_space(),) * 3,
+    )
 
 
 def swap(value, axis, d):
@@ -613,23 +699,23 @@
     seat = lax.axis_index("tile")
     aligned = chunk % LANES == 0
     team = BLOCK_TILES // tile_count
+    assert team == 4
     blocks = along // team
 
-    if aligned:
-        parts = cut(group, params, shards)
-    else:
+    info, parts = pack(group, params, target, hit_shard, hit_local, shards, aligned)
+    if not aligned:
         parts = [
             lax.dynamic_slice_in_dim(params, (group ^ d) * chunk, chunk, axis=1)
             for d in range(shards)
         ]
-    info = pack(group, width, target, hit_shard, hit_local, shards, parts[0])
     parts = [swap(parts[d], "gs", d) for d in range(shards)]
-    info, parts[1] = lax.optimization_barrier((info, parts[1]))
-    infos = [swap(info, "tile", d) for d in range(team)]
+    beside = swap(info, "tile", 1)
+    beyond = swap(join(info, beside), "tile", 2)
     if not aligned:
         parts = [jnp.concatenate(parts, axis=1)]
     where = jnp.stack([seat % team, seat // team, jnp.int32(chunk)]).astype(jnp.int32)
-    rendered, packets = render(tile_ids, cameras, where, parts, infos, tile_count, blocks)
+    rendered, rows, partial = near(tile_ids, cameras, where, info, beside, parts, tile_count)
+    packets = far(tile_ids, where, rows, partial, beyond, len(parts), tile_count, blocks)
     if not aligned:
         packets = [packets[0][:, d * chunk : (d + 1) * chunk] for d in range(shards)]
     packets = [swap(packets[d], "gs", d) for d in range(shards)]

time: 30.5 us -> 28.7 us (0.941)
  waiting for transfers between devices: 6.72 us -> 3.7 us
  Pallas kernels: 11.4 us -> 11.9 us
  local copies, waits for them, and re-layouts: 1.93 us -> 2.33 us
    ppermute x9 -> x8, waiting for transfers between devices: 6.72 us -> 3.7 us  [swap(): lax.ppermute(value, axis, [(k, k ^ d) for k in range(lax.axis_size(axis))])]
    pallas_call x4 -> x5, Pallas kernels: 11.4 us -> 11.9 us  [call(): pl.pallas_call(kernel, out_shape=out_shape, in_specs=in_specs, out_specs=...]
    unnamed x18, local copies, waits for them, and re-layouts: 1.93 us -> 2.33 us
    ppermute x9 -> x8, starting transfers between devices: 9.56 us -> 9.73 us  [swap(): lax.ppermute(value, axis, [(k, k ^ d) for k in range(lax.axis_size(axis))])]
  transfers between devices with their start and end apart: 9 -> 8, of which waited for: 4 -> 3; matrix products, arithmetic and copies ran while one was open for 0% -> 0% of each run, Pallas kernels for 1% -> 17%
where the time goes in v4:
time: 28.7 us; the launch traced here: 28.4 us
  Pallas kernels  11.9 us (41%)
  starting transfers between devices  9.73 us (34%)
  waiting for transfers between devices  3.7 us (13%)
  local copies, waits for them, and re-layouts  2.33 us (8%)
  between operations  0.72 us (3%)
    pallas_call x5, Pallas kernels, call(): pl.pallas_call(kernel, out_shape=out_shape, in_specs=in_specs, out_specs=...  11.9 us
    ppermute x8, starting transfers between devices, swap(): lax.ppermute(value, axis, [(k, k ^ d) for k in range(lax.axis_size(axis))])  9.73 us
    ppermute x8, waiting for transfers between devices, swap(): lax.ppermute(value, axis, [(k, k ^ d) for k in range(lax.axis_size(axis))])  3.7 us
    unnamed x18, local copies, waits for them, and re-layouts  2.33 us
  transfers between devices with their start and end apart: 8, of which 3 were waited for; matrix products, arithmetic and copies ran while one was open for 0% of the time, Pallas kernels for 17%

profile of v4, /device:TPU:0, one launch (start us, length us, event | category | flops | bytes accessed | tf_op | source)
XLA Modules:
  0.0 28.4 jit_solution(9469947260461301896)
XLA Ops:
  0.6 0.0 copy-start.5
  0.6 0.0 copy-start.6
  0.7 0.7 %copy-done.5 = f32[3,512]{1,0:T(4,128)S(1)} copy-done((f32[3,512]{1,0:T(4,128)S(1)}, f32[3,512]{1,0:T(4,128)}, u32[]{:S(2)}) %copy-start.5) | copy-done | bytes 6168
  1.3 0.0 copy-done.6
  1.3 0.0 copy-start
  1.3 0.9 %copy-done = f32[59,1024]{1,0:T(8,128)S(1)} copy-done((f32[59,1024]{1,0:T(8,128)S(1)}, f32[59,1024]{1,0:T(8,128)}, u32[]{:S(2)}) %copy-start) | copy-done | bytes 241688
  2.3 0.0 copy-start.7
  2.3 0.7 %copy-done.7 = s32[2,256]{1,0:T(2,128)S(1)} copy-done((s32[2,256]{1,0:T(2,128)S(1)}, s32[2,256]{1,0:T(2,128)}, u32[]{:S(2)}) %copy-start.7) | copy-done | bytes 2072
  3.0 0.0 copy-start.3
  3.0 0.4 %pack.1 = (f32[8,512]{1,0:T(8,128)S(1)}, f32[59,256]{1,0:T(8,128)S(1)}, f32[59,256]{1,0:T(8,128)S(1)}, f32[59,256]{1,0:T(8,128)S(1)}, f32[59,256]{1,0:T(8,128)S(1)}) custom-call(s32[1]{0:T(128)} %bitcast.2.where, s32[2,1,256]{2,1,0:T(1,128)S(1)} %bitcast.4, s32[2,256]{1,0:T(2,128)S(1)} %copy-done.7, f32[3,512]{1,0:T(4,128)S(1)} %copy-done.5, ...), custom_call_target="tpu_custom_call" | custom-call | tf_op jit(solution)/shard_map/pack/pallas_call | solution.py:599
  3.3 3.1 %collective-permute-start = (f32[8,512]{1,0:T(8,128)S(1)}, f32[8,512]{1,0:T(8,128)S(1)}, u32[]{:S(2)}, u32[]{:S(2)}) collective-permute-start(f32[8,512]{1,0:T(8,128)S(1)} %get-tuple-element.19.own.first), channel_id=1, source_target_pairs={{0,1},{1,0},{2,3},{3,2},{4,5},{5,4},{6,7},{7,6},{8,9},{9,8},{10,11... | collective-permute-start | bytes 49160 | tf_op jit(solution)/shard_map/ppermute | solution.py:689
  6.4 0.0 collective-permute-start.1
  6.4 1.5 %collective-permute-start.2 = (f32[59,256]{1,0:T(8,128)S(1)}, f32[59,256]{1,0:T(8,128)S(1)}, u32[]{:S(2)}, u32[]{:S(2)}) collective-permute-start(f32[59,256]{1,0:T(8,128)S(1)} %get-tuple-element.22), channel_id=1, source_target_pairs={{0,8},{4,12},{8,0},{12,4},{1,9},{5,13},{9,1},{13,5},{2,10},{6,14},... | collective-permute-start | bytes 181256 | tf_op jit(solution)/shard_map/ppermute | solution.py:689
  7.9 0.4 %collective-permute-start.3 = (f32[59,256]{1,0:T(8,128)S(1)}, f32[59,256]{1,0:T(8,128)S(1)}, u32[]{:S(2)}, u32[]{:S(2)}) collective-permute-start(f32[59,256]{1,0:T(8,128)S(1)} %get-tuple-element.23), channel_id=1, source_target_pairs={{0,12},{4,8},{8,4},{12,0},{1,13},{5,9},{9,5},{13,1},{2,14},{6,10},... | collective-permute-start | bytes 181256 | tf_op jit(solution)/shard_map/ppermute | solution.py:689
  8.3 0.0 copy-start.4
  8.3 0.0 copy-start.8
  8.3 0.0 copy-start.1
  8.3 0.0 copy-start.2
  8.3 0.0 collective-permute-done.other.second
  8.3 2.9 %collective-permute-start.4 = (f32[16,512]{1,0:T(8,128)S(1)}, f32[16,512]{1,0:T(8,128)S(1)}, u32[]{:S(2)}, u32[]{:S(2)}) collective-permute-start(f32[16,512]{1,0:T(8,128)S(1)} %join.1), channel_id=1, source_target_pairs={{0,2},{1,3},{2,0},{3,1},{4,6},{5,7},{6,4},{7,5},{8,10},{9,11},{10,... | collective-permute-start | bytes 98312 | tf_op jit(solution)/shard_map/ppermute | solution.py:689
  11.2 0.1 pad_add_fusion.where
  11.3 0.0 collective-permute-done.1.refs_1_
  11.3 0.0 collective-permute-done.2.refs_2_
  11.3 0.8 %collective-permute-done.3.refs_3_ = f32[59,256]{1,0:T(8,128)S(1)} collective-permute-done((f32[59,256]{1,0:T(8,128)S(1)}, f32[59,256]{1,0:T(8,128)S(1)}, u32[]{:S(2)}, u32[]{:S(2)}) %collective-permute-start.3) | collective-permute-done | bytes 60448 | tf_op jit(solution)/shard_map/ppermute | solution.py:689
  12.1 0.0 copy-done.4
  12.1 0.0 copy-done.8
  12.1 4.9 %near.1 = (f32[3,512]{1,0:T(4,128)}, f32[128,128]{1,0:T(8,128)S(1)}, f32[16,1024]{1,0:T(8,128)S(1)}) custom-call(s32[2]{0:T(128)S(1)} %copy-done.8, f32[4,12]{1,0:T(4,128)S(1)} %copy-done.4, s32[3]{0:T(128)S(1)} %pad_add_fusion.where, f32[8,512]{1,0:T(8,128)S(1)} %get-tuple-element.19.own.first, f32[8,512]{1,0:T(8,128)S(1)} %collective-permute-done.other.second, ...), custom_call_target="tpu_custom_call" | custom-call | tf_op jit(solution)/shard_map/near/pallas_call | solution.py:599
  17.0 0.0 collective-permute-done.4.infos
  17.0 4.7 %far.1 = (f32[16,256]{1,0:T(8,128)S(1)}, f32[16,256]{1,0:T(8,128)S(1)}, f32[16,256]{1,0:T(8,128)S(1)}, f32[16,256]{1,0:T(8,128)S(1)}) custom-call(s32[2]{0:T(128)S(1)} %copy-done.8, s32[3]{0:T(128)S(1)} %pad_add_fusion.where, f32[128,128]{1,0:T(8,128)S(1)} %get-tuple-element.25.rows, f32[16,1024]{1,0:T(8,128)S(1)} %get-tuple-element.26.partial, ...), custom_call_target="tpu_custom_call" | custom-call | tf_op jit(solution)/shard_map/far/pallas_call | solution.py:599
  21.7 0.2 collective-permute-start.5
  21.9 1.5 %collective-permute-start.6 = (f32[16,256]{1,0:T(8,128)S(1)}, f32[16,256]{1,0:T(8,128)S(1)}, u32[]{:S(2)}, u32[]{:S(2)}) collective-permute-start(f32[16,256]{1,0:T(8,128)S(1)} %get-tuple-element.29), channel_id=1, source_target_pairs={{0,8},{4,12},{8,0},{12,4},{1,9},{5,13},{9,1},{13,5},{2,10},{6,14},... | collective-permute-start | bytes 49160 | tf_op jit(solution)/shard_map/ppermute | solution.py:689
  23.4 0.3 collective-permute-start.7
  23.6 0.0 collective-permute-done.5.refs_1_
  23.6 2.0 %collective-permute-done.6.refs_2_ = f32[16,256]{1,0:T(8,128)S(1)} collective-permute-done((f32[16,256]{1,0:T(8,128)S(1)}, f32[16,256]{1,0:T(8,128)S(1)}, u32[]{:S(2)}, u32[]{:S(2)}) %collective-permute-start.6) | collective-permute-done | bytes 16416 | tf_op jit(solution)/shard_map/ppermute | solution.py:689
  25.7 0.9 %collective-permute-done.7.refs_3_ = f32[16,256]{1,0:T(8,128)S(1)} collective-permute-done((f32[16,256]{1,0:T(8,128)S(1)}, f32[16,256]{1,0:T(8,128)S(1)}, u32[]{:S(2)}, u32[]{:S(2)}) %collective-permute-start.7) | collective-permute-done | bytes 16416 | tf_op jit(solution)/shard_map/ppermute | solution.py:689
  26.6 0.0 copy-done.3
  26.6 0.0 copy-done.1
  26.6 0.0 copy-done.2
  26.6 1.9 %update.1 = (f32[59,1024]{1,0:T(8,128)}, f32[59,1024]{1,0:T(8,128)}, f32[59,1024]{1,0:T(8,128)}) custom-call(s32[1]{0:T(128)} %bitcast.2.where, f32[4,12]{1,0:T(4,128)S(1)} %copy-done.4, f32[16,256]{1,0:T(8,128)S(1)} %get-tuple-element.27.refs_0_, f32[16,256]{1,0:T(8,128)S(1)} %collective-permute-done.5.refs_1_, ...), custom_call_target="tpu_custom_call" | custom-call | tf_op jit(solution)/shard_map/update/pallas_call | solution.py:599
  (1 shorter events, 0.0 us)
Async XLA Ops:
  0.6 0.7 %copy-start.5 = (f32[3,512]{1,0:T(4,128)S(1)}, f32[3,512]{1,0:T(4,128)}, u32[]{:S(2)}) copy-start(f32[3,512]{1,0:T(4,128)} %refs_2_.1) | copy-start | bytes 18436
  0.6 0.7 %copy-start.6 = (s32[2,256,1]{1,2,0:T(1,128)S(1)}, s32[2,256,1]{1,2,0:T(1,128)}, u32[]{:S(2)}) copy-start(s32[2,256,1]{1,2,0:T(1,128)} %param.14) | copy-start | bytes 6148
  1.3 1.0 %copy-start = (f32[59,1024]{1,0:T(8,128)S(1)}, f32[59,1024]{1,0:T(8,128)}, u32[]{:S(2)}) copy-start(f32[59,1024]{1,0:T(8,128)} %refs_4_.1) | copy-start | bytes 724996
  2.3 0.7 %copy-start.7 = (s32[2,256]{1,0:T(2,128)S(1)}, s32[2,256]{1,0:T(2,128)}, u32[]{:S(2)}) copy-start(s32[2,256]{1,0:T(2,128)} %refs_1_.1) | copy-start | bytes 6148
  3.0 23.6 %copy-start.3 = (f32[59,1024]{1,0:T(8,128)S(1)}, f32[59,1024]{1,0:T(8,128)}, u32[]{:S(2)}) copy-start(f32[59,1024]{1,0:T(8,128)} %refs_6_.1) | copy-start | bytes 724996
  3.3 5.0 %collective-permute-start = (f32[8,512]{1,0:T(8,128)S(1)}, f32[8,512]{1,0:T(8,128)S(1)}, u32[]{:S(2)}, u32[]{:S(2)}) collective-permute-start(f32[8,512]{1,0:T(8,128)S(1)} %get-tuple-element.19.own.first), channel_id=1, source_target_pairs={{0,1},{1,0},{2,3},{3,2},{4,5},{5,4},{6,7},{7,6},{8,9},{9,8},{10,11... | collective-permute-start | bytes 49160 | tf_op jit(solution)/shard_map/ppermute | solution.py:689
  6.4 4.8 %collective-permute-start.1 = (f32[59,256]{1,0:T(8,128)S(1)}, f32[59,256]{1,0:T(8,128)S(1)}, u32[]{:S(2)}, u32[]{:S(2)}) collective-permute-start(f32[59,256]{1,0:T(8,128)S(1)} %get-tuple-element.21), channel_id=1, source_target_pairs={{0,4},{4,0},{8,12},{12,8},{1,5},{5,1},{9,13},{13,9},{2,6},{6,2},{1... | collective-permute-start | bytes 181256 | tf_op jit(solution)/shard_map/ppermute | solution.py:689
  6.4 4.8 %collective-permute-start.2 = (f32[59,256]{1,0:T(8,128)S(1)}, f32[59,256]{1,0:T(8,128)S(1)}, u32[]{:S(2)}, u32[]{:S(2)}) collective-permute-start(f32[59,256]{1,0:T(8,128)S(1)} %get-tuple-element.22), channel_id=1, source_target_pairs={{0,8},{4,12},{8,0},{12,4},{1,9},{5,13},{9,1},{13,5},{2,10},{6,14},... | collective-permute-start | bytes 181256 | tf_op jit(solution)/shard_map/ppermute | solution.py:689
  7.9 4.1 %collective-permute-start.3 = (f32[59,256]{1,0:T(8,128)S(1)}, f32[59,256]{1,0:T(8,128)S(1)}, u32[]{:S(2)}, u32[]{:S(2)}) collective-permute-start(f32[59,256]{1,0:T(8,128)S(1)} %get-tuple-element.23), channel_id=1, source_target_pairs={{0,12},{4,8},{8,4},{12,0},{1,13},{5,9},{9,5},{13,1},{2,14},{6,10},... | collective-permute-start | bytes 181256 | tf_op jit(solution)/shard_map/ppermute | solution.py:689
  8.3 3.8 %copy-start.4 = (f32[4,12]{1,0:T(4,128)S(1)}, f32[4,12]{1,0:T(4,128)}, u32[]{:S(2)}) copy-start(f32[4,12]{1,0:T(4,128)} %cams.3) | copy-start | bytes 580
  8.3 3.8 %copy-start.8 = (s32[2]{0:T(128)S(1)}, s32[2]{0:T(128)}, u32[]{:S(2)}) copy-start(s32[2]{0:T(128)} %tile_ids.3) | copy-start | bytes 28
  8.3 18.3 %copy-start.1 = (f32[59,1024]{1,0:T(8,128)S(1)}, f32[59,1024]{1,0:T(8,128)}, u32[]{:S(2)}) copy-start(f32[59,1024]{1,0:T(8,128)} %refs_4_.1) | copy-start | bytes 724996
  8.3 18.3 %copy-start.2 = (f32[59,1024]{1,0:T(8,128)S(1)}, f32[59,1024]{1,0:T(8,128)}, u32[]{:S(2)}) copy-start(f32[59,1024]{1,0:T(8,128)} %refs_5_.1) | copy-start | bytes 724996
  8.3 8.7 %collective-permute-start.4 = (f32[16,512]{1,0:T(8,128)S(1)}, f32[16,512]{1,0:T(8,128)S(1)}, u32[]{:S(2)}, u32[]{:S(2)}) collective-permute-start(f32[16,512]{1,0:T(8,128)S(1)} %join.1), channel_id=1, source_target_pairs={{0,2},{1,3},{2,0},{3,1},{4,6},{5,7},{6,4},{7,5},{8,10},{9,11},{10,... | collective-permute-start | bytes 98312 | tf_op jit(solution)/shard_map/ppermute | solution.py:689
  21.7 1.9 %collective-permute-start.5 = (f32[16,256]{1,0:T(8,128)S(1)}, f32[16,256]{1,0:T(8,128)S(1)}, u32[]{:S(2)}, u32[]{:S(2)}) collective-permute-start(f32[16,256]{1,0:T(8,128)S(1)} %get-tuple-element.28), channel_id=1, source_target_pairs={{0,4},{4,0},{8,12},{12,8},{1,5},{5,1},{9,13},{13,9},{2,6},{6,2},{1... | collective-permute-start | bytes 49160 | tf_op jit(solution)/shard_map/ppermute | solution.py:689
  21.9 3.8 %collective-permute-start.6 = (f32[16,256]{1,0:T(8,128)S(1)}, f32[16,256]{1,0:T(8,128)S(1)}, u32[]{:S(2)}, u32[]{:S(2)}) collective-permute-start(f32[16,256]{1,0:T(8,128)S(1)} %get-tuple-element.29), channel_id=1, source_target_pairs={{0,8},{4,12},{8,0},{12,4},{1,9},{5,13},{9,1},{13,5},{2,10},{6,14},... | collective-permute-start | bytes 49160 | tf_op jit(solution)/shard_map/ppermute | solution.py:689
  23.4 3.2 %collective-permute-start.7 = (f32[16,256]{1,0:T(8,128)S(1)}, f32[16,256]{1,0:T(8,128)S(1)}, u32[]{:S(2)}, u32[]{:S(2)}) collective-permute-start(f32[16,256]{1,0:T(8,128)S(1)} %get-tuple-element.30), channel_id=1, source_target_pairs={{0,12},{4,8},{8,4},{12,0},{1,13},{5,9},{9,5},{13,1},{2,14},{6,10},... | collective-permute-start | bytes 49160 | tf_op jit(solution)/shard_map/ppermute | solution.py:689

commit v5 on v4

--- a/solution.py
+++ b/solution.py
@@ -321,7 +321,7 @@
             pltpu.SemaphoreType.DMA((3,)),
             pltpu.SemaphoreType.DMA((shards,)),
         ],
-        (group.reshape(1),) + args,
+        (group.reshape(1),) + tuple(pltpu.with_memory_space_constraint(a, pltpu.HBM) for a in args),
     )
     return out[0], list(out[1:])
 
@@ -595,14 +595,14 @@
     return pl.BlockSpec(memory_space=pl.ANY)
 
 
-def call(kernel, name, out_shape, in_specs, scratch, args, out_specs=None):
+def call(kernel, name, out_shape, in_specs, scratch, args, out_specs=None, grant=32):
     return pl.pallas_call(
         kernel,
         out_shape=out_shape,
         in_specs=in_specs,
         out_specs=out_specs or tuple(vmem() for _ in out_shape),
         scratch_shapes=scratch,
-        compiler_params=pltpu.CompilerParams(vmem_limit_bytes=32 * 1024 * 1024),
+        compiler_params=pltpu.CompilerParams(vmem_limit_bytes=grant * 1024 * 1024),
         name=name,
     )(*args)
 

time: 28.7 us -> 27.1 us (0.944)
  local copies, waits for them, and re-layouts: 2.33 us -> 0.02 us
  Pallas kernels: 11.9 us -> 12.7 us
    unnamed x18 -> x10, local copies, waits for them, and re-layouts: 2.33 us -> 0.02 us
    pallas_call x5, Pallas kernels: 11.9 us -> 12.7 us  [call(): pl.pallas_call(kernel, out_shape=out_shape, in_specs=in_specs, out_specs=...]
  transfers between devices with their start and end apart: 8 -> 8, of which waited for: 3 -> 3; matrix products, arithmetic and copies ran while one was open for 0% -> 0% of each run, Pallas kernels for 17% -> 18%
where the time goes in v5:
time: 27.1 us; the launch traced here: 26.9 us
  Pallas kernels  12.7 us (47%)
  starting transfers between devices  9.73 us (36%)
  waiting for transfers between devices  3.7 us (14%)
  between operations  0.7 us (3%)
    pallas_call x5, Pallas kernels, call(): pl.pallas_call(kernel, out_shape=out_shape, in_specs=in_specs, out_specs=...  12.7 us
    ppermute x8, starting transfers between devices, swap(): lax.ppermute(value, axis, [(k, k ^ d) for k in range(lax.axis_size(axis))])  9.73 us
    ppermute x8, waiting for transfers between devices, swap(): lax.ppermute(value, axis, [(k, k ^ d) for k in range(lax.axis_size(axis))])  3.7 us
  transfers between devices with their start and end apart: 8, of which 3 were waited for; matrix products, arithmetic and copies ran while one was open for 0% of the time, Pallas kernels for 18%

profile of v5, /device:TPU:0, one launch (start us, length us, event | category | flops | bytes accessed | tf_op | source)
XLA Modules:
  0.0 26.9 jit_solution(4855276600187803111)
XLA Ops:
  0.6 0.0 copy-start.2
  0.6 1.2 %pack.1 = (f32[8,512]{1,0:T(8,128)S(1)}, f32[59,256]{1,0:T(8,128)S(1)}, f32[59,256]{1,0:T(8,128)S(1)}, f32[59,256]{1,0:T(8,128)S(1)}, f32[59,256]{1,0:T(8,128)S(1)}) custom-call(s32[1]{0:T(128)} %bitcast.2.where, s32[2,1,256]{2,1,0:T(1,128)} %bitcast.4, s32[2,256]{1,0:T(2,128)} %refs_1_.1, f32[3,512]{1,0:T(4,128)} %refs_2_.1, f32[59,1024]{1,0:T(8,128)} %refs_4_.1), custom_call_target="tpu_custom_call" | custom-call | tf_op jit(solution)/shard_map/pack/pallas_call | solution.py:599
  1.8 3.1 %collective-permute-start = (f32[8,512]{1,0:T(8,128)S(1)}, f32[8,512]{1,0:T(8,128)S(1)}, u32[]{:S(2)}, u32[]{:S(2)}) collective-permute-start(f32[8,512]{1,0:T(8,128)S(1)} %get-tuple-element.19.own.first), channel_id=1, source_target_pairs={{0,1},{1,0},{2,3},{3,2},{4,5},{5,4},{6,7},{7,6},{8,9},{9,8},{10,11... | collective-permute-start | bytes 49160 | tf_op jit(solution)/shard_map/ppermute | solution.py:689
  4.9 0.0 collective-permute-start.1
  4.9 1.5 %collective-permute-start.2 = (f32[59,256]{1,0:T(8,128)S(1)}, f32[59,256]{1,0:T(8,128)S(1)}, u32[]{:S(2)}, u32[]{:S(2)}) collective-permute-start(f32[59,256]{1,0:T(8,128)S(1)} %get-tuple-element.22), channel_id=1, source_target_pairs={{0,8},{4,12},{8,0},{12,4},{1,9},{5,13},{9,1},{13,5},{2,10},{6,14},... | collective-permute-start | bytes 181256 | tf_op jit(solution)/shard_map/ppermute | solution.py:689
  6.4 0.4 %collective-permute-start.3 = (f32[59,256]{1,0:T(8,128)S(1)}, f32[59,256]{1,0:T(8,128)S(1)}, u32[]{:S(2)}, u32[]{:S(2)}) collective-permute-start(f32[59,256]{1,0:T(8,128)S(1)} %get-tuple-element.23), channel_id=1, source_target_pairs={{0,12},{4,8},{8,4},{12,0},{1,13},{5,9},{9,5},{13,1},{2,14},{6,10},... | collective-permute-start | bytes 181256 | tf_op jit(solution)/shard_map/ppermute | solution.py:689
  6.8 0.0 copy-start.3
  6.8 0.0 copy-start.4
  6.8 0.0 copy-start
  6.8 0.0 copy-start.1
  6.8 0.0 collective-permute-done.other.second
  6.8 2.9 %collective-permute-start.4 = (f32[16,512]{1,0:T(8,128)S(1)}, f32[16,512]{1,0:T(8,128)S(1)}, u32[]{:S(2)}, u32[]{:S(2)}) collective-permute-start(f32[16,512]{1,0:T(8,128)S(1)} %join.1), channel_id=1, source_target_pairs={{0,2},{1,3},{2,0},{3,1},{4,6},{5,7},{6,4},{7,5},{8,10},{9,11},{10,... | collective-permute-start | bytes 98312 | tf_op jit(solution)/shard_map/ppermute | solution.py:689
  9.7 0.1 pad_add_fusion.where
  9.8 0.0 collective-permute-done.1.refs_1_
  9.8 0.0 collective-permute-done.2.refs_2_
  9.8 0.8 %collective-permute-done.3.refs_3_ = f32[59,256]{1,0:T(8,128)S(1)} collective-permute-done((f32[59,256]{1,0:T(8,128)S(1)}, f32[59,256]{1,0:T(8,128)S(1)}, u32[]{:S(2)}, u32[]{:S(2)}) %collective-permute-start.3) | collective-permute-done | bytes 60448 | tf_op jit(solution)/shard_map/ppermute | solution.py:689
  10.5 0.0 copy-done.3
  10.5 0.0 copy-done.4
  10.6 4.9 %near.1 = (f32[3,512]{1,0:T(4,128)}, f32[128,128]{1,0:T(8,128)S(1)}, f32[16,1024]{1,0:T(8,128)S(1)}) custom-call(s32[2]{0:T(128)S(1)} %copy-done.4, f32[4,12]{1,0:T(4,128)S(1)} %copy-done.3, s32[3]{0:T(128)S(1)} %pad_add_fusion.where, f32[8,512]{1,0:T(8,128)S(1)} %get-tuple-element.19.own.first, f32[8,512]{1,0:T(8,128)S(1)} %collective-permute-done.other.second, ...), custom_call_target="tpu_custom_call" | custom-call | tf_op jit(solution)/shard_map/near/pallas_call | solution.py:599
  15.5 0.0 collective-permute-done.4.infos
  15.5 4.7 %far.1 = (f32[16,256]{1,0:T(8,128)S(1)}, f32[16,256]{1,0:T(8,128)S(1)}, f32[16,256]{1,0:T(8,128)S(1)}, f32[16,256]{1,0:T(8,128)S(1)}) custom-call(s32[2]{0:T(128)S(1)} %copy-done.4, s32[3]{0:T(128)S(1)} %pad_add_fusion.where, f32[128,128]{1,0:T(8,128)S(1)} %get-tuple-element.25.rows, f32[16,1024]{1,0:T(8,128)S(1)} %get-tuple-element.26.partial, ...), custom_call_target="tpu_custom_call" | custom-call | tf_op jit(solution)/shard_map/far/pallas_call | solution.py:599
  20.2 0.2 collective-permute-start.5
  20.4 1.5 %collective-permute-start.6 = (f32[16,256]{1,0:T(8,128)S(1)}, f32[16,256]{1,0:T(8,128)S(1)}, u32[]{:S(2)}, u32[]{:S(2)}) collective-permute-start(f32[16,256]{1,0:T(8,128)S(1)} %get-tuple-element.29), channel_id=1, source_target_pairs={{0,8},{4,12},{8,0},{12,4},{1,9},{5,13},{9,1},{13,5},{2,10},{6,14},... | collective-permute-start | bytes 49160 | tf_op jit(solution)/shard_map/ppermute | solution.py:689
  21.9 0.2 collective-permute-start.7
  22.1 0.0 collective-permute-done.5.refs_1_
  22.1 2.0 %collective-permute-done.6.refs_2_ = f32[16,256]{1,0:T(8,128)S(1)} collective-permute-done((f32[16,256]{1,0:T(8,128)S(1)}, f32[16,256]{1,0:T(8,128)S(1)}, u32[]{:S(2)}, u32[]{:S(2)}) %collective-permute-start.6) | collective-permute-done | bytes 16416 | tf_op jit(solution)/shard_map/ppermute | solution.py:689
  24.2 0.9 %collective-permute-done.7.refs_3_ = f32[16,256]{1,0:T(8,128)S(1)} collective-permute-done((f32[16,256]{1,0:T(8,128)S(1)}, f32[16,256]{1,0:T(8,128)S(1)}, u32[]{:S(2)}, u32[]{:S(2)}) %collective-permute-start.7) | collective-permute-done | bytes 16416 | tf_op jit(solution)/shard_map/ppermute | solution.py:689
  25.1 0.0 copy-done.2
  25.1 0.0 copy-done
  25.1 0.0 copy-done.1
  25.1 1.9 %update.1 = (f32[59,1024]{1,0:T(8,128)}, f32[59,1024]{1,0:T(8,128)}, f32[59,1024]{1,0:T(8,128)}) custom-call(s32[1]{0:T(128)} %bitcast.2.where, f32[4,12]{1,0:T(4,128)S(1)} %copy-done.3, f32[16,256]{1,0:T(8,128)S(1)} %get-tuple-element.27.refs_0_, f32[16,256]{1,0:T(8,128)S(1)} %collective-permute-done.5.refs_1_, ...), custom_call_target="tpu_custom_call" | custom-call | tf_op jit(solution)/shard_map/update/pallas_call | solution.py:599
  (1 shorter events, 0.0 us)
Async XLA Ops:
  0.6 24.4 %copy-start.2 = (f32[59,1024]{1,0:T(8,128)S(1)}, f32[59,1024]{1,0:T(8,128)}, u32[]{:S(2)}) copy-start(f32[59,1024]{1,0:T(8,128)} %refs_6_.1) | copy-start | bytes 724996
  1.8 5.0 %collective-permute-start = (f32[8,512]{1,0:T(8,128)S(1)}, f32[8,512]{1,0:T(8,128)S(1)}, u32[]{:S(2)}, u32[]{:S(2)}) collective-permute-start(f32[8,512]{1,0:T(8,128)S(1)} %get-tuple-element.19.own.first), channel_id=1, source_target_pairs={{0,1},{1,0},{2,3},{3,2},{4,5},{5,4},{6,7},{7,6},{8,9},{9,8},{10,11... | collective-permute-start | bytes 49160 | tf_op jit(solution)/shard_map/ppermute | solution.py:689
  4.9 4.8 %collective-permute-start.1 = (f32[59,256]{1,0:T(8,128)S(1)}, f32[59,256]{1,0:T(8,128)S(1)}, u32[]{:S(2)}, u32[]{:S(2)}) collective-permute-start(f32[59,256]{1,0:T(8,128)S(1)} %get-tuple-element.21), channel_id=1, source_target_pairs={{0,4},{4,0},{8,12},{12,8},{1,5},{5,1},{9,13},{13,9},{2,6},{6,2},{1... | collective-permute-start | bytes 181256 | tf_op jit(solution)/shard_map/ppermute | solution.py:689
  4.9 4.8 %collective-permute-start.2 = (f32[59,256]{1,0:T(8,128)S(1)}, f32[59,256]{1,0:T(8,128)S(1)}, u32[]{:S(2)}, u32[]{:S(2)}) collective-permute-start(f32[59,256]{1,0:T(8,128)S(1)} %get-tuple-element.22), channel_id=1, source_target_pairs={{0,8},{4,12},{8,0},{12,4},{1,9},{5,13},{9,1},{13,5},{2,10},{6,14},... | collective-permute-start | bytes 181256 | tf_op jit(solution)/shard_map/ppermute | solution.py:689
  6.4 4.1 %collective-permute-start.3 = (f32[59,256]{1,0:T(8,128)S(1)}, f32[59,256]{1,0:T(8,128)S(1)}, u32[]{:S(2)}, u32[]{:S(2)}) collective-permute-start(f32[59,256]{1,0:T(8,128)S(1)} %get-tuple-element.23), channel_id=1, source_target_pairs={{0,12},{4,8},{8,4},{12,0},{1,13},{5,9},{9,5},{13,1},{2,14},{6,10},... | collective-permute-start | bytes 181256 | tf_op jit(solution)/shard_map/ppermute | solution.py:689
  6.8 3.8 %copy-start.3 = (f32[4,12]{1,0:T(4,128)S(1)}, f32[4,12]{1,0:T(4,128)}, u32[]{:S(2)}) copy-start(f32[4,12]{1,0:T(4,128)} %cams.3) | copy-start | bytes 580
  6.8 3.8 %copy-start.4 = (s32[2]{0:T(128)S(1)}, s32[2]{0:T(128)}, u32[]{:S(2)}) copy-start(s32[2]{0:T(128)} %tile_ids.3) | copy-start | bytes 28
  6.8 18.3 %copy-start = (f32[59,1024]{1,0:T(8,128)S(1)}, f32[59,1024]{1,0:T(8,128)}, u32[]{:S(2)}) copy-start(f32[59,1024]{1,0:T(8,128)} %refs_4_.1) | copy-start | bytes 724996
  6.8 18.3 %copy-start.1 = (f32[59,1024]{1,0:T(8,128)S(1)}, f32[59,1024]{1,0:T(8,128)}, u32[]{:S(2)}) copy-start(f32[59,1024]{1,0:T(8,128)} %refs_5_.1) | copy-start | bytes 724996
  6.8 8.7 %collective-permute-start.4 = (f32[16,512]{1,0:T(8,128)S(1)}, f32[16,512]{1,0:T(8,128)S(1)}, u32[]{:S(2)}, u32[]{:S(2)}) collective-permute-start(f32[16,512]{1,0:T(8,128)S(1)} %join.1), channel_id=1, source_target_pairs={{0,2},{1,3},{2,0},{3,1},{4,6},{5,7},{6,4},{7,5},{8,10},{9,11},{10,... | collective-permute-start | bytes 98312 | tf_op jit(solution)/shard_map/ppermute | solution.py:689
  20.2 1.9 %collective-permute-start.5 = (f32[16,256]{1,0:T(8,128)S(1)}, f32[16,256]{1,0:T(8,128)S(1)}, u32[]{:S(2)}, u32[]{:S(2)}) collective-permute-start(f32[16,256]{1,0:T(8,128)S(1)} %get-tuple-element.28), channel_id=1, source_target_pairs={{0,4},{4,0},{8,12},{12,8},{1,5},{5,1},{9,13},{13,9},{2,6},{6,2},{1... | collective-permute-start | bytes 49160 | tf_op jit(solution)/shard_map/ppermute | solution.py:689
  20.4 3.8 %collective-permute-start.6 = (f32[16,256]{1,0:T(8,128)S(1)}, f32[16,256]{1,0:T(8,128)S(1)}, u32[]{:S(2)}, u32[]{:S(2)}) collective-permute-start(f32[16,256]{1,0:T(8,128)S(1)} %get-tuple-element.29), channel_id=1, source_target_pairs={{0,8},{4,12},{8,0},{12,4},{1,9},{5,13},{9,1},{13,5},{2,10},{6,14},... | collective-permute-start | bytes 49160 | tf_op jit(solution)/shard_map/ppermute | solution.py:689
  21.9 3.2 %collective-permute-start.7 = (f32[16,256]{1,0:T(8,128)S(1)}, f32[16,256]{1,0:T(8,128)S(1)}, u32[]{:S(2)}, u32[]{:S(2)}) collective-permute-start(f32[16,256]{1,0:T(8,128)S(1)} %get-tuple-element.30), channel_id=1, source_target_pairs={{0,12},{4,8},{8,4},{12,0},{1,13},{5,9},{9,5},{13,1},{2,14},{6,10},... | collective-permute-start | bytes 49160 | tf_op jit(solution)/shard_map/ppermute | solution.py:689

commit v6 on v5

--- a/solution.py
+++ b/solution.py
@@ -136,12 +136,11 @@
     cov_yy = sum(wide[1][k] * axes[1][k] for k in range(3)) + dilation
     rdet = 1.0 / (cov_xx * cov_yy - cov_xy * cov_xy)
     conic = (cov_yy * rdet, -cov_xy * rdet, cov_xx * rdet)
-    opacity = 1.0 / (1.0 + jnp.exp(-feat(10)))
     rlen = lax.rsqrt(off[0] * off[0] + off[1] * off[1] + off[2] * off[2])
     way = [off[a] * rlen for a in range(3)]
     return dict(
         rot=rot, inv=inv, u=u, v=v, finv=finv, scale=scale, rnorm=rnorm, rotor=(w, x, y, z), turn=turn,
-        screen=screen, axes=axes, wide=wide, conic=conic, opacity=opacity, rlen=rlen, way=way,
+        screen=screen, axes=axes, wide=wide, conic=conic, rlen=rlen, way=way,
     )
 
 
@@ -156,7 +155,9 @@
         colours.append(total)
     mean_x = focal_length * part["u"] + center_x
     mean_y = focal_length * part["v"] + center_y
-    return [mean_x, mean_y, *part["conic"], part["opacity"], *colours]
+    logit = feat(10)
+    log_opacity = jnp.minimum(logit, 0.0) - jnp.log(1.0 + jnp.exp(-jnp.abs(logit)))
+    return [mean_x, mean_y, *part["conic"], log_opacity, *colours]
 
 
 def project_pull(feat, cam, grads, put):
@@ -177,7 +178,7 @@
     g_way = sh_pull(pulled, *way)
     along = way[0] * g_way[0] + way[1] * g_way[1] + way[2] * g_way[2]
     g_off = [(g_way[a] - way[a] * along) * rlen for a in range(3)]
-    put(10, g_o * part["opacity"] * (1.0 - part["opacity"]))
+    put(10, g_o / (1.0 + jnp.exp(feat(10))))
     a, b, c = part["conic"]
     g_xx = -(a * a * g_a + a * b * g_b + b * b * g_c)
     g_xy = -(2.0 * a * b * g_a + (a * c + b * b) * g_b + 2.0 * b * c * g_c)
@@ -326,20 +327,32 @@
     return out[0], list(out[1:])
 
 
+def pixel_basis(pixels):
+    pixel = lax.broadcasted_iota(jnp.int32, (8, pixels), 1)
+    row = lax.broadcasted_iota(jnp.int32, (8, pixels), 0)
+    middle = 0.5 * TILE_SIDE - 0.5
+    u = (pixel % TILE_SIDE).astype(F32) - middle
+    v = (pixel // TILE_SIDE).astype(F32) - middle
+    value = jnp.where(row == 0, 1.0, 0.0)
+    for at, term in ((1, u), (2, v), (3, u * u), (4, u * v), (5, v * v)):
+        value = jnp.where(row == at, term, value)
+    return value
+
+
 def composite(tiles, first_group, me, rows, info_s, rendered, work):
-    e_s, t_s, d_s, hi_s, lo_s, acc_s = work
-    tile_count, pixels, listed = e_s.shape
+    alpha_s, weight_s, push_s, colour_s, goal_s, coef_s, mix_s, acc_s = work
+    groups, tile_count, _, listed = acc_s.shape
+    pixels = info_s.shape[2] // tile_count
+    parts = pixels // LANES
+    spans = groups * tile_count * parts
     slabs = rows.shape[0] // ROWS
     side = TILE_SIDE
     first_col, first_row = tiles
-    row_i = lax.broadcasted_iota(jnp.int32, (listed, listed), 0)
-    col_i = lax.broadcasted_iota(jnp.int32, (listed, listed), 1)
-    earlier = jnp.where(row_i < col_i, 1.0, 0.0).astype(BF16)
-    later = jnp.where(row_i > col_i, 1.0, 0.0).astype(BF16)
-    step = lax.broadcasted_iota(jnp.int32, (side, listed), 0).astype(F32)
-
-    def one_group(g, carry):
-        lists = []
+    basis = pixel_basis(pixels)
+    basis_3 = jnp.concatenate([basis, basis, basis], axis=0).astype(BF16)
+
+    means = []
+    for g in range(groups):
         for t in range(tile_count):
             halves = []
             for first in range(t * listed, (t + 1) * listed, LANES):
@@ -353,100 +366,121 @@
                     )
                     found = jnp.where(slab == s, here, found)
                 halves.append(found)
-            lists.append(jnp.concatenate(halves, axis=1))
-
-        setup = []
+            entry = jnp.concatenate(halves, axis=1)
+            slot = (me ^ (first_group + g)) * tile_count + t
+            mean_u = entry[0:1] - (((first_col + slot % 4) * side).astype(F32) + 0.5 * side)
+            mean_v = entry[1:2] - (((first_row + slot // 4) * side).astype(F32) + 0.5 * side)
+            quad_a, quad_b, quad_c = -0.5 * entry[2:3], -entry[3:4], -0.5 * entry[4:5]
+            means.append((mean_u, mean_v, quad_a, quad_b, quad_c))
+            slope_u = 2.0 * quad_a * mean_u + quad_b * mean_v
+            slope_v = 2.0 * quad_c * mean_v + quad_b * mean_u
+            level = 0.5 * (slope_u * mean_u + slope_v * mean_v) + entry[5:6]
+            zero = jnp.zeros_like(level)
+            coef = jnp.concatenate(
+                [level, -slope_u, -slope_v, quad_a, quad_b, quad_c, zero, zero], axis=0
+            )
+            for part in range(3):
+                term = coef.astype(BF16).astype(F32)
+                coef_s[part * 8 : part * 8 + 8, :] = term
+                coef = coef - term
+            power = matmul(coef_s[...].astype(BF16), basis_3, ((0,), (0,)))
+            n = g * tile_count + t
+            for part in range(parts):
+                span = n * parts + part
+                at = slice(part * LANES, (part + 1) * LANES)
+                alpha_s[pl.ds(span, listed, stride=spans), :] = jnp.exp(power[:, at])
+                for k in range(3):
+                    colour_s[k, span : span + 1, :] = entry[6 + k : 7 + k]
+                    first = t * pixels + part * LANES
+                    goal_s[k, span : span + 1, :] = info_s[g, k : k + 1, first : first + LANES]
+
+    unroll = 32
+    steps = listed // unroll
+
+    def colours_of(step):
+        first = step * unroll
+        at = pl.ds(pl.multiple_of(first // LANES * LANES, LANES), LANES)
+        turn = (LANES - first % LANES) % LANES
+        return [pltpu.roll(colour_s[k, :, at], turn, 1) for k in range(3)]
+
+    def forward(step, carry):
+        passed, *image = carry
+        colours = colours_of(step)
+        for j in range(unroll):
+            at = pl.ds(pl.multiple_of((step * unroll + j) * spans, spans), spans)
+            alpha = alpha_s[at, :]
+            weight = alpha * passed
+            passed = passed * (1.0 - alpha)
+            weight_s[at, :] = weight
+            image = [
+                image[k] + weight * jnp.broadcast_to(colours[k][:, j : j + 1], (spans, LANES))
+                for k in range(3)
+            ]
+        return (passed, *image)
+
+    nought = jnp.zeros((spans, LANES), F32)
+    _, *image = lax.fori_loop(0, steps, forward, (nought + 1.0, nought, nought, nought))
+    if rendered is not None:
+        for k in range(3):
+            for span in range(tile_count * parts):
+                rendered[k : k + 1, span * LANES : (span + 1) * LANES] = image[k][span : span + 1]
+    error = [image[k] - goal_s[k] for k in range(3)]
+
+    def backward(back, behind):
+        step = steps - 1 - back
+        colours = colours_of(step)
+        for j in reversed(range(unroll)):
+            at = pl.ds(pl.multiple_of((step * unroll + j) * spans, spans), spans)
+            alpha, weight = alpha_s[at, :], weight_s[at, :]
+            pull = sum(
+                error[k] * jnp.broadcast_to(colours[k][:, j : j + 1], (spans, LANES))
+                for k in range(3)
+            )
+            push_s[at, :] = weight * (pull - behind)
+            behind = behind * (1.0 - alpha) + alpha * pull
+        return behind
+
+    lax.fori_loop(0, steps, backward, nought)
+
+    error_hi = [each.astype(BF16).astype(F32) for each in error]
+    error_lo = [error[k] - error_hi[k] for k in range(3)]
+    mix_s[...] = jnp.zeros(mix_s.shape, F32)
+    for n in range(groups * tile_count):
+        for part in range(parts):
+            span = n * parts + part
+            at = slice(span * LANES, (span + 1) * LANES)
+            mix_s[0, n * ROWS : n * ROWS + 8, at] = basis[:, part * LANES : (part + 1) * LANES]
+            for k in range(3):
+                row = n * ROWS + 6 + k
+                mix_s[1, row : row + 1, at] = error_hi[k][span : span + 1]
+                mix_s[1, row + 3 : row + 4, at] = error_lo[k][span : span + 1]
+    sums = 0.0
+    for which, source in ((0, push_s), (1, weight_s)):
+        whole = jnp.concatenate(
+            [source[pl.ds(span, listed, stride=spans), :] for span in range(spans)], axis=1
+        )
+        high, low = split(whole)
+        mix = mix_s[which].astype(BF16)
+        sums = sums + matmul(high, mix, ((1,), (1,))) + matmul(low, mix, ((1,), (1,)))
+    sums = sums.T
+    for g in range(groups):
         for t in range(tile_count):
-            entry = lists[t]
-            slot = (me ^ (first_group + g)) * tile_count + t
-            x_0 = ((first_col + slot % 4) * side).astype(F32) + 0.5
-            y_0 = ((first_row + slot // 4) * side).astype(F32) + 0.5
-            quad_a, quad_b, quad_c = -0.5 * entry[2:3], -entry[3:4], -0.5 * entry[4:5]
-            opacity = entry[5:6]
-            dx = (step + x_0) - entry[0:1]
-            dy = (step + y_0) - entry[1:2]
-            adx2 = quad_a * dx * dx
-            bdy = quad_b * dy
-            cdy2 = quad_c * dy * dy
-            setup.append((entry, quad_a, quad_b, quad_c, opacity, dx, dy))
-            for row in range(side):
-                at = slice(row * side, (row + 1) * side)
-                power = adx2 + dx * bdy[row : row + 1] + cdy2[row : row + 1]
-                bell = jnp.exp(power)
-                e_s[t, at, :] = bell
-                hi_s[t, at, :], lo_s[t, at, :] = split(jnp.log(1.0 - opacity * bell))
-
-        for t in range(tile_count):
-            t_s[t] = matmul(hi_s[t], earlier) + matmul(lo_s[t], earlier)
-
-        for t in range(tile_count):
-            entry, opacity = setup[t][0], setup[t][4]
-            for row in range(side):
-                at = slice(row * side, (row + 1) * side)
-                passed = jnp.exp(t_s[t, at, :])
-                t_s[t, at, :] = passed
-                hi_s[t, at, :], lo_s[t, at, :] = split(opacity * e_s[t, at, :] * passed)
-            c_hi, c_lo = split(entry[6:9])
-            both = ((1,), (1,))
-            image = (
-                matmul(c_hi, hi_s[t], both)
-                + matmul(c_lo, hi_s[t], both)
-                + matmul(c_hi, lo_s[t], both)
-            )
-            here = slice(t * pixels, (t + 1) * pixels)
-            if rendered is not None:
-
-                @pl.when(g == 0)
-                def _():
-                    rendered[:, here] = image
-
-            error = image - info_s[g, 0:3, here]
-            g_hi, g_lo = split(error)
-            first = ((0,), (0,))
-            d_s[t] = (
-                matmul(g_hi, c_hi, first) + matmul(g_lo, c_hi, first) + matmul(g_hi, c_lo, first)
-            )
-            g_colours = matmul(g_hi, hi_s[t]) + matmul(g_lo, hi_s[t]) + matmul(g_hi, lo_s[t])
-            acc_s[g, t, 6:9, :] = g_colours
-
-        for t in range(tile_count):
-            opacity = setup[t][4]
-            for row in range(side):
-                at = slice(row * side, (row + 1) * side)
-                pushed = t_s[t, at, :] * d_s[t, at, :]
-                t_s[t, at, :] = pushed
-                hi_s[t, at, :], lo_s[t, at, :] = split(opacity * e_s[t, at, :] * pushed)
-            d_s[t] = matmul(hi_s[t], later) + matmul(lo_s[t], later)
-
-        for t in range(tile_count):
-            entry, quad_a, quad_b, quad_c, opacity, dx, dy = setup[t]
-            r_0 = r_1 = r_2 = None
-            for row in range(side):
-                at = slice(row * side, (row + 1) * side)
-                bell = e_s[t, at, :]
-                flow = bell * (t_s[t, at, :] - d_s[t, at, :] / (1.0 - opacity * bell))
-                one = flow * dy[row : row + 1]
-                two = one * dy[row : row + 1]
-                r_0 = flow if r_0 is None else r_0 + flow
-                r_1 = one if r_1 is None else r_1 + one
-                r_2 = two if r_2 is None else r_2 + two
-            rdx = r_0 * dx
-            m_00 = jnp.sum(r_0, axis=0, keepdims=True)
-            m_10 = jnp.sum(rdx, axis=0, keepdims=True)
-            m_20 = jnp.sum(rdx * dx, axis=0, keepdims=True)
-            m_01 = jnp.sum(r_1, axis=0, keepdims=True)
-            m_11 = jnp.sum(r_1 * dx, axis=0, keepdims=True)
-            m_02 = jnp.sum(r_2, axis=0, keepdims=True)
-            acc_s[g, t, 0:1, :] = -opacity * (2.0 * quad_a * m_10 + quad_b * m_01)
-            acc_s[g, t, 1:2, :] = -opacity * (2.0 * quad_c * m_01 + quad_b * m_10)
-            acc_s[g, t, 2:3, :] = -0.5 * opacity * m_20
-            acc_s[g, t, 3:4, :] = -opacity * m_11
-            acc_s[g, t, 4:5, :] = -0.5 * opacity * m_02
+            n = g * tile_count + t
+            mean_u, mean_v, quad_a, quad_b, quad_c = means[n]
+            m_00, m_10, m_01, m_20, m_11, m_02 = [
+                sums[n * ROWS + m : n * ROWS + m + 1] for m in range(6)
+            ]
+            n_10 = m_10 - mean_u * m_00
+            n_01 = m_01 - mean_v * m_00
+            acc_s[g, t, 0:1, :] = -(2.0 * quad_a * n_10 + quad_b * n_01)
+            acc_s[g, t, 1:2, :] = -(2.0 * quad_c * n_01 + quad_b * n_10)
+            acc_s[g, t, 2:3, :] = -0.5 * (m_20 - mean_u * (m_10 + n_10))
+            acc_s[g, t, 3:4, :] = -(m_11 - mean_u * m_01 - mean_v * n_10)
+            acc_s[g, t, 4:5, :] = -0.5 * (m_02 - mean_v * (m_01 + n_01))
             acc_s[g, t, 5:6, :] = m_00
+            at = n * ROWS + 6
+            acc_s[g, t, 6:9, :] = sums[at : at + 3] + sums[at + 3 : at + 6]
             acc_s[g, t, 9:16, :] = jnp.zeros((7, listed), F32)
-        return carry
-
-    lax.fori_loop(0, acc_s.shape[0], one_group, 0)
 
 
 def pool_sum(slab, info_s, acc_s):
@@ -498,8 +532,8 @@
 
 
 def far_kernel(blocks, tile_ids, where, rows, partial, infos, *refs):
-    *packets, info_s = refs[: len(refs) - 6]
-    work = refs[len(refs) - 6 :]
+    *packets, info_s = refs[: len(refs) - 8]
+    work = refs[len(refs) - 8 :]
     half = infos.shape[0] // 2
     info_s[0] = infos[:half, :]
     info_s[1] = infos[half:, :]
@@ -608,13 +642,15 @@
 
 
 def work_shapes(tile_count, pixels, listed):
-    square = (tile_count, pixels, listed)
+    spans = 2 * tile_count * pixels // LANES
     return [
-        pltpu.VMEM(square, F32),
-        pltpu.VMEM(square, F32),
-        pltpu.VMEM(square, F32),
-        pltpu.VMEM(square, BF16),
-        pltpu.VMEM(square, BF16),
+        pltpu.VMEM((listed * spans, LANES), F32),
+        pltpu.VMEM((listed * spans, LANES), F32),
+        pltpu.VMEM((listed * spans, LANES), F32),
+        pltpu.VMEM((3, spans, listed), F32),
+        pltpu.VMEM((3, spans, LANES), F32),
+        pltpu.VMEM((24, listed), F32),
+        pltpu.VMEM((2, LANES, spans * LANES), F32),
         pltpu.VMEM((2, tile_count, ROWS, listed), F32),
     ]
 

time: 27.1 us -> 31.9 us (1.18)
  Pallas kernels: 12.7 us -> 17.5 us
    pallas_call x5, Pallas kernels: 12.7 us -> 17.5 us  [call(): pl.pallas_call(kernel, out_shape=out_shape, in_specs=in_specs, out_specs=...]
  transfers between devices with their start and end apart: 8 -> 8, of which waited for: 3 -> 3; matrix products, arithmetic and copies ran while one was open for 0% -> 0% of each run, Pallas kernels for 18% -> 23%
where the time goes in v6:
time: 31.9 us; the launch traced here: 31.7 us
  Pallas kernels  17.5 us (55%)
  starting transfers between devices  9.73 us (31%)
  waiting for transfers between devices  3.7 us (12%)
  between operations  0.7 us (2%)
    pallas_call x5, Pallas kernels, call(): pl.pallas_call(kernel, out_shape=out_shape, in_specs=in_specs, out_specs=...  17.5 us
    ppermute x8, starting transfers between devices, swap(): lax.ppermute(value, axis, [(k, k ^ d) for k in range(lax.axis_size(axis))])  9.73 us
    ppermute x8, waiting for transfers between devices, swap(): lax.ppermute(value, axis, [(k, k ^ d) for k in range(lax.axis_size(axis))])  3.7 us
  transfers between devices with their start and end apart: 8, of which 3 were waited for; matrix products, arithmetic and copies ran while one was open for 0% of the time, Pallas kernels for 23%

profile of v6, /device:TPU:0, one launch (start us, length us, event | category | flops | bytes accessed | tf_op | source)
XLA Modules:
  0.0 31.7 jit_solution(18436912385780667877)
XLA Ops:
  0.6 0.0 copy-start.2
  0.6 1.2 %pack.1 = (f32[8,512]{1,0:T(8,128)S(1)}, f32[59,256]{1,0:T(8,128)S(1)}, f32[59,256]{1,0:T(8,128)S(1)}, f32[59,256]{1,0:T(8,128)S(1)}, f32[59,256]{1,0:T(8,128)S(1)}) custom-call(s32[1]{0:T(128)} %bitcast.2.where, s32[2,1,256]{2,1,0:T(1,128)} %bitcast.4, s32[2,256]{1,0:T(2,128)} %refs_1_.1, f32[3,512]{1,0:T(4,128)} %refs_2_.1, f32[59,1024]{1,0:T(8,128)} %refs_4_.1), custom_call_target="tpu_custom_call" | custom-call | tf_op jit(solution)/shard_map/pack/pallas_call | solution.py:633
  1.8 3.1 %collective-permute-start = (f32[8,512]{1,0:T(8,128)S(1)}, f32[8,512]{1,0:T(8,128)S(1)}, u32[]{:S(2)}, u32[]{:S(2)}) collective-permute-start(f32[8,512]{1,0:T(8,128)S(1)} %get-tuple-element.19.own.first), channel_id=1, source_target_pairs={{0,1},{1,0},{2,3},{3,2},{4,5},{5,4},{6,7},{7,6},{8,9},{9,8},{10,11... | collective-permute-start | bytes 49160 | tf_op jit(solution)/shard_map/ppermute | solution.py:725
  4.9 0.0 collective-permute-start.1
  4.9 1.5 %collective-permute-start.2 = (f32[59,256]{1,0:T(8,128)S(1)}, f32[59,256]{1,0:T(8,128)S(1)}, u32[]{:S(2)}, u32[]{:S(2)}) collective-permute-start(f32[59,256]{1,0:T(8,128)S(1)} %get-tuple-element.22), channel_id=1, source_target_pairs={{0,8},{4,12},{8,0},{12,4},{1,9},{5,13},{9,1},{13,5},{2,10},{6,14},... | collective-permute-start | bytes 181256 | tf_op jit(solution)/shard_map/ppermute | solution.py:725
  6.4 0.4 %collective-permute-start.3 = (f32[59,256]{1,0:T(8,128)S(1)}, f32[59,256]{1,0:T(8,128)S(1)}, u32[]{:S(2)}, u32[]{:S(2)}) collective-permute-start(f32[59,256]{1,0:T(8,128)S(1)} %get-tuple-element.23), channel_id=1, source_target_pairs={{0,12},{4,8},{8,4},{12,0},{1,13},{5,9},{9,5},{13,1},{2,14},{6,10},... | collective-permute-start | bytes 181256 | tf_op jit(solution)/shard_map/ppermute | solution.py:725
  6.8 0.0 copy-start.3
  6.8 0.0 copy-start.4
  6.8 0.0 copy-start
  6.8 0.0 copy-start.1
  6.8 0.0 collective-permute-done.other.second
  6.8 2.9 %collective-permute-start.4 = (f32[16,512]{1,0:T(8,128)S(1)}, f32[16,512]{1,0:T(8,128)S(1)}, u32[]{:S(2)}, u32[]{:S(2)}) collective-permute-start(f32[16,512]{1,0:T(8,128)S(1)} %join.1), channel_id=1, source_target_pairs={{0,2},{1,3},{2,0},{3,1},{4,6},{5,7},{6,4},{7,5},{8,10},{9,11},{10,... | collective-permute-start | bytes 98312 | tf_op jit(solution)/shard_map/ppermute | solution.py:725
  9.7 0.1 pad_add_fusion.where
  9.8 0.0 collective-permute-done.1.refs_1_
  9.8 0.0 collective-permute-done.2.refs_2_
  9.8 0.8 %collective-permute-done.3.refs_3_ = f32[59,256]{1,0:T(8,128)S(1)} collective-permute-done((f32[59,256]{1,0:T(8,128)S(1)}, f32[59,256]{1,0:T(8,128)S(1)}, u32[]{:S(2)}, u32[]{:S(2)}) %collective-permute-start.3) | collective-permute-done | bytes 60448 | tf_op jit(solution)/shard_map/ppermute | solution.py:725
  10.5 0.0 copy-done.3
  10.5 0.0 copy-done.4
  10.6 7.3 %near.1 = (f32[3,512]{1,0:T(4,128)}, f32[128,128]{1,0:T(8,128)S(1)}, f32[16,1024]{1,0:T(8,128)S(1)}) custom-call(s32[2]{0:T(128)S(1)} %copy-done.4, f32[4,12]{1,0:T(4,128)S(1)} %copy-done.3, s32[3]{0:T(128)S(1)} %pad_add_fusion.where, f32[8,512]{1,0:T(8,128)S(1)} %get-tuple-element.19.own.first, f32[8,512]{1,0:T(8,128)S(1)} %collective-permute-done.other.second, ...), custom_call_target="tpu_custom_call" | custom-call | tf_op jit(solution)/shard_map/near/pallas_call | solution.py:633
  17.8 0.0 collective-permute-done.4.infos
  17.9 7.1 %far.1 = (f32[16,256]{1,0:T(8,128)S(1)}, f32[16,256]{1,0:T(8,128)S(1)}, f32[16,256]{1,0:T(8,128)S(1)}, f32[16,256]{1,0:T(8,128)S(1)}) custom-call(s32[2]{0:T(128)S(1)} %copy-done.4, s32[3]{0:T(128)S(1)} %pad_add_fusion.where, f32[128,128]{1,0:T(8,128)S(1)} %get-tuple-element.25.rows, f32[16,1024]{1,0:T(8,128)S(1)} %get-tuple-element.26.partial, ...), custom_call_target="tpu_custom_call" | custom-call | tf_op jit(solution)/shard_map/far/pallas_call | solution.py:633
  25.0 0.2 collective-permute-start.5
  25.2 1.5 %collective-permute-start.6 = (f32[16,256]{1,0:T(8,128)S(1)}, f32[16,256]{1,0:T(8,128)S(1)}, u32[]{:S(2)}, u32[]{:S(2)}) collective-permute-start(f32[16,256]{1,0:T(8,128)S(1)} %get-tuple-element.29), channel_id=1, source_target_pairs={{0,8},{4,12},{8,0},{12,4},{1,9},{5,13},{9,1},{13,5},{2,10},{6,14},... | collective-permute-start | bytes 49160 | tf_op jit(solution)/shard_map/ppermute | solution.py:725
  26.7 0.3 collective-permute-start.7
  26.9 0.0 collective-permute-done.5.refs_1_
  26.9 2.0 %collective-permute-done.6.refs_2_ = f32[16,256]{1,0:T(8,128)S(1)} collective-permute-done((f32[16,256]{1,0:T(8,128)S(1)}, f32[16,256]{1,0:T(8,128)S(1)}, u32[]{:S(2)}, u32[]{:S(2)}) %collective-permute-start.6) | collective-permute-done | bytes 16416 | tf_op jit(solution)/shard_map/ppermute | solution.py:725
  28.9 0.9 %collective-permute-done.7.refs_3_ = f32[16,256]{1,0:T(8,128)S(1)} collective-permute-done((f32[16,256]{1,0:T(8,128)S(1)}, f32[16,256]{1,0:T(8,128)S(1)}, u32[]{:S(2)}, u32[]{:S(2)}) %collective-permute-start.7) | collective-permute-done | bytes 16416 | tf_op jit(solution)/shard_map/ppermute | solution.py:725
  29.8 0.0 copy-done.2
  29.8 0.0 copy-done
  29.8 0.0 copy-done.1
  29.8 1.9 %update.1 = (f32[59,1024]{1,0:T(8,128)}, f32[59,1024]{1,0:T(8,128)}, f32[59,1024]{1,0:T(8,128)}) custom-call(s32[1]{0:T(128)} %bitcast.2.where, f32[4,12]{1,0:T(4,128)S(1)} %copy-done.3, f32[16,256]{1,0:T(8,128)S(1)} %get-tuple-element.27.refs_0_, f32[16,256]{1,0:T(8,128)S(1)} %collective-permute-done.5.refs_1_, ...), custom_call_target="tpu_custom_call" | custom-call | tf_op jit(solution)/shard_map/update/pallas_call | solution.py:633
  (1 shorter events, 0.0 us)
Async XLA Ops:
  0.6 29.2 %copy-start.2 = (f32[59,1024]{1,0:T(8,128)S(1)}, f32[59,1024]{1,0:T(8,128)}, u32[]{:S(2)}) copy-start(f32[59,1024]{1,0:T(8,128)} %refs_6_.1) | copy-start | bytes 724996
  1.8 5.0 %collective-permute-start = (f32[8,512]{1,0:T(8,128)S(1)}, f32[8,512]{1,0:T(8,128)S(1)}, u32[]{:S(2)}, u32[]{:S(2)}) collective-permute-start(f32[8,512]{1,0:T(8,128)S(1)} %get-tuple-element.19.own.first), channel_id=1, source_target_pairs={{0,1},{1,0},{2,3},{3,2},{4,5},{5,4},{6,7},{7,6},{8,9},{9,8},{10,11... | collective-permute-start | bytes 49160 | tf_op jit(solution)/shard_map/ppermute | solution.py:725
  4.9 4.8 %collective-permute-start.1 = (f32[59,256]{1,0:T(8,128)S(1)}, f32[59,256]{1,0:T(8,128)S(1)}, u32[]{:S(2)}, u32[]{:S(2)}) collective-permute-start(f32[59,256]{1,0:T(8,128)S(1)} %get-tuple-element.21), channel_id=1, source_target_pairs={{0,4},{4,0},{8,12},{12,8},{1,5},{5,1},{9,13},{13,9},{2,6},{6,2},{1... | collective-permute-start | bytes 181256 | tf_op jit(solution)/shard_map/ppermute | solution.py:725
  4.9 4.8 %collective-permute-start.2 = (f32[59,256]{1,0:T(8,128)S(1)}, f32[59,256]{1,0:T(8,128)S(1)}, u32[]{:S(2)}, u32[]{:S(2)}) collective-permute-start(f32[59,256]{1,0:T(8,128)S(1)} %get-tuple-element.22), channel_id=1, source_target_pairs={{0,8},{4,12},{8,0},{12,4},{1,9},{5,13},{9,1},{13,5},{2,10},{6,14},... | collective-permute-start | bytes 181256 | tf_op jit(solution)/shard_map/ppermute | solution.py:725
  6.4 4.1 %collective-permute-start.3 = (f32[59,256]{1,0:T(8,128)S(1)}, f32[59,256]{1,0:T(8,128)S(1)}, u32[]{:S(2)}, u32[]{:S(2)}) collective-permute-start(f32[59,256]{1,0:T(8,128)S(1)} %get-tuple-element.23), channel_id=1, source_target_pairs={{0,12},{4,8},{8,4},{12,0},{1,13},{5,9},{9,5},{13,1},{2,14},{6,10},... | collective-permute-start | bytes 181256 | tf_op jit(solution)/shard_map/ppermute | solution.py:725
  6.8 3.8 %copy-start.3 = (f32[4,12]{1,0:T(4,128)S(1)}, f32[4,12]{1,0:T(4,128)}, u32[]{:S(2)}) copy-start(f32[4,12]{1,0:T(4,128)} %cams.3) | copy-start | bytes 580
  6.8 3.8 %copy-start.4 = (s32[2]{0:T(128)S(1)}, s32[2]{0:T(128)}, u32[]{:S(2)}) copy-start(s32[2]{0:T(128)} %tile_ids.3) | copy-start | bytes 28
  6.8 23.0 %copy-start = (f32[59,1024]{1,0:T(8,128)S(1)}, f32[59,1024]{1,0:T(8,128)}, u32[]{:S(2)}) copy-start(f32[59,1024]{1,0:T(8,128)} %refs_4_.1) | copy-start | bytes 724996
  6.8 23.0 %copy-start.1 = (f32[59,1024]{1,0:T(8,128)S(1)}, f32[59,1024]{1,0:T(8,128)}, u32[]{:S(2)}) copy-start(f32[59,1024]{1,0:T(8,128)} %refs_5_.1) | copy-start | bytes 724996
  6.8 11.0 %collective-permute-start.4 = (f32[16,512]{1,0:T(8,128)S(1)}, f32[16,512]{1,0:T(8,128)S(1)}, u32[]{:S(2)}, u32[]{:S(2)}) collective-permute-start(f32[16,512]{1,0:T(8,128)S(1)} %join.1), channel_id=1, source_target_pairs={{0,2},{1,3},{2,0},{3,1},{4,6},{5,7},{6,4},{7,5},{8,10},{9,11},{10,... | collective-permute-start | bytes 98312 | tf_op jit(solution)/shard_map/ppermute | solution.py:725
  25.0 1.9 %collective-permute-start.5 = (f32[16,256]{1,0:T(8,128)S(1)}, f32[16,256]{1,0:T(8,128)S(1)}, u32[]{:S(2)}, u32[]{:S(2)}) collective-permute-start(f32[16,256]{1,0:T(8,128)S(1)} %get-tuple-element.28), channel_id=1, source_target_pairs={{0,4},{4,0},{8,12},{12,8},{1,5},{5,1},{9,13},{13,9},{2,6},{6,2},{1... | collective-permute-start | bytes 49160 | tf_op jit(solution)/shard_map/ppermute | solution.py:725
  25.2 3.8 %collective-permute-start.6 = (f32[16,256]{1,0:T(8,128)S(1)}, f32[16,256]{1,0:T(8,128)S(1)}, u32[]{:S(2)}, u32[]{:S(2)}) collective-permute-start(f32[16,256]{1,0:T(8,128)S(1)} %get-tuple-element.29), channel_id=1, source_target_pairs={{0,8},{4,12},{8,0},{12,4},{1,9},{5,13},{9,1},{13,5},{2,10},{6,14},... | collective-permute-start | bytes 49160 | tf_op jit(solution)/shard_map/ppermute | solution.py:725
  26.7 3.2 %collective-permute-start.7 = (f32[16,256]{1,0:T(8,128)S(1)}, f32[16,256]{1,0:T(8,128)S(1)}, u32[]{:S(2)}, u32[]{:S(2)}) collective-permute-start(f32[16,256]{1,0:T(8,128)S(1)} %get-tuple-element.30), channel_id=1, source_target_pairs={{0,12},{4,8},{8,4},{12,0},{1,13},{5,9},{9,5},{13,1},{2,14},{6,10},... | collective-permute-start | bytes 49160 | tf_op jit(solution)/shard_map/ppermute | solution.py:725

commit v7 on v6

--- a/solution.py
+++ b/solution.py
@@ -13,6 +13,7 @@
 BLOCK_TILES = 8
 LANES = 128
 ROWS = 16
+SPAN_STEP, LIST_STEP = 3, 25
 F32 = jnp.float32
 BF16 = jnp.bfloat16
 
@@ -340,7 +341,7 @@
 
 
 def composite(tiles, first_group, me, rows, info_s, rendered, work):
-    alpha_s, weight_s, push_s, colour_s, goal_s, coef_s, mix_s, acc_s = work
+    alpha_s, weight_s, pull_s, push_s, weight_hi, weight_lo, coef_s, mix_s, acc_s = work
     groups, tile_count, _, listed = acc_s.shape
     pixels = info_s.shape[2] // tile_count
     parts = pixels // LANES
@@ -348,10 +349,17 @@
     slabs = rows.shape[0] // ROWS
     side = TILE_SIDE
     first_col, first_row = tiles
+
+    def of_span(span):
+        return pl.ds(span * SPAN_STEP, listed, stride=LIST_STEP)
+
+    def of_place(place):
+        return pl.ds(place * LIST_STEP, spans, stride=SPAN_STEP)
+
     basis = pixel_basis(pixels)
     basis_3 = jnp.concatenate([basis, basis, basis], axis=0).astype(BF16)
 
-    means = []
+    means, colours = [], []
     for g in range(groups):
         for t in range(tile_count):
             halves = []
@@ -386,82 +394,75 @@
             power = matmul(coef_s[...].astype(BF16), basis_3, ((0,), (0,)))
             n = g * tile_count + t
             for part in range(parts):
-                span = n * parts + part
                 at = slice(part * LANES, (part + 1) * LANES)
-                alpha_s[pl.ds(span, listed, stride=spans), :] = jnp.exp(power[:, at])
-                for k in range(3):
-                    colour_s[k, span : span + 1, :] = entry[6 + k : 7 + k]
-                    first = t * pixels + part * LANES
-                    goal_s[k, span : span + 1, :] = info_s[g, k : k + 1, first : first + LANES]
+                alpha_s[of_span(n * parts + part), :] = jnp.exp(power[:, at])
+            high = entry[6:9].astype(BF16).astype(F32)
+            low = entry[6:9] - high
+            zero = jnp.zeros((2, listed), F32)
+            colours.append(jnp.concatenate([high, low, zero], axis=0).astype(BF16))
 
     unroll = 32
     steps = listed // unroll
 
-    def colours_of(step):
-        first = step * unroll
-        at = pl.ds(pl.multiple_of(first // LANES * LANES, LANES), LANES)
-        turn = (LANES - first % LANES) % LANES
-        return [pltpu.roll(colour_s[k, :, at], turn, 1) for k in range(3)]
-
-    def forward(step, carry):
-        passed, *image = carry
-        colours = colours_of(step)
+    def forward(step, passed):
         for j in range(unroll):
-            at = pl.ds(pl.multiple_of((step * unroll + j) * spans, spans), spans)
+            at = of_place(step * unroll + j)
             alpha = alpha_s[at, :]
-            weight = alpha * passed
+            weight_s[at, :] = alpha * passed
             passed = passed * (1.0 - alpha)
-            weight_s[at, :] = weight
-            image = [
-                image[k] + weight * jnp.broadcast_to(colours[k][:, j : j + 1], (spans, LANES))
-                for k in range(3)
-            ]
-        return (passed, *image)
+        return passed
 
     nought = jnp.zeros((spans, LANES), F32)
-    _, *image = lax.fori_loop(0, steps, forward, (nought + 1.0, nought, nought, nought))
-    if rendered is not None:
-        for k in range(3):
-            for span in range(tile_count * parts):
-                rendered[k : k + 1, span * LANES : (span + 1) * LANES] = image[k][span : span + 1]
-    error = [image[k] - goal_s[k] for k in range(3)]
+    lax.fori_loop(0, steps, forward, nought + 1.0)
+
+    errors = []
+    for n in range(groups * tile_count):
+        g, t = n // tile_count, n % tile_count
+        for part in range(parts):
+            at = slice((n * parts + part) * LANES, (n * parts + part + 1) * LANES)
+            weight_hi[:, at], weight_lo[:, at] = split(weight_s[of_span(n * parts + part), :])
+        at = slice(n * pixels, (n + 1) * pixels)
+        image = matmul(colours[n], weight_hi[:, at])
+        image = image[0:3] + image[3:6] + matmul(colours[n], weight_lo[:, at])[0:3]
+        here = slice(t * pixels, (t + 1) * pixels)
+        if rendered is not None and g == 0:
+            rendered[:, here] = image
+        error = image - info_s[g, 0:3, here]
+        high = error.astype(BF16).astype(F32)
+        low = error - high
+        errors.append((high, low))
+        zero = jnp.zeros((2, pixels), F32)
+        both = jnp.concatenate([high, high, zero], axis=0).astype(BF16)
+        rest = jnp.concatenate([low, jnp.zeros((5, pixels), F32)], axis=0).astype(BF16)
+        first = ((0,), (0,))
+        pull = matmul(colours[n], both, first) + matmul(colours[n], rest, first)
+        for part in range(parts):
+            at = slice(part * LANES, (part + 1) * LANES)
+            pull_s[of_span(n * parts + part), :] = pull[:, at]
 
     def backward(back, behind):
-        step = steps - 1 - back
-        colours = colours_of(step)
-        for j in reversed(range(unroll)):
-            at = pl.ds(pl.multiple_of((step * unroll + j) * spans, spans), spans)
-            alpha, weight = alpha_s[at, :], weight_s[at, :]
-            pull = sum(
-                error[k] * jnp.broadcast_to(colours[k][:, j : j + 1], (spans, LANES))
-                for k in range(3)
-            )
-            push_s[at, :] = weight * (pull - behind)
+        for j in range(unroll):
+            at = of_place(listed - 1 - (back * unroll + j))
+            alpha, pull = alpha_s[at, :], pull_s[at, :]
+            push_s[at, :] = weight_s[at, :] * (pull - behind)
             behind = behind * (1.0 - alpha) + alpha * pull
         return behind
 
     lax.fori_loop(0, steps, backward, nought)
 
-    error_hi = [each.astype(BF16).astype(F32) for each in error]
-    error_lo = [error[k] - error_hi[k] for k in range(3)]
     mix_s[...] = jnp.zeros(mix_s.shape, F32)
     for n in range(groups * tile_count):
-        for part in range(parts):
-            span = n * parts + part
-            at = slice(span * LANES, (span + 1) * LANES)
-            mix_s[0, n * ROWS : n * ROWS + 8, at] = basis[:, part * LANES : (part + 1) * LANES]
-            for k in range(3):
-                row = n * ROWS + 6 + k
-                mix_s[1, row : row + 1, at] = error_hi[k][span : span + 1]
-                mix_s[1, row + 3 : row + 4, at] = error_lo[k][span : span + 1]
-    sums = 0.0
-    for which, source in ((0, push_s), (1, weight_s)):
-        whole = jnp.concatenate(
-            [source[pl.ds(span, listed, stride=spans), :] for span in range(spans)], axis=1
-        )
-        high, low = split(whole)
-        mix = mix_s[which].astype(BF16)
-        sums = sums + matmul(high, mix, ((1,), (1,))) + matmul(low, mix, ((1,), (1,)))
+        at = slice(n * pixels, (n + 1) * pixels)
+        mix_s[0, n * ROWS : n * ROWS + 8, at] = basis
+        high, low = errors[n]
+        mix_s[1, n * ROWS + 6 : n * ROWS + 9, at] = high
+        mix_s[1, n * ROWS + 9 : n * ROWS + 12, at] = low
+    moments, colour_sums = mix_s[0].astype(BF16), mix_s[1].astype(BF16)
+    high, low = split(jnp.concatenate([push_s[of_span(span), :] for span in range(spans)], axis=1))
+    across = ((1,), (1,))
+    sums = matmul(high, moments, across) + matmul(low, moments, across)
+    sums = sums + matmul(weight_hi[...], colour_sums, across)
+    sums = sums + matmul(weight_lo[...], colour_sums, across)
     sums = sums.T
     for g in range(groups):
         for t in range(tile_count):
@@ -532,8 +533,8 @@
 
 
 def far_kernel(blocks, tile_ids, where, rows, partial, infos, *refs):
-    *packets, info_s = refs[: len(refs) - 8]
-    work = refs[len(refs) - 8 :]
+    *packets, info_s = refs[: len(refs) - 9]
+    work = refs[len(refs) - 9 :]
     half = infos.shape[0] // 2
     info_s[0] = infos[:half, :]
     info_s[1] = infos[half:, :]
@@ -643,12 +644,10 @@
 
 def work_shapes(tile_count, pixels, listed):
     spans = 2 * tile_count * pixels // LANES
-    return [
-        pltpu.VMEM((listed * spans, LANES), F32),
-        pltpu.VMEM((listed * spans, LANES), F32),
-        pltpu.VMEM((listed * spans, LANES), F32),
-        pltpu.VMEM((3, spans, listed), F32),
-        pltpu.VMEM((3, spans, LANES), F32),
+    assert (spans - 1) * SPAN_STEP < LIST_STEP
+    return [pltpu.VMEM((listed * LIST_STEP, LANES), F32)] * 4 + [
+        pltpu.VMEM((listed, spans * LANES), BF16),
+        pltpu.VMEM((listed, spans * LANES), BF16),
         pltpu.VMEM((24, listed), F32),
         pltpu.VMEM((2, LANES, spans * LANES), F32),
         pltpu.VMEM((2, tile_count, ROWS, listed), F32),

time: 31.9 us -> 26.5 us (0.83)
  Pallas kernels: 17.5 us -> 12.1 us
    pallas_call x5, Pallas kernels: 17.5 us -> 12.1 us  [call(): pl.pallas_call(kernel, out_shape=out_shape, in_specs=in_specs, out_specs=...]
  transfers between devices with their start and end apart: 8 -> 8, of which waited for: 3 -> 3; matrix products, arithmetic and copies ran while one was open for 0% -> 0% of each run, Pallas kernels for 23% -> 17%
where the time goes in v7:
time: 26.5 us; the launch traced here: 26.3 us
  Pallas kernels  12.1 us (46%)
  starting transfers between devices  9.77 us (37%)
  waiting for transfers between devices  3.66 us (14%)
  between operations  0.7 us (3%)
    pallas_call x5, Pallas kernels, call(): pl.pallas_call(kernel, out_shape=out_shape, in_specs=in_specs, out_specs=...  12.1 us
    ppermute x8, starting transfers between devices, swap(): lax.ppermute(value, axis, [(k, k ^ d) for k in range(lax.axis_size(axis))])  9.77 us
    ppermute x8, waiting for transfers between devices, swap(): lax.ppermute(value, axis, [(k, k ^ d) for k in range(lax.axis_size(axis))])  3.66 us
  transfers between devices with their start and end apart: 8, of which 3 were waited for; matrix products, arithmetic and copies ran while one was open for 0% of the time, Pallas kernels for 17%

profile of v7, /device:TPU:0, one launch (start us, length us, event | category | flops | bytes accessed | tf_op | source)
XLA Modules:
  0.0 26.3 jit_solution(7985561401571879987)
XLA Ops:
  0.6 0.0 copy-start.2
  0.6 1.2 %pack.1 = (f32[8,512]{1,0:T(8,128)S(1)}, f32[59,256]{1,0:T(8,128)S(1)}, f32[59,256]{1,0:T(8,128)S(1)}, f32[59,256]{1,0:T(8,128)S(1)}, f32[59,256]{1,0:T(8,128)S(1)}) custom-call(s32[1]{0:T(128)} %bitcast.2.where, s32[2,1,256]{2,1,0:T(1,128)} %bitcast.4, s32[2,256]{1,0:T(2,128)} %refs_1_.1, f32[3,512]{1,0:T(4,128)} %refs_2_.1, f32[59,1024]{1,0:T(8,128)} %refs_4_.1), custom_call_target="tpu_custom_call" | custom-call | tf_op jit(solution)/shard_map/pack/pallas_call | solution.py:634
  1.8 3.1 %collective-permute-start = (f32[8,512]{1,0:T(8,128)S(1)}, f32[8,512]{1,0:T(8,128)S(1)}, u32[]{:S(2)}, u32[]{:S(2)}) collective-permute-start(f32[8,512]{1,0:T(8,128)S(1)} %get-tuple-element.19.own.first), channel_id=1, source_target_pairs={{0,1},{1,0},{2,3},{3,2},{4,5},{5,4},{6,7},{7,6},{8,9},{9,8},{10,11... | collective-permute-start | bytes 49160 | tf_op jit(solution)/shard_map/ppermute | solution.py:724
  4.9 0.0 collective-permute-start.1
  4.9 1.5 %collective-permute-start.2 = (f32[59,256]{1,0:T(8,128)S(1)}, f32[59,256]{1,0:T(8,128)S(1)}, u32[]{:S(2)}, u32[]{:S(2)}) collective-permute-start(f32[59,256]{1,0:T(8,128)S(1)} %get-tuple-element.22), channel_id=1, source_target_pairs={{0,8},{4,12},{8,0},{12,4},{1,9},{5,13},{9,1},{13,5},{2,10},{6,14},... | collective-permute-start | bytes 181256 | tf_op jit(solution)/shard_map/ppermute | solution.py:724
  6.4 0.4 %collective-permute-start.3 = (f32[59,256]{1,0:T(8,128)S(1)}, f32[59,256]{1,0:T(8,128)S(1)}, u32[]{:S(2)}, u32[]{:S(2)}) collective-permute-start(f32[59,256]{1,0:T(8,128)S(1)} %get-tuple-element.23), channel_id=1, source_target_pairs={{0,12},{4,8},{8,4},{12,0},{1,13},{5,9},{9,5},{13,1},{2,14},{6,10},... | collective-permute-start | bytes 181256 | tf_op jit(solution)/shard_map/ppermute | solution.py:724
  6.8 0.0 copy-start.3
  6.8 0.0 copy-start.4
  6.8 0.0 copy-start
  6.8 0.0 copy-start.1
  6.8 0.0 collective-permute-done.other.second
  6.8 2.9 %collective-permute-start.4 = (f32[16,512]{1,0:T(8,128)S(1)}, f32[16,512]{1,0:T(8,128)S(1)}, u32[]{:S(2)}, u32[]{:S(2)}) collective-permute-start(f32[16,512]{1,0:T(8,128)S(1)} %join.1), channel_id=1, source_target_pairs={{0,2},{1,3},{2,0},{3,1},{4,6},{5,7},{6,4},{7,5},{8,10},{9,11},{10,... | collective-permute-start | bytes 98312 | tf_op jit(solution)/shard_map/ppermute | solution.py:724
  9.7 0.1 pad_add_fusion.where
  9.8 0.0 collective-permute-done.1.refs_1_
  9.8 0.0 collective-permute-done.2.refs_2_
  9.8 0.8 %collective-permute-done.3.refs_3_ = f32[59,256]{1,0:T(8,128)S(1)} collective-permute-done((f32[59,256]{1,0:T(8,128)S(1)}, f32[59,256]{1,0:T(8,128)S(1)}, u32[]{:S(2)}, u32[]{:S(2)}) %collective-permute-start.3) | collective-permute-done | bytes 60448 | tf_op jit(solution)/shard_map/ppermute | solution.py:724
  10.5 0.0 copy-done.3
  10.5 0.0 copy-done.4
  10.6 4.6 %near.1 = (f32[3,512]{1,0:T(4,128)}, f32[128,128]{1,0:T(8,128)S(1)}, f32[16,1024]{1,0:T(8,128)S(1)}) custom-call(s32[2]{0:T(128)S(1)} %copy-done.4, f32[4,12]{1,0:T(4,128)S(1)} %copy-done.3, s32[3]{0:T(128)S(1)} %pad_add_fusion.where, f32[8,512]{1,0:T(8,128)S(1)} %get-tuple-element.19.own.first, f32[8,512]{1,0:T(8,128)S(1)} %collective-permute-done.other.second, ...), custom_call_target="tpu_custom_call" | custom-call | tf_op jit(solution)/shard_map/near/pallas_call | solution.py:634
  15.1 0.0 collective-permute-done.4.infos
  15.1 4.5 %far.1 = (f32[16,256]{1,0:T(8,128)S(1)}, f32[16,256]{1,0:T(8,128)S(1)}, f32[16,256]{1,0:T(8,128)S(1)}, f32[16,256]{1,0:T(8,128)S(1)}) custom-call(s32[2]{0:T(128)S(1)} %copy-done.4, s32[3]{0:T(128)S(1)} %pad_add_fusion.where, f32[128,128]{1,0:T(8,128)S(1)} %get-tuple-element.25.rows, f32[16,1024]{1,0:T(8,128)S(1)} %get-tuple-element.26.partial, ...), custom_call_target="tpu_custom_call" | custom-call | tf_op jit(solution)/shard_map/far/pallas_call | solution.py:634
  19.6 0.2 collective-permute-start.5
  19.8 1.5 %collective-permute-start.6 = (f32[16,256]{1,0:T(8,128)S(1)}, f32[16,256]{1,0:T(8,128)S(1)}, u32[]{:S(2)}, u32[]{:S(2)}) collective-permute-start(f32[16,256]{1,0:T(8,128)S(1)} %get-tuple-element.29), channel_id=1, source_target_pairs={{0,8},{4,12},{8,0},{12,4},{1,9},{5,13},{9,1},{13,5},{2,10},{6,14},... | collective-permute-start | bytes 49160 | tf_op jit(solution)/shard_map/ppermute | solution.py:724
  21.3 0.3 %collective-permute-start.7 = (f32[16,256]{1,0:T(8,128)S(1)}, f32[16,256]{1,0:T(8,128)S(1)}, u32[]{:S(2)}, u32[]{:S(2)}) collective-permute-start(f32[16,256]{1,0:T(8,128)S(1)} %get-tuple-element.30), channel_id=1, source_target_pairs={{0,12},{4,8},{8,4},{12,0},{1,13},{5,9},{9,5},{13,1},{2,14},{6,10},... | collective-permute-start | bytes 49160 | tf_op jit(solution)/shard_map/ppermute | solution.py:724
  21.6 0.0 collective-permute-done.5.refs_1_
  21.6 2.0 %collective-permute-done.6.refs_2_ = f32[16,256]{1,0:T(8,128)S(1)} collective-permute-done((f32[16,256]{1,0:T(8,128)S(1)}, f32[16,256]{1,0:T(8,128)S(1)}, u32[]{:S(2)}, u32[]{:S(2)}) %collective-permute-start.6) | collective-permute-done | bytes 16416 | tf_op jit(solution)/shard_map/ppermute | solution.py:724
  23.5 0.9 %collective-permute-done.7.refs_3_ = f32[16,256]{1,0:T(8,128)S(1)} collective-permute-done((f32[16,256]{1,0:T(8,128)S(1)}, f32[16,256]{1,0:T(8,128)S(1)}, u32[]{:S(2)}, u32[]{:S(2)}) %collective-permute-start.7) | collective-permute-done | bytes 16416 | tf_op jit(solution)/shard_map/ppermute | solution.py:724
  24.4 0.0 copy-done.2
  24.4 0.0 copy-done
  24.4 0.0 copy-done.1
  24.4 1.9 %update.1 = (f32[59,1024]{1,0:T(8,128)}, f32[59,1024]{1,0:T(8,128)}, f32[59,1024]{1,0:T(8,128)}) custom-call(s32[1]{0:T(128)} %bitcast.2.where, f32[4,12]{1,0:T(4,128)S(1)} %copy-done.3, f32[16,256]{1,0:T(8,128)S(1)} %get-tuple-element.27.refs_0_, f32[16,256]{1,0:T(8,128)S(1)} %collective-permute-done.5.refs_1_, ...), custom_call_target="tpu_custom_call" | custom-call | tf_op jit(solution)/shard_map/update/pallas_call | solution.py:634
  (1 shorter events, 0.0 us)
Async XLA Ops:
  0.6 23.8 %copy-start.2 = (f32[59,1024]{1,0:T(8,128)S(1)}, f32[59,1024]{1,0:T(8,128)}, u32[]{:S(2)}) copy-start(f32[59,1024]{1,0:T(8,128)} %refs_6_.1) | copy-start | bytes 724996
  1.8 5.0 %collective-permute-start = (f32[8,512]{1,0:T(8,128)S(1)}, f32[8,512]{1,0:T(8,128)S(1)}, u32[]{:S(2)}, u32[]{:S(2)}) collective-permute-start(f32[8,512]{1,0:T(8,128)S(1)} %get-tuple-element.19.own.first), channel_id=1, source_target_pairs={{0,1},{1,0},{2,3},{3,2},{4,5},{5,4},{6,7},{7,6},{8,9},{9,8},{10,11... | collective-permute-start | bytes 49160 | tf_op jit(solution)/shard_map/ppermute | solution.py:724
  4.9 4.8 %collective-permute-start.1 = (f32[59,256]{1,0:T(8,128)S(1)}, f32[59,256]{1,0:T(8,128)S(1)}, u32[]{:S(2)}, u32[]{:S(2)}) collective-permute-start(f32[59,256]{1,0:T(8,128)S(1)} %get-tuple-element.21), channel_id=1, source_target_pairs={{0,4},{4,0},{8,12},{12,8},{1,5},{5,1},{9,13},{13,9},{2,6},{6,2},{1... | collective-permute-start | bytes 181256 | tf_op jit(solution)/shard_map/ppermute | solution.py:724
  4.9 4.8 %collective-permute-start.2 = (f32[59,256]{1,0:T(8,128)S(1)}, f32[59,256]{1,0:T(8,128)S(1)}, u32[]{:S(2)}, u32[]{:S(2)}) collective-permute-start(f32[59,256]{1,0:T(8,128)S(1)} %get-tuple-element.22), channel_id=1, source_target_pairs={{0,8},{4,12},{8,0},{12,4},{1,9},{5,13},{9,1},{13,5},{2,10},{6,14},... | collective-permute-start | bytes 181256 | tf_op jit(solution)/shard_map/ppermute | solution.py:724
  6.4 4.1 %collective-permute-start.3 = (f32[59,256]{1,0:T(8,128)S(1)}, f32[59,256]{1,0:T(8,128)S(1)}, u32[]{:S(2)}, u32[]{:S(2)}) collective-permute-start(f32[59,256]{1,0:T(8,128)S(1)} %get-tuple-element.23), channel_id=1, source_target_pairs={{0,12},{4,8},{8,4},{12,0},{1,13},{5,9},{9,5},{13,1},{2,14},{6,10},... | collective-permute-start | bytes 181256 | tf_op jit(solution)/shard_map/ppermute | solution.py:724
  6.8 3.8 %copy-start.3 = (f32[4,12]{1,0:T(4,128)S(1)}, f32[4,12]{1,0:T(4,128)}, u32[]{:S(2)}) copy-start(f32[4,12]{1,0:T(4,128)} %cams.3) | copy-start | bytes 580
  6.8 3.8 %copy-start.4 = (s32[2]{0:T(128)S(1)}, s32[2]{0:T(128)}, u32[]{:S(2)}) copy-start(s32[2]{0:T(128)} %tile_ids.3) | copy-start | bytes 28
  6.8 17.6 %copy-start = (f32[59,1024]{1,0:T(8,128)S(1)}, f32[59,1024]{1,0:T(8,128)}, u32[]{:S(2)}) copy-start(f32[59,1024]{1,0:T(8,128)} %refs_4_.1) | copy-start | bytes 724996
  6.8 17.6 %copy-start.1 = (f32[59,1024]{1,0:T(8,128)S(1)}, f32[59,1024]{1,0:T(8,128)}, u32[]{:S(2)}) copy-start(f32[59,1024]{1,0:T(8,128)} %refs_5_.1) | copy-start | bytes 724996
  6.8 8.3 %collective-permute-start.4 = (f32[16,512]{1,0:T(8,128)S(1)}, f32[16,512]{1,0:T(8,128)S(1)}, u32[]{:S(2)}, u32[]{:S(2)}) collective-permute-start(f32[16,512]{1,0:T(8,128)S(1)} %join.1), channel_id=1, source_target_pairs={{0,2},{1,3},{2,0},{3,1},{4,6},{5,7},{6,4},{7,5},{8,10},{9,11},{10,... | collective-permute-start | bytes 98312 | tf_op jit(solution)/shard_map/ppermute | solution.py:724
  19.6 2.0 %collective-permute-start.5 = (f32[16,256]{1,0:T(8,128)S(1)}, f32[16,256]{1,0:T(8,128)S(1)}, u32[]{:S(2)}, u32[]{:S(2)}) collective-permute-start(f32[16,256]{1,0:T(8,128)S(1)} %get-tuple-element.28), channel_id=1, source_target_pairs={{0,4},{4,0},{8,12},{12,8},{1,5},{5,1},{9,13},{13,9},{2,6},{6,2},{1... | collective-permute-start | bytes 49160 | tf_op jit(solution)/shard_map/ppermute | solution.py:724
  19.8 3.7 %collective-permute-start.6 = (f32[16,256]{1,0:T(8,128)S(1)}, f32[16,256]{1,0:T(8,128)S(1)}, u32[]{:S(2)}, u32[]{:S(2)}) collective-permute-start(f32[16,256]{1,0:T(8,128)S(1)} %get-tuple-element.29), channel_id=1, source_target_pairs={{0,8},{4,12},{8,0},{12,4},{1,9},{5,13},{9,1},{13,5},{2,10},{6,14},... | collective-permute-start | bytes 49160 | tf_op jit(solution)/shard_map/ppermute | solution.py:724
  21.3 3.2 %collective-permute-start.7 = (f32[16,256]{1,0:T(8,128)S(1)}, f32[16,256]{1,0:T(8,128)S(1)}, u32[]{:S(2)}, u32[]{:S(2)}) collective-permute-start(f32[16,256]{1,0:T(8,128)S(1)} %get-tuple-element.30), channel_id=1, source_target_pairs={{0,12},{4,8},{8,4},{12,0},{1,13},{5,9},{9,5},{13,1},{2,14},{6,10},... | collective-permute-start | bytes 49160 | tf_op jit(solution)/shard_map/ppermute | solution.py:724

commit v8 on v7

--- a/solution.py
+++ b/solution.py
@@ -341,11 +341,13 @@
 
 
 def composite(tiles, first_group, me, rows, info_s, rendered, work):
-    alpha_s, weight_s, pull_s, push_s, weight_hi, weight_lo, coef_s, mix_s, acc_s = work
+    alpha_s, weight_s, pull_s, push_s, weight_2, coef_s, colour_s, error_s, mix_s, index_s, acc_s = work
     groups, tile_count, _, listed = acc_s.shape
     pixels = info_s.shape[2] // tile_count
     parts = pixels // LANES
-    spans = groups * tile_count * parts
+    halves = listed // LANES
+    tiles_here = groups * tile_count
+    spans = tiles_here * parts
     slabs = rows.shape[0] // ROWS
     side = TILE_SIDE
     first_col, first_row = tiles
@@ -356,156 +358,199 @@
     def of_place(place):
         return pl.ds(place * LIST_STEP, spans, stride=SPAN_STEP)
 
+    def lane_gather(source, lane):
+        return jnp.take_along_axis(source, lane, axis=1, mode="promise_in_bounds")
+
     basis = pixel_basis(pixels)
     basis_3 = jnp.concatenate([basis, basis, basis], axis=0).astype(BF16)
 
-    means, colours = [], []
-    for g in range(groups):
-        for t in range(tile_count):
-            halves = []
-            for first in range(t * listed, (t + 1) * listed, LANES):
-                at = info_s[g, 3:4, first : first + LANES].astype(jnp.int32)
-                at = jnp.broadcast_to(at, (ROWS, LANES))
-                lane, slab = at & (LANES - 1), at >> 7
-                found = jnp.zeros((ROWS, LANES), F32)
-                for s in range(slabs):
-                    here = jnp.take_along_axis(
-                        rows[s * ROWS : (s + 1) * ROWS, :], lane, axis=1, mode="promise_in_bounds"
-                    )
-                    found = jnp.where(slab == s, here, found)
-                halves.append(found)
-            entry = jnp.concatenate(halves, axis=1)
-            slot = (me ^ (first_group + g)) * tile_count + t
-            mean_u = entry[0:1] - (((first_col + slot % 4) * side).astype(F32) + 0.5 * side)
-            mean_v = entry[1:2] - (((first_row + slot // 4) * side).astype(F32) + 0.5 * side)
-            quad_a, quad_b, quad_c = -0.5 * entry[2:3], -entry[3:4], -0.5 * entry[4:5]
-            means.append((mean_u, mean_v, quad_a, quad_b, quad_c))
-            slope_u = 2.0 * quad_a * mean_u + quad_b * mean_v
-            slope_v = 2.0 * quad_c * mean_v + quad_b * mean_u
-            level = 0.5 * (slope_u * mean_u + slope_v * mean_v) + entry[5:6]
-            zero = jnp.zeros_like(level)
-            coef = jnp.concatenate(
-                [level, -slope_u, -slope_v, quad_a, quad_b, quad_c, zero, zero], axis=0
+    entries = []
+    for n in range(tiles_here):
+        g, t = n // tile_count, n % tile_count
+        found = []
+        for h in range(halves):
+            first = t * listed + h * LANES
+            at = info_s[g, 3:4, first : first + LANES].astype(jnp.int32)
+            index_s[n * halves + h : n * halves + h + 1, :] = at
+            at = jnp.broadcast_to(at, (8, LANES))
+            lane, slab = at & (LANES - 1), at >> 7
+            value = lane_gather(rows[0:8, :], lane)
+            for s in range(1, slabs):
+                value = jnp.where(
+                    slab == s, lane_gather(rows[s * ROWS : s * ROWS + 8, :], lane), value
+                )
+            found.append(value)
+        entries.append(jnp.concatenate(found, axis=1))
+    at = index_s[...]
+    lane, slab = at & (LANES - 1), at >> 7
+    ninth = lane_gather(rows[8:16, :], lane)
+    for s in range(1, slabs):
+        ninth = jnp.where(
+            slab == s, lane_gather(rows[s * ROWS + 8 : s * ROWS + 16, :], lane), ninth
+        )
+
+    means = []
+    colour_s[...] = jnp.zeros(colour_s.shape, F32)
+    for n in range(tiles_here):
+        g, t = n // tile_count, n % tile_count
+        entry = entries[n]
+        slot = (me ^ (first_group + g)) * tile_count + t
+        mean_u = entry[0:1] - (((first_col + slot % 4) * side).astype(F32) + 0.5 * side)
+        mean_v = entry[1:2] - (((first_row + slot // 4) * side).astype(F32) + 0.5 * side)
+        quad_a, quad_b, quad_c = -0.5 * entry[2:3], -entry[3:4], -0.5 * entry[4:5]
+        means.append((mean_u, mean_v, quad_a, quad_b, quad_c))
+        slope_u = 2.0 * quad_a * mean_u + quad_b * mean_v
+        slope_v = 2.0 * quad_c * mean_v + quad_b * mean_u
+        level = 0.5 * (slope_u * mean_u + slope_v * mean_v) + entry[5:6]
+        zero = jnp.zeros_like(level)
+        coef = jnp.concatenate(
+            [level, -slope_u, -slope_v, quad_a, quad_b, quad_c, zero, zero], axis=0
+        )
+        here = slice(n * listed, (n + 1) * listed)
+        for part in range(3):
+            term = coef.astype(BF16).astype(F32)
+            coef_s[part * 8 : part * 8 + 8, here] = term
+            coef = coef - term
+        last = [ninth[n * halves + h : n * halves + h + 1] for h in range(halves)]
+        colours = jnp.concatenate([entry[6:8], jnp.concatenate(last, axis=1)], axis=0)
+        high = colours.astype(BF16).astype(F32)
+        colour_s[n * ROWS : n * ROWS + 3, here] = high
+        colour_s[n * ROWS + 3 : n * ROWS + 6, here] = colours - high
+        colour_s[n * ROWS + 6 : n * ROWS + 9, here] = high
+
+    down = ((0,), (0,))
+    power = matmul(coef_s[...].astype(BF16), basis_3, down)
+    for n in range(tiles_here):
+        for part in range(parts):
+            alpha_s[of_span(n * parts + part), :] = jnp.exp(
+                power[n * listed : (n + 1) * listed, part * LANES : (part + 1) * LANES]
             )
-            for part in range(3):
-                term = coef.astype(BF16).astype(F32)
-                coef_s[part * 8 : part * 8 + 8, :] = term
-                coef = coef - term
-            power = matmul(coef_s[...].astype(BF16), basis_3, ((0,), (0,)))
-            n = g * tile_count + t
-            for part in range(parts):
-                at = slice(part * LANES, (part + 1) * LANES)
-                alpha_s[of_span(n * parts + part), :] = jnp.exp(power[:, at])
-            high = entry[6:9].astype(BF16).astype(F32)
-            low = entry[6:9] - high
-            zero = jnp.zeros((2, listed), F32)
-            colours.append(jnp.concatenate([high, low, zero], axis=0).astype(BF16))
-
-    unroll = 32
+
+    unroll, quad = 32, 4
     steps = listed // unroll
 
     def forward(step, passed):
-        for j in range(unroll):
-            at = of_place(step * unroll + j)
-            alpha = alpha_s[at, :]
-            weight_s[at, :] = alpha * passed
-            passed = passed * (1.0 - alpha)
+        for j in range(0, unroll, quad):
+            at = [of_place(step * unroll + j + i) for i in range(quad)]
+            alpha = [alpha_s[at[i], :] for i in range(quad)]
+            keep = [1.0 - alpha[i] for i in range(quad)]
+            two = keep[0] * keep[1]
+            three = two * keep[2]
+            weight_s[at[0], :] = alpha[0] * passed
+            weight_s[at[1], :] = (alpha[1] * keep[0]) * passed
+            weight_s[at[2], :] = (alpha[2] * two) * passed
+            weight_s[at[3], :] = (alpha[3] * three) * passed
+            passed = passed * (two * (keep[2] * keep[3]))
         return passed
 
     nought = jnp.zeros((spans, LANES), F32)
     lax.fori_loop(0, steps, forward, nought + 1.0)
 
-    errors = []
-    for n in range(groups * tile_count):
+    error_s[...] = jnp.zeros(error_s.shape, F32)
+    mix_s[...] = jnp.zeros(mix_s.shape, F32)
+    for n in range(tiles_here):
         g, t = n // tile_count, n % tile_count
         for part in range(parts):
             at = slice((n * parts + part) * LANES, (n * parts + part + 1) * LANES)
-            weight_hi[:, at], weight_lo[:, at] = split(weight_s[of_span(n * parts + part), :])
+            weight_2[:listed, at], weight_2[listed:, at] = split(
+                weight_s[of_span(n * parts + part), :]
+            )
         at = slice(n * pixels, (n + 1) * pixels)
-        image = matmul(colours[n], weight_hi[:, at])
-        image = image[0:3] + image[3:6] + matmul(colours[n], weight_lo[:, at])[0:3]
+        colours = colour_s[n * ROWS : (n + 1) * ROWS, n * listed : (n + 1) * listed].astype(BF16)
+        image = matmul(colours, weight_2[:listed, at])
+        image = image[0:3] + image[3:6] + matmul(colours, weight_2[listed:, at])[0:3]
         here = slice(t * pixels, (t + 1) * pixels)
         if rendered is not None and g == 0:
             rendered[:, here] = image
         error = image - info_s[g, 0:3, here]
         high = error.astype(BF16).astype(F32)
         low = error - high
-        errors.append((high, low))
-        zero = jnp.zeros((2, pixels), F32)
-        both = jnp.concatenate([high, high, zero], axis=0).astype(BF16)
-        rest = jnp.concatenate([low, jnp.zeros((5, pixels), F32)], axis=0).astype(BF16)
-        first = ((0,), (0,))
-        pull = matmul(colours[n], both, first) + matmul(colours[n], rest, first)
-        for part in range(parts):
-            at = slice(part * LANES, (part + 1) * LANES)
-            pull_s[of_span(n * parts + part), :] = pull[:, at]
-
-    def backward(back, behind):
-        for j in range(unroll):
-            at = of_place(listed - 1 - (back * unroll + j))
-            alpha, pull = alpha_s[at, :], pull_s[at, :]
-            push_s[at, :] = weight_s[at, :] * (pull - behind)
-            behind = behind * (1.0 - alpha) + alpha * pull
-        return behind
-
-    lax.fori_loop(0, steps, backward, nought)
-
-    mix_s[...] = jnp.zeros(mix_s.shape, F32)
-    for n in range(groups * tile_count):
-        at = slice(n * pixels, (n + 1) * pixels)
+        error_s[n * ROWS : n * ROWS + 3, :] = high
+        error_s[n * ROWS + 3 : n * ROWS + 6, :] = high
+        error_s[n * ROWS + 6 : n * ROWS + 9, :] = low
         mix_s[0, n * ROWS : n * ROWS + 8, at] = basis
-        high, low = errors[n]
         mix_s[1, n * ROWS + 6 : n * ROWS + 9, at] = high
         mix_s[1, n * ROWS + 9 : n * ROWS + 12, at] = low
-    moments, colour_sums = mix_s[0].astype(BF16), mix_s[1].astype(BF16)
+    pull = matmul(colour_s[...].astype(BF16), error_s[...].astype(BF16), down)
+    for n in range(tiles_here):
+        for part in range(parts):
+            pull_s[of_span(n * parts + part), :] = pull[
+                n * listed : (n + 1) * listed, part * LANES : (part + 1) * LANES
+            ]
+
+    def backward(back, behind):
+        for j in range(0, unroll, quad):
+            at = [of_place(listed - 1 - (back * unroll + j + i)) for i in range(quad)]
+            alpha = [alpha_s[at[i], :] for i in range(quad)]
+            pull = [pull_s[at[i], :] for i in range(quad)]
+            keep = [1.0 - alpha[i] for i in range(quad)]
+            own = alpha[0] * pull[0]
+            seen, through = behind, keep[0]
+            for i in range(quad):
+                push_s[at[i], :] = weight_s[at[i], :] * (pull[i] - seen)
+                if i > 0:
+                    own = own * keep[i] + alpha[i] * pull[i]
+                    through = through * keep[i]
+                seen = behind * through + own
+            behind = seen
+        return behind
+
+    lax.fori_loop(0, steps, backward, nought)
+
+    across = ((1,), (1,))
     high, low = split(jnp.concatenate([push_s[of_span(span), :] for span in range(spans)], axis=1))
-    across = ((1,), (1,))
-    sums = matmul(high, moments, across) + matmul(low, moments, across)
-    sums = sums + matmul(weight_hi[...], colour_sums, across)
-    sums = sums + matmul(weight_lo[...], colour_sums, across)
-    sums = sums.T
-    for g in range(groups):
-        for t in range(tile_count):
-            n = g * tile_count + t
-            mean_u, mean_v, quad_a, quad_b, quad_c = means[n]
-            m_00, m_10, m_01, m_20, m_11, m_02 = [
-                sums[n * ROWS + m : n * ROWS + m + 1] for m in range(6)
-            ]
-            n_10 = m_10 - mean_u * m_00
-            n_01 = m_01 - mean_v * m_00
-            acc_s[g, t, 0:1, :] = -(2.0 * quad_a * n_10 + quad_b * n_01)
-            acc_s[g, t, 1:2, :] = -(2.0 * quad_c * n_01 + quad_b * n_10)
-            acc_s[g, t, 2:3, :] = -0.5 * (m_20 - mean_u * (m_10 + n_10))
-            acc_s[g, t, 3:4, :] = -(m_11 - mean_u * m_01 - mean_v * n_10)
-            acc_s[g, t, 4:5, :] = -0.5 * (m_02 - mean_v * (m_01 + n_01))
-            acc_s[g, t, 5:6, :] = m_00
-            at = n * ROWS + 6
-            acc_s[g, t, 6:9, :] = sums[at : at + 3] + sums[at + 3 : at + 6]
-            acc_s[g, t, 9:16, :] = jnp.zeros((7, listed), F32)
+    sums = matmul(jnp.concatenate([high, low], axis=0), mix_s[0].astype(BF16), across)
+    sums = sums + matmul(weight_2[...], mix_s[1].astype(BF16), across)
+    sums = (sums[:listed] + sums[listed:]).T
+    for n in range(tiles_here):
+        g, t = n // tile_count, n % tile_count
+        mean_u, mean_v, quad_a, quad_b, quad_c = means[n]
+        m_00, m_10, m_01, m_20, m_11, m_02 = [
+            sums[n * ROWS + m : n * ROWS + m + 1] for m in range(6)
+        ]
+        n_10 = m_10 - mean_u * m_00
+        n_01 = m_01 - mean_v * m_00
+        acc_s[g, t, 0:1, :] = -(2.0 * quad_a * n_10 + quad_b * n_01)
+        acc_s[g, t, 1:2, :] = -(2.0 * quad_c * n_01 + quad_b * n_10)
+        acc_s[g, t, 2:3, :] = -0.5 * (m_20 - mean_u * (m_10 + n_10))
+        acc_s[g, t, 3:4, :] = -(m_11 - mean_u * m_01 - mean_v * n_10)
+        acc_s[g, t, 4:5, :] = -0.5 * (m_02 - mean_v * (m_01 + n_01))
+        acc_s[g, t, 5:6, :] = m_00
+        at = n * ROWS + 6
+        grads = sums[at : at + 3] + sums[at + 3 : at + 6]
+        acc_s[g, t, 6:8, :] = grads[0:2]
+        for h in range(halves):
+            row = n * halves + h
+            acc_s[0, 0, 8 + row : 9 + row, :LANES] = grads[2:3, h * LANES : (h + 1) * LANES]
 
 
 def pool_sum(slab, info_s, acc_s):
-    _, tile_count, _, listed = acc_s.shape
+    groups, tile_count, _, listed = acc_s.shape
+    halves = listed // LANES
     width = info_s.shape[2]
     rows_each = (info_s.shape[1] - 4) // tile_count
-    totals = []
-    for g in range(2):
-        total = jnp.zeros((ROWS, LANES), F32)
+    row_of = lax.broadcasted_iota(jnp.int32, (8, LANES), 0)
+
+    def lane_gather(source, lane):
+        return jnp.take_along_axis(source, lane, axis=1, mode="promise_in_bounds")
+
+    totals, every = [], None
+    for g in range(groups):
+        total = jnp.zeros((8, LANES), F32)
         for t in range(tile_count):
             row, first = 4 + t * rows_each + slab * LANES // width, slab * LANES % width
             at = info_s[g, row : row + 1, first : first + LANES].astype(jnp.int32)
-            at = jnp.broadcast_to(at, (ROWS, LANES))
+            at = jnp.broadcast_to(at, (8, LANES))
+            n = g * tile_count + t
+            every = at if every is None else jnp.where(row_of >= n * halves, at, every)
             lane, half = at & (LANES - 1), at >> 7
-            for h in range(listed // LANES):
-                here = jnp.take_along_axis(
-                    acc_s[g, t, :, h * LANES : (h + 1) * LANES],
-                    lane,
-                    axis=1,
-                    mode="promise_in_bounds",
-                )
+            for h in range(halves):
+                here = lane_gather(acc_s[g, t, 0:8, h * LANES : (h + 1) * LANES], lane)
                 total = total + jnp.where(half == h, here, 0.0)
         totals.append(total)
-    return totals[0] + totals[1]
+    here = lane_gather(acc_s[0, 0, 8:16, :LANES], every & (LANES - 1))
+    ninth = jnp.where(every >> 7 == row_of % halves, here, 0.0)
+    return totals[0] + totals[1], jnp.sum(ninth, axis=0, keepdims=True)
 
 
 def block_start(tile_id):
@@ -522,36 +567,41 @@
     projected = project_rows(lambda f: feats[f * slabs : (f + 1) * slabs, :], cam)
     for f, value in enumerate(projected):
         rows[pl.ds(f, slabs, stride=ROWS), :] = value
-    zero_row = jnp.zeros((slabs, LANES), F32)
     for f in range(len(projected), ROWS):
-        rows[pl.ds(f, slabs, stride=ROWS), :] = zero_row
+        rows[pl.ds(f, slabs, stride=ROWS), :] = projected[8]
     info_s[0] = own[...]
     info_s[1] = other[...]
     composite(block_start(tile_ids[0]), 0, where[0], rows, info_s, rendered, work)
     for s in range(slabs):
-        partial[:, s * LANES : (s + 1) * LANES] = pool_sum(s, info_s, work[-1])
+        at = slice(s * LANES, (s + 1) * LANES)
+        partial[0:8, at], partial[8:9, at] = pool_sum(s, info_s, work[-1])
 
 
 def far_kernel(blocks, tile_ids, where, rows, partial, infos, *refs):
-    *packets, info_s = refs[: len(refs) - 9]
-    work = refs[len(refs) - 9 :]
+    *packets, info_s = refs[: len(refs) - 11]
+    work = refs[len(refs) - 11 :]
     half = infos.shape[0] // 2
     info_s[0] = infos[:half, :]
     info_s[1] = infos[half:, :]
     composite(block_start(tile_ids[0]), 2, where[0], rows, info_s, None, work)
     share = (tile_ids[0] // (TILES_X * TILES_Y)).astype(F32)
-    row_of = lax.broadcasted_iota(jnp.int32, (ROWS, LANES), 0)
-    lane_of = lax.broadcasted_iota(jnp.int32, (ROWS, LANES), 1)
+    row_of = lax.broadcasted_iota(jnp.int32, (8, LANES), 0)
+    lane_of = lax.broadcasted_iota(jnp.int32, (8, LANES), 1)
     chunk = packets[0].shape[1]
     for s in range(rows.shape[0] // ROWS):
-        total = partial[:, s * LANES : (s + 1) * LANES] + pool_sum(s, info_s, work[-1])
+        total, ninth = pool_sum(s, info_s, work[-1])
+        total = total + partial[0:8, s * LANES : (s + 1) * LANES]
+        ninth = ninth + partial[8:9, s * LANES : (s + 1) * LANES]
         if blocks == 1:
             mine = share
         else:
             column = s * LANES + lane_of
             mine = jnp.where(column % where[2] // (where[2] // blocks) == where[1], share, 0.0)
-        total = jnp.where(row_of == 9, mine, total)
-        packets[s * LANES // chunk][:, s * LANES % chunk : s * LANES % chunk + LANES] = total
+        at = slice(s * LANES % chunk, s * LANES % chunk + LANES)
+        packets[s * LANES // chunk][0:8, at] = total
+        packets[s * LANES // chunk][8:16, at] = jnp.where(
+            row_of == 0, jnp.broadcast_to(ninth, (8, LANES)), mine
+        )
 
 
 def join_kernel(first, second, out):
@@ -643,13 +693,16 @@
 
 
 def work_shapes(tile_count, pixels, listed):
-    spans = 2 * tile_count * pixels // LANES
-    assert (spans - 1) * SPAN_STEP < LIST_STEP
+    tiles = 2 * tile_count
+    spans = tiles * pixels // LANES
+    assert (spans - 1) * SPAN_STEP < LIST_STEP and tiles * listed // LANES == 8
     return [pltpu.VMEM((listed * LIST_STEP, LANES), F32)] * 4 + [
-        pltpu.VMEM((listed, spans * LANES), BF16),
-        pltpu.VMEM((listed, spans * LANES), BF16),
-        pltpu.VMEM((24, listed), F32),
+        pltpu.VMEM((2 * listed, spans * LANES), BF16),
+        pltpu.VMEM((24, tiles * listed), F32),
+        pltpu.VMEM((tiles * ROWS, tiles * listed), F32),
+        pltpu.VMEM((tiles * ROWS, pixels), F32),
         pltpu.VMEM((2, LANES, spans * LANES), F32),
+        pltpu.VMEM((8, LANES), jnp.int32),
         pltpu.VMEM((2, tile_count, ROWS, listed), F32),
     ]
 

time: 26.5 us -> 25.6 us (0.966)
  Pallas kernels: 12.1 us -> 11.2 us
    pallas_call x5, Pallas kernels: 12.1 us -> 11.2 us  [call(): pl.pallas_call(kernel, out_shape=out_shape, in_specs=in_specs, out_specs=...]
  transfers between devices with their start and end apart: 8 -> 8, of which waited for: 3 -> 3; matrix products, arithmetic and copies ran while one was open for 0% -> 0% of each run, Pallas kernels for 17% -> 16%
where the time goes in v8:
time: 25.6 us; the launch traced here: 25.4 us
  Pallas kernels  11.2 us (44%)
  starting transfers between devices  9.73 us (38%)
  waiting for transfers between devices  3.71 us (14%)
  between operations  0.7 us (3%)
    pallas_call x5, Pallas kernels, call(): pl.pallas_call(kernel, out_shape=out_shape, in_specs=in_specs, out_specs=...  11.2 us
    ppermute x8, starting transfers between devices, swap(): lax.ppermute(value, axis, [(k, k ^ d) for k in range(lax.axis_size(axis))])  9.73 us
    ppermute x8, waiting for transfers between devices, swap(): lax.ppermute(value, axis, [(k, k ^ d) for k in range(lax.axis_size(axis))])  3.71 us
  transfers between devices with their start and end apart: 8, of which 3 were waited for; matrix products, arithmetic and copies ran while one was open for 0% of the time, Pallas kernels for 16%

profile of v8, /device:TPU:0, one launch (start us, length us, event | category | flops | bytes accessed | tf_op | source)
XLA Modules:
  0.0 25.4 jit_solution(14476468902044577345)
XLA Ops:
  0.6 0.0 copy-start.2
  0.6 1.2 %pack.1 = (f32[8,512]{1,0:T(8,128)S(1)}, f32[59,256]{1,0:T(8,128)S(1)}, f32[59,256]{1,0:T(8,128)S(1)}, f32[59,256]{1,0:T(8,128)S(1)}, f32[59,256]{1,0:T(8,128)S(1)}) custom-call(s32[1]{0:T(128)} %bitcast.2.where, s32[2,1,256]{2,1,0:T(1,128)} %bitcast.4, s32[2,256]{1,0:T(2,128)} %refs_1_.1, f32[3,512]{1,0:T(4,128)} %refs_2_.1, f32[59,1024]{1,0:T(8,128)} %refs_4_.1), custom_call_target="tpu_custom_call" | custom-call | tf_op jit(solution)/shard_map/pack/pallas_call | solution.py:684
  1.8 3.1 %collective-permute-start = (f32[8,512]{1,0:T(8,128)S(1)}, f32[8,512]{1,0:T(8,128)S(1)}, u32[]{:S(2)}, u32[]{:S(2)}) collective-permute-start(f32[8,512]{1,0:T(8,128)S(1)} %get-tuple-element.19.own.first), channel_id=1, source_target_pairs={{0,1},{1,0},{2,3},{3,2},{4,5},{5,4},{6,7},{7,6},{8,9},{9,8},{10,11... | collective-permute-start | bytes 49160 | tf_op jit(solution)/shard_map/ppermute | solution.py:777
  4.9 0.0 collective-permute-start.1
  4.9 1.5 %collective-permute-start.2 = (f32[59,256]{1,0:T(8,128)S(1)}, f32[59,256]{1,0:T(8,128)S(1)}, u32[]{:S(2)}, u32[]{:S(2)}) collective-permute-start(f32[59,256]{1,0:T(8,128)S(1)} %get-tuple-element.22), channel_id=1, source_target_pairs={{0,8},{4,12},{8,0},{12,4},{1,9},{5,13},{9,1},{13,5},{2,10},{6,14},... | collective-permute-start | bytes 181256 | tf_op jit(solution)/shard_map/ppermute | solution.py:777
  6.4 0.4 %collective-permute-start.3 = (f32[59,256]{1,0:T(8,128)S(1)}, f32[59,256]{1,0:T(8,128)S(1)}, u32[]{:S(2)}, u32[]{:S(2)}) collective-permute-start(f32[59,256]{1,0:T(8,128)S(1)} %get-tuple-element.23), channel_id=1, source_target_pairs={{0,12},{4,8},{8,4},{12,0},{1,13},{5,9},{9,5},{13,1},{2,14},{6,10},... | collective-permute-start | bytes 181256 | tf_op jit(solution)/shard_map/ppermute | solution.py:777
  6.8 0.0 copy-start.3
  6.8 0.0 copy-start.4
  6.8 0.0 copy-start
  6.8 0.0 copy-start.1
  6.8 0.0 collective-permute-done.other.second
  6.8 2.9 %collective-permute-start.4 = (f32[16,512]{1,0:T(8,128)S(1)}, f32[16,512]{1,0:T(8,128)S(1)}, u32[]{:S(2)}, u32[]{:S(2)}) collective-permute-start(f32[16,512]{1,0:T(8,128)S(1)} %join.1), channel_id=1, source_target_pairs={{0,2},{1,3},{2,0},{3,1},{4,6},{5,7},{6,4},{7,5},{8,10},{9,11},{10,... | collective-permute-start | bytes 98312 | tf_op jit(solution)/shard_map/ppermute | solution.py:777
  9.7 0.1 pad_add_fusion.where
  9.8 0.0 collective-permute-done.1.refs_1_
  9.8 0.0 collective-permute-done.2.refs_2_
  9.8 0.8 %collective-permute-done.3.refs_3_ = f32[59,256]{1,0:T(8,128)S(1)} collective-permute-done((f32[59,256]{1,0:T(8,128)S(1)}, f32[59,256]{1,0:T(8,128)S(1)}, u32[]{:S(2)}, u32[]{:S(2)}) %collective-permute-start.3) | collective-permute-done | bytes 60448 | tf_op jit(solution)/shard_map/ppermute | solution.py:777
  10.5 0.0 copy-done.3
  10.5 0.0 copy-done.4
  10.6 4.1 %near.1 = (f32[3,512]{1,0:T(4,128)}, f32[128,128]{1,0:T(8,128)S(1)}, f32[16,1024]{1,0:T(8,128)S(1)}) custom-call(s32[2]{0:T(128)S(1)} %copy-done.4, f32[4,12]{1,0:T(4,128)S(1)} %copy-done.3, s32[3]{0:T(128)S(1)} %pad_add_fusion.where, f32[8,512]{1,0:T(8,128)S(1)} %get-tuple-element.19.own.first, f32[8,512]{1,0:T(8,128)S(1)} %collective-permute-done.other.second, ...), custom_call_target="tpu_custom_call" | custom-call | tf_op jit(solution)/shard_map/near/pallas_call | solution.py:684
  14.7 0.0 collective-permute-done.4.infos
  14.7 4.0 %far.1 = (f32[16,256]{1,0:T(8,128)S(1)}, f32[16,256]{1,0:T(8,128)S(1)}, f32[16,256]{1,0:T(8,128)S(1)}, f32[16,256]{1,0:T(8,128)S(1)}) custom-call(s32[2]{0:T(128)S(1)} %copy-done.4, s32[3]{0:T(128)S(1)} %pad_add_fusion.where, f32[128,128]{1,0:T(8,128)S(1)} %get-tuple-element.25.rows, f32[16,1024]{1,0:T(8,128)S(1)} %get-tuple-element.26.partial, ...), custom_call_target="tpu_custom_call" | custom-call | tf_op jit(solution)/shard_map/far/pallas_call | solution.py:684
  18.7 0.2 collective-permute-start.5
  18.9 1.5 %collective-permute-start.6 = (f32[16,256]{1,0:T(8,128)S(1)}, f32[16,256]{1,0:T(8,128)S(1)}, u32[]{:S(2)}, u32[]{:S(2)}) collective-permute-start(f32[16,256]{1,0:T(8,128)S(1)} %get-tuple-element.29), channel_id=1, source_target_pairs={{0,8},{4,12},{8,0},{12,4},{1,9},{5,13},{9,1},{13,5},{2,10},{6,14},... | collective-permute-start | bytes 49160 | tf_op jit(solution)/shard_map/ppermute | solution.py:777
  20.4 0.2 collective-permute-start.7
  20.6 0.0 collective-permute-done.5.refs_1_
  20.6 2.0 %collective-permute-done.6.refs_2_ = f32[16,256]{1,0:T(8,128)S(1)} collective-permute-done((f32[16,256]{1,0:T(8,128)S(1)}, f32[16,256]{1,0:T(8,128)S(1)}, u32[]{:S(2)}, u32[]{:S(2)}) %collective-permute-start.6) | collective-permute-done | bytes 16416 | tf_op jit(solution)/shard_map/ppermute | solution.py:777
  22.6 0.9 %collective-permute-done.7.refs_3_ = f32[16,256]{1,0:T(8,128)S(1)} collective-permute-done((f32[16,256]{1,0:T(8,128)S(1)}, f32[16,256]{1,0:T(8,128)S(1)}, u32[]{:S(2)}, u32[]{:S(2)}) %collective-permute-start.7) | collective-permute-done | bytes 16416 | tf_op jit(solution)/shard_map/ppermute | solution.py:777
  23.5 0.0 copy-done.2
  23.5 0.0 copy-done
  23.5 0.0 copy-done.1
  23.6 1.9 %update.1 = (f32[59,1024]{1,0:T(8,128)}, f32[59,1024]{1,0:T(8,128)}, f32[59,1024]{1,0:T(8,128)}) custom-call(s32[1]{0:T(128)} %bitcast.2.where, f32[4,12]{1,0:T(4,128)S(1)} %copy-done.3, f32[16,256]{1,0:T(8,128)S(1)} %get-tuple-element.27.refs_0_, f32[16,256]{1,0:T(8,128)S(1)} %collective-permute-done.5.refs_1_, ...), custom_call_target="tpu_custom_call" | custom-call | tf_op jit(solution)/shard_map/update/pallas_call | solution.py:684
  (1 shorter events, 0.0 us)
Async XLA Ops:
  0.6 22.9 %copy-start.2 = (f32[59,1024]{1,0:T(8,128)S(1)}, f32[59,1024]{1,0:T(8,128)}, u32[]{:S(2)}) copy-start(f32[59,1024]{1,0:T(8,128)} %refs_6_.1) | copy-start | bytes 724996
  1.8 5.0 %collective-permute-start = (f32[8,512]{1,0:T(8,128)S(1)}, f32[8,512]{1,0:T(8,128)S(1)}, u32[]{:S(2)}, u32[]{:S(2)}) collective-permute-start(f32[8,512]{1,0:T(8,128)S(1)} %get-tuple-element.19.own.first), channel_id=1, source_target_pairs={{0,1},{1,0},{2,3},{3,2},{4,5},{5,4},{6,7},{7,6},{8,9},{9,8},{10,11... | collective-permute-start | bytes 49160 | tf_op jit(solution)/shard_map/ppermute | solution.py:777
  4.9 4.8 %collective-permute-start.1 = (f32[59,256]{1,0:T(8,128)S(1)}, f32[59,256]{1,0:T(8,128)S(1)}, u32[]{:S(2)}, u32[]{:S(2)}) collective-permute-start(f32[59,256]{1,0:T(8,128)S(1)} %get-tuple-element.21), channel_id=1, source_target_pairs={{0,4},{4,0},{8,12},{12,8},{1,5},{5,1},{9,13},{13,9},{2,6},{6,2},{1... | collective-permute-start | bytes 181256 | tf_op jit(solution)/shard_map/ppermute | solution.py:777
  4.9 4.8 %collective-permute-start.2 = (f32[59,256]{1,0:T(8,128)S(1)}, f32[59,256]{1,0:T(8,128)S(1)}, u32[]{:S(2)}, u32[]{:S(2)}) collective-permute-start(f32[59,256]{1,0:T(8,128)S(1)} %get-tuple-element.22), channel_id=1, source_target_pairs={{0,8},{4,12},{8,0},{12,4},{1,9},{5,13},{9,1},{13,5},{2,10},{6,14},... | collective-permute-start | bytes 181256 | tf_op jit(solution)/shard_map/ppermute | solution.py:777
  6.4 4.1 %collective-permute-start.3 = (f32[59,256]{1,0:T(8,128)S(1)}, f32[59,256]{1,0:T(8,128)S(1)}, u32[]{:S(2)}, u32[]{:S(2)}) collective-permute-start(f32[59,256]{1,0:T(8,128)S(1)} %get-tuple-element.23), channel_id=1, source_target_pairs={{0,12},{4,8},{8,4},{12,0},{1,13},{5,9},{9,5},{13,1},{2,14},{6,10},... | collective-permute-start | bytes 181256 | tf_op jit(solution)/shard_map/ppermute | solution.py:777
  6.8 3.8 %copy-start.3 = (f32[4,12]{1,0:T(4,128)S(1)}, f32[4,12]{1,0:T(4,128)}, u32[]{:S(2)}) copy-start(f32[4,12]{1,0:T(4,128)} %cams.3) | copy-start | bytes 580
  6.8 3.8 %copy-start.4 = (s32[2]{0:T(128)S(1)}, s32[2]{0:T(128)}, u32[]{:S(2)}) copy-start(s32[2]{0:T(128)} %tile_ids.3) | copy-start | bytes 28
  6.8 16.8 %copy-start = (f32[59,1024]{1,0:T(8,128)S(1)}, f32[59,1024]{1,0:T(8,128)}, u32[]{:S(2)}) copy-start(f32[59,1024]{1,0:T(8,128)} %refs_4_.1) | copy-start | bytes 724996
  6.8 16.8 %copy-start.1 = (f32[59,1024]{1,0:T(8,128)S(1)}, f32[59,1024]{1,0:T(8,128)}, u32[]{:S(2)}) copy-start(f32[59,1024]{1,0:T(8,128)} %refs_5_.1) | copy-start | bytes 724996
  6.8 7.9 %collective-permute-start.4 = (f32[16,512]{1,0:T(8,128)S(1)}, f32[16,512]{1,0:T(8,128)S(1)}, u32[]{:S(2)}, u32[]{:S(2)}) collective-permute-start(f32[16,512]{1,0:T(8,128)S(1)} %join.1), channel_id=1, source_target_pairs={{0,2},{1,3},{2,0},{3,1},{4,6},{5,7},{6,4},{7,5},{8,10},{9,11},{10,... | collective-permute-start | bytes 98312 | tf_op jit(solution)/shard_map/ppermute | solution.py:777
  18.7 1.9 %collective-permute-start.5 = (f32[16,256]{1,0:T(8,128)S(1)}, f32[16,256]{1,0:T(8,128)S(1)}, u32[]{:S(2)}, u32[]{:S(2)}) collective-permute-start(f32[16,256]{1,0:T(8,128)S(1)} %get-tuple-element.28), channel_id=1, source_target_pairs={{0,4},{4,0},{8,12},{12,8},{1,5},{5,1},{9,13},{13,9},{2,6},{6,2},{1... | collective-permute-start | bytes 49160 | tf_op jit(solution)/shard_map/ppermute | solution.py:777
  18.9 3.8 %collective-permute-start.6 = (f32[16,256]{1,0:T(8,128)S(1)}, f32[16,256]{1,0:T(8,128)S(1)}, u32[]{:S(2)}, u32[]{:S(2)}) collective-permute-start(f32[16,256]{1,0:T(8,128)S(1)} %get-tuple-element.29), channel_id=1, source_target_pairs={{0,8},{4,12},{8,0},{12,4},{1,9},{5,13},{9,1},{13,5},{2,10},{6,14},... | collective-permute-start | bytes 49160 | tf_op jit(solution)/shard_map/ppermute | solution.py:777
  20.4 3.2 %collective-permute-start.7 = (f32[16,256]{1,0:T(8,128)S(1)}, f32[16,256]{1,0:T(8,128)S(1)}, u32[]{:S(2)}, u32[]{:S(2)}) collective-permute-start(f32[16,256]{1,0:T(8,128)S(1)} %get-tuple-element.30), channel_id=1, source_target_pairs={{0,12},{4,8},{8,4},{12,0},{1,13},{5,9},{9,5},{13,1},{2,14},{6,10},... | collective-permute-start | bytes 49160 | tf_op jit(solution)/shard_map/ppermute | solution.py:777

commit v9 on v5

--- a/solution.py
+++ b/solution.py
@@ -136,12 +136,11 @@
     cov_yy = sum(wide[1][k] * axes[1][k] for k in range(3)) + dilation
     rdet = 1.0 / (cov_xx * cov_yy - cov_xy * cov_xy)
     conic = (cov_yy * rdet, -cov_xy * rdet, cov_xx * rdet)
-    opacity = 1.0 / (1.0 + jnp.exp(-feat(10)))
     rlen = lax.rsqrt(off[0] * off[0] + off[1] * off[1] + off[2] * off[2])
     way = [off[a] * rlen for a in range(3)]
     return dict(
         rot=rot, inv=inv, u=u, v=v, finv=finv, scale=scale, rnorm=rnorm, rotor=(w, x, y, z), turn=turn,
-        screen=screen, axes=axes, wide=wide, conic=conic, opacity=opacity, rlen=rlen, way=way,
+        screen=screen, axes=axes, wide=wide, conic=conic, rlen=rlen, way=way,
     )
 
 
@@ -156,7 +155,9 @@
         colours.append(total)
     mean_x = focal_length * part["u"] + center_x
     mean_y = focal_length * part["v"] + center_y
-    return [mean_x, mean_y, *part["conic"], part["opacity"], *colours]
+    logit = feat(10)
+    log_opacity = jnp.minimum(logit, 0.0) - jnp.log(1.0 + jnp.exp(-jnp.abs(logit)))
+    return [mean_x, mean_y, *part["conic"], log_opacity, *colours]
 
 
 def project_pull(feat, cam, grads, put):
@@ -177,7 +178,7 @@
     g_way = sh_pull(pulled, *way)
     along = way[0] * g_way[0] + way[1] * g_way[1] + way[2] * g_way[2]
     g_off = [(g_way[a] - way[a] * along) * rlen for a in range(3)]
-    put(10, g_o * part["opacity"] * (1.0 - part["opacity"]))
+    put(10, g_o / (1.0 + jnp.exp(feat(10))))
     a, b, c = part["conic"]
     g_xx = -(a * a * g_a + a * b * g_b + b * b * g_c)
     g_xy = -(2.0 * a * b * g_a + (a * c + b * b) * g_b + 2.0 * b * c * g_c)
@@ -326,151 +327,251 @@
     return out[0], list(out[1:])
 
 
+def lane_gather(source, lane):
+    return jnp.take_along_axis(source, lane, axis=1, mode="promise_in_bounds")
+
+
+def spread(row):
+    return jnp.broadcast_to(row, (8, LANES))
+
+
 def composite(tiles, first_group, me, rows, info_s, rendered, work):
-    e_s, t_s, d_s, hi_s, lo_s, acc_s = work
-    tile_count, pixels, listed = e_s.shape
+    alpha_s, weight_s, left_s, image_s, before_s, behind_s, error_s, joined_s, wrong_s, coef_s, line_s, sum_s, acc_s = work
+    groups, tile_count, _, listed = acc_s.shape
+    pixels = info_s.shape[2] // tile_count
+    tiles_here = groups * tile_count
+    segments = LANES // tiles_here
+    steps = listed // segments
+    halves = listed // LANES
     slabs = rows.shape[0] // ROWS
     side = TILE_SIDE
+    middle = 0.5 * side - 0.5
     first_col, first_row = tiles
-    row_i = lax.broadcasted_iota(jnp.int32, (listed, listed), 0)
-    col_i = lax.broadcasted_iota(jnp.int32, (listed, listed), 1)
-    earlier = jnp.where(row_i < col_i, 1.0, 0.0).astype(BF16)
-    later = jnp.where(row_i > col_i, 1.0, 0.0).astype(BF16)
-    step = lax.broadcasted_iota(jnp.int32, (side, listed), 0).astype(F32)
-
-    def one_group(g, carry):
-        lists = []
-        for t in range(tile_count):
-            halves = []
-            for first in range(t * listed, (t + 1) * listed, LANES):
-                at = info_s[g, 3:4, first : first + LANES].astype(jnp.int32)
-                at = jnp.broadcast_to(at, (ROWS, LANES))
-                lane, slab = at & (LANES - 1), at >> 7
-                found = jnp.zeros((ROWS, LANES), F32)
-                for s in range(slabs):
-                    here = jnp.take_along_axis(
-                        rows[s * ROWS : (s + 1) * ROWS, :], lane, axis=1, mode="promise_in_bounds"
-                    )
-                    found = jnp.where(slab == s, here, found)
-                halves.append(found)
-            lists.append(jnp.concatenate(halves, axis=1))
-
-        setup = []
-        for t in range(tile_count):
-            entry = lists[t]
-            slot = (me ^ (first_group + g)) * tile_count + t
-            x_0 = ((first_col + slot % 4) * side).astype(F32) + 0.5
-            y_0 = ((first_row + slot // 4) * side).astype(F32) + 0.5
-            quad_a, quad_b, quad_c = -0.5 * entry[2:3], -entry[3:4], -0.5 * entry[4:5]
-            opacity = entry[5:6]
-            dx = (step + x_0) - entry[0:1]
-            dy = (step + y_0) - entry[1:2]
-            adx2 = quad_a * dx * dx
-            bdy = quad_b * dy
-            cdy2 = quad_c * dy * dy
-            setup.append((entry, quad_a, quad_b, quad_c, opacity, dx, dy))
-            for row in range(side):
-                at = slice(row * side, (row + 1) * side)
-                power = adx2 + dx * bdy[row : row + 1] + cdy2[row : row + 1]
-                bell = jnp.exp(power)
-                e_s[t, at, :] = bell
-                hi_s[t, at, :], lo_s[t, at, :] = split(jnp.log(1.0 - opacity * bell))
-
-        for t in range(tile_count):
-            t_s[t] = matmul(hi_s[t], earlier) + matmul(lo_s[t], earlier)
-
-        for t in range(tile_count):
-            entry, opacity = setup[t][0], setup[t][4]
-            for row in range(side):
-                at = slice(row * side, (row + 1) * side)
-                passed = jnp.exp(t_s[t, at, :])
-                t_s[t, at, :] = passed
-                hi_s[t, at, :], lo_s[t, at, :] = split(opacity * e_s[t, at, :] * passed)
-            c_hi, c_lo = split(entry[6:9])
-            both = ((1,), (1,))
-            image = (
-                matmul(c_hi, hi_s[t], both)
-                + matmul(c_lo, hi_s[t], both)
-                + matmul(c_hi, lo_s[t], both)
-            )
+    lane = lax.broadcasted_iota(jnp.int32, (8, LANES), 1)
+    sub = lax.broadcasted_iota(jnp.int32, (8, LANES), 0)
+    segment = lane % segments
+
+    pattern = (lane % (LANES // steps)) * steps + sub
+    place = jnp.zeros((8, LANES), F32)
+    col_0 = row_0 = jnp.zeros((8, LANES), F32)
+    for n in range(tiles_here):
+        g, t = n // tile_count, n % tile_count
+        for h in range(halves):
+            first = t * listed + h * LANES
+            here = lane_gather(spread(info_s[g, 3:4, first : first + LANES]), pattern)
+            place = jnp.where(lane // (LANES // steps) == n * halves + h, here, place)
+        slot = (me ^ (first_group + g)) * tile_count + t
+        own = lane // segments == n
+        col_0 = jnp.where(own, ((first_col + slot % 4) * side).astype(F32) + 0.5 * side, col_0)
+        row_0 = jnp.where(own, ((first_row + slot // 4) * side).astype(F32) + 0.5 * side, row_0)
+    place = place.astype(jnp.int32)
+    at, slab = place & (LANES - 1), place >> 7
+    entry = []
+    for f in range(9):
+        value = lane_gather(spread(rows[f : f + 1, :]), at)
+        for s in range(1, slabs):
+            here = lane_gather(spread(rows[s * ROWS + f : s * ROWS + f + 1, :]), at)
+            value = jnp.where(slab == s, here, value)
+        entry.append(value)
+    mean_u, mean_v = entry[0] - col_0, entry[1] - row_0
+    quad_a, quad_b, quad_c = -0.5 * entry[2], -entry[3], -0.5 * entry[4]
+    slope_u = 2.0 * quad_a * mean_u + quad_b * mean_v
+    slope_v = 2.0 * quad_c * mean_v + quad_b * mean_u
+    level = 0.5 * (slope_u * mean_u + slope_v * mean_v) + entry[5]
+    for f, value in enumerate(
+        (level, -slope_u, quad_a, -slope_v, quad_b, quad_c, entry[6], entry[7], entry[8])
+    ):
+        coef_s[f] = value
+    for s in range(steps):
+        c = [spread(coef_s[f, s : s + 1, :]) for f in range(5)]
+        for half in range(side // 8):
+            u = sub.astype(F32) + (8.0 * half - middle)
+            line_s[0, s, half] = c[0] + u * (c[1] + u * c[2])
+            line_s[1, s, half] = c[3] + u * c[4]
+
+    rows_each = 2
+
+    def forward(i, carry):
+        for j in range(rows_each):
+            row = i * rows_each + j
+            v = row.astype(F32) - middle
+            left = [None] * (side // 8)
+            image = [[None] * 3 for _ in left]
+            for s in range(steps):
+                quad = spread(coef_s[5, s : s + 1, :]) * v
+                colour = [spread(coef_s[6 + k, s : s + 1, :]) for k in range(3)]
+                for half in range(side // 8):
+                    power = line_s[0, s, half] + v * (line_s[1, s, half] + quad)
+                    alpha = jnp.exp(power)
+                    at = pl.ds(pl.multiple_of(row * side, side) + (s * pixels + half * 8), 8)
+                    alpha_s[at, :] = alpha
+                    if s == 0:
+                        weight = alpha
+                        left[half] = 1.0 - alpha
+                        image[half] = [weight * colour[k] for k in range(3)]
+                    else:
+                        weight = alpha * left[half]
+                        left[half] = left[half] - weight
+                        image[half] = [
+                            image[half][k] + weight * colour[k] for k in range(3)
+                        ]
+                    weight_s[at, :] = weight
+            for half in range(side // 8):
+                at = pl.ds(pl.multiple_of(row * side, side) + half * 8, 8)
+                left_s[at, :] = left[half]
+                for k in range(3):
+                    image_s[k, at, :] = image[half][k]
+        return carry
+
+    lax.fori_loop(0, side // rows_each, forward, 0)
+
+    tall = 32
+    segment_t = lax.broadcasted_iota(jnp.int32, (tall, LANES), 1) % segments
+    for first in range(0, pixels, tall):
+        at = slice(first, first + tall)
+        passed = left_s[at, :]
+        step = 1
+        while step < segments:
+            passed = passed * jnp.where(segment_t >= step, pltpu.roll(passed, step, 1), 1.0)
+            step *= 2
+        before = jnp.where(segment_t >= 1, pltpu.roll(passed, 1, 1), 1.0)
+        before_s[at, :] = before
+        for k in range(3):
+            joined_s[k, at, :LANES], joined_s[k, at, LANES:] = split(before * image_s[k, at, :])
+    pick = lax.broadcasted_iota(jnp.int32, (16, 2 * LANES), 1) % LANES // segments
+    pick = jnp.where(
+        pick == lax.broadcasted_iota(jnp.int32, (16, 2 * LANES), 0), 1.0, 0.0
+    ).astype(BF16)
+    wrong_s[...] = jnp.zeros(wrong_s.shape, F32)
+    for k in range(3):
+        image = matmul(pick, joined_s[k], ((1,), (1,)))
+        for n in range(tiles_here):
+            g, t = n // tile_count, n % tile_count
             here = slice(t * pixels, (t + 1) * pixels)
-            if rendered is not None:
-
-                @pl.when(g == 0)
-                def _():
-                    rendered[:, here] = image
-
-            error = image - info_s[g, 0:3, here]
-            g_hi, g_lo = split(error)
-            first = ((0,), (0,))
-            d_s[t] = (
-                matmul(g_hi, c_hi, first) + matmul(g_lo, c_hi, first) + matmul(g_hi, c_lo, first)
-            )
-            g_colours = matmul(g_hi, hi_s[t]) + matmul(g_lo, hi_s[t]) + matmul(g_hi, lo_s[t])
-            acc_s[g, t, 6:9, :] = g_colours
-
-        for t in range(tile_count):
-            opacity = setup[t][4]
-            for row in range(side):
-                at = slice(row * side, (row + 1) * side)
-                pushed = t_s[t, at, :] * d_s[t, at, :]
-                t_s[t, at, :] = pushed
-                hi_s[t, at, :], lo_s[t, at, :] = split(opacity * e_s[t, at, :] * pushed)
-            d_s[t] = matmul(hi_s[t], later) + matmul(lo_s[t], later)
-
-        for t in range(tile_count):
-            entry, quad_a, quad_b, quad_c, opacity, dx, dy = setup[t]
-            r_0 = r_1 = r_2 = None
-            for row in range(side):
-                at = slice(row * side, (row + 1) * side)
-                bell = e_s[t, at, :]
-                flow = bell * (t_s[t, at, :] - d_s[t, at, :] / (1.0 - opacity * bell))
-                one = flow * dy[row : row + 1]
-                two = one * dy[row : row + 1]
-                r_0 = flow if r_0 is None else r_0 + flow
-                r_1 = one if r_1 is None else r_1 + one
-                r_2 = two if r_2 is None else r_2 + two
-            rdx = r_0 * dx
-            m_00 = jnp.sum(r_0, axis=0, keepdims=True)
-            m_10 = jnp.sum(rdx, axis=0, keepdims=True)
-            m_20 = jnp.sum(rdx * dx, axis=0, keepdims=True)
-            m_01 = jnp.sum(r_1, axis=0, keepdims=True)
-            m_11 = jnp.sum(r_1 * dx, axis=0, keepdims=True)
-            m_02 = jnp.sum(r_2, axis=0, keepdims=True)
-            acc_s[g, t, 0:1, :] = -opacity * (2.0 * quad_a * m_10 + quad_b * m_01)
-            acc_s[g, t, 1:2, :] = -opacity * (2.0 * quad_c * m_01 + quad_b * m_10)
-            acc_s[g, t, 2:3, :] = -0.5 * opacity * m_20
-            acc_s[g, t, 3:4, :] = -opacity * m_11
-            acc_s[g, t, 4:5, :] = -0.5 * opacity * m_02
-            acc_s[g, t, 5:6, :] = m_00
-            acc_s[g, t, 9:16, :] = jnp.zeros((7, listed), F32)
+            if rendered is not None and g == 0:
+                rendered[k : k + 1, here] = image[n : n + 1]
+            wrong = image[n : n + 1] - info_s[g, k : k + 1, here]
+            high = wrong.astype(BF16).astype(F32)
+            wrong_s[k, n : n + 1, :] = high
+            wrong_s[k, 8 + n : 9 + n, :] = wrong - high
+    back = lax.broadcasted_iota(jnp.int32, (16, LANES), 1) // segments
+    back = jnp.where(
+        back == lax.broadcasted_iota(jnp.int32, (16, LANES), 0) % 8, 1.0, 0.0
+    ).astype(BF16)
+    for k in range(3):
+        error_s[k] = matmul(wrong_s[k].astype(BF16), back, ((0,), (0,)))
+
+    for first in range(0, pixels, tall):
+        at = slice(first, first + tall)
+        error = [error_s[k, at, :] for k in range(3)]
+        through = left_s[at, :]
+        own = sum(error[k] * image_s[k, at, :] for k in range(3))
+        step = 1
+        while step < segments:
+            inside = segment_t < segments - step
+            own = own + through * jnp.where(inside, pltpu.roll(own, LANES - step, 1), 0.0)
+            if 2 * step < segments:
+                through = through * jnp.where(inside, pltpu.roll(through, LANES - step, 1), 1.0)
+            step *= 2
+        before = before_s[at, :]
+        behind = jnp.where(segment_t < segments - 1, pltpu.roll(own, LANES - 1, 1), 0.0)
+        behind_s[at, :] = before * behind
+        for k in range(3):
+            error_s[k, at, :] = before * error[k]
+
+    def backward(i, carry):
+        s = steps - 1 - i
+        colour = [spread(coef_s[6 + k, pl.ds(s, 1), :]) for k in range(3)]
+        plain = [[None] * 3 for _ in range(side // 8)]
+        hues = [None] * 3
+        for row in range(side):
+            v = row - middle
+            for half in range(side // 8):
+                at = pl.ds(row * side + half * 8, 8)
+                of_step = pl.ds(pl.multiple_of(s * pixels, pixels) + (row * side + half * 8), 8)
+                weight = weight_s[of_step, :]
+                error = [error_s[k, at, :] for k in range(3)]
+                pull = error[0] * colour[0] + error[1] * colour[1] + error[2] * colour[2]
+                behind = behind_s[at, :]
+                gap = pull - behind
+                behind_s[at, :] = behind + alpha_s[of_step, :] * gap
+                push = weight * gap
+                terms = (push, v * push, (v * v) * push)
+                hue = [weight * error[k] for k in range(3)]
+                if row == 0:
+                    plain[half] = list(terms)
+                else:
+                    plain[half] = [plain[half][m] + terms[m] for m in range(3)]
+                hues = [hue[k] if hues[k] is None else hues[k] + hue[k] for k in range(3)]
+        u = [sub.astype(F32) + (8.0 * half - middle) for half in range(side // 8)]
+
+        def over(m, power):
+            total = 0.0
+            for half in range(side // 8):
+                value = plain[half][m]
+                for _ in range(power):
+                    value = value * u[half]
+                total = total + value
+            return total
+
+        for m, value in enumerate(
+            (over(0, 0), over(0, 1), over(1, 0), over(0, 2), over(1, 1), over(2, 0), *hues)
+        ):
+            sum_s[m, pl.ds(s, 1), :] = jnp.sum(value, axis=0, keepdims=True)
         return carry
 
-    lax.fori_loop(0, acc_s.shape[0], one_group, 0)
+    lax.fori_loop(0, steps, backward, 0)
+
+    m_00, m_10, m_01, m_20, m_11, m_02, *grads = [sum_s[m] for m in range(9)]
+    n_10 = m_10 - mean_u * m_00
+    n_01 = m_01 - mean_v * m_00
+    grads = [
+        -(2.0 * quad_a * n_10 + quad_b * n_01),
+        -(2.0 * quad_c * n_01 + quad_b * n_10),
+        -0.5 * (m_20 - mean_u * (m_10 + n_10)),
+        -(m_11 - mean_u * m_01 - mean_v * n_10),
+        -0.5 * (m_02 - mean_v * (m_01 + n_01)),
+        m_00,
+    ] + grads
+    mine = sub == lane % steps
+    for n in range(tiles_here):
+        g, t = n // tile_count, n % tile_count
+        for h in range(halves):
+            at = lane // steps + (n * segments + h * (LANES // steps))
+            for f in range(9):
+                row = jnp.sum(
+                    jnp.where(mine, lane_gather(grads[f], at), 0.0), axis=0, keepdims=True
+                )
+                if f < 8:
+                    acc_s[g, t, f : f + 1, h * LANES : (h + 1) * LANES] = row
+                else:
+                    acc_s[0, 0, 8 + n * halves + h : 9 + n * halves + h, :LANES] = row
 
 
 def pool_sum(slab, info_s, acc_s):
-    _, tile_count, _, listed = acc_s.shape
+    groups, tile_count, _, listed = acc_s.shape
+    halves = listed // LANES
     width = info_s.shape[2]
     rows_each = (info_s.shape[1] - 4) // tile_count
-    totals = []
-    for g in range(2):
-        total = jnp.zeros((ROWS, LANES), F32)
+    row_of = lax.broadcasted_iota(jnp.int32, (8, LANES), 0)
+
+    totals, every = [], None
+    for g in range(groups):
+        total = jnp.zeros((8, LANES), F32)
         for t in range(tile_count):
             row, first = 4 + t * rows_each + slab * LANES // width, slab * LANES % width
             at = info_s[g, row : row + 1, first : first + LANES].astype(jnp.int32)
-            at = jnp.broadcast_to(at, (ROWS, LANES))
+            at = jnp.broadcast_to(at, (8, LANES))
+            n = g * tile_count + t
+            every = at if every is None else jnp.where(row_of >= n * halves, at, every)
             lane, half = at & (LANES - 1), at >> 7
-            for h in range(listed // LANES):
-                here = jnp.take_along_axis(
-                    acc_s[g, t, :, h * LANES : (h + 1) * LANES],
-                    lane,
-                    axis=1,
-                    mode="promise_in_bounds",
-                )
+            for h in range(halves):
+                here = lane_gather(acc_s[g, t, 0:8, h * LANES : (h + 1) * LANES], lane)
                 total = total + jnp.where(half == h, here, 0.0)
         totals.append(total)
-    return totals[0] + totals[1]
+    here = lane_gather(acc_s[0, 0, 8:16, :LANES], every & (LANES - 1))
+    ninth = jnp.where(every >> 7 == row_of % halves, here, 0.0)
+    return totals[0] + totals[1], jnp.sum(ninth, axis=0, keepdims=True)
 
 
 def block_start(tile_id):
@@ -487,36 +588,39 @@
     projected = project_rows(lambda f: feats[f * slabs : (f + 1) * slabs, :], cam)
     for f, value in enumerate(projected):
         rows[pl.ds(f, slabs, stride=ROWS), :] = value
-    zero_row = jnp.zeros((slabs, LANES), F32)
-    for f in range(len(projected), ROWS):
-        rows[pl.ds(f, slabs, stride=ROWS), :] = zero_row
     info_s[0] = own[...]
     info_s[1] = other[...]
     composite(block_start(tile_ids[0]), 0, where[0], rows, info_s, rendered, work)
     for s in range(slabs):
-        partial[:, s * LANES : (s + 1) * LANES] = pool_sum(s, info_s, work[-1])
+        at = slice(s * LANES, (s + 1) * LANES)
+        partial[0:8, at], partial[8:9, at] = pool_sum(s, info_s, work[-1])
 
 
 def far_kernel(blocks, tile_ids, where, rows, partial, infos, *refs):
-    *packets, info_s = refs[: len(refs) - 6]
-    work = refs[len(refs) - 6 :]
+    *packets, info_s = refs[: len(refs) - 13]
+    work = refs[len(refs) - 13 :]
     half = infos.shape[0] // 2
     info_s[0] = infos[:half, :]
     info_s[1] = infos[half:, :]
     composite(block_start(tile_ids[0]), 2, where[0], rows, info_s, None, work)
     share = (tile_ids[0] // (TILES_X * TILES_Y)).astype(F32)
-    row_of = lax.broadcasted_iota(jnp.int32, (ROWS, LANES), 0)
-    lane_of = lax.broadcasted_iota(jnp.int32, (ROWS, LANES), 1)
+    row_of = lax.broadcasted_iota(jnp.int32, (8, LANES), 0)
+    lane_of = lax.broadcasted_iota(jnp.int32, (8, LANES), 1)
     chunk = packets[0].shape[1]
     for s in range(rows.shape[0] // ROWS):
-        total = partial[:, s * LANES : (s + 1) * LANES] + pool_sum(s, info_s, work[-1])
+        total, ninth = pool_sum(s, info_s, work[-1])
+        total = total + partial[0:8, s * LANES : (s + 1) * LANES]
+        ninth = ninth + partial[8:9, s * LANES : (s + 1) * LANES]
         if blocks == 1:
             mine = share
         else:
             column = s * LANES + lane_of
             mine = jnp.where(column % where[2] // (where[2] // blocks) == where[1], share, 0.0)
-        total = jnp.where(row_of == 9, mine, total)
-        packets[s * LANES // chunk][:, s * LANES % chunk : s * LANES % chunk + LANES] = total
+        at = slice(s * LANES % chunk, s * LANES % chunk + LANES)
+        packets[s * LANES // chunk][0:8, at] = total
+        packets[s * LANES // chunk][8:16, at] = jnp.where(
+            row_of == 0, jnp.broadcast_to(ninth, (8, LANES)), mine
+        )
 
 
 def join_kernel(first, second, out):
@@ -608,13 +712,21 @@
 
 
 def work_shapes(tile_count, pixels, listed):
-    square = (tile_count, pixels, listed)
+    steps = 2 * tile_count * listed // LANES
+    assert steps == 8
     return [
-        pltpu.VMEM(square, F32),
-        pltpu.VMEM(square, F32),
-        pltpu.VMEM(square, F32),
-        pltpu.VMEM(square, BF16),
-        pltpu.VMEM(square, BF16),
+        pltpu.VMEM((steps * pixels, LANES), F32),
+        pltpu.VMEM((steps * pixels, LANES), F32),
+        pltpu.VMEM((pixels, LANES), F32),
+        pltpu.VMEM((3, pixels, LANES), F32),
+        pltpu.VMEM((pixels, LANES), F32),
+        pltpu.VMEM((pixels, LANES), F32),
+        pltpu.VMEM((3, pixels, LANES), F32),
+        pltpu.VMEM((3, pixels, 2 * LANES), BF16),
+        pltpu.VMEM((3, 16, pixels), F32),
+        pltpu.VMEM((9, steps, LANES), F32),
+        pltpu.VMEM((2, steps, TILE_SIDE // 8, 8, LANES), F32),
+        pltpu.VMEM((9, steps, LANES), F32),
         pltpu.VMEM((2, tile_count, ROWS, listed), F32),
     ]
 

time: 27.1 us -> 26.4 us (0.974)
  Pallas kernels: 12.7 us -> 12 us
    pallas_call x5, Pallas kernels: 12.7 us -> 12 us  [call(): pl.pallas_call(kernel, out_shape=out_shape, in_specs=in_specs, out_specs=...]
  transfers between devices with their start and end apart: 8 -> 8, of which waited for: 3 -> 3; matrix products, arithmetic and copies ran while one was open for 0% -> 0% of each run, Pallas kernels for 18% -> 17%
where the time goes in v9:
time: 26.4 us; the launch traced here: 26.3 us
  Pallas kernels  12 us (45%)
  starting transfers between devices  9.73 us (37%)
  waiting for transfers between devices  3.7 us (14%)
  between operations  0.69 us (3%)
    pallas_call x5, Pallas kernels, call(): pl.pallas_call(kernel, out_shape=out_shape, in_specs=in_specs, out_specs=...  12 us
    ppermute x8, starting transfers between devices, swap(): lax.ppermute(value, axis, [(k, k ^ d) for k in range(lax.axis_size(axis))])  9.73 us
    ppermute x8, waiting for transfers between devices, swap(): lax.ppermute(value, axis, [(k, k ^ d) for k in range(lax.axis_size(axis))])  3.7 us
  transfers between devices with their start and end apart: 8, of which 3 were waited for; matrix products, arithmetic and copies ran while one was open for 0% of the time, Pallas kernels for 17%

profile of v9, /device:TPU:0, one launch (start us, length us, event | category | flops | bytes accessed | tf_op | source)
XLA Modules:
  0.0 26.3 jit_solution(17317668440390513774)
XLA Ops:
  0.6 0.0 copy-start.2
  0.6 1.2 %pack.1 = (f32[8,512]{1,0:T(8,128)S(1)}, f32[59,256]{1,0:T(8,128)S(1)}, f32[59,256]{1,0:T(8,128)S(1)}, f32[59,256]{1,0:T(8,128)S(1)}, f32[59,256]{1,0:T(8,128)S(1)}) custom-call(s32[1]{0:T(128)} %bitcast.2.where, s32[2,1,256]{2,1,0:T(1,128)} %bitcast.4, s32[2,256]{1,0:T(2,128)} %refs_1_.1, f32[3,512]{1,0:T(4,128)} %refs_2_.1, f32[59,1024]{1,0:T(8,128)} %refs_4_.1), custom_call_target="tpu_custom_call" | custom-call | tf_op jit(solution)/shard_map/pack/pallas_call | solution.py:703
  1.8 3.1 %collective-permute-start = (f32[8,512]{1,0:T(8,128)S(1)}, f32[8,512]{1,0:T(8,128)S(1)}, u32[]{:S(2)}, u32[]{:S(2)}) collective-permute-start(f32[8,512]{1,0:T(8,128)S(1)} %get-tuple-element.19.own.first), channel_id=1, source_target_pairs={{0,1},{1,0},{2,3},{3,2},{4,5},{5,4},{6,7},{7,6},{8,9},{9,8},{10,11... | collective-permute-start | bytes 49160 | tf_op jit(solution)/shard_map/ppermute | solution.py:801
  4.9 0.0 collective-permute-start.1
  4.9 1.5 %collective-permute-start.2 = (f32[59,256]{1,0:T(8,128)S(1)}, f32[59,256]{1,0:T(8,128)S(1)}, u32[]{:S(2)}, u32[]{:S(2)}) collective-permute-start(f32[59,256]{1,0:T(8,128)S(1)} %get-tuple-element.22), channel_id=1, source_target_pairs={{0,8},{4,12},{8,0},{12,4},{1,9},{5,13},{9,1},{13,5},{2,10},{6,14},... | collective-permute-start | bytes 181256 | tf_op jit(solution)/shard_map/ppermute | solution.py:801
  6.4 0.4 %collective-permute-start.3 = (f32[59,256]{1,0:T(8,128)S(1)}, f32[59,256]{1,0:T(8,128)S(1)}, u32[]{:S(2)}, u32[]{:S(2)}) collective-permute-start(f32[59,256]{1,0:T(8,128)S(1)} %get-tuple-element.23), channel_id=1, source_target_pairs={{0,12},{4,8},{8,4},{12,0},{1,13},{5,9},{9,5},{13,1},{2,14},{6,10},... | collective-permute-start | bytes 181256 | tf_op jit(solution)/shard_map/ppermute | solution.py:801
  6.8 0.0 copy-start.3
  6.8 0.0 copy-start.4
  6.8 0.0 copy-start
  6.8 0.0 copy-start.1
  6.8 0.0 collective-permute-done.other.second
  6.8 2.9 %collective-permute-start.4 = (f32[16,512]{1,0:T(8,128)S(1)}, f32[16,512]{1,0:T(8,128)S(1)}, u32[]{:S(2)}, u32[]{:S(2)}) collective-permute-start(f32[16,512]{1,0:T(8,128)S(1)} %join.1), channel_id=1, source_target_pairs={{0,2},{1,3},{2,0},{3,1},{4,6},{5,7},{6,4},{7,5},{8,10},{9,11},{10,... | collective-permute-start | bytes 98312 | tf_op jit(solution)/shard_map/ppermute | solution.py:801
  9.7 0.1 pad_add_fusion.where
  9.8 0.0 collective-permute-done.1.refs_1_
  9.8 0.0 collective-permute-done.2.refs_2_
  9.8 0.8 %collective-permute-done.3.refs_3_ = f32[59,256]{1,0:T(8,128)S(1)} collective-permute-done((f32[59,256]{1,0:T(8,128)S(1)}, f32[59,256]{1,0:T(8,128)S(1)}, u32[]{:S(2)}, u32[]{:S(2)}) %collective-permute-start.3) | collective-permute-done | bytes 60448 | tf_op jit(solution)/shard_map/ppermute | solution.py:801
  10.5 0.0 copy-done.3
  10.5 0.0 copy-done.4
  10.6 4.6 %near.1 = (f32[3,512]{1,0:T(4,128)}, f32[128,128]{1,0:T(8,128)S(1)}, f32[16,1024]{1,0:T(8,128)S(1)}) custom-call(s32[2]{0:T(128)S(1)} %copy-done.4, f32[4,12]{1,0:T(4,128)S(1)} %copy-done.3, s32[3]{0:T(128)S(1)} %pad_add_fusion.where, f32[8,512]{1,0:T(8,128)S(1)} %get-tuple-element.19.own.first, f32[8,512]{1,0:T(8,128)S(1)} %collective-permute-done.other.second, ...), custom_call_target="tpu_custom_call" | custom-call | tf_op jit(solution)/shard_map/near/pallas_call | solution.py:703
  15.1 0.0 collective-permute-done.4.infos
  15.1 4.4 %far.1 = (f32[16,256]{1,0:T(8,128)S(1)}, f32[16,256]{1,0:T(8,128)S(1)}, f32[16,256]{1,0:T(8,128)S(1)}, f32[16,256]{1,0:T(8,128)S(1)}) custom-call(s32[2]{0:T(128)S(1)} %copy-done.4, s32[3]{0:T(128)S(1)} %pad_add_fusion.where, f32[128,128]{1,0:T(8,128)S(1)} %get-tuple-element.25.rows, f32[16,1024]{1,0:T(8,128)S(1)} %get-tuple-element.26.partial, ...), custom_call_target="tpu_custom_call" | custom-call | tf_op jit(solution)/shard_map/far/pallas_call | solution.py:703
  19.5 0.2 collective-permute-start.5
  19.7 1.5 %collective-permute-start.6 = (f32[16,256]{1,0:T(8,128)S(1)}, f32[16,256]{1,0:T(8,128)S(1)}, u32[]{:S(2)}, u32[]{:S(2)}) collective-permute-start(f32[16,256]{1,0:T(8,128)S(1)} %get-tuple-element.29), channel_id=1, source_target_pairs={{0,8},{4,12},{8,0},{12,4},{1,9},{5,13},{9,1},{13,5},{2,10},{6,14},... | collective-permute-start | bytes 49160 | tf_op jit(solution)/shard_map/ppermute | solution.py:801
  21.2 0.3 collective-permute-start.7
  21.5 0.0 collective-permute-done.5.refs_1_
  21.5 2.0 %collective-permute-done.6.refs_2_ = f32[16,256]{1,0:T(8,128)S(1)} collective-permute-done((f32[16,256]{1,0:T(8,128)S(1)}, f32[16,256]{1,0:T(8,128)S(1)}, u32[]{:S(2)}, u32[]{:S(2)}) %collective-permute-start.6) | collective-permute-done | bytes 16416 | tf_op jit(solution)/shard_map/ppermute | solution.py:801
  23.5 0.9 %collective-permute-done.7.refs_3_ = f32[16,256]{1,0:T(8,128)S(1)} collective-permute-done((f32[16,256]{1,0:T(8,128)S(1)}, f32[16,256]{1,0:T(8,128)S(1)}, u32[]{:S(2)}, u32[]{:S(2)}) %collective-permute-start.7) | collective-permute-done | bytes 16416 | tf_op jit(solution)/shard_map/ppermute | solution.py:801
  24.4 0.0 copy-done.2
  24.4 0.0 copy-done
  24.4 0.0 copy-done.1
  24.4 1.9 %update.1 = (f32[59,1024]{1,0:T(8,128)}, f32[59,1024]{1,0:T(8,128)}, f32[59,1024]{1,0:T(8,128)}) custom-call(s32[1]{0:T(128)} %bitcast.2.where, f32[4,12]{1,0:T(4,128)S(1)} %copy-done.3, f32[16,256]{1,0:T(8,128)S(1)} %get-tuple-element.27.refs_0_, f32[16,256]{1,0:T(8,128)S(1)} %collective-permute-done.5.refs_1_, ...), custom_call_target="tpu_custom_call" | custom-call | tf_op jit(solution)/shard_map/update/pallas_call | solution.py:703
  (1 shorter events, 0.0 us)
Async XLA Ops:
  0.6 23.7 %copy-start.2 = (f32[59,1024]{1,0:T(8,128)S(1)}, f32[59,1024]{1,0:T(8,128)}, u32[]{:S(2)}) copy-start(f32[59,1024]{1,0:T(8,128)} %refs_6_.1) | copy-start | bytes 724996
  1.8 5.0 %collective-permute-start = (f32[8,512]{1,0:T(8,128)S(1)}, f32[8,512]{1,0:T(8,128)S(1)}, u32[]{:S(2)}, u32[]{:S(2)}) collective-permute-start(f32[8,512]{1,0:T(8,128)S(1)} %get-tuple-element.19.own.first), channel_id=1, source_target_pairs={{0,1},{1,0},{2,3},{3,2},{4,5},{5,4},{6,7},{7,6},{8,9},{9,8},{10,11... | collective-permute-start | bytes 49160 | tf_op jit(solution)/shard_map/ppermute | solution.py:801
  4.9 4.8 %collective-permute-start.1 = (f32[59,256]{1,0:T(8,128)S(1)}, f32[59,256]{1,0:T(8,128)S(1)}, u32[]{:S(2)}, u32[]{:S(2)}) collective-permute-start(f32[59,256]{1,0:T(8,128)S(1)} %get-tuple-element.21), channel_id=1, source_target_pairs={{0,4},{4,0},{8,12},{12,8},{1,5},{5,1},{9,13},{13,9},{2,6},{6,2},{1... | collective-permute-start | bytes 181256 | tf_op jit(solution)/shard_map/ppermute | solution.py:801
  4.9 4.8 %collective-permute-start.2 = (f32[59,256]{1,0:T(8,128)S(1)}, f32[59,256]{1,0:T(8,128)S(1)}, u32[]{:S(2)}, u32[]{:S(2)}) collective-permute-start(f32[59,256]{1,0:T(8,128)S(1)} %get-tuple-element.22), channel_id=1, source_target_pairs={{0,8},{4,12},{8,0},{12,4},{1,9},{5,13},{9,1},{13,5},{2,10},{6,14},... | collective-permute-start | bytes 181256 | tf_op jit(solution)/shard_map/ppermute | solution.py:801
  6.4 4.1 %collective-permute-start.3 = (f32[59,256]{1,0:T(8,128)S(1)}, f32[59,256]{1,0:T(8,128)S(1)}, u32[]{:S(2)}, u32[]{:S(2)}) collective-permute-start(f32[59,256]{1,0:T(8,128)S(1)} %get-tuple-element.23), channel_id=1, source_target_pairs={{0,12},{4,8},{8,4},{12,0},{1,13},{5,9},{9,5},{13,1},{2,14},{6,10},... | collective-permute-start | bytes 181256 | tf_op jit(solution)/shard_map/ppermute | solution.py:801
  6.8 3.8 %copy-start.3 = (f32[4,12]{1,0:T(4,128)S(1)}, f32[4,12]{1,0:T(4,128)}, u32[]{:S(2)}) copy-start(f32[4,12]{1,0:T(4,128)} %cams.3) | copy-start | bytes 580
  6.8 3.8 %copy-start.4 = (s32[2]{0:T(128)S(1)}, s32[2]{0:T(128)}, u32[]{:S(2)}) copy-start(s32[2]{0:T(128)} %tile_ids.3) | copy-start | bytes 28
  6.8 17.6 %copy-start = (f32[59,1024]{1,0:T(8,128)S(1)}, f32[59,1024]{1,0:T(8,128)}, u32[]{:S(2)}) copy-start(f32[59,1024]{1,0:T(8,128)} %refs_4_.1) | copy-start | bytes 724996
  6.8 17.6 %copy-start.1 = (f32[59,1024]{1,0:T(8,128)S(1)}, f32[59,1024]{1,0:T(8,128)}, u32[]{:S(2)}) copy-start(f32[59,1024]{1,0:T(8,128)} %refs_5_.1) | copy-start | bytes 724996
  6.8 8.3 %collective-permute-start.4 = (f32[16,512]{1,0:T(8,128)S(1)}, f32[16,512]{1,0:T(8,128)S(1)}, u32[]{:S(2)}, u32[]{:S(2)}) collective-permute-start(f32[16,512]{1,0:T(8,128)S(1)} %join.1), channel_id=1, source_target_pairs={{0,2},{1,3},{2,0},{3,1},{4,6},{5,7},{6,4},{7,5},{8,10},{9,11},{10,... | collective-permute-start | bytes 98312 | tf_op jit(solution)/shard_map/ppermute | solution.py:801
  19.5 1.9 %collective-permute-start.5 = (f32[16,256]{1,0:T(8,128)S(1)}, f32[16,256]{1,0:T(8,128)S(1)}, u32[]{:S(2)}, u32[]{:S(2)}) collective-permute-start(f32[16,256]{1,0:T(8,128)S(1)} %get-tuple-element.28), channel_id=1, source_target_pairs={{0,4},{4,0},{8,12},{12,8},{1,5},{5,1},{9,13},{13,9},{2,6},{6,2},{1... | collective-permute-start | bytes 49160 | tf_op jit(solution)/shard_map/ppermute | solution.py:801
  19.7 3.8 %collective-permute-start.6 = (f32[16,256]{1,0:T(8,128)S(1)}, f32[16,256]{1,0:T(8,128)S(1)}, u32[]{:S(2)}, u32[]{:S(2)}) collective-permute-start(f32[16,256]{1,0:T(8,128)S(1)} %get-tuple-element.29), channel_id=1, source_target_pairs={{0,8},{4,12},{8,0},{12,4},{1,9},{5,13},{9,1},{13,5},{2,10},{6,14},... | collective-permute-start | bytes 49160 | tf_op jit(solution)/shard_map/ppermute | solution.py:801
  21.2 3.2 %collective-permute-start.7 = (f32[16,256]{1,0:T(8,128)S(1)}, f32[16,256]{1,0:T(8,128)S(1)}, u32[]{:S(2)}, u32[]{:S(2)}) collective-permute-start(f32[16,256]{1,0:T(8,128)S(1)} %get-tuple-element.30), channel_id=1, source_target_pairs={{0,12},{4,8},{8,4},{12,0},{1,13},{5,9},{9,5},{13,1},{2,14},{6,10},... | collective-permute-start | bytes 49160 | tf_op jit(solution)/shard_map/ppermute | solution.py:801

commit v10 on v9

--- a/solution.py
+++ b/solution.py
@@ -327,6 +327,18 @@
     return out[0], list(out[1:])
 
 
+def pixel_basis(pixels):
+    pixel = lax.broadcasted_iota(jnp.int32, (8, pixels), 1)
+    row = lax.broadcasted_iota(jnp.int32, (8, pixels), 0)
+    middle = 0.5 * TILE_SIDE - 0.5
+    u = (pixel % TILE_SIDE).astype(F32) - middle
+    v = (pixel // TILE_SIDE).astype(F32) - middle
+    value = jnp.where(row == 0, 1.0, 0.0)
+    for at, term in ((1, u), (2, v), (3, u * u), (4, u * v), (5, v * v)):
+        value = jnp.where(row == at, term, value)
+    return value
+
+
 def lane_gather(source, lane):
     return jnp.take_along_axis(source, lane, axis=1, mode="promise_in_bounds")
 
@@ -336,7 +348,10 @@
 
 
 def composite(tiles, first_group, me, rows, info_s, rendered, work):
-    alpha_s, weight_s, left_s, image_s, before_s, behind_s, error_s, joined_s, wrong_s, coef_s, line_s, sum_s, acc_s = work
+    (
+        alpha_s, weight_s, pull_s, left_s, image_s, before_s, behind_s, error_s,
+        joined_s, wrong_s, colour_s, term_s, hue_s, sum_s, acc_s,
+    ) = work
     groups, tile_count, _, listed = acc_s.shape
     pixels = info_s.shape[2] // tile_count
     tiles_here = groups * tile_count
@@ -378,33 +393,47 @@
     slope_u = 2.0 * quad_a * mean_u + quad_b * mean_v
     slope_v = 2.0 * quad_c * mean_v + quad_b * mean_u
     level = 0.5 * (slope_u * mean_u + slope_v * mean_v) + entry[5]
-    for f, value in enumerate(
-        (level, -slope_u, quad_a, -slope_v, quad_b, quad_c, entry[6], entry[7], entry[8])
-    ):
-        coef_s[f] = value
-    for s in range(steps):
-        c = [spread(coef_s[f, s : s + 1, :]) for f in range(5)]
-        for half in range(side // 8):
-            u = sub.astype(F32) + (8.0 * half - middle)
-            line_s[0, s, half] = c[0] + u * (c[1] + u * c[2])
-            line_s[1, s, half] = c[3] + u * c[4]
+    zero = jnp.zeros((8, LANES), F32)
+    for f, value in enumerate((level, -slope_u, -slope_v, quad_a, quad_b, quad_c, zero, zero)):
+        for term in range(3):
+            high = value.astype(BF16).astype(F32)
+            term_s[pl.ds(8 * term + f, steps, stride=24), :] = high
+            value = value - high
+    down = ((0,), (0,))
+
+    def by_step(ref, count):
+        return jnp.concatenate(
+            [ref[s * count : (s + 1) * count, :] for s in range(steps)], axis=1
+        ).astype(BF16)
+
+    basis = pixel_basis(pixels)
+    basis = jnp.concatenate([basis, basis, basis], axis=0).astype(BF16)
+    alpha_s[...] = jnp.exp(matmul(basis, by_step(term_s, 24), down))
+    hue_s[...] = jnp.zeros(hue_s.shape, F32)
+    for k in range(3):
+        colour_s[k] = entry[6 + k]
+        high = entry[6 + k].astype(BF16).astype(F32)
+        low = entry[6 + k] - high
+        for n in range(tiles_here):
+            own = lane // segments == n
+            for at, value in ((0, high), (3, low), (6, high)):
+                hue_s[pl.ds(n * 16 + at + k, steps, stride=16 * tiles_here), :] = jnp.where(
+                    own, value, 0.0
+                )
 
     rows_each = 2
 
     def forward(i, carry):
         for j in range(rows_each):
             row = i * rows_each + j
-            v = row.astype(F32) - middle
             left = [None] * (side // 8)
             image = [[None] * 3 for _ in left]
             for s in range(steps):
-                quad = spread(coef_s[5, s : s + 1, :]) * v
-                colour = [spread(coef_s[6 + k, s : s + 1, :]) for k in range(3)]
+                colour = [spread(colour_s[k, s : s + 1, :]) for k in range(3)]
+                of_step = slice(s * LANES, (s + 1) * LANES)
                 for half in range(side // 8):
-                    power = line_s[0, s, half] + v * (line_s[1, s, half] + quad)
-                    alpha = jnp.exp(power)
-                    at = pl.ds(pl.multiple_of(row * side, side) + (s * pixels + half * 8), 8)
-                    alpha_s[at, :] = alpha
+                    at = pl.ds(pl.multiple_of(row * side, side) + half * 8, 8)
+                    alpha = alpha_s[at, of_step]
                     if s == 0:
                         weight = alpha
                         left[half] = 1.0 - alpha
@@ -415,7 +444,7 @@
                         image[half] = [
                             image[half][k] + weight * colour[k] for k in range(3)
                         ]
-                    weight_s[at, :] = weight
+                    weight_s[at, of_step] = weight
             for half in range(side // 8):
                 at = pl.ds(pl.multiple_of(row * side, side) + half * 8, 8)
                 left_s[at, :] = left[half]
@@ -452,14 +481,16 @@
                 rendered[k : k + 1, here] = image[n : n + 1]
             wrong = image[n : n + 1] - info_s[g, k : k + 1, here]
             high = wrong.astype(BF16).astype(F32)
-            wrong_s[k, n : n + 1, :] = high
-            wrong_s[k, 8 + n : 9 + n, :] = wrong - high
-    back = lax.broadcasted_iota(jnp.int32, (16, LANES), 1) // segments
-    back = jnp.where(
-        back == lax.broadcasted_iota(jnp.int32, (16, LANES), 0) % 8, 1.0, 0.0
-    ).astype(BF16)
+            wrong_s[n * 16 + k : n * 16 + k + 1, :] = high
+            wrong_s[n * 16 + 3 + k : n * 16 + 4 + k, :] = high
+            wrong_s[n * 16 + 6 + k : n * 16 + 7 + k, :] = wrong - high
+    wrong = wrong_s[...].astype(BF16)
+    pull_s[...] = matmul(wrong, by_step(hue_s, 16 * tiles_here), down)
+    row_of = lax.broadcasted_iota(jnp.int32, (16 * tiles_here, LANES), 0)
+    own = lax.broadcasted_iota(jnp.int32, (16 * tiles_here, LANES), 1) // segments == row_of // 16
     for k in range(3):
-        error_s[k] = matmul(wrong_s[k].astype(BF16), back, ((0,), (0,)))
+        pick = own & ((row_of % 16 == k) | (row_of % 16 == 6 + k))
+        error_s[k] = matmul(wrong, jnp.where(pick, 1.0, 0.0).astype(BF16), down)
 
     for first in range(0, pixels, tall):
         at = slice(first, first + tall)
@@ -481,29 +512,31 @@
 
     def backward(i, carry):
         s = steps - 1 - i
-        colour = [spread(coef_s[6 + k, pl.ds(s, 1), :]) for k in range(3)]
+        of_step = pl.ds(pl.multiple_of(s * LANES, LANES), LANES)
         plain = [[None] * 3 for _ in range(side // 8)]
         hues = [None] * 3
         for row in range(side):
-            v = row - middle
             for half in range(side // 8):
                 at = pl.ds(row * side + half * 8, 8)
-                of_step = pl.ds(pl.multiple_of(s * pixels, pixels) + (row * side + half * 8), 8)
-                weight = weight_s[of_step, :]
-                error = [error_s[k, at, :] for k in range(3)]
-                pull = error[0] * colour[0] + error[1] * colour[1] + error[2] * colour[2]
+                weight = weight_s[at, of_step]
                 behind = behind_s[at, :]
-                gap = pull - behind
-                behind_s[at, :] = behind + alpha_s[of_step, :] * gap
+                gap = before_s[at, :] * pull_s[at, of_step] - behind
+                behind_s[at, :] = behind + alpha_s[at, of_step] * gap
                 push = weight * gap
-                terms = (push, v * push, (v * v) * push)
-                hue = [weight * error[k] for k in range(3)]
                 if row == 0:
-                    plain[half] = list(terms)
+                    plain[half] = [push, push, push]
                 else:
-                    plain[half] = [plain[half][m] + terms[m] for m in range(3)]
+                    plain[half][0] = plain[half][0] + push
+                    plain[half][1] = plain[half][1] + plain[half][0]
+                    plain[half][2] = plain[half][2] + plain[half][1]
+                hue = [weight * error_s[k, at, :] for k in range(3)]
                 hues = [hue[k] if hues[k] is None else hues[k] + hue[k] for k in range(3)]
         u = [sub.astype(F32) + (8.0 * half - middle) for half in range(side // 8)]
+        shift = side - middle
+        for half in range(side // 8):
+            one, two, three = plain[half]
+            plain[half][1] = shift * one - two
+            plain[half][2] = shift * shift * one - (2.0 * shift + 1.0) * two + 2.0 * three
 
         def over(m, power):
             total = 0.0
@@ -597,8 +630,8 @@
 
 
 def far_kernel(blocks, tile_ids, where, rows, partial, infos, *refs):
-    *packets, info_s = refs[: len(refs) - 13]
-    work = refs[len(refs) - 13 :]
+    *packets, info_s = refs[: len(refs) - 15]
+    work = refs[len(refs) - 15 :]
     half = infos.shape[0] // 2
     info_s[0] = infos[:half, :]
     info_s[1] = infos[half:, :]
@@ -712,20 +745,20 @@
 
 
 def work_shapes(tile_count, pixels, listed):
-    steps = 2 * tile_count * listed // LANES
+    tiles = 2 * tile_count
+    steps = tiles * listed // LANES
     assert steps == 8
-    return [
-        pltpu.VMEM((steps * pixels, LANES), F32),
-        pltpu.VMEM((steps * pixels, LANES), F32),
+    return [pltpu.VMEM((pixels, steps * LANES), F32)] * 3 + [
         pltpu.VMEM((pixels, LANES), F32),
         pltpu.VMEM((3, pixels, LANES), F32),
         pltpu.VMEM((pixels, LANES), F32),
         pltpu.VMEM((pixels, LANES), F32),
         pltpu.VMEM((3, pixels, LANES), F32),
         pltpu.VMEM((3, pixels, 2 * LANES), BF16),
-        pltpu.VMEM((3, 16, pixels), F32),
-        pltpu.VMEM((9, steps, LANES), F32),
-        pltpu.VMEM((2, steps, TILE_SIDE // 8, 8, LANES), F32),
+        pltpu.VMEM((tiles * 16, pixels), F32),
+        pltpu.VMEM((3, steps, LANES), F32),
+        pltpu.VMEM((steps * 24, LANES), F32),
+        pltpu.VMEM((steps * 16 * tiles, LANES), F32),
         pltpu.VMEM((9, steps, LANES), F32),
         pltpu.VMEM((2, tile_count, ROWS, listed), F32),
     ]

time: 26.4 us -> 27.1 us (1.027)
  Pallas kernels: 12 us -> 12.7 us
    pallas_call x5, Pallas kernels: 12 us -> 12.7 us  [call(): pl.pallas_call(kernel, out_shape=out_shape, in_specs=in_specs, out_specs=...]
  transfers between devices with their start and end apart: 8 -> 8, of which waited for: 3 -> 3; matrix products, arithmetic and copies ran while one was open for 0% -> 0% of each run, Pallas kernels for 17% -> 18%
where the time goes in v10:
time: 27.1 us; the launch traced here: 26.9 us
  Pallas kernels  12.7 us (47%)
  starting transfers between devices  9.76 us (36%)
  waiting for transfers between devices  3.67 us (14%)
  between operations  0.69 us (3%)
    pallas_call x5, Pallas kernels, call(): pl.pallas_call(kernel, out_shape=out_shape, in_specs=in_specs, out_specs=...  12.7 us
    ppermute x8, starting transfers between devices, swap(): lax.ppermute(value, axis, [(k, k ^ d) for k in range(lax.axis_size(axis))])  9.76 us
    ppermute x8, waiting for transfers between devices, swap(): lax.ppermute(value, axis, [(k, k ^ d) for k in range(lax.axis_size(axis))])  3.67 us
  transfers between devices with their start and end apart: 8, of which 3 were waited for; matrix products, arithmetic and copies ran while one was open for 0% of the time, Pallas kernels for 18%

profile of v10, /device:TPU:0, one launch (start us, length us, event | category | flops | bytes accessed | tf_op | source)
XLA Modules:
  0.0 26.9 jit_solution(4139149298361026146)
XLA Ops:
  0.6 0.0 copy-start.2
  0.6 1.2 %pack.1 = (f32[8,512]{1,0:T(8,128)S(1)}, f32[59,256]{1,0:T(8,128)S(1)}, f32[59,256]{1,0:T(8,128)S(1)}, f32[59,256]{1,0:T(8,128)S(1)}, f32[59,256]{1,0:T(8,128)S(1)}) custom-call(s32[1]{0:T(128)} %bitcast.2.where, s32[2,1,256]{2,1,0:T(1,128)} %bitcast.4, s32[2,256]{1,0:T(2,128)} %refs_1_.1, f32[3,512]{1,0:T(4,128)} %refs_2_.1, f32[59,1024]{1,0:T(8,128)} %refs_4_.1), custom_call_target="tpu_custom_call" | custom-call | tf_op jit(solution)/shard_map/pack/pallas_call | solution.py:736
  1.8 3.1 %collective-permute-start = (f32[8,512]{1,0:T(8,128)S(1)}, f32[8,512]{1,0:T(8,128)S(1)}, u32[]{:S(2)}, u32[]{:S(2)}) collective-permute-start(f32[8,512]{1,0:T(8,128)S(1)} %get-tuple-element.19.own.first), channel_id=1, source_target_pairs={{0,1},{1,0},{2,3},{3,2},{4,5},{5,4},{6,7},{7,6},{8,9},{9,8},{10,11... | collective-permute-start | bytes 49160 | tf_op jit(solution)/shard_map/ppermute | solution.py:834
  4.9 0.0 collective-permute-start.1
  4.9 1.5 %collective-permute-start.2 = (f32[59,256]{1,0:T(8,128)S(1)}, f32[59,256]{1,0:T(8,128)S(1)}, u32[]{:S(2)}, u32[]{:S(2)}) collective-permute-start(f32[59,256]{1,0:T(8,128)S(1)} %get-tuple-element.22), channel_id=1, source_target_pairs={{0,8},{4,12},{8,0},{12,4},{1,9},{5,13},{9,1},{13,5},{2,10},{6,14},... | collective-permute-start | bytes 181256 | tf_op jit(solution)/shard_map/ppermute | solution.py:834
  6.4 0.4 %collective-permute-start.3 = (f32[59,256]{1,0:T(8,128)S(1)}, f32[59,256]{1,0:T(8,128)S(1)}, u32[]{:S(2)}, u32[]{:S(2)}) collective-permute-start(f32[59,256]{1,0:T(8,128)S(1)} %get-tuple-element.23), channel_id=1, source_target_pairs={{0,12},{4,8},{8,4},{12,0},{1,13},{5,9},{9,5},{13,1},{2,14},{6,10},... | collective-permute-start | bytes 181256 | tf_op jit(solution)/shard_map/ppermute | solution.py:834
  6.8 0.0 copy-start.3
  6.8 0.0 copy-start.4
  6.8 0.0 copy-start
  6.8 0.0 copy-start.1
  6.8 0.0 collective-permute-done.other.second
  6.8 2.9 %collective-permute-start.4 = (f32[16,512]{1,0:T(8,128)S(1)}, f32[16,512]{1,0:T(8,128)S(1)}, u32[]{:S(2)}, u32[]{:S(2)}) collective-permute-start(f32[16,512]{1,0:T(8,128)S(1)} %join.1), channel_id=1, source_target_pairs={{0,2},{1,3},{2,0},{3,1},{4,6},{5,7},{6,4},{7,5},{8,10},{9,11},{10,... | collective-permute-start | bytes 98312 | tf_op jit(solution)/shard_map/ppermute | solution.py:834
  9.7 0.1 pad_add_fusion.where
  9.8 0.0 collective-permute-done.1.refs_1_
  9.8 0.0 collective-permute-done.2.refs_2_
  9.8 0.8 %collective-permute-done.3.refs_3_ = f32[59,256]{1,0:T(8,128)S(1)} collective-permute-done((f32[59,256]{1,0:T(8,128)S(1)}, f32[59,256]{1,0:T(8,128)S(1)}, u32[]{:S(2)}, u32[]{:S(2)}) %collective-permute-start.3) | collective-permute-done | bytes 60448 | tf_op jit(solution)/shard_map/ppermute | solution.py:834
  10.5 0.0 copy-done.3
  10.5 0.0 copy-done.4
  10.6 4.9 %near.1 = (f32[3,512]{1,0:T(4,128)}, f32[128,128]{1,0:T(8,128)S(1)}, f32[16,1024]{1,0:T(8,128)S(1)}) custom-call(s32[2]{0:T(128)S(1)} %copy-done.4, f32[4,12]{1,0:T(4,128)S(1)} %copy-done.3, s32[3]{0:T(128)S(1)} %pad_add_fusion.where, f32[8,512]{1,0:T(8,128)S(1)} %get-tuple-element.19.own.first, f32[8,512]{1,0:T(8,128)S(1)} %collective-permute-done.other.second, ...), custom_call_target="tpu_custom_call" | custom-call | tf_op jit(solution)/shard_map/near/pallas_call | solution.py:736
  15.4 0.0 collective-permute-done.4.infos
  15.4 4.8 %far.1 = (f32[16,256]{1,0:T(8,128)S(1)}, f32[16,256]{1,0:T(8,128)S(1)}, f32[16,256]{1,0:T(8,128)S(1)}, f32[16,256]{1,0:T(8,128)S(1)}) custom-call(s32[2]{0:T(128)S(1)} %copy-done.4, s32[3]{0:T(128)S(1)} %pad_add_fusion.where, f32[128,128]{1,0:T(8,128)S(1)} %get-tuple-element.25.rows, f32[16,1024]{1,0:T(8,128)S(1)} %get-tuple-element.26.partial, ...), custom_call_target="tpu_custom_call" | custom-call | tf_op jit(solution)/shard_map/far/pallas_call | solution.py:736
  20.2 0.2 collective-permute-start.5
  20.4 1.5 %collective-permute-start.6 = (f32[16,256]{1,0:T(8,128)S(1)}, f32[16,256]{1,0:T(8,128)S(1)}, u32[]{:S(2)}, u32[]{:S(2)}) collective-permute-start(f32[16,256]{1,0:T(8,128)S(1)} %get-tuple-element.29), channel_id=1, source_target_pairs={{0,8},{4,12},{8,0},{12,4},{1,9},{5,13},{9,1},{13,5},{2,10},{6,14},... | collective-permute-start | bytes 49160 | tf_op jit(solution)/shard_map/ppermute | solution.py:834
  21.9 0.3 %collective-permute-start.7 = (f32[16,256]{1,0:T(8,128)S(1)}, f32[16,256]{1,0:T(8,128)S(1)}, u32[]{:S(2)}, u32[]{:S(2)}) collective-permute-start(f32[16,256]{1,0:T(8,128)S(1)} %get-tuple-element.30), channel_id=1, source_target_pairs={{0,12},{4,8},{8,4},{12,0},{1,13},{5,9},{9,5},{13,1},{2,14},{6,10},... | collective-permute-start | bytes 49160 | tf_op jit(solution)/shard_map/ppermute | solution.py:834
  22.1 0.0 collective-permute-done.5.refs_1_
  22.1 2.0 %collective-permute-done.6.refs_2_ = f32[16,256]{1,0:T(8,128)S(1)} collective-permute-done((f32[16,256]{1,0:T(8,128)S(1)}, f32[16,256]{1,0:T(8,128)S(1)}, u32[]{:S(2)}, u32[]{:S(2)}) %collective-permute-start.6) | collective-permute-done | bytes 16416 | tf_op jit(solution)/shard_map/ppermute | solution.py:834
  24.1 0.9 %collective-permute-done.7.refs_3_ = f32[16,256]{1,0:T(8,128)S(1)} collective-permute-done((f32[16,256]{1,0:T(8,128)S(1)}, f32[16,256]{1,0:T(8,128)S(1)}, u32[]{:S(2)}, u32[]{:S(2)}) %collective-permute-start.7) | collective-permute-done | bytes 16416 | tf_op jit(solution)/shard_map/ppermute | solution.py:834
  25.0 0.0 copy-done.2
  25.0 0.0 copy-done
  25.0 0.0 copy-done.1
  25.0 1.9 %update.1 = (f32[59,1024]{1,0:T(8,128)}, f32[59,1024]{1,0:T(8,128)}, f32[59,1024]{1,0:T(8,128)}) custom-call(s32[1]{0:T(128)} %bitcast.2.where, f32[4,12]{1,0:T(4,128)S(1)} %copy-done.3, f32[16,256]{1,0:T(8,128)S(1)} %get-tuple-element.27.refs_0_, f32[16,256]{1,0:T(8,128)S(1)} %collective-permute-done.5.refs_1_, ...), custom_call_target="tpu_custom_call" | custom-call | tf_op jit(solution)/shard_map/update/pallas_call | solution.py:736
  (1 shorter events, 0.0 us)
Async XLA Ops:
  0.6 24.4 %copy-start.2 = (f32[59,1024]{1,0:T(8,128)S(1)}, f32[59,1024]{1,0:T(8,128)}, u32[]{:S(2)}) copy-start(f32[59,1024]{1,0:T(8,128)} %refs_6_.1) | copy-start | bytes 724996
  1.8 5.0 %collective-permute-start = (f32[8,512]{1,0:T(8,128)S(1)}, f32[8,512]{1,0:T(8,128)S(1)}, u32[]{:S(2)}, u32[]{:S(2)}) collective-permute-start(f32[8,512]{1,0:T(8,128)S(1)} %get-tuple-element.19.own.first), channel_id=1, source_target_pairs={{0,1},{1,0},{2,3},{3,2},{4,5},{5,4},{6,7},{7,6},{8,9},{9,8},{10,11... | collective-permute-start | bytes 49160 | tf_op jit(solution)/shard_map/ppermute | solution.py:834
  4.9 4.8 %collective-permute-start.1 = (f32[59,256]{1,0:T(8,128)S(1)}, f32[59,256]{1,0:T(8,128)S(1)}, u32[]{:S(2)}, u32[]{:S(2)}) collective-permute-start(f32[59,256]{1,0:T(8,128)S(1)} %get-tuple-element.21), channel_id=1, source_target_pairs={{0,4},{4,0},{8,12},{12,8},{1,5},{5,1},{9,13},{13,9},{2,6},{6,2},{1... | collective-permute-start | bytes 181256 | tf_op jit(solution)/shard_map/ppermute | solution.py:834
  4.9 4.8 %collective-permute-start.2 = (f32[59,256]{1,0:T(8,128)S(1)}, f32[59,256]{1,0:T(8,128)S(1)}, u32[]{:S(2)}, u32[]{:S(2)}) collective-permute-start(f32[59,256]{1,0:T(8,128)S(1)} %get-tuple-element.22), channel_id=1, source_target_pairs={{0,8},{4,12},{8,0},{12,4},{1,9},{5,13},{9,1},{13,5},{2,10},{6,14},... | collective-permute-start | bytes 181256 | tf_op jit(solution)/shard_map/ppermute | solution.py:834
  6.4 4.1 %collective-permute-start.3 = (f32[59,256]{1,0:T(8,128)S(1)}, f32[59,256]{1,0:T(8,128)S(1)}, u32[]{:S(2)}, u32[]{:S(2)}) collective-permute-start(f32[59,256]{1,0:T(8,128)S(1)} %get-tuple-element.23), channel_id=1, source_target_pairs={{0,12},{4,8},{8,4},{12,0},{1,13},{5,9},{9,5},{13,1},{2,14},{6,10},... | collective-permute-start | bytes 181256 | tf_op jit(solution)/shard_map/ppermute | solution.py:834
  6.8 3.8 %copy-start.3 = (f32[4,12]{1,0:T(4,128)S(1)}, f32[4,12]{1,0:T(4,128)}, u32[]{:S(2)}) copy-start(f32[4,12]{1,0:T(4,128)} %cams.3) | copy-start | bytes 580
  6.8 3.8 %copy-start.4 = (s32[2]{0:T(128)S(1)}, s32[2]{0:T(128)}, u32[]{:S(2)}) copy-start(s32[2]{0:T(128)} %tile_ids.3) | copy-start | bytes 28
  6.8 18.2 %copy-start = (f32[59,1024]{1,0:T(8,128)S(1)}, f32[59,1024]{1,0:T(8,128)}, u32[]{:S(2)}) copy-start(f32[59,1024]{1,0:T(8,128)} %refs_4_.1) | copy-start | bytes 724996
  6.8 18.2 %copy-start.1 = (f32[59,1024]{1,0:T(8,128)S(1)}, f32[59,1024]{1,0:T(8,128)}, u32[]{:S(2)}) copy-start(f32[59,1024]{1,0:T(8,128)} %refs_5_.1) | copy-start | bytes 724996
  6.8 8.6 %collective-permute-start.4 = (f32[16,512]{1,0:T(8,128)S(1)}, f32[16,512]{1,0:T(8,128)S(1)}, u32[]{:S(2)}, u32[]{:S(2)}) collective-permute-start(f32[16,512]{1,0:T(8,128)S(1)} %join.1), channel_id=1, source_target_pairs={{0,2},{1,3},{2,0},{3,1},{4,6},{5,7},{6,4},{7,5},{8,10},{9,11},{10,... | collective-permute-start | bytes 98312 | tf_op jit(solution)/shard_map/ppermute | solution.py:834
  20.2 2.0 %collective-permute-start.5 = (f32[16,256]{1,0:T(8,128)S(1)}, f32[16,256]{1,0:T(8,128)S(1)}, u32[]{:S(2)}, u32[]{:S(2)}) collective-permute-start(f32[16,256]{1,0:T(8,128)S(1)} %get-tuple-element.28), channel_id=1, source_target_pairs={{0,4},{4,0},{8,12},{12,8},{1,5},{5,1},{9,13},{13,9},{2,6},{6,2},{1... | collective-permute-start | bytes 49160 | tf_op jit(solution)/shard_map/ppermute | solution.py:834
  20.4 3.7 %collective-permute-start.6 = (f32[16,256]{1,0:T(8,128)S(1)}, f32[16,256]{1,0:T(8,128)S(1)}, u32[]{:S(2)}, u32[]{:S(2)}) collective-permute-start(f32[16,256]{1,0:T(8,128)S(1)} %get-tuple-element.29), channel_id=1, source_target_pairs={{0,8},{4,12},{8,0},{12,4},{1,9},{5,13},{9,1},{13,5},{2,10},{6,14},... | collective-permute-start | bytes 49160 | tf_op jit(solution)/shard_map/ppermute | solution.py:834
  21.9 3.2 %collective-permute-start.7 = (f32[16,256]{1,0:T(8,128)S(1)}, f32[16,256]{1,0:T(8,128)S(1)}, u32[]{:S(2)}, u32[]{:S(2)}) collective-permute-start(f32[16,256]{1,0:T(8,128)S(1)} %get-tuple-element.30), channel_id=1, source_target_pairs={{0,12},{4,8},{8,4},{12,0},{1,13},{5,9},{9,5},{13,1},{2,14},{6,10},... | collective-permute-start | bytes 49160 | tf_op jit(solution)/shard_map/ppermute | solution.py:834

commit v11 on v9

--- a/solution.py
+++ b/solution.py
@@ -331,12 +331,31 @@
     return jnp.take_along_axis(source, lane, axis=1, mode="promise_in_bounds")
 
 
+def fold(values):
+    sub = lax.broadcasted_iota(jnp.int32, (8, LANES), 0)
+    values = list(values)
+    step = 4
+    while step:
+        low = (sub & step) == 0
+        moved = [jnp.where(low, values[i + step], values[i]) for i in range(step)]
+        if step < 4:
+            moved = [
+                jnp.where(low, pltpu.roll(each, 8 - step, 0), pltpu.roll(each, step, 0))
+                for each in moved
+            ]
+        else:
+            moved = [pltpu.roll(each, step, 0) for each in moved]
+        values = [jnp.where(low, values[i], values[i + step]) + moved[i] for i in range(step)]
+        step //= 2
+    return values[0]
+
+
 def spread(row):
     return jnp.broadcast_to(row, (8, LANES))
 
 
 def composite(tiles, first_group, me, rows, info_s, rendered, work):
-    alpha_s, weight_s, left_s, image_s, before_s, behind_s, error_s, joined_s, wrong_s, coef_s, line_s, sum_s, acc_s = work
+    alpha_s, weight_s, left_s, image_s, before_s, behind_s, error_s, joined_s, wrong_s, coef_s, line_s, part_s, acc_s = work
     groups, tile_count, _, listed = acc_s.shape
     pixels = info_s.shape[2] // tile_count
     tiles_here = groups * tile_count
@@ -389,7 +408,7 @@
             line_s[0, s, half] = c[0] + u * (c[1] + u * c[2])
             line_s[1, s, half] = c[3] + u * c[4]
 
-    rows_each = 2
+    rows_each = 4
 
     def forward(i, carry):
         for j in range(rows_each):
@@ -485,7 +504,6 @@
         plain = [[None] * 3 for _ in range(side // 8)]
         hues = [None] * 3
         for row in range(side):
-            v = row - middle
             for half in range(side // 8):
                 at = pl.ds(row * side + half * 8, 8)
                 of_step = pl.ds(pl.multiple_of(s * pixels, pixels) + (row * side + half * 8), 8)
@@ -496,33 +514,38 @@
                 gap = pull - behind
                 behind_s[at, :] = behind + alpha_s[of_step, :] * gap
                 push = weight * gap
-                terms = (push, v * push, (v * v) * push)
                 hue = [weight * error[k] for k in range(3)]
                 if row == 0:
-                    plain[half] = list(terms)
+                    plain[half] = [push, push, push]
                 else:
-                    plain[half] = [plain[half][m] + terms[m] for m in range(3)]
+                    plain[half][0] = plain[half][0] + push
+                    plain[half][1] = plain[half][1] + plain[half][0]
+                    plain[half][2] = plain[half][2] + plain[half][1]
                 hues = [hue[k] if hues[k] is None else hues[k] + hue[k] for k in range(3)]
-        u = [sub.astype(F32) + (8.0 * half - middle) for half in range(side // 8)]
-
-        def over(m, power):
-            total = 0.0
-            for half in range(side // 8):
-                value = plain[half][m]
-                for _ in range(power):
-                    value = value * u[half]
-                total = total + value
-            return total
-
-        for m, value in enumerate(
-            (over(0, 0), over(0, 1), over(1, 0), over(0, 2), over(1, 1), over(2, 0), *hues)
-        ):
-            sum_s[m, pl.ds(s, 1), :] = jnp.sum(value, axis=0, keepdims=True)
+        for half in range(side // 8):
+            for m in range(3):
+                part_s[3 * half + m, s] = plain[half][m]
+        for k in range(3):
+            part_s[6 + k, s] = hues[k]
         return carry
 
     lax.fori_loop(0, steps, backward, 0)
 
-    m_00, m_10, m_01, m_20, m_11, m_02, *grads = [sum_s[m] for m in range(9)]
+    shift = side - middle
+    u = [sub.astype(F32) + (8.0 * half - middle) for half in range(side // 8)]
+    parts = []
+    for s in range(steps):
+        moments = [0.0] * 6
+        for half in range(side // 8):
+            one, two, three = [part_s[3 * half + m, s] for m in range(3)]
+            by_v = shift * one - two
+            by_vv = shift * shift * one - (2.0 * shift + 1.0) * two + 2.0 * three
+            by_u = u[half] * one
+            terms = (one, by_u, by_v, u[half] * by_u, u[half] * by_v, by_vv)
+            moments = [moments[m] + terms[m] for m in range(6)]
+        parts.append(moments + [part_s[6 + k, s] for k in range(3)])
+    sums = [fold([parts[s][m] for s in range(steps)]) for m in range(9)]
+    m_00, m_10, m_01, m_20, m_11, m_02, *grads = sums
     n_10 = m_10 - mean_u * m_00
     n_01 = m_01 - mean_v * m_00
     grads = [
@@ -534,18 +557,15 @@
         m_00,
     ] + grads
     mine = sub == lane % steps
+    last = []
     for n in range(tiles_here):
         g, t = n // tile_count, n % tile_count
         for h in range(halves):
             at = lane // steps + (n * segments + h * (LANES // steps))
-            for f in range(9):
-                row = jnp.sum(
-                    jnp.where(mine, lane_gather(grads[f], at), 0.0), axis=0, keepdims=True
-                )
-                if f < 8:
-                    acc_s[g, t, f : f + 1, h * LANES : (h + 1) * LANES] = row
-                else:
-                    acc_s[0, 0, 8 + n * halves + h : 9 + n * halves + h, :LANES] = row
+            found = [jnp.where(mine, lane_gather(grads[f], at), 0.0) for f in range(9)]
+            acc_s[g, t, 0:8, h * LANES : (h + 1) * LANES] = fold(found[:8])
+            last.append(found[8])
+    acc_s[0, 0, 8:16, :LANES] = fold(last)
 
 
 def pool_sum(slab, info_s, acc_s):
@@ -726,7 +746,7 @@
         pltpu.VMEM((3, 16, pixels), F32),
         pltpu.VMEM((9, steps, LANES), F32),
         pltpu.VMEM((2, steps, TILE_SIDE // 8, 8, LANES), F32),
-        pltpu.VMEM((9, steps, LANES), F32),
+        pltpu.VMEM((9, steps, 8, LANES), F32),
         pltpu.VMEM((2, tile_count, ROWS, listed), F32),
     ]
 

time: 26.4 us -> 26.2 us (level)
  no operation moved by 1% of the time
where the time goes in v11:
time: 26.2 us; the launch traced here: 26 us
  Pallas kernels  11.8 us (45%)
  starting transfers between devices  9.73 us (37%)
  waiting for transfers between devices  3.7 us (14%)
  between operations  0.69 us (3%)
    pallas_call x5, Pallas kernels, call(): pl.pallas_call(kernel, out_shape=out_shape, in_specs=in_specs, out_specs=...  11.8 us
    ppermute x8, starting transfers between devices, swap(): lax.ppermute(value, axis, [(k, k ^ d) for k in range(lax.axis_size(axis))])  9.73 us
    ppermute x8, waiting for transfers between devices, swap(): lax.ppermute(value, axis, [(k, k ^ d) for k in range(lax.axis_size(axis))])  3.7 us
  transfers between devices with their start and end apart: 8, of which 3 were waited for; matrix products, arithmetic and copies ran while one was open for 0% of the time, Pallas kernels for 17%

profile of v11, /device:TPU:0, one launch (start us, length us, event | category | flops | bytes accessed | tf_op | source)
XLA Modules:
  0.0 26.0 jit_solution(3024832062119390744)
XLA Ops:
  0.6 0.0 copy-start.2
  0.6 1.2 %pack.1 = (f32[8,512]{1,0:T(8,128)S(1)}, f32[59,256]{1,0:T(8,128)S(1)}, f32[59,256]{1,0:T(8,128)S(1)}, f32[59,256]{1,0:T(8,128)S(1)}, f32[59,256]{1,0:T(8,128)S(1)}) custom-call(s32[1]{0:T(128)} %bitcast.2.where, s32[2,1,256]{2,1,0:T(1,128)} %bitcast.4, s32[2,256]{1,0:T(2,128)} %refs_1_.1, f32[3,512]{1,0:T(4,128)} %refs_2_.1, f32[59,1024]{1,0:T(8,128)} %refs_4_.1), custom_call_target="tpu_custom_call" | custom-call | tf_op jit(solution)/shard_map/pack/pallas_call | solution.py:723
  1.8 3.1 %collective-permute-start = (f32[8,512]{1,0:T(8,128)S(1)}, f32[8,512]{1,0:T(8,128)S(1)}, u32[]{:S(2)}, u32[]{:S(2)}) collective-permute-start(f32[8,512]{1,0:T(8,128)S(1)} %get-tuple-element.19.own.first), channel_id=1, source_target_pairs={{0,1},{1,0},{2,3},{3,2},{4,5},{5,4},{6,7},{7,6},{8,9},{9,8},{10,11... | collective-permute-start | bytes 49160 | tf_op jit(solution)/shard_map/ppermute | solution.py:821
  4.9 0.0 collective-permute-start.1
  4.9 1.5 %collective-permute-start.2 = (f32[59,256]{1,0:T(8,128)S(1)}, f32[59,256]{1,0:T(8,128)S(1)}, u32[]{:S(2)}, u32[]{:S(2)}) collective-permute-start(f32[59,256]{1,0:T(8,128)S(1)} %get-tuple-element.22), channel_id=1, source_target_pairs={{0,8},{4,12},{8,0},{12,4},{1,9},{5,13},{9,1},{13,5},{2,10},{6,14},... | collective-permute-start | bytes 181256 | tf_op jit(solution)/shard_map/ppermute | solution.py:821
  6.4 0.4 %collective-permute-start.3 = (f32[59,256]{1,0:T(8,128)S(1)}, f32[59,256]{1,0:T(8,128)S(1)}, u32[]{:S(2)}, u32[]{:S(2)}) collective-permute-start(f32[59,256]{1,0:T(8,128)S(1)} %get-tuple-element.23), channel_id=1, source_target_pairs={{0,12},{4,8},{8,4},{12,0},{1,13},{5,9},{9,5},{13,1},{2,14},{6,10},... | collective-permute-start | bytes 181256 | tf_op jit(solution)/shard_map/ppermute | solution.py:821
  6.8 0.0 copy-start.3
  6.8 0.0 copy-start.4
  6.8 0.0 copy-start
  6.8 0.0 copy-start.1
  6.8 0.0 collective-permute-done.other.second
  6.8 2.9 %collective-permute-start.4 = (f32[16,512]{1,0:T(8,128)S(1)}, f32[16,512]{1,0:T(8,128)S(1)}, u32[]{:S(2)}, u32[]{:S(2)}) collective-permute-start(f32[16,512]{1,0:T(8,128)S(1)} %join.1), channel_id=1, source_target_pairs={{0,2},{1,3},{2,0},{3,1},{4,6},{5,7},{6,4},{7,5},{8,10},{9,11},{10,... | collective-permute-start | bytes 98312 | tf_op jit(solution)/shard_map/ppermute | solution.py:821
  9.7 0.1 pad_add_fusion.where
  9.8 0.0 collective-permute-done.1.refs_1_
  9.8 0.0 collective-permute-done.2.refs_2_
  9.8 0.8 %collective-permute-done.3.refs_3_ = f32[59,256]{1,0:T(8,128)S(1)} collective-permute-done((f32[59,256]{1,0:T(8,128)S(1)}, f32[59,256]{1,0:T(8,128)S(1)}, u32[]{:S(2)}, u32[]{:S(2)}) %collective-permute-start.3) | collective-permute-done | bytes 60448 | tf_op jit(solution)/shard_map/ppermute | solution.py:821
  10.5 0.0 copy-done.3
  10.5 0.0 copy-done.4
  10.6 4.5 %near.1 = (f32[3,512]{1,0:T(4,128)}, f32[128,128]{1,0:T(8,128)S(1)}, f32[16,1024]{1,0:T(8,128)S(1)}) custom-call(s32[2]{0:T(128)S(1)} %copy-done.4, f32[4,12]{1,0:T(4,128)S(1)} %copy-done.3, s32[3]{0:T(128)S(1)} %pad_add_fusion.where, f32[8,512]{1,0:T(8,128)S(1)} %get-tuple-element.19.own.first, f32[8,512]{1,0:T(8,128)S(1)} %collective-permute-done.other.second, ...), custom_call_target="tpu_custom_call" | custom-call | tf_op jit(solution)/shard_map/near/pallas_call | solution.py:723
  15.0 0.0 collective-permute-done.4.infos
  15.0 4.3 %far.1 = (f32[16,256]{1,0:T(8,128)S(1)}, f32[16,256]{1,0:T(8,128)S(1)}, f32[16,256]{1,0:T(8,128)S(1)}, f32[16,256]{1,0:T(8,128)S(1)}) custom-call(s32[2]{0:T(128)S(1)} %copy-done.4, s32[3]{0:T(128)S(1)} %pad_add_fusion.where, f32[128,128]{1,0:T(8,128)S(1)} %get-tuple-element.25.rows, f32[16,1024]{1,0:T(8,128)S(1)} %get-tuple-element.26.partial, ...), custom_call_target="tpu_custom_call" | custom-call | tf_op jit(solution)/shard_map/far/pallas_call | solution.py:723
  19.3 0.2 collective-permute-start.5
  19.5 1.5 %collective-permute-start.6 = (f32[16,256]{1,0:T(8,128)S(1)}, f32[16,256]{1,0:T(8,128)S(1)}, u32[]{:S(2)}, u32[]{:S(2)}) collective-permute-start(f32[16,256]{1,0:T(8,128)S(1)} %get-tuple-element.29), channel_id=1, source_target_pairs={{0,8},{4,12},{8,0},{12,4},{1,9},{5,13},{9,1},{13,5},{2,10},{6,14},... | collective-permute-start | bytes 49160 | tf_op jit(solution)/shard_map/ppermute | solution.py:821
  21.0 0.3 collective-permute-start.7
  21.2 0.0 collective-permute-done.5.refs_1_
  21.2 2.0 %collective-permute-done.6.refs_2_ = f32[16,256]{1,0:T(8,128)S(1)} collective-permute-done((f32[16,256]{1,0:T(8,128)S(1)}, f32[16,256]{1,0:T(8,128)S(1)}, u32[]{:S(2)}, u32[]{:S(2)}) %collective-permute-start.6) | collective-permute-done | bytes 16416 | tf_op jit(solution)/shard_map/ppermute | solution.py:821
  23.2 0.9 %collective-permute-done.7.refs_3_ = f32[16,256]{1,0:T(8,128)S(1)} collective-permute-done((f32[16,256]{1,0:T(8,128)S(1)}, f32[16,256]{1,0:T(8,128)S(1)}, u32[]{:S(2)}, u32[]{:S(2)}) %collective-permute-start.7) | collective-permute-done | bytes 16416 | tf_op jit(solution)/shard_map/ppermute | solution.py:821
  24.1 0.0 copy-done.2
  24.1 0.0 copy-done
  24.1 0.0 copy-done.1
  24.1 1.9 %update.1 = (f32[59,1024]{1,0:T(8,128)}, f32[59,1024]{1,0:T(8,128)}, f32[59,1024]{1,0:T(8,128)}) custom-call(s32[1]{0:T(128)} %bitcast.2.where, f32[4,12]{1,0:T(4,128)S(1)} %copy-done.3, f32[16,256]{1,0:T(8,128)S(1)} %get-tuple-element.27.refs_0_, f32[16,256]{1,0:T(8,128)S(1)} %collective-permute-done.5.refs_1_, ...), custom_call_target="tpu_custom_call" | custom-call | tf_op jit(solution)/shard_map/update/pallas_call | solution.py:723
  (1 shorter events, 0.0 us)
Async XLA Ops:
  0.6 23.5 %copy-start.2 = (f32[59,1024]{1,0:T(8,128)S(1)}, f32[59,1024]{1,0:T(8,128)}, u32[]{:S(2)}) copy-start(f32[59,1024]{1,0:T(8,128)} %refs_6_.1) | copy-start | bytes 724996
  1.8 5.0 %collective-permute-start = (f32[8,512]{1,0:T(8,128)S(1)}, f32[8,512]{1,0:T(8,128)S(1)}, u32[]{:S(2)}, u32[]{:S(2)}) collective-permute-start(f32[8,512]{1,0:T(8,128)S(1)} %get-tuple-element.19.own.first), channel_id=1, source_target_pairs={{0,1},{1,0},{2,3},{3,2},{4,5},{5,4},{6,7},{7,6},{8,9},{9,8},{10,11... | collective-permute-start | bytes 49160 | tf_op jit(solution)/shard_map/ppermute | solution.py:821
  4.9 4.8 %collective-permute-start.1 = (f32[59,256]{1,0:T(8,128)S(1)}, f32[59,256]{1,0:T(8,128)S(1)}, u32[]{:S(2)}, u32[]{:S(2)}) collective-permute-start(f32[59,256]{1,0:T(8,128)S(1)} %get-tuple-element.21), channel_id=1, source_target_pairs={{0,4},{4,0},{8,12},{12,8},{1,5},{5,1},{9,13},{13,9},{2,6},{6,2},{1... | collective-permute-start | bytes 181256 | tf_op jit(solution)/shard_map/ppermute | solution.py:821
  4.9 4.8 %collective-permute-start.2 = (f32[59,256]{1,0:T(8,128)S(1)}, f32[59,256]{1,0:T(8,128)S(1)}, u32[]{:S(2)}, u32[]{:S(2)}) collective-permute-start(f32[59,256]{1,0:T(8,128)S(1)} %get-tuple-element.22), channel_id=1, source_target_pairs={{0,8},{4,12},{8,0},{12,4},{1,9},{5,13},{9,1},{13,5},{2,10},{6,14},... | collective-permute-start | bytes 181256 | tf_op jit(solution)/shard_map/ppermute | solution.py:821
  6.4 4.1 %collective-permute-start.3 = (f32[59,256]{1,0:T(8,128)S(1)}, f32[59,256]{1,0:T(8,128)S(1)}, u32[]{:S(2)}, u32[]{:S(2)}) collective-permute-start(f32[59,256]{1,0:T(8,128)S(1)} %get-tuple-element.23), channel_id=1, source_target_pairs={{0,12},{4,8},{8,4},{12,0},{1,13},{5,9},{9,5},{13,1},{2,14},{6,10},... | collective-permute-start | bytes 181256 | tf_op jit(solution)/shard_map/ppermute | solution.py:821
  6.8 3.8 %copy-start.3 = (f32[4,12]{1,0:T(4,128)S(1)}, f32[4,12]{1,0:T(4,128)}, u32[]{:S(2)}) copy-start(f32[4,12]{1,0:T(4,128)} %cams.3) | copy-start | bytes 580
  6.8 3.8 %copy-start.4 = (s32[2]{0:T(128)S(1)}, s32[2]{0:T(128)}, u32[]{:S(2)}) copy-start(s32[2]{0:T(128)} %tile_ids.3) | copy-start | bytes 28
  6.8 17.3 %copy-start = (f32[59,1024]{1,0:T(8,128)S(1)}, f32[59,1024]{1,0:T(8,128)}, u32[]{:S(2)}) copy-start(f32[59,1024]{1,0:T(8,128)} %refs_4_.1) | copy-start | bytes 724996
  6.8 17.3 %copy-start.1 = (f32[59,1024]{1,0:T(8,128)S(1)}, f32[59,1024]{1,0:T(8,128)}, u32[]{:S(2)}) copy-start(f32[59,1024]{1,0:T(8,128)} %refs_5_.1) | copy-start | bytes 724996
  6.8 8.2 %collective-permute-start.4 = (f32[16,512]{1,0:T(8,128)S(1)}, f32[16,512]{1,0:T(8,128)S(1)}, u32[]{:S(2)}, u32[]{:S(2)}) collective-permute-start(f32[16,512]{1,0:T(8,128)S(1)} %join.1), channel_id=1, source_target_pairs={{0,2},{1,3},{2,0},{3,1},{4,6},{5,7},{6,4},{7,5},{8,10},{9,11},{10,... | collective-permute-start | bytes 98312 | tf_op jit(solution)/shard_map/ppermute | solution.py:821
  19.3 1.9 %collective-permute-start.5 = (f32[16,256]{1,0:T(8,128)S(1)}, f32[16,256]{1,0:T(8,128)S(1)}, u32[]{:S(2)}, u32[]{:S(2)}) collective-permute-start(f32[16,256]{1,0:T(8,128)S(1)} %get-tuple-element.28), channel_id=1, source_target_pairs={{0,4},{4,0},{8,12},{12,8},{1,5},{5,1},{9,13},{13,9},{2,6},{6,2},{1... | collective-permute-start | bytes 49160 | tf_op jit(solution)/shard_map/ppermute | solution.py:821
  19.5 3.8 %collective-permute-start.6 = (f32[16,256]{1,0:T(8,128)S(1)}, f32[16,256]{1,0:T(8,128)S(1)}, u32[]{:S(2)}, u32[]{:S(2)}) collective-permute-start(f32[16,256]{1,0:T(8,128)S(1)} %get-tuple-element.29), channel_id=1, source_target_pairs={{0,8},{4,12},{8,0},{12,4},{1,9},{5,13},{9,1},{13,5},{2,10},{6,14},... | collective-permute-start | bytes 49160 | tf_op jit(solution)/shard_map/ppermute | solution.py:821
  21.0 3.2 %collective-permute-start.7 = (f32[16,256]{1,0:T(8,128)S(1)}, f32[16,256]{1,0:T(8,128)S(1)}, u32[]{:S(2)}, u32[]{:S(2)}) collective-permute-start(f32[16,256]{1,0:T(8,128)S(1)} %get-tuple-element.30), channel_id=1, source_target_pairs={{0,12},{4,8},{8,4},{12,0},{1,13},{5,9},{9,5},{13,1},{2,14},{6,10},... | collective-permute-start | bytes 49160 | tf_op jit(solution)/shard_map/ppermute | solution.py:821

commit v12 on v8

--- a/solution.py
+++ b/solution.py
@@ -610,20 +610,17 @@
     out[half:, :] = second[...]
 
 
-def update_kernel(pieces, where, cams, *refs):
-    packets = refs[:pieces]
-    sources, sinks = refs[pieces : pieces + 3], refs[pieces + 3 : pieces + 6]
-    feats, rows, grads, held, made, in_sems, out_sems = refs[pieces + 6 :]
-    params, adam_m, adam_v = held.at[0], held.at[1], held.at[2]
-    features, width = params.shape
-    loads = [pltpu.make_async_copy(sources[k], held.at[k], in_sems.at[k]) for k in range(3)]
-    for load in loads:
-        load.start()
+def update_kernel(pieces, follows, where, cams, params, adam_m, adam_v, *refs):
+    packets, refs = refs[:pieces], refs[pieces + 3 * follows :]
+    sinks, (feats, rows, grads, made, sems) = refs[:3], refs[3:]
+    features = params.shape[0]
     chunk = packets[0].shape[1]
+    width = pieces * chunk
     slabs = width // LANES
+    start = (where[0] ^ where[1]) // pieces * pieces * chunk
     for d in range(pieces):
         for h in range(chunk // LANES):
-            slab = (where[0] ^ d) * (chunk // LANES) + h
+            slab = (where[0] ^ where[1] ^ d) % pieces * (chunk // LANES) + h
             rows[pl.ds(slab, ROWS, stride=slabs), :] = packets[d][:, h * LANES : (h + 1) * LANES]
     pulled = [rows[f * slabs : (f + 1) * slabs, :] for f in range(10)]
     view = pulled[9]
@@ -637,30 +634,39 @@
     def put(f, value):
         grads[f * slabs : (f + 1) * slabs, :] = value
 
-    loads[0].wait()
-    spread_features([params], feats, features)
+    def column(s):
+        return pl.ds(pl.multiple_of(start + s * LANES, LANES), LANES)
+
+    for s in range(slabs):
+        for row in range(0, features, 8):
+            count = min(8, features - row)
+            feats[pl.ds(row * slabs + s, count, stride=slabs), :] = params[
+                row : row + count, column(s)
+            ]
     project_pull(lambda f: feats[f * slabs : (f + 1) * slabs, :], cam, pulled[:9], put)
     rate = learn_rate / (1.0 - beta_one**adam_steps)
     unbias = 1.0 / (1.0 - beta_two**adam_steps)
-    loads[1].wait()
-    loads[2].wait()
     stores = []
     for row in range(0, features, 8):
         count = min(8, features - row)
+        span = slice(row, row + count)
         for s in range(slabs):
-            at = (slice(row, row + count), slice(s * LANES, (s + 1) * LANES))
+            here = (span, slice(s * LANES, (s + 1) * LANES))
             grad = grads[pl.ds(row * slabs + s, count, stride=slabs), :]
-            moment = beta_one * adam_m[at] + (1.0 - beta_one) * grad
-            second = beta_two * adam_v[at] + (1.0 - beta_two) * grad * grad
-            made.at[1][at] = moment
-            made.at[2][at] = second
-            made.at[0][at] = params[at] - rate * moment / (jnp.sqrt(second * unbias) + adam_eps)
+            moment = beta_one * adam_m[span, column(s)] + (1.0 - beta_one) * grad
+            second = beta_two * adam_v[span, column(s)] + (1.0 - beta_two) * grad * grad
+            made.at[1][here] = moment
+            made.at[2][here] = second
+            made.at[0][here] = params[span, column(s)] - rate * moment / (
+                jnp.sqrt(second * unbias) + adam_eps
+            )
         if row % 16 == 8 or row + count == features:
             first = row // 16 * 16
             span = pl.ds(first, row + count - first)
+            columns = pl.ds(pl.multiple_of(start, LANES), width)
             for k in range(3):
                 store = pltpu.make_async_copy(
-                    made.at[k, span], sinks[k].at[span], out_sems.at[k, first // 16]
+                    made.at[k, span], sinks[k].at[span, columns], sems.at[k, first // 16]
                 )
                 store.start()
                 stores.append(store)
@@ -748,26 +754,32 @@
     )[0]
 
 
-def update(where, cameras, params, adam_m, adam_v, packets):
-    features, width = params.shape
+def update(own, first, cameras, params, adam_m, adam_v, packets, before):
+    features = params.shape[0]
+    width = sum(packet.shape[1] for packet in packets)
     slabs = width // LANES
     shape = jax.ShapeDtypeStruct(params.shape, F32)
-    return call(
-        functools.partial(update_kernel, len(packets)),
-        "update",
-        (shape, shape, shape),
-        [smem()] * 2 + [vmem()] * len(packets) + [any_space()] * 3,
-        [
+    at = 5 + len(packets)
+    return pl.pallas_call(
+        functools.partial(update_kernel, len(packets), len(before) > 0),
+        out_shape=(shape, shape, shape),
+        in_specs=[smem()] * 2
+        + [vmem()] * (3 + len(packets))
+        + [any_space()] * len(before),
+        out_specs=(any_space(),) * 3,
+        scratch_shapes=[
             pltpu.VMEM((features * slabs, LANES), F32),
             pltpu.VMEM((ROWS * slabs, LANES), F32),
             pltpu.VMEM((features * slabs, LANES), F32),
-            pltpu.VMEM((3,) + params.shape, F32),
-            pltpu.VMEM((3,) + params.shape, F32),
-            pltpu.SemaphoreType.DMA((3,)),
+            pltpu.VMEM((3, features, width), F32),
             pltpu.SemaphoreType.DMA((3, (features + 15) // 16)),
         ],
-        (where, cameras, *packets, params, adam_m, adam_v),
-        (any_space(),) * 3,
+        input_output_aliases={at + k: k for k in range(len(before))},
+        compiler_params=pltpu.CompilerParams(vmem_limit_bytes=32 * 1024 * 1024),
+        name="update",
+    )(
+        jnp.stack([own, jnp.int32(first)]).astype(jnp.int32),
+        cameras, params, adam_m, adam_v, *packets, *before,
     )
 
 
@@ -814,9 +826,13 @@
     else:
         packets = [jnp.stack(packets)[jnp.arange(shards) ^ group].transpose(1, 0, 2).reshape(ROWS, -1)]
         own = jnp.int32(0)
-    new_params, new_m, new_v = update(
-        own.reshape(1), cameras, params, adam_m, adam_v, packets
-    )
+    made = ()
+    count = max(1, len(packets) // 2)
+    for first in range(0, len(packets), count):
+        made = update(
+            own, first, cameras, params, adam_m, adam_v, packets[first : first + count], made
+        )
+    new_params, new_m, new_v = made
     return (rendered, new_params, new_m, new_v)
 
 

time: 25.6 us -> 25.1 us (0.980)
  waiting for transfers between devices: 3.71 us -> 1.58 us
  Pallas kernels: 11.2 us -> 12.5 us
    pallas_call x0 -> x2, Pallas kernels: none -> 3.19 us  [update(): pl.pallas_call(functools.partial(update_kernel, len(packets), len(before)...]
    ppermute x8, waiting for transfers between devices: 3.71 us -> 1.58 us  [swap(): lax.ppermute(value, axis, [(k, k ^ d) for k in range(lax.axis_size(axis))])]
    pallas_call x5 -> x4, Pallas kernels: 11.2 us -> 9.31 us  [call(): pl.pallas_call(kernel, out_shape=out_shape, in_specs=in_specs, out_specs=...]
  transfers between devices with their start and end apart: 8 -> 8, of which waited for: 3 -> 2; matrix products, arithmetic and copies ran while one was open for 0% -> 1% of each run, Pallas kernels for 16% -> 23%
where the time goes in v12:
time: 25.1 us; the launch traced here: 25 us
  Pallas kernels  12.5 us (50%)
  starting transfers between devices  9.94 us (40%)
  waiting for transfers between devices  1.58 us (6%)
  between operations  0.72 us (3%)
    ppermute x8, starting transfers between devices, swap(): lax.ppermute(value, axis, [(k, k ^ d) for k in range(lax.axis_size(axis))])  9.94 us
    pallas_call x4, Pallas kernels, call(): pl.pallas_call(kernel, out_shape=out_shape, in_specs=in_specs, out_specs=...  9.31 us
    pallas_call x2, Pallas kernels, update(): pl.pallas_call(functools.partial(update_kernel, len(packets), len(before)...  3.19 us
    ppermute x8, waiting for transfers between devices, swap(): lax.ppermute(value, axis, [(k, k ^ d) for k in range(lax.axis_size(axis))])  1.58 us
  transfers between devices with their start and end apart: 8, of which 2 were waited for; matrix products, arithmetic and copies ran while one was open for 1% of the time, Pallas kernels for 23%

profile of v12, /device:TPU:0, one launch (start us, length us, event | category | flops | bytes accessed | tf_op | source)
XLA Modules:
  0.0 25.0 jit_solution(2175648413144535598)
XLA Ops:
  0.6 0.0 copy-start.2
  0.6 1.2 %pack.1 = (f32[8,512]{1,0:T(8,128)S(1)}, f32[59,256]{1,0:T(8,128)S(1)}, f32[59,256]{1,0:T(8,128)S(1)}, f32[59,256]{1,0:T(8,128)S(1)}, f32[59,256]{1,0:T(8,128)S(1)}) custom-call(s32[1]{0:T(128)} %bitcast.2.where, s32[2,1,256]{2,1,0:T(1,128)} %bitcast.4, s32[2,256]{1,0:T(2,128)} %refs_1_.1, f32[3,512]{1,0:T(4,128)} %refs_2_.1, f32[59,1024]{1,0:T(8,128)} %params.3), custom_call_target="tpu_custom_call" | custom-call | tf_op jit(solution)/shard_map/pack/pallas_call | solution.py:690
  1.8 3.1 %collective-permute-start = (f32[8,512]{1,0:T(8,128)S(1)}, f32[8,512]{1,0:T(8,128)S(1)}, u32[]{:S(2)}, u32[]{:S(2)}) collective-permute-start(f32[8,512]{1,0:T(8,128)S(1)} %get-tuple-element.22.own.first), channel_id=1, source_target_pairs={{0,1},{1,0},{2,3},{3,2},{4,5},{5,4},{6,7},{7,6},{8,9},{9,8},{10,11... | collective-permute-start | bytes 49160 | tf_op jit(solution)/shard_map/ppermute | solution.py:789
  4.9 0.0 collective-permute-start.1
  4.9 1.5 %collective-permute-start.2 = (f32[59,256]{1,0:T(8,128)S(1)}, f32[59,256]{1,0:T(8,128)S(1)}, u32[]{:S(2)}, u32[]{:S(2)}) collective-permute-start(f32[59,256]{1,0:T(8,128)S(1)} %get-tuple-element.25), channel_id=1, source_target_pairs={{0,8},{4,12},{8,0},{12,4},{1,9},{5,13},{9,1},{13,5},{2,10},{6,14},... | collective-permute-start | bytes 181256 | tf_op jit(solution)/shard_map/ppermute | solution.py:789
  6.4 0.4 %collective-permute-start.3 = (f32[59,256]{1,0:T(8,128)S(1)}, f32[59,256]{1,0:T(8,128)S(1)}, u32[]{:S(2)}, u32[]{:S(2)}) collective-permute-start(f32[59,256]{1,0:T(8,128)S(1)} %get-tuple-element.26), channel_id=1, source_target_pairs={{0,12},{4,8},{8,4},{12,0},{1,13},{5,9},{9,5},{13,1},{2,14},{6,10},... | collective-permute-start | bytes 181256 | tf_op jit(solution)/shard_map/ppermute | solution.py:789
  6.8 0.1 pad_add_fusion.2.where
  6.9 0.0 copy-start.3
  6.9 0.0 copy-start.4
  6.9 0.0 copy-start
  6.9 0.0 copy-start.1
  6.9 0.0 collective-permute-done.other.second
  6.9 2.8 %collective-permute-start.4 = (f32[16,512]{1,0:T(8,128)S(1)}, f32[16,512]{1,0:T(8,128)S(1)}, u32[]{:S(2)}, u32[]{:S(2)}) collective-permute-start(f32[16,512]{1,0:T(8,128)S(1)} %join.1), channel_id=1, source_target_pairs={{0,2},{1,3},{2,0},{3,1},{4,6},{5,7},{6,4},{7,5},{8,10},{9,11},{10,... | collective-permute-start | bytes 98312 | tf_op jit(solution)/shard_map/ppermute | solution.py:789
  9.7 0.1 pad_add_fusion.where
  9.8 0.0 collective-permute-done.1.refs_1_
  9.8 0.0 collective-permute-done.2.refs_2_
  9.8 0.8 %collective-permute-done.3.refs_3_ = f32[59,256]{1,0:T(8,128)S(1)} collective-permute-done((f32[59,256]{1,0:T(8,128)S(1)}, f32[59,256]{1,0:T(8,128)S(1)}, u32[]{:S(2)}, u32[]{:S(2)}) %collective-permute-start.3) | collective-permute-done | bytes 60448 | tf_op jit(solution)/shard_map/ppermute | solution.py:789
  10.5 0.0 copy-done.3
  10.5 0.0 copy-done.4
  10.6 4.1 %near.1 = (f32[3,512]{1,0:T(4,128)}, f32[128,128]{1,0:T(8,128)S(1)}, f32[16,1024]{1,0:T(8,128)S(1)}) custom-call(s32[2]{0:T(128)S(1)} %copy-done.4, f32[4,12]{1,0:T(4,128)S(1)} %copy-done.3, s32[3]{0:T(128)S(1)} %pad_add_fusion.where, f32[8,512]{1,0:T(8,128)S(1)} %get-tuple-element.22.own.first, f32[8,512]{1,0:T(8,128)S(1)} %collective-permute-done.other.second, ...), custom_call_target="tpu_custom_call" | custom-call | tf_op jit(solution)/shard_map/near/pallas_call | solution.py:690
  14.7 0.0 collective-permute-done.4.infos
  14.7 4.0 %far.1 = (f32[16,256]{1,0:T(8,128)S(1)}, f32[16,256]{1,0:T(8,128)S(1)}, f32[16,256]{1,0:T(8,128)S(1)}, f32[16,256]{1,0:T(8,128)S(1)}) custom-call(s32[2]{0:T(128)S(1)} %copy-done.4, s32[3]{0:T(128)S(1)} %pad_add_fusion.where, f32[128,128]{1,0:T(8,128)S(1)} %get-tuple-element.28.rows, f32[16,1024]{1,0:T(8,128)S(1)} %get-tuple-element.29.partial, ...), custom_call_target="tpu_custom_call" | custom-call | tf_op jit(solution)/shard_map/far/pallas_call | solution.py:690
  18.7 1.5 %collective-permute-start.5 = (f32[16,256]{1,0:T(8,128)S(1)}, f32[16,256]{1,0:T(8,128)S(1)}, u32[]{:S(2)}, u32[]{:S(2)}) collective-permute-start(f32[16,256]{1,0:T(8,128)S(1)} %get-tuple-element.30), channel_id=1, source_target_pairs={{0,8},{4,12},{8,0},{12,4},{1,9},{5,13},{9,1},{13,5},{2,10},{6,14},... | collective-permute-start | bytes 49160 | tf_op jit(solution)/shard_map/ppermute | solution.py:789
  20.2 0.1 collective-permute-start.6
  20.2 0.7 %collective-permute-start.7 = (f32[16,256]{1,0:T(8,128)S(1)}, f32[16,256]{1,0:T(8,128)S(1)}, u32[]{:S(2)}, u32[]{:S(2)}) collective-permute-start(f32[16,256]{1,0:T(8,128)S(1)} %get-tuple-element.33), channel_id=1, source_target_pairs={{0,4},{4,0},{8,12},{12,8},{1,5},{5,1},{9,13},{13,9},{2,6},{6,2},{1... | collective-permute-start | bytes 49160 | tf_op jit(solution)/shard_map/ppermute | solution.py:789
  20.9 0.1 pad_add_fusion.1.where
  21.0 0.8 %collective-permute-done.7.refs_1_ = f32[16,256]{1,0:T(8,128)S(1)} collective-permute-done((f32[16,256]{1,0:T(8,128)S(1)}, f32[16,256]{1,0:T(8,128)S(1)}, u32[]{:S(2)}, u32[]{:S(2)}) %collective-permute-start.7) | collective-permute-done | bytes 16416 | tf_op jit(solution)/shard_map/ppermute | solution.py:789
  21.7 0.0 copy-done.2
  21.7 0.0 copy-done
  21.7 0.0 copy-done.1
  21.7 1.6 %update.2 = (f32[59,1024]{1,0:T(8,128)}, f32[59,1024]{1,0:T(8,128)}, f32[59,1024]{1,0:T(8,128)}) custom-call(s32[2]{0:T(128)S(1)} %pad_add_fusion.2.where, f32[4,12]{1,0:T(4,128)S(1)} %copy-done.3, f32[59,1024]{1,0:T(8,128)S(1)} %copy-done, f32[59,1024]{1,0:T(8,128)S(1)} %copy-done.1, f32[59,1024]{1,0:T(8,128)S(1)} %copy-done.2, ...), custom_call_target="tpu_custom_call" | custom-call | tf_op jit(solution)/shard_map/update/pallas_call | solution.py:763
  23.4 0.0 collective-permute-done.5.refs_0_
  23.4 0.0 collective-permute-done.6.refs_1_
  23.4 1.6 %update.3 = (f32[59,1024]{1,0:T(8,128)}, f32[59,1024]{1,0:T(8,128)}, f32[59,1024]{1,0:T(8,128)}) custom-call(s32[2]{0:T(128)S(1)} %pad_add_fusion.1.where, f32[4,12]{1,0:T(4,128)S(1)} %copy-done.3, f32[59,1024]{1,0:T(8,128)S(1)} %copy-done, f32[59,1024]{1,0:T(8,128)S(1)} %copy-done.1, ...), custom_call_target="tpu_custom_call", output_to_operand_aliasing={{0}: (7, {}), {1}: (8, {}), {2}: (9, {})} | custom-call | tf_op jit(solution)/shard_map/update/pallas_call | solution.py:763
  (1 shorter events, 0.0 us)
Async XLA Ops:
  0.6 21.1 %copy-start.2 = (f32[59,1024]{1,0:T(8,128)S(1)}, f32[59,1024]{1,0:T(8,128)}, u32[]{:S(2)}) copy-start(f32[59,1024]{1,0:T(8,128)} %adam_v.3) | copy-start | bytes 724996
  1.8 5.0 %collective-permute-start = (f32[8,512]{1,0:T(8,128)S(1)}, f32[8,512]{1,0:T(8,128)S(1)}, u32[]{:S(2)}, u32[]{:S(2)}) collective-permute-start(f32[8,512]{1,0:T(8,128)S(1)} %get-tuple-element.22.own.first), channel_id=1, source_target_pairs={{0,1},{1,0},{2,3},{3,2},{4,5},{5,4},{6,7},{7,6},{8,9},{9,8},{10,11... | collective-permute-start | bytes 49160 | tf_op jit(solution)/shard_map/ppermute | solution.py:789
  4.9 4.8 %collective-permute-start.1 = (f32[59,256]{1,0:T(8,128)S(1)}, f32[59,256]{1,0:T(8,128)S(1)}, u32[]{:S(2)}, u32[]{:S(2)}) collective-permute-start(f32[59,256]{1,0:T(8,128)S(1)} %get-tuple-element.24), channel_id=1, source_target_pairs={{0,4},{4,0},{8,12},{12,8},{1,5},{5,1},{9,13},{13,9},{2,6},{6,2},{1... | collective-permute-start | bytes 181256 | tf_op jit(solution)/shard_map/ppermute | solution.py:789
  4.9 4.8 %collective-permute-start.2 = (f32[59,256]{1,0:T(8,128)S(1)}, f32[59,256]{1,0:T(8,128)S(1)}, u32[]{:S(2)}, u32[]{:S(2)}) collective-permute-start(f32[59,256]{1,0:T(8,128)S(1)} %get-tuple-element.25), channel_id=1, source_target_pairs={{0,8},{4,12},{8,0},{12,4},{1,9},{5,13},{9,1},{13,5},{2,10},{6,14},... | collective-permute-start | bytes 181256 | tf_op jit(solution)/shard_map/ppermute | solution.py:789
  6.4 4.1 %collective-permute-start.3 = (f32[59,256]{1,0:T(8,128)S(1)}, f32[59,256]{1,0:T(8,128)S(1)}, u32[]{:S(2)}, u32[]{:S(2)}) collective-permute-start(f32[59,256]{1,0:T(8,128)S(1)} %get-tuple-element.26), channel_id=1, source_target_pairs={{0,12},{4,8},{8,4},{12,0},{1,13},{5,9},{9,5},{13,1},{2,14},{6,10},... | collective-permute-start | bytes 181256 | tf_op jit(solution)/shard_map/ppermute | solution.py:789
  6.9 3.7 %copy-start.3 = (f32[4,12]{1,0:T(4,128)S(1)}, f32[4,12]{1,0:T(4,128)}, u32[]{:S(2)}) copy-start(f32[4,12]{1,0:T(4,128)} %cams.5) | copy-start | bytes 580
  6.9 3.7 %copy-start.4 = (s32[2]{0:T(128)S(1)}, s32[2]{0:T(128)}, u32[]{:S(2)}) copy-start(s32[2]{0:T(128)} %tile_ids.3) | copy-start | bytes 28
  6.9 14.9 %copy-start = (f32[59,1024]{1,0:T(8,128)S(1)}, f32[59,1024]{1,0:T(8,128)}, u32[]{:S(2)}) copy-start(f32[59,1024]{1,0:T(8,128)} %params.3) | copy-start | bytes 724996
  6.9 14.9 %copy-start.1 = (f32[59,1024]{1,0:T(8,128)S(1)}, f32[59,1024]{1,0:T(8,128)}, u32[]{:S(2)}) copy-start(f32[59,1024]{1,0:T(8,128)} %adam_m.3) | copy-start | bytes 724996
  6.9 7.8 %collective-permute-start.4 = (f32[16,512]{1,0:T(8,128)S(1)}, f32[16,512]{1,0:T(8,128)S(1)}, u32[]{:S(2)}, u32[]{:S(2)}) collective-permute-start(f32[16,512]{1,0:T(8,128)S(1)} %join.1), channel_id=1, source_target_pairs={{0,2},{1,3},{2,0},{3,1},{4,6},{5,7},{6,4},{7,5},{8,10},{9,11},{10,... | collective-permute-start | bytes 98312 | tf_op jit(solution)/shard_map/ppermute | solution.py:789
  18.7 4.7 %collective-permute-start.5 = (f32[16,256]{1,0:T(8,128)S(1)}, f32[16,256]{1,0:T(8,128)S(1)}, u32[]{:S(2)}, u32[]{:S(2)}) collective-permute-start(f32[16,256]{1,0:T(8,128)S(1)} %get-tuple-element.30), channel_id=1, source_target_pairs={{0,8},{4,12},{8,0},{12,4},{1,9},{5,13},{9,1},{13,5},{2,10},{6,14},... | collective-permute-start | bytes 49160 | tf_op jit(solution)/shard_map/ppermute | solution.py:789
  20.2 3.2 %collective-permute-start.6 = (f32[16,256]{1,0:T(8,128)S(1)}, f32[16,256]{1,0:T(8,128)S(1)}, u32[]{:S(2)}, u32[]{:S(2)}) collective-permute-start(f32[16,256]{1,0:T(8,128)S(1)} %get-tuple-element.31), channel_id=1, source_target_pairs={{0,12},{4,8},{8,4},{12,0},{1,13},{5,9},{9,5},{13,1},{2,14},{6,10},... | collective-permute-start | bytes 49160 | tf_op jit(solution)/shard_map/ppermute | solution.py:789
  20.2 1.5 %collective-permute-start.7 = (f32[16,256]{1,0:T(8,128)S(1)}, f32[16,256]{1,0:T(8,128)S(1)}, u32[]{:S(2)}, u32[]{:S(2)}) collective-permute-start(f32[16,256]{1,0:T(8,128)S(1)} %get-tuple-element.33), channel_id=1, source_target_pairs={{0,4},{4,0},{8,12},{12,8},{1,5},{5,1},{9,13},{13,9},{2,6},{6,2},{1... | collective-permute-start | bytes 49160 | tf_op jit(solution)/shard_map/ppermute | solution.py:789

commit v13 on v12

--- a/solution.py
+++ b/solution.py
@@ -145,20 +145,26 @@
     )
 
 
-def project_rows(feat, cam):
-    part = project_parts(feat, cam)
-    basis = sh_basis(*part["way"])
+def shade(feat, cam):
+    off = [feat(a) - cam[9 + a] for a in range(3)]
+    rlen = lax.rsqrt(off[0] * off[0] + off[1] * off[1] + off[2] * off[2])
+    basis = sh_basis(*[off[a] * rlen for a in range(3)])
     colours = []
     for k in range(3):
         total = 0.5 + sh_const[0] * feat(11 + 16 * k)
         for b in range(1, 16):
             total = total + feat(11 + 16 * k + b) * basis[b]
         colours.append(total)
+    return colours
+
+
+def project_rows(feat, cam):
+    part = project_parts(feat, cam)
     mean_x = focal_length * part["u"] + center_x
     mean_y = focal_length * part["v"] + center_y
     logit = feat(10)
     log_opacity = jnp.minimum(logit, 0.0) - jnp.log(1.0 + jnp.exp(-jnp.abs(logit)))
-    return [mean_x, mean_y, *part["conic"], log_opacity, *colours]
+    return [mean_x, mean_y, *part["conic"], log_opacity]
 
 
 def project_pull(feat, cam, grads, put):
@@ -251,21 +257,13 @@
     return tiles
 
 
-def pack_kernel(shards, pieces, where, *refs):
-    sources, refs = refs[: 3 + (pieces > 0)], refs[3 + (pieces > 0) :]
-    info, parts, refs = refs[0], refs[1 : 1 + pieces], refs[1 + pieces :]
-    shard_of, local_of, goal, place_s, sems, cut_sems = refs
+def pack_kernel(shards, where, *refs):
+    sources, (info, params, shard_of, local_of, goal, place_s, sems) = refs[:4], refs[4:]
     group = where[0]
     loads = [
         pltpu.make_async_copy(source, held, sems.at[k])
-        for k, (source, held) in enumerate(zip(sources, (shard_of, local_of, goal)))
+        for k, (source, held) in enumerate(zip(sources, (shard_of, local_of, goal, params)))
     ]
-    for d in range(pieces):
-        chunk = parts[d].shape[1]
-        first = pl.multiple_of((group ^ d) * chunk, LANES)
-        loads.append(
-            pltpu.make_async_copy(sources[3].at[:, pl.ds(first, chunk)], parts[d], cut_sems.at[d])
-        )
     for load in loads:
         load.start()
     for load in loads[:3]:
@@ -298,34 +296,77 @@
             best = jnp.max(best, axis=0, keepdims=True)
             row, at = 4 + t * rows_each + s * LANES // width, s * LANES % width
             info[row : row + 1, at : at + LANES] = best
-    for load in loads[3:]:
-        load.wait()
-
-
-def pack(group, params, target, hit_shard, hit_local, shards, aligned):
-    features, columns = params.shape
+    loads[3].wait()
+
+
+def pack(group, params, target, hit_shard, hit_local, shards):
+    columns = params.shape[1]
     tile_count, listed = hit_local.shape
     width = target.shape[1]
     rows = 4 + tile_count * (columns // width)
-    pieces = shards if aligned else 0
-    piece = jax.ShapeDtypeStruct((features, columns // shards), F32)
-    args = (hit_shard.reshape(tile_count, 1, listed), hit_local, target) + (params,) * aligned
-    out = call(
-        functools.partial(pack_kernel, shards, pieces),
+    args = (hit_shard.reshape(tile_count, 1, listed), hit_local, target, params)
+    return call(
+        functools.partial(pack_kernel, shards),
         "pack",
-        (jax.ShapeDtypeStruct((rows, width), F32),) + (piece,) * pieces,
-        [smem()] + [pl.BlockSpec(memory_space=pltpu.HBM)] * len(args),
+        (jax.ShapeDtypeStruct((rows, width), F32), jax.ShapeDtypeStruct(params.shape, F32)),
+        [smem()] + [pl.BlockSpec(memory_space=pltpu.HBM)] * 4,
         [
             pltpu.VMEM((tile_count, 1, listed), jnp.int32),
             pltpu.VMEM((tile_count, listed), jnp.int32),
             pltpu.VMEM(target.shape, F32),
             pltpu.VMEM((listed, LANES), F32),
-            pltpu.SemaphoreType.DMA((3,)),
-            pltpu.SemaphoreType.DMA((shards,)),
+            pltpu.SemaphoreType.DMA((4,)),
         ],
         (group.reshape(1),) + tuple(pltpu.with_memory_space_constraint(a, pltpu.HBM) for a in args),
+        (vmem(), any_space()),
     )
-    return out[0], list(out[1:])
+
+
+def sent_rows(views):
+    return (11 + 3 * views + 7) // 8 * 8
+
+
+def cut_kernel(pieces, where, cams, params, *refs):
+    parts, (feats, rows) = refs[:pieces], refs[pieces:]
+    views = cams.shape[0]
+    count = sent_rows(views)
+    slabs = spread_features([params], feats, params.shape[0])
+
+    def feat(f):
+        return feats[f * slabs : (f + 1) * slabs, :]
+
+    values = [feat(f) for f in range(11)]
+    for v in range(views):
+        values += shade(feat, [cams[v, i] for i in range(12)])
+    values += [jnp.zeros((slabs, LANES), F32)] * (count - len(values))
+    for f, value in enumerate(values):
+        rows[pl.ds(f, slabs, stride=count), :] = value
+    each = slabs // pieces
+    for d in range(pieces):
+        for h in range(each):
+            first = (((where[0] ^ d) % pieces) * each + h) * count
+            parts[d][:, h * LANES : (h + 1) * LANES] = rows[
+                pl.ds(pl.multiple_of(first, 8), count), :
+            ]
+
+
+def cut(group, cameras, params, pieces):
+    features, columns = params.shape
+    slabs = columns // LANES
+    count = sent_rows(cameras.shape[0])
+    return list(
+        call(
+            functools.partial(cut_kernel, pieces),
+            "cut",
+            (jax.ShapeDtypeStruct((count, columns // pieces), F32),) * pieces,
+            [smem()] * 2 + [vmem()],
+            [
+                pltpu.VMEM((features * slabs, LANES), F32),
+                pltpu.VMEM((count * slabs, LANES), F32),
+            ],
+            (group.reshape(1), cameras, params),
+        )
+    )
 
 
 def pixel_basis(pixels):
@@ -565,6 +606,9 @@
     cam = [cams[view, i] for i in range(12)]
     slabs = spread_features(parts, feats, parts[0].shape[0])
     projected = project_rows(lambda f: feats[f * slabs : (f + 1) * slabs, :], cam)
+    for k in range(3):
+        first = pl.multiple_of((11 + 3 * view + k) * slabs, slabs)
+        projected.append(feats[pl.ds(first, slabs), :])
     for f, value in enumerate(projected):
         rows[pl.ds(f, slabs, stride=ROWS), :] = value
     for f in range(len(projected), ROWS):
@@ -647,7 +691,8 @@
     rate = learn_rate / (1.0 - beta_one**adam_steps)
     unbias = 1.0 / (1.0 - beta_two**adam_steps)
     stores = []
-    for row in range(0, features, 8):
+    order = list(range(16, features, 8)) + [0, 8]
+    for row in order:
         count = min(8, features - row)
         span = slice(row, row + count)
         for s in range(slabs):
@@ -802,10 +847,11 @@
     assert team == 4
     blocks = along // team
 
-    info, parts = pack(group, params, target, hit_shard, hit_local, shards, aligned)
+    info, params = pack(group, params, target, hit_shard, hit_local, shards)
+    parts = cut(group, cameras, params, shards if aligned else 1)
     if not aligned:
         parts = [
-            lax.dynamic_slice_in_dim(params, (group ^ d) * chunk, chunk, axis=1)
+            lax.dynamic_slice_in_dim(parts[0], (group ^ d) * chunk, chunk, axis=1)
             for d in range(shards)
         ]
     parts = [swap(parts[d], "gs", d) for d in range(shards)]

time: 25.1 us -> 25 us (level)
  waiting for transfers between devices: 1.58 us -> 1 us
  Pallas kernels: 12.5 us -> 13 us
    ppermute x8, waiting for transfers between devices: 1.58 us -> 1 us  [swap(): lax.ppermute(value, axis, [(k, k ^ d) for k in range(lax.axis_size(axis))])]
    pallas_call x4 -> x5, Pallas kernels: 9.31 us -> 9.83 us  [call(): pl.pallas_call(kernel, out_shape=out_shape, in_specs=in_specs, out_specs=...]
  transfers between devices with their start and end apart: 8 -> 8, of which waited for: 2 -> 3; matrix products, arithmetic and copies ran while one was open for 1% -> 1% of each run, Pallas kernels for 23% -> 26%
where the time goes in v13:
time: 25 us; the launch traced here: 24.8 us
  Pallas kernels  13 us (52%)
  starting transfers between devices  9.85 us (39%)
  waiting for transfers between devices  1 us (4%)
  between operations  0.71 us (3%)
    ppermute x8, starting transfers between devices, swap(): lax.ppermute(value, axis, [(k, k ^ d) for k in range(lax.axis_size(axis))])  9.85 us
    pallas_call x5, Pallas kernels, call(): pl.pallas_call(kernel, out_shape=out_shape, in_specs=in_specs, out_specs=...  9.83 us
    pallas_call x2, Pallas kernels, update(): pl.pallas_call(functools.partial(update_kernel, len(packets), len(before)...  3.18 us
    ppermute x8, waiting for transfers between devices, swap(): lax.ppermute(value, axis, [(k, k ^ d) for k in range(lax.axis_size(axis))])  1 us
  transfers between devices with their start and end apart: 8, of which 3 were waited for; matrix products, arithmetic and copies ran while one was open for 1% of the time, Pallas kernels for 26%

profile of v13, /device:TPU:0, one launch (start us, length us, event | category | flops | bytes accessed | tf_op | source)
XLA Modules:
  0.0 24.8 jit_solution(13309927997659766666)
XLA Ops:
  0.6 1.0 %pack.1 = (f32[8,512]{1,0:T(8,128)S(1)}, f32[59,1024]{1,0:T(8,128)S(1)}) custom-call(s32[1]{0:T(128)} %bitcast.2.where, s32[2,1,256]{2,1,0:T(1,128)} %bitcast.4, s32[2,256]{1,0:T(2,128)} %refs_1_.1, f32[3,512]{1,0:T(4,128)} %refs_2_.1, f32[59,1024]{1,0:T(8,128)} %refs_3_.1), custom_call_target="tpu_custom_call" | custom-call | tf_op jit(solution)/shard_map/pack/pallas_call | solution.py:735
  1.7 0.0 copy-start.2
  1.7 3.1 %collective-permute-start = (f32[8,512]{1,0:T(8,128)S(1)}, f32[8,512]{1,0:T(8,128)S(1)}, u32[]{:S(2)}, u32[]{:S(2)}) collective-permute-start(f32[8,512]{1,0:T(8,128)S(1)} %get-tuple-element.23.own.first), channel_id=1, source_target_pairs={{0,1},{1,0},{2,3},{3,2},{4,5},{5,4},{6,7},{7,6},{8,9},{9,8},{10,11... | collective-permute-start | bytes 49160 | tf_op jit(solution)/shard_map/ppermute | solution.py:834
  4.8 0.0 copy-done.2
  4.8 0.0 copy-start.3
  4.8 0.0 copy-start.1
  4.8 0.7 %cut.1 = (f32[24,256]{1,0:T(8,128)S(1)}, f32[24,256]{1,0:T(8,128)S(1)}, f32[24,256]{1,0:T(8,128)S(1)}, f32[24,256]{1,0:T(8,128)S(1)}) custom-call(s32[1]{0:T(128)} %bitcast.2.where, f32[4,12]{1,0:T(4,128)S(1)} %copy-done.2, f32[59,1024]{1,0:T(8,128)S(1)} %get-tuple-element.24.params), custom_call_target="tpu_custom_call" | custom-call | tf_op jit(solution)/shard_map/cut/pallas_call | solution.py:735
  5.5 0.0 copy-start
  5.5 0.1 collective-permute-start.1
  5.6 1.6 %collective-permute-start.2 = (f32[24,256]{1,0:T(8,128)S(1)}, f32[24,256]{1,0:T(8,128)S(1)}, u32[]{:S(2)}, u32[]{:S(2)}) collective-permute-start(f32[24,256]{1,0:T(8,128)S(1)} %get-tuple-element.27), channel_id=1, source_target_pairs={{0,8},{4,12},{8,0},{12,4},{1,9},{5,13},{9,1},{13,5},{2,10},{6,14},... | collective-permute-start | bytes 73736 | tf_op jit(solution)/shard_map/ppermute | solution.py:834
  7.2 0.3 %collective-permute-start.3 = (f32[24,256]{1,0:T(8,128)S(1)}, f32[24,256]{1,0:T(8,128)S(1)}, u32[]{:S(2)}, u32[]{:S(2)}) collective-permute-start(f32[24,256]{1,0:T(8,128)S(1)} %get-tuple-element.28), channel_id=1, source_target_pairs={{0,12},{4,8},{8,4},{12,0},{1,13},{5,9},{9,5},{13,1},{2,14},{6,10},... | collective-permute-start | bytes 73736 | tf_op jit(solution)/shard_map/ppermute | solution.py:834
  7.5 0.1 pad_add_fusion.2.where
  7.5 0.0 collective-permute-done.other.second
  7.5 2.6 %collective-permute-start.4 = (f32[16,512]{1,0:T(8,128)S(1)}, f32[16,512]{1,0:T(8,128)S(1)}, u32[]{:S(2)}, u32[]{:S(2)}) collective-permute-start(f32[16,512]{1,0:T(8,128)S(1)} %join.1), channel_id=1, source_target_pairs={{0,2},{1,3},{2,0},{3,1},{4,6},{5,7},{6,4},{7,5},{8,10},{9,11},{10,... | collective-permute-start | bytes 98312 | tf_op jit(solution)/shard_map/ppermute | solution.py:834
  10.2 0.1 pad_add_fusion.where
  10.2 0.0 collective-permute-done.1.refs_1_
  10.2 0.0 collective-permute-done.2.refs_2_
  10.2 0.2 collective-permute-done.3.refs_3_
  10.4 0.0 copy-done.3
  10.4 4.1 %near.1 = (f32[3,512]{1,0:T(4,128)}, f32[128,128]{1,0:T(8,128)S(1)}, f32[16,1024]{1,0:T(8,128)S(1)}) custom-call(s32[2]{0:T(128)S(1)} %copy-done.3, f32[4,12]{1,0:T(4,128)S(1)} %copy-done.2, s32[3]{0:T(128)S(1)} %pad_add_fusion.where, f32[8,512]{1,0:T(8,128)S(1)} %get-tuple-element.23.own.first, f32[8,512]{1,0:T(8,128)S(1)} %collective-permute-done.other.second, ...), custom_call_target="tpu_custom_call" | custom-call | tf_op jit(solution)/shard_map/near/pallas_call | solution.py:735
  14.5 0.0 collective-permute-done.4.infos
  14.5 4.0 %far.1 = (f32[16,256]{1,0:T(8,128)S(1)}, f32[16,256]{1,0:T(8,128)S(1)}, f32[16,256]{1,0:T(8,128)S(1)}, f32[16,256]{1,0:T(8,128)S(1)}) custom-call(s32[2]{0:T(128)S(1)} %copy-done.3, s32[3]{0:T(128)S(1)} %pad_add_fusion.where, f32[128,128]{1,0:T(8,128)S(1)} %get-tuple-element.30.rows, f32[16,1024]{1,0:T(8,128)S(1)} %get-tuple-element.31.partial, ...), custom_call_target="tpu_custom_call" | custom-call | tf_op jit(solution)/shard_map/far/pallas_call | solution.py:735
  18.5 1.4 %collective-permute-start.5 = (f32[16,256]{1,0:T(8,128)S(1)}, f32[16,256]{1,0:T(8,128)S(1)}, u32[]{:S(2)}, u32[]{:S(2)}) collective-permute-start(f32[16,256]{1,0:T(8,128)S(1)} %get-tuple-element.32), channel_id=1, source_target_pairs={{0,8},{4,12},{8,0},{12,4},{1,9},{5,13},{9,1},{13,5},{2,10},{6,14},... | collective-permute-start | bytes 49160 | tf_op jit(solution)/shard_map/ppermute | solution.py:834
  19.9 0.2 collective-permute-start.6
  20.1 0.6 %collective-permute-start.7 = (f32[16,256]{1,0:T(8,128)S(1)}, f32[16,256]{1,0:T(8,128)S(1)}, u32[]{:S(2)}, u32[]{:S(2)}) collective-permute-start(f32[16,256]{1,0:T(8,128)S(1)} %get-tuple-element.35), channel_id=1, source_target_pairs={{0,4},{4,0},{8,12},{12,8},{1,5},{5,1},{9,13},{13,9},{2,6},{6,2},{1... | collective-permute-start | bytes 49160 | tf_op jit(solution)/shard_map/ppermute | solution.py:834
  20.7 0.1 pad_add_fusion.1.where
  20.8 0.8 %collective-permute-done.7.refs_1_ = f32[16,256]{1,0:T(8,128)S(1)} collective-permute-done((f32[16,256]{1,0:T(8,128)S(1)}, f32[16,256]{1,0:T(8,128)S(1)}, u32[]{:S(2)}, u32[]{:S(2)}) %collective-permute-start.7) | collective-permute-done | bytes 16416 | tf_op jit(solution)/shard_map/ppermute | solution.py:834
  21.6 0.0 copy-done.1
  21.6 0.0 copy-done
  21.6 1.6 %update.2 = (f32[59,1024]{1,0:T(8,128)}, f32[59,1024]{1,0:T(8,128)}, f32[59,1024]{1,0:T(8,128)}) custom-call(s32[2]{0:T(128)S(1)} %pad_add_fusion.2.where, f32[4,12]{1,0:T(4,128)S(1)} %copy-done.2, f32[59,1024]{1,0:T(8,128)S(1)} %get-tuple-element.24.params, f32[59,1024]{1,0:T(8,128)S(1)} %copy-done, f32[59,1024]{1,0:T(8,128)S(1)} %copy-done.1, ...), custom_call_target="tpu_custom_call" | custom-call | tf_op jit(solution)/shard_map/update/pallas_call | solution.py:808
  23.2 0.0 collective-permute-done.5.refs_0_
  23.2 0.1 collective-permute-done.6.refs_1_
  23.2 1.6 %update.3 = (f32[59,1024]{1,0:T(8,128)}, f32[59,1024]{1,0:T(8,128)}, f32[59,1024]{1,0:T(8,128)}) custom-call(s32[2]{0:T(128)S(1)} %pad_add_fusion.1.where, f32[4,12]{1,0:T(4,128)S(1)} %copy-done.2, f32[59,1024]{1,0:T(8,128)S(1)} %get-tuple-element.24.params, f32[59,1024]{1,0:T(8,128)S(1)} %copy-done, ...), custom_call_target="tpu_custom_call", output_to_operand_aliasing={{0}: (7, {}), {1}: (8, {}), {2}: (9, {})} | custom-call | tf_op jit(solution)/shard_map/update/pallas_call | solution.py:808
  (1 shorter events, 0.0 us)
Async XLA Ops:
  1.7 3.1 %copy-start.2 = (f32[4,12]{1,0:T(4,128)S(1)}, f32[4,12]{1,0:T(4,128)}, u32[]{:S(2)}) copy-start(f32[4,12]{1,0:T(4,128)} %cams.7) | copy-start | bytes 580
  1.7 5.8 %collective-permute-start = (f32[8,512]{1,0:T(8,128)S(1)}, f32[8,512]{1,0:T(8,128)S(1)}, u32[]{:S(2)}, u32[]{:S(2)}) collective-permute-start(f32[8,512]{1,0:T(8,128)S(1)} %get-tuple-element.23.own.first), channel_id=1, source_target_pairs={{0,1},{1,0},{2,3},{3,2},{4,5},{5,4},{6,7},{7,6},{8,9},{9,8},{10,11... | collective-permute-start | bytes 49160 | tf_op jit(solution)/shard_map/ppermute | solution.py:834
  4.8 5.6 %copy-start.3 = (s32[2]{0:T(128)S(1)}, s32[2]{0:T(128)}, u32[]{:S(2)}) copy-start(s32[2]{0:T(128)} %tile_ids.3) | copy-start | bytes 28
  4.8 16.8 %copy-start.1 = (f32[59,1024]{1,0:T(8,128)S(1)}, f32[59,1024]{1,0:T(8,128)}, u32[]{:S(2)}) copy-start(f32[59,1024]{1,0:T(8,128)} %adam_v.3) | copy-start | bytes 724996
  5.5 16.0 %copy-start = (f32[59,1024]{1,0:T(8,128)S(1)}, f32[59,1024]{1,0:T(8,128)}, u32[]{:S(2)}) copy-start(f32[59,1024]{1,0:T(8,128)} %adam_m.3) | copy-start | bytes 724996
  5.5 4.7 %collective-permute-start.1 = (f32[24,256]{1,0:T(8,128)S(1)}, f32[24,256]{1,0:T(8,128)S(1)}, u32[]{:S(2)}, u32[]{:S(2)}) collective-permute-start(f32[24,256]{1,0:T(8,128)S(1)} %get-tuple-element.26), channel_id=1, source_target_pairs={{0,4},{4,0},{8,12},{12,8},{1,5},{5,1},{9,13},{13,9},{2,6},{6,2},{1... | collective-permute-start | bytes 73736 | tf_op jit(solution)/shard_map/ppermute | solution.py:834
  5.6 4.6 %collective-permute-start.2 = (f32[24,256]{1,0:T(8,128)S(1)}, f32[24,256]{1,0:T(8,128)S(1)}, u32[]{:S(2)}, u32[]{:S(2)}) collective-permute-start(f32[24,256]{1,0:T(8,128)S(1)} %get-tuple-element.27), channel_id=1, source_target_pairs={{0,8},{4,12},{8,0},{12,4},{1,9},{5,13},{9,1},{13,5},{2,10},{6,14},... | collective-permute-start | bytes 73736 | tf_op jit(solution)/shard_map/ppermute | solution.py:834
  7.2 3.3 %collective-permute-start.3 = (f32[24,256]{1,0:T(8,128)S(1)}, f32[24,256]{1,0:T(8,128)S(1)}, u32[]{:S(2)}, u32[]{:S(2)}) collective-permute-start(f32[24,256]{1,0:T(8,128)S(1)} %get-tuple-element.28), channel_id=1, source_target_pairs={{0,12},{4,8},{8,4},{12,0},{1,13},{5,9},{9,5},{13,1},{2,14},{6,10},... | collective-permute-start | bytes 73736 | tf_op jit(solution)/shard_map/ppermute | solution.py:834
  7.5 7.0 %collective-permute-start.4 = (f32[16,512]{1,0:T(8,128)S(1)}, f32[16,512]{1,0:T(8,128)S(1)}, u32[]{:S(2)}, u32[]{:S(2)}) collective-permute-start(f32[16,512]{1,0:T(8,128)S(1)} %join.1), channel_id=1, source_target_pairs={{0,2},{1,3},{2,0},{3,1},{4,6},{5,7},{6,4},{7,5},{8,10},{9,11},{10,... | collective-permute-start | bytes 98312 | tf_op jit(solution)/shard_map/ppermute | solution.py:834
  18.5 4.7 %collective-permute-start.5 = (f32[16,256]{1,0:T(8,128)S(1)}, f32[16,256]{1,0:T(8,128)S(1)}, u32[]{:S(2)}, u32[]{:S(2)}) collective-permute-start(f32[16,256]{1,0:T(8,128)S(1)} %get-tuple-element.32), channel_id=1, source_target_pairs={{0,8},{4,12},{8,0},{12,4},{1,9},{5,13},{9,1},{13,5},{2,10},{6,14},... | collective-permute-start | bytes 49160 | tf_op jit(solution)/shard_map/ppermute | solution.py:834
  19.9 3.3 %collective-permute-start.6 = (f32[16,256]{1,0:T(8,128)S(1)}, f32[16,256]{1,0:T(8,128)S(1)}, u32[]{:S(2)}, u32[]{:S(2)}) collective-permute-start(f32[16,256]{1,0:T(8,128)S(1)} %get-tuple-element.33), channel_id=1, source_target_pairs={{0,12},{4,8},{8,4},{12,0},{1,13},{5,9},{9,5},{13,1},{2,14},{6,10},... | collective-permute-start | bytes 49160 | tf_op jit(solution)/shard_map/ppermute | solution.py:834
  20.1 1.5 %collective-permute-start.7 = (f32[16,256]{1,0:T(8,128)S(1)}, f32[16,256]{1,0:T(8,128)S(1)}, u32[]{:S(2)}, u32[]{:S(2)}) collective-permute-start(f32[16,256]{1,0:T(8,128)S(1)} %get-tuple-element.35), channel_id=1, source_target_pairs={{0,4},{4,0},{8,12},{12,8},{1,5},{5,1},{9,13},{13,9},{2,6},{6,2},{1... | collective-permute-start | bytes 49160 | tf_op jit(solution)/shard_map/ppermute | solution.py:834

commit v14 on v13

--- a/solution.py
+++ b/solution.py
@@ -369,6 +369,10 @@
     )
 
 
+def lane_gather(source, lane):
+    return jnp.take_along_axis(source, lane, axis=1, mode="promise_in_bounds")
+
+
 def pixel_basis(pixels):
     pixel = lax.broadcasted_iota(jnp.int32, (8, pixels), 1)
     row = lax.broadcasted_iota(jnp.int32, (8, pixels), 0)
@@ -382,8 +386,10 @@
 
 
 def composite(tiles, first_group, me, rows, info_s, rendered, work):
-    alpha_s, weight_s, pull_s, push_s, weight_2, coef_s, colour_s, error_s, mix_s, index_s, acc_s = work
-    groups, tile_count, _, listed = acc_s.shape
+    alpha_s, weight_s, pull_s, push_s, weight_2, entry_s, coef_s, colour_s, sums_s, index_s, acc_s, ninth_s = work
+    groups = info_s.shape[0]
+    listed = acc_s.shape[0] * LANES
+    tile_count = info_s.shape[2] // listed
     pixels = info_s.shape[2] // tile_count
     parts = pixels // LANES
     halves = listed // LANES
@@ -399,11 +405,9 @@
     def of_place(place):
         return pl.ds(place * LIST_STEP, spans, stride=SPAN_STEP)
 
-    def lane_gather(source, lane):
-        return jnp.take_along_axis(source, lane, axis=1, mode="promise_in_bounds")
-
     basis = pixel_basis(pixels)
     basis_3 = jnp.concatenate([basis, basis, basis], axis=0).astype(BF16)
+    row_of = lax.broadcasted_iota(jnp.int32, (8, listed), 0)
 
     entries = []
     for n in range(tiles_here):
@@ -422,6 +426,8 @@
                 )
             found.append(value)
         entries.append(jnp.concatenate(found, axis=1))
+        for h in range(halves):
+            entry_s[h, 8 * n : 8 * n + 8, :] = found[h]
     at = index_s[...]
     lane, slab = at & (LANES - 1), at >> 7
     ninth = lane_gather(rows[8:16, :], lane)
@@ -430,42 +436,47 @@
             slab == s, lane_gather(rows[s * ROWS + 8 : s * ROWS + 16, :], lane), ninth
         )
 
-    means = []
-    colour_s[...] = jnp.zeros(colour_s.shape, F32)
-    for n in range(tiles_here):
-        g, t = n // tile_count, n % tile_count
-        entry = entries[n]
-        slot = (me ^ (first_group + g)) * tile_count + t
-        mean_u = entry[0:1] - (((first_col + slot % 4) * side).astype(F32) + 0.5 * side)
-        mean_v = entry[1:2] - (((first_row + slot // 4) * side).astype(F32) + 0.5 * side)
-        quad_a, quad_b, quad_c = -0.5 * entry[2:3], -entry[3:4], -0.5 * entry[4:5]
-        means.append((mean_u, mean_v, quad_a, quad_b, quad_c))
-        slope_u = 2.0 * quad_a * mean_u + quad_b * mean_v
-        slope_v = 2.0 * quad_c * mean_v + quad_b * mean_u
-        level = 0.5 * (slope_u * mean_u + slope_v * mean_v) + entry[5:6]
-        zero = jnp.zeros_like(level)
-        coef = jnp.concatenate(
-            [level, -slope_u, -slope_v, quad_a, quad_b, quad_c, zero, zero], axis=0
-        )
-        here = slice(n * listed, (n + 1) * listed)
-        for part in range(3):
-            term = coef.astype(BF16).astype(F32)
-            coef_s[part * 8 : part * 8 + 8, here] = term
-            coef = coef - term
-        last = [ninth[n * halves + h : n * halves + h + 1] for h in range(halves)]
-        colours = jnp.concatenate([entry[6:8], jnp.concatenate(last, axis=1)], axis=0)
-        high = colours.astype(BF16).astype(F32)
-        colour_s[n * ROWS : n * ROWS + 3, here] = high
-        colour_s[n * ROWS + 3 : n * ROWS + 6, here] = colours - high
-        colour_s[n * ROWS + 6 : n * ROWS + 9, here] = high
-
+    def of_lists(ref, f):
+        at = pl.ds(f, tiles_here, stride=8)
+        return jnp.concatenate([ref[h, at, :] for h in range(halves)], axis=1)
+
+    tile_of = lax.broadcasted_iota(jnp.int32, (tiles_here, listed), 0)
+    slot = (me ^ (first_group + tile_of // tile_count)) * tile_count + tile_of % tile_count
+    mean_u = of_lists(entry_s, 2) - (((first_col + slot % 4) * side).astype(F32) + 0.5 * side)
+    mean_v = of_lists(entry_s, 3) - (((first_row + slot // 4) * side).astype(F32) + 0.5 * side)
+    quad_a = -0.5 * of_lists(entry_s, 4)
+    quad_b = -of_lists(entry_s, 5)
+    quad_c = -0.5 * of_lists(entry_s, 6)
+    slope_u = 2.0 * quad_a * mean_u + quad_b * mean_v
+    slope_v = 2.0 * quad_c * mean_v + quad_b * mean_u
+    level = 0.5 * (slope_u * mean_u + slope_v * mean_v) + of_lists(entry_s, 7)
+    for f, value in enumerate((level, -slope_u, -slope_v, quad_a, quad_b, quad_c)):
+        for n in range(tiles_here):
+            coef_s[f : f + 1, n * listed : (n + 1) * listed] = value[n : n + 1]
+    coef_s[6:8, :] = jnp.zeros((2, tiles_here * listed), F32)
+    coef = coef_s[...]
+    terms = []
+    for _ in range(3):
+        terms.append(coef.astype(BF16).astype(F32))
+        coef = coef - terms[-1]
     down = ((0,), (0,))
-    power = matmul(coef_s[...].astype(BF16), basis_3, down)
+    power = matmul(jnp.concatenate(terms, axis=0).astype(BF16), basis_3, down)
     for n in range(tiles_here):
         for part in range(parts):
             alpha_s[of_span(n * parts + part), :] = jnp.exp(
                 power[n * listed : (n + 1) * listed, part * LANES : (part + 1) * LANES]
             )
+    colour_s[...] = jnp.zeros(colour_s.shape, F32)
+    hues = []
+    for n in range(tiles_here):
+        last = jnp.concatenate([ninth[n * halves + h : n * halves + h + 1] for h in range(halves)], axis=1)
+        colours = jnp.where(row_of < 2, entries[n], jnp.where(row_of == 2, last, 0.0))
+        high = colours.astype(BF16).astype(F32)
+        low = colours - high
+        here = slice(n * listed, (n + 1) * listed)
+        for at, value in ((0, high), (8, low), (16, high)):
+            colour_s[24 * n + at : 24 * n + at + 8, here] = value
+        hues.append(jnp.concatenate([high, low], axis=0).astype(BF16))
 
     unroll, quad = 32, 4
     steps = listed // unroll
@@ -487,8 +498,7 @@
     nought = jnp.zeros((spans, LANES), F32)
     lax.fori_loop(0, steps, forward, nought + 1.0)
 
-    error_s[...] = jnp.zeros(error_s.shape, F32)
-    mix_s[...] = jnp.zeros(mix_s.shape, F32)
+    errors, wrongs, moments = [], [], []
     for n in range(tiles_here):
         g, t = n // tile_count, n % tile_count
         for part in range(parts):
@@ -497,22 +507,28 @@
                 weight_s[of_span(n * parts + part), :]
             )
         at = slice(n * pixels, (n + 1) * pixels)
-        colours = colour_s[n * ROWS : (n + 1) * ROWS, n * listed : (n + 1) * listed].astype(BF16)
-        image = matmul(colours, weight_2[:listed, at])
-        image = image[0:3] + image[3:6] + matmul(colours, weight_2[listed:, at])[0:3]
+        image = matmul(hues[n], weight_2[:listed, at])
+        image = image[0:8] + image[8:16] + matmul(hues[n], weight_2[listed:, at])[0:8]
         here = slice(t * pixels, (t + 1) * pixels)
         if rendered is not None and g == 0:
-            rendered[:, here] = image
-        error = image - info_s[g, 0:3, here]
+            rendered[:, here] = image[0:3]
+        error = image - info_s[g, 0:8, here]
         high = error.astype(BF16).astype(F32)
         low = error - high
-        error_s[n * ROWS : n * ROWS + 3, :] = high
-        error_s[n * ROWS + 3 : n * ROWS + 6, :] = high
-        error_s[n * ROWS + 6 : n * ROWS + 9, :] = low
-        mix_s[0, n * ROWS : n * ROWS + 8, at] = basis
-        mix_s[1, n * ROWS + 6 : n * ROWS + 9, at] = high
-        mix_s[1, n * ROWS + 9 : n * ROWS + 12, at] = low
-    pull = matmul(colour_s[...].astype(BF16), error_s[...].astype(BF16), down)
+        errors += [high, high, low]
+
+        def block(values, first, total):
+            rows_in = sum(value.shape[0] for value in values)
+            return jnp.concatenate(
+                [jnp.zeros((first, pixels), F32)] * (first > 0)
+                + values
+                + [jnp.zeros((total - first - rows_in, pixels), F32)],
+                axis=0,
+            ).astype(BF16)
+
+        wrongs.append(block([high, low], 16 * n, LANES))
+        moments.append(block([basis], 16 * tiles_here + 8 * n, LANES))
+    pull = matmul(colour_s[...].astype(BF16), jnp.concatenate(errors, axis=0).astype(BF16), down)
     for n in range(tiles_here):
         for part in range(parts):
             pull_s[of_span(n * parts + part), :] = pull[
@@ -540,40 +556,43 @@
 
     across = ((1,), (1,))
     high, low = split(jnp.concatenate([push_s[of_span(span), :] for span in range(spans)], axis=1))
-    sums = matmul(jnp.concatenate([high, low], axis=0), mix_s[0].astype(BF16), across)
-    sums = sums + matmul(weight_2[...], mix_s[1].astype(BF16), across)
+    sums = matmul(weight_2[...], jnp.concatenate(wrongs, axis=1), across)
+    sums = sums + matmul(
+        jnp.concatenate([high, low], axis=0), jnp.concatenate(moments, axis=1), across
+    )
     sums = (sums[:listed] + sums[listed:]).T
+    for h in range(halves):
+        sums_s[h] = sums[:, h * LANES : (h + 1) * LANES]
+    m_00, m_10, m_01, m_20, m_11, m_02 = [
+        of_lists(sums_s, 16 * tiles_here + m) for m in range(6)
+    ]
+    n_10 = m_10 - mean_u * m_00
+    n_01 = m_01 - mean_v * m_00
     for n in range(tiles_here):
-        g, t = n // tile_count, n % tile_count
-        mean_u, mean_v, quad_a, quad_b, quad_c = means[n]
-        m_00, m_10, m_01, m_20, m_11, m_02 = [
-            sums[n * ROWS + m : n * ROWS + m + 1] for m in range(6)
-        ]
-        n_10 = m_10 - mean_u * m_00
-        n_01 = m_01 - mean_v * m_00
-        acc_s[g, t, 0:1, :] = -(2.0 * quad_a * n_10 + quad_b * n_01)
-        acc_s[g, t, 1:2, :] = -(2.0 * quad_c * n_01 + quad_b * n_10)
-        acc_s[g, t, 2:3, :] = -0.5 * (m_20 - mean_u * (m_10 + n_10))
-        acc_s[g, t, 3:4, :] = -(m_11 - mean_u * m_01 - mean_v * n_10)
-        acc_s[g, t, 4:5, :] = -0.5 * (m_02 - mean_v * (m_01 + n_01))
-        acc_s[g, t, 5:6, :] = m_00
-        at = n * ROWS + 6
-        grads = sums[at : at + 3] + sums[at + 3 : at + 6]
-        acc_s[g, t, 6:8, :] = grads[0:2]
         for h in range(halves):
+            grads = sums_s[h, 16 * n : 16 * n + 8, :] + sums_s[h, 16 * n + 8 : 16 * n + 16, :]
+            acc_s[h, 8 * n : 8 * n + 8, :] = grads
             row = n * halves + h
-            acc_s[0, 0, 8 + row : 9 + row, :LANES] = grads[2:3, h * LANES : (h + 1) * LANES]
-
-
-def pool_sum(slab, info_s, acc_s):
-    groups, tile_count, _, listed = acc_s.shape
+            ninth_s[row : row + 1, :] = grads[2:3, :]
+    for f, value in (
+        (2, -(2.0 * quad_a * n_10 + quad_b * n_01)),
+        (3, -(2.0 * quad_c * n_01 + quad_b * n_10)),
+        (4, -0.5 * (m_20 - mean_u * (m_10 + n_10))),
+        (5, -(m_11 - mean_u * m_01 - mean_v * n_10)),
+        (6, -0.5 * (m_02 - mean_v * (m_01 + n_01))),
+        (7, m_00),
+    ):
+        for h in range(halves):
+            acc_s[h, pl.ds(f, tiles_here, stride=8), :] = value[:, h * LANES : (h + 1) * LANES]
+
+
+def pool_sum(slab, info_s, acc_s, ninth_s):
+    groups, _, width = info_s.shape
+    listed = acc_s.shape[0] * LANES
+    tile_count = width // listed
     halves = listed // LANES
-    width = info_s.shape[2]
     rows_each = (info_s.shape[1] - 4) // tile_count
     row_of = lax.broadcasted_iota(jnp.int32, (8, LANES), 0)
-
-    def lane_gather(source, lane):
-        return jnp.take_along_axis(source, lane, axis=1, mode="promise_in_bounds")
 
     totals, every = [], None
     for g in range(groups):
@@ -586,10 +605,10 @@
             every = at if every is None else jnp.where(row_of >= n * halves, at, every)
             lane, half = at & (LANES - 1), at >> 7
             for h in range(halves):
-                here = lane_gather(acc_s[g, t, 0:8, h * LANES : (h + 1) * LANES], lane)
+                here = lane_gather(acc_s[h, 8 * n : 8 * n + 8, :], lane)
                 total = total + jnp.where(half == h, here, 0.0)
         totals.append(total)
-    here = lane_gather(acc_s[0, 0, 8:16, :LANES], every & (LANES - 1))
+    here = lane_gather(ninth_s[...], every & (LANES - 1))
     ninth = jnp.where(every >> 7 == row_of % halves, here, 0.0)
     return totals[0] + totals[1], jnp.sum(ninth, axis=0, keepdims=True)
 
@@ -606,24 +625,23 @@
     cam = [cams[view, i] for i in range(12)]
     slabs = spread_features(parts, feats, parts[0].shape[0])
     projected = project_rows(lambda f: feats[f * slabs : (f + 1) * slabs, :], cam)
+    colours = []
     for k in range(3):
         first = pl.multiple_of((11 + 3 * view + k) * slabs, slabs)
-        projected.append(feats[pl.ds(first, slabs), :])
-    for f, value in enumerate(projected):
+        colours.append(feats[pl.ds(first, slabs), :])
+    for f, value in enumerate(colours[:2] + projected + [colours[2]] * 8):
         rows[pl.ds(f, slabs, stride=ROWS), :] = value
-    for f in range(len(projected), ROWS):
-        rows[pl.ds(f, slabs, stride=ROWS), :] = projected[8]
     info_s[0] = own[...]
     info_s[1] = other[...]
     composite(block_start(tile_ids[0]), 0, where[0], rows, info_s, rendered, work)
     for s in range(slabs):
         at = slice(s * LANES, (s + 1) * LANES)
-        partial[0:8, at], partial[8:9, at] = pool_sum(s, info_s, work[-1])
+        partial[0:8, at], partial[8:9, at] = pool_sum(s, info_s, *work[-2:])
 
 
 def far_kernel(blocks, tile_ids, where, rows, partial, infos, *refs):
-    *packets, info_s = refs[: len(refs) - 11]
-    work = refs[len(refs) - 11 :]
+    *packets, info_s = refs[: len(refs) - 12]
+    work = refs[len(refs) - 12 :]
     half = infos.shape[0] // 2
     info_s[0] = infos[:half, :]
     info_s[1] = infos[half:, :]
@@ -633,7 +651,7 @@
     lane_of = lax.broadcasted_iota(jnp.int32, (8, LANES), 1)
     chunk = packets[0].shape[1]
     for s in range(rows.shape[0] // ROWS):
-        total, ninth = pool_sum(s, info_s, work[-1])
+        total, ninth = pool_sum(s, info_s, *work[-2:])
         total = total + partial[0:8, s * LANES : (s + 1) * LANES]
         ninth = ninth + partial[8:9, s * LANES : (s + 1) * LANES]
         if blocks == 1:
@@ -687,7 +705,9 @@
             feats[pl.ds(row * slabs + s, count, stride=slabs), :] = params[
                 row : row + count, column(s)
             ]
-    project_pull(lambda f: feats[f * slabs : (f + 1) * slabs, :], cam, pulled[:9], put)
+    project_pull(
+        lambda f: feats[f * slabs : (f + 1) * slabs, :], cam, pulled[2:8] + pulled[:2] + pulled[8:9], put
+    )
     rate = learn_rate / (1.0 - beta_one**adam_steps)
     unbias = 1.0 / (1.0 - beta_two**adam_steps)
     stores = []
@@ -746,15 +766,16 @@
 def work_shapes(tile_count, pixels, listed):
     tiles = 2 * tile_count
     spans = tiles * pixels // LANES
-    assert (spans - 1) * SPAN_STEP < LIST_STEP and tiles * listed // LANES == 8
+    assert (spans - 1) * SPAN_STEP < LIST_STEP and tiles * listed // LANES == 8 and tiles == 4
     return [pltpu.VMEM((listed * LIST_STEP, LANES), F32)] * 4 + [
         pltpu.VMEM((2 * listed, spans * LANES), BF16),
-        pltpu.VMEM((24, tiles * listed), F32),
-        pltpu.VMEM((tiles * ROWS, tiles * listed), F32),
-        pltpu.VMEM((tiles * ROWS, pixels), F32),
-        pltpu.VMEM((2, LANES, spans * LANES), F32),
+        pltpu.VMEM((listed // LANES, 8 * tiles, LANES), F32),
+        pltpu.VMEM((8, tiles * listed), F32),
+        pltpu.VMEM((24 * tiles, tiles * listed), F32),
+        pltpu.VMEM((listed // LANES, LANES, LANES), F32),
         pltpu.VMEM((8, LANES), jnp.int32),
-        pltpu.VMEM((2, tile_count, ROWS, listed), F32),
+        pltpu.VMEM((listed // LANES, 8 * tiles, LANES), F32),
+        pltpu.VMEM((8, LANES), F32),
     ]
 
 

time: 25 us -> 24.7 us (0.988)
  transfers between devices with their start and end apart: 8 -> 8, of which waited for: 3 -> 3; matrix products, arithmetic and copies ran while one was open for 1% -> 1% of each run, Pallas kernels for 26% -> 25%
where the time goes in v14:
time: 24.7 us; the launch traced here: 24.6 us
  Pallas kernels  12.8 us (52%)
  starting transfers between devices  9.85 us (40%)
  waiting for transfers between devices  0.99 us (4%)
  between operations  0.72 us (3%)
    ppermute x8, starting transfers between devices, swap(): lax.ppermute(value, axis, [(k, k ^ d) for k in range(lax.axis_size(axis))])  9.85 us
    pallas_call x5, Pallas kernels, call(): pl.pallas_call(kernel, out_shape=out_shape, in_specs=in_specs, out_specs=...  9.59 us
    pallas_call x2, Pallas kernels, update(): pl.pallas_call(functools.partial(update_kernel, len(packets), len(before)...  3.18 us
    ppermute x8, waiting for transfers between devices, swap(): lax.ppermute(value, axis, [(k, k ^ d) for k in range(lax.axis_size(axis))])  0.99 us
  transfers between devices with their start and end apart: 8, of which 3 were waited for; matrix products, arithmetic and copies ran while one was open for 1% of the time, Pallas kernels for 25%

profile of v14, /device:TPU:0, one launch (start us, length us, event | category | flops | bytes accessed | tf_op | source)
XLA Modules:
  0.0 24.6 jit_solution(17830056127262706270)
XLA Ops:
  0.6 1.0 %pack.1 = (f32[8,512]{1,0:T(8,128)S(1)}, f32[59,1024]{1,0:T(8,128)S(1)}) custom-call(s32[1]{0:T(128)} %bitcast.2.where, s32[2,1,256]{2,1,0:T(1,128)} %bitcast.4, s32[2,256]{1,0:T(2,128)} %refs_1_.1, f32[3,512]{1,0:T(4,128)} %refs_2_.1, f32[59,1024]{1,0:T(8,128)} %refs_3_.1), custom_call_target="tpu_custom_call" | custom-call | tf_op jit(solution)/shard_map/pack/pallas_call | solution.py:755
  1.7 0.0 copy-start.2
  1.7 3.1 %collective-permute-start = (f32[8,512]{1,0:T(8,128)S(1)}, f32[8,512]{1,0:T(8,128)S(1)}, u32[]{:S(2)}, u32[]{:S(2)}) collective-permute-start(f32[8,512]{1,0:T(8,128)S(1)} %get-tuple-element.23.own.first), channel_id=1, source_target_pairs={{0,1},{1,0},{2,3},{3,2},{4,5},{5,4},{6,7},{7,6},{8,9},{9,8},{10,11... | collective-permute-start | bytes 49160 | tf_op jit(solution)/shard_map/ppermute | solution.py:855
  4.8 0.0 copy-done.2
  4.8 0.0 copy-start.3
  4.8 0.0 copy-start.1
  4.8 0.7 %cut.1 = (f32[24,256]{1,0:T(8,128)S(1)}, f32[24,256]{1,0:T(8,128)S(1)}, f32[24,256]{1,0:T(8,128)S(1)}, f32[24,256]{1,0:T(8,128)S(1)}) custom-call(s32[1]{0:T(128)} %bitcast.2.where, f32[4,12]{1,0:T(4,128)S(1)} %copy-done.2, f32[59,1024]{1,0:T(8,128)S(1)} %get-tuple-element.24.params), custom_call_target="tpu_custom_call" | custom-call | tf_op jit(solution)/shard_map/cut/pallas_call | solution.py:755
  5.5 0.0 copy-start
  5.5 0.1 collective-permute-start.1
  5.6 1.6 %collective-permute-start.2 = (f32[24,256]{1,0:T(8,128)S(1)}, f32[24,256]{1,0:T(8,128)S(1)}, u32[]{:S(2)}, u32[]{:S(2)}) collective-permute-start(f32[24,256]{1,0:T(8,128)S(1)} %get-tuple-element.27), channel_id=1, source_target_pairs={{0,8},{4,12},{8,0},{12,4},{1,9},{5,13},{9,1},{13,5},{2,10},{6,14},... | collective-permute-start | bytes 73736 | tf_op jit(solution)/shard_map/ppermute | solution.py:855
  7.2 0.3 %collective-permute-start.3 = (f32[24,256]{1,0:T(8,128)S(1)}, f32[24,256]{1,0:T(8,128)S(1)}, u32[]{:S(2)}, u32[]{:S(2)}) collective-permute-start(f32[24,256]{1,0:T(8,128)S(1)} %get-tuple-element.28), channel_id=1, source_target_pairs={{0,12},{4,8},{8,4},{12,0},{1,13},{5,9},{9,5},{13,1},{2,14},{6,10},... | collective-permute-start | bytes 73736 | tf_op jit(solution)/shard_map/ppermute | solution.py:855
  7.5 0.1 pad_add_fusion.2.where
  7.5 0.0 collective-permute-done.other.second
  7.5 2.6 %collective-permute-start.4 = (f32[16,512]{1,0:T(8,128)S(1)}, f32[16,512]{1,0:T(8,128)S(1)}, u32[]{:S(2)}, u32[]{:S(2)}) collective-permute-start(f32[16,512]{1,0:T(8,128)S(1)} %join.1), channel_id=1, source_target_pairs={{0,2},{1,3},{2,0},{3,1},{4,6},{5,7},{6,4},{7,5},{8,10},{9,11},{10,... | collective-permute-start | bytes 98312 | tf_op jit(solution)/shard_map/ppermute | solution.py:855
  10.2 0.1 pad_add_fusion.where
  10.2 0.0 collective-permute-done.1.refs_1_
  10.2 0.0 collective-permute-done.2.refs_2_
  10.2 0.2 collective-permute-done.3.refs_3_
  10.4 0.0 copy-done.3
  10.4 4.0 %near.1 = (f32[3,512]{1,0:T(4,128)}, f32[128,128]{1,0:T(8,128)S(1)}, f32[16,1024]{1,0:T(8,128)S(1)}) custom-call(s32[2]{0:T(128)S(1)} %copy-done.3, f32[4,12]{1,0:T(4,128)S(1)} %copy-done.2, s32[3]{0:T(128)S(1)} %pad_add_fusion.where, f32[8,512]{1,0:T(8,128)S(1)} %get-tuple-element.23.own.first, f32[8,512]{1,0:T(8,128)S(1)} %collective-permute-done.other.second, ...), custom_call_target="tpu_custom_call" | custom-call | tf_op jit(solution)/shard_map/near/pallas_call | solution.py:755
  14.4 0.0 collective-permute-done.4.infos
  14.4 3.9 %far.1 = (f32[16,256]{1,0:T(8,128)S(1)}, f32[16,256]{1,0:T(8,128)S(1)}, f32[16,256]{1,0:T(8,128)S(1)}, f32[16,256]{1,0:T(8,128)S(1)}) custom-call(s32[2]{0:T(128)S(1)} %copy-done.3, s32[3]{0:T(128)S(1)} %pad_add_fusion.where, f32[128,128]{1,0:T(8,128)S(1)} %get-tuple-element.30.rows, f32[16,1024]{1,0:T(8,128)S(1)} %get-tuple-element.31.partial, ...), custom_call_target="tpu_custom_call" | custom-call | tf_op jit(solution)/shard_map/far/pallas_call | solution.py:755
  18.3 1.4 %collective-permute-start.5 = (f32[16,256]{1,0:T(8,128)S(1)}, f32[16,256]{1,0:T(8,128)S(1)}, u32[]{:S(2)}, u32[]{:S(2)}) collective-permute-start(f32[16,256]{1,0:T(8,128)S(1)} %get-tuple-element.32), channel_id=1, source_target_pairs={{0,8},{4,12},{8,0},{12,4},{1,9},{5,13},{9,1},{13,5},{2,10},{6,14},... | collective-permute-start | bytes 49160 | tf_op jit(solution)/shard_map/ppermute | solution.py:855
  19.7 0.2 collective-permute-start.6
  19.9 0.6 %collective-permute-start.7 = (f32[16,256]{1,0:T(8,128)S(1)}, f32[16,256]{1,0:T(8,128)S(1)}, u32[]{:S(2)}, u32[]{:S(2)}) collective-permute-start(f32[16,256]{1,0:T(8,128)S(1)} %get-tuple-element.35), channel_id=1, source_target_pairs={{0,4},{4,0},{8,12},{12,8},{1,5},{5,1},{9,13},{13,9},{2,6},{6,2},{1... | collective-permute-start | bytes 49160 | tf_op jit(solution)/shard_map/ppermute | solution.py:855
  20.5 0.1 pad_add_fusion.1.where
  20.6 0.8 %collective-permute-done.7.refs_1_ = f32[16,256]{1,0:T(8,128)S(1)} collective-permute-done((f32[16,256]{1,0:T(8,128)S(1)}, f32[16,256]{1,0:T(8,128)S(1)}, u32[]{:S(2)}, u32[]{:S(2)}) %collective-permute-start.7) | collective-permute-done | bytes 16416 | tf_op jit(solution)/shard_map/ppermute | solution.py:855
  21.3 0.0 copy-done.1
  21.3 0.0 copy-done
  21.3 1.6 %update.2 = (f32[59,1024]{1,0:T(8,128)}, f32[59,1024]{1,0:T(8,128)}, f32[59,1024]{1,0:T(8,128)}) custom-call(s32[2]{0:T(128)S(1)} %pad_add_fusion.2.where, f32[4,12]{1,0:T(4,128)S(1)} %copy-done.2, f32[59,1024]{1,0:T(8,128)S(1)} %get-tuple-element.24.params, f32[59,1024]{1,0:T(8,128)S(1)} %copy-done, f32[59,1024]{1,0:T(8,128)S(1)} %copy-done.1, ...), custom_call_target="tpu_custom_call" | custom-call | tf_op jit(solution)/shard_map/update/pallas_call | solution.py:829
  22.9 0.0 collective-permute-done.5.refs_0_
  22.9 0.1 collective-permute-done.6.refs_1_
  23.0 1.6 %update.3 = (f32[59,1024]{1,0:T(8,128)}, f32[59,1024]{1,0:T(8,128)}, f32[59,1024]{1,0:T(8,128)}) custom-call(s32[2]{0:T(128)S(1)} %pad_add_fusion.1.where, f32[4,12]{1,0:T(4,128)S(1)} %copy-done.2, f32[59,1024]{1,0:T(8,128)S(1)} %get-tuple-element.24.params, f32[59,1024]{1,0:T(8,128)S(1)} %copy-done, ...), custom_call_target="tpu_custom_call", output_to_operand_aliasing={{0}: (7, {}), {1}: (8, {}), {2}: (9, {})} | custom-call | tf_op jit(solution)/shard_map/update/pallas_call | solution.py:829
  (1 shorter events, 0.0 us)
Async XLA Ops:
  1.7 3.1 %copy-start.2 = (f32[4,12]{1,0:T(4,128)S(1)}, f32[4,12]{1,0:T(4,128)}, u32[]{:S(2)}) copy-start(f32[4,12]{1,0:T(4,128)} %cams.7) | copy-start | bytes 580
  1.7 5.8 %collective-permute-start = (f32[8,512]{1,0:T(8,128)S(1)}, f32[8,512]{1,0:T(8,128)S(1)}, u32[]{:S(2)}, u32[]{:S(2)}) collective-permute-start(f32[8,512]{1,0:T(8,128)S(1)} %get-tuple-element.23.own.first), channel_id=1, source_target_pairs={{0,1},{1,0},{2,3},{3,2},{4,5},{5,4},{6,7},{7,6},{8,9},{9,8},{10,11... | collective-permute-start | bytes 49160 | tf_op jit(solution)/shard_map/ppermute | solution.py:855
  4.8 5.6 %copy-start.3 = (s32[2]{0:T(128)S(1)}, s32[2]{0:T(128)}, u32[]{:S(2)}) copy-start(s32[2]{0:T(128)} %tile_ids.3) | copy-start | bytes 28
  4.8 16.5 %copy-start.1 = (f32[59,1024]{1,0:T(8,128)S(1)}, f32[59,1024]{1,0:T(8,128)}, u32[]{:S(2)}) copy-start(f32[59,1024]{1,0:T(8,128)} %adam_v.3) | copy-start | bytes 724996
  5.5 15.8 %copy-start = (f32[59,1024]{1,0:T(8,128)S(1)}, f32[59,1024]{1,0:T(8,128)}, u32[]{:S(2)}) copy-start(f32[59,1024]{1,0:T(8,128)} %adam_m.3) | copy-start | bytes 724996
  5.5 4.7 %collective-permute-start.1 = (f32[24,256]{1,0:T(8,128)S(1)}, f32[24,256]{1,0:T(8,128)S(1)}, u32[]{:S(2)}, u32[]{:S(2)}) collective-permute-start(f32[24,256]{1,0:T(8,128)S(1)} %get-tuple-element.26), channel_id=1, source_target_pairs={{0,4},{4,0},{8,12},{12,8},{1,5},{5,1},{9,13},{13,9},{2,6},{6,2},{1... | collective-permute-start | bytes 73736 | tf_op jit(solution)/shard_map/ppermute | solution.py:855
  5.6 4.6 %collective-permute-start.2 = (f32[24,256]{1,0:T(8,128)S(1)}, f32[24,256]{1,0:T(8,128)S(1)}, u32[]{:S(2)}, u32[]{:S(2)}) collective-permute-start(f32[24,256]{1,0:T(8,128)S(1)} %get-tuple-element.27), channel_id=1, source_target_pairs={{0,8},{4,12},{8,0},{12,4},{1,9},{5,13},{9,1},{13,5},{2,10},{6,14},... | collective-permute-start | bytes 73736 | tf_op jit(solution)/shard_map/ppermute | solution.py:855
  7.2 3.3 %collective-permute-start.3 = (f32[24,256]{1,0:T(8,128)S(1)}, f32[24,256]{1,0:T(8,128)S(1)}, u32[]{:S(2)}, u32[]{:S(2)}) collective-permute-start(f32[24,256]{1,0:T(8,128)S(1)} %get-tuple-element.28), channel_id=1, source_target_pairs={{0,12},{4,8},{8,4},{12,0},{1,13},{5,9},{9,5},{13,1},{2,14},{6,10},... | collective-permute-start | bytes 73736 | tf_op jit(solution)/shard_map/ppermute | solution.py:855
  7.5 6.8 %collective-permute-start.4 = (f32[16,512]{1,0:T(8,128)S(1)}, f32[16,512]{1,0:T(8,128)S(1)}, u32[]{:S(2)}, u32[]{:S(2)}) collective-permute-start(f32[16,512]{1,0:T(8,128)S(1)} %join.1), channel_id=1, source_target_pairs={{0,2},{1,3},{2,0},{3,1},{4,6},{5,7},{6,4},{7,5},{8,10},{9,11},{10,... | collective-permute-start | bytes 98312 | tf_op jit(solution)/shard_map/ppermute | solution.py:855
  18.3 4.7 %collective-permute-start.5 = (f32[16,256]{1,0:T(8,128)S(1)}, f32[16,256]{1,0:T(8,128)S(1)}, u32[]{:S(2)}, u32[]{:S(2)}) collective-permute-start(f32[16,256]{1,0:T(8,128)S(1)} %get-tuple-element.32), channel_id=1, source_target_pairs={{0,8},{4,12},{8,0},{12,4},{1,9},{5,13},{9,1},{13,5},{2,10},{6,14},... | collective-permute-start | bytes 49160 | tf_op jit(solution)/shard_map/ppermute | solution.py:855
  19.7 3.3 %collective-permute-start.6 = (f32[16,256]{1,0:T(8,128)S(1)}, f32[16,256]{1,0:T(8,128)S(1)}, u32[]{:S(2)}, u32[]{:S(2)}) collective-permute-start(f32[16,256]{1,0:T(8,128)S(1)} %get-tuple-element.33), channel_id=1, source_target_pairs={{0,12},{4,8},{8,4},{12,0},{1,13},{5,9},{9,5},{13,1},{2,14},{6,10},... | collective-permute-start | bytes 49160 | tf_op jit(solution)/shard_map/ppermute | solution.py:855
  19.9 1.5 %collective-permute-start.7 = (f32[16,256]{1,0:T(8,128)S(1)}, f32[16,256]{1,0:T(8,128)S(1)}, u32[]{:S(2)}, u32[]{:S(2)}) collective-permute-start(f32[16,256]{1,0:T(8,128)S(1)} %get-tuple-element.35), channel_id=1, source_target_pairs={{0,4},{4,0},{8,12},{12,8},{1,5},{5,1},{9,13},{13,9},{2,6},{6,2},{1... | collective-permute-start | bytes 49160 | tf_op jit(solution)/shard_map/ppermute | solution.py:855

commit v15 on v14

--- a/solution.py
+++ b/solution.py
@@ -13,7 +13,7 @@
 BLOCK_TILES = 8
 LANES = 128
 ROWS = 16
-SPAN_STEP, LIST_STEP = 3, 25
+LIST_STEP = 9
 F32 = jnp.float32
 BF16 = jnp.bfloat16
 
@@ -400,10 +400,10 @@
     first_col, first_row = tiles
 
     def of_span(span):
-        return pl.ds(span * SPAN_STEP, listed, stride=LIST_STEP)
+        return pl.ds(span, listed, stride=LIST_STEP)
 
     def of_place(place):
-        return pl.ds(place * LIST_STEP, spans, stride=SPAN_STEP)
+        return pl.ds(place * LIST_STEP, spans)
 
     basis = pixel_basis(pixels)
     basis_3 = jnp.concatenate([basis, basis, basis], axis=0).astype(BF16)
@@ -766,7 +766,7 @@
 def work_shapes(tile_count, pixels, listed):
     tiles = 2 * tile_count
     spans = tiles * pixels // LANES
-    assert (spans - 1) * SPAN_STEP < LIST_STEP and tiles * listed // LANES == 8 and tiles == 4
+    assert spans < LIST_STEP and tiles * listed // LANES == 8 and tiles == 4
     return [pltpu.VMEM((listed * LIST_STEP, LANES), F32)] * 4 + [
         pltpu.VMEM((2 * listed, spans * LANES), BF16),
         pltpu.VMEM((listed // LANES, 8 * tiles, LANES), F32),

time: 24.7 us -> 24.7 us (level)
  transfers between devices with their start and end apart: 8 -> 8, of which waited for: 3 -> 3; matrix products, arithmetic and copies ran while one was open for 1% -> 1% of each run, Pallas kernels for 25% -> 26%
where the time goes in v15:
time: 24.7 us; the launch traced here: 24.6 us
  Pallas kernels  12.8 us (52%)
  starting transfers between devices  9.85 us (40%)
  waiting for transfers between devices  0.99 us (4%)
  between operations  0.72 us (3%)
    ppermute x8, starting transfers between devices, swap(): lax.ppermute(value, axis, [(k, k ^ d) for k in range(lax.axis_size(axis))])  9.85 us
    pallas_call x5, Pallas kernels, call(): pl.pallas_call(kernel, out_shape=out_shape, in_specs=in_specs, out_specs=...  9.59 us
    pallas_call x2, Pallas kernels, update(): pl.pallas_call(functools.partial(update_kernel, len(packets), len(before)...  3.18 us
    ppermute x8, waiting for transfers between devices, swap(): lax.ppermute(value, axis, [(k, k ^ d) for k in range(lax.axis_size(axis))])  0.99 us
  transfers between devices with their start and end apart: 8, of which 3 were waited for; matrix products, arithmetic and copies ran while one was open for 1% of the time, Pallas kernels for 26%

profile of v15, /device:TPU:0, one launch (start us, length us, event | category | flops | bytes accessed | tf_op | source)
XLA Modules:
  0.0 24.6 jit_solution(8468966280883839224)
XLA Ops:
  0.6 1.0 %pack.1 = (f32[8,512]{1,0:T(8,128)S(1)}, f32[59,1024]{1,0:T(8,128)S(1)}) custom-call(s32[1]{0:T(128)} %bitcast.2.where, s32[2,1,256]{2,1,0:T(1,128)} %bitcast.4, s32[2,256]{1,0:T(2,128)} %refs_1_.1, f32[3,512]{1,0:T(4,128)} %refs_2_.1, f32[59,1024]{1,0:T(8,128)} %refs_3_.1), custom_call_target="tpu_custom_call" | custom-call | tf_op jit(solution)/shard_map/pack/pallas_call | solution.py:755
  1.7 0.0 copy-start.2
  1.7 3.1 %collective-permute-start = (f32[8,512]{1,0:T(8,128)S(1)}, f32[8,512]{1,0:T(8,128)S(1)}, u32[]{:S(2)}, u32[]{:S(2)}) collective-permute-start(f32[8,512]{1,0:T(8,128)S(1)} %get-tuple-element.23.own.first), channel_id=1, source_target_pairs={{0,1},{1,0},{2,3},{3,2},{4,5},{5,4},{6,7},{7,6},{8,9},{9,8},{10,11... | collective-permute-start | bytes 49160 | tf_op jit(solution)/shard_map/ppermute | solution.py:855
  4.8 0.0 copy-done.2
  4.8 0.0 copy-start.3
  4.8 0.0 copy-start.1
  4.8 0.7 %cut.1 = (f32[24,256]{1,0:T(8,128)S(1)}, f32[24,256]{1,0:T(8,128)S(1)}, f32[24,256]{1,0:T(8,128)S(1)}, f32[24,256]{1,0:T(8,128)S(1)}) custom-call(s32[1]{0:T(128)} %bitcast.2.where, f32[4,12]{1,0:T(4,128)S(1)} %copy-done.2, f32[59,1024]{1,0:T(8,128)S(1)} %get-tuple-element.24.params), custom_call_target="tpu_custom_call" | custom-call | tf_op jit(solution)/shard_map/cut/pallas_call | solution.py:755
  5.5 0.0 copy-start
  5.5 0.1 collective-permute-start.1
  5.6 1.6 %collective-permute-start.2 = (f32[24,256]{1,0:T(8,128)S(1)}, f32[24,256]{1,0:T(8,128)S(1)}, u32[]{:S(2)}, u32[]{:S(2)}) collective-permute-start(f32[24,256]{1,0:T(8,128)S(1)} %get-tuple-element.27), channel_id=1, source_target_pairs={{0,8},{4,12},{8,0},{12,4},{1,9},{5,13},{9,1},{13,5},{2,10},{6,14},... | collective-permute-start | bytes 73736 | tf_op jit(solution)/shard_map/ppermute | solution.py:855
  7.2 0.3 %collective-permute-start.3 = (f32[24,256]{1,0:T(8,128)S(1)}, f32[24,256]{1,0:T(8,128)S(1)}, u32[]{:S(2)}, u32[]{:S(2)}) collective-permute-start(f32[24,256]{1,0:T(8,128)S(1)} %get-tuple-element.28), channel_id=1, source_target_pairs={{0,12},{4,8},{8,4},{12,0},{1,13},{5,9},{9,5},{13,1},{2,14},{6,10},... | collective-permute-start | bytes 73736 | tf_op jit(solution)/shard_map/ppermute | solution.py:855
  7.5 0.1 pad_add_fusion.2.where
  7.5 0.0 collective-permute-done.other.second
  7.5 2.6 %collective-permute-start.4 = (f32[16,512]{1,0:T(8,128)S(1)}, f32[16,512]{1,0:T(8,128)S(1)}, u32[]{:S(2)}, u32[]{:S(2)}) collective-permute-start(f32[16,512]{1,0:T(8,128)S(1)} %join.1), channel_id=1, source_target_pairs={{0,2},{1,3},{2,0},{3,1},{4,6},{5,7},{6,4},{7,5},{8,10},{9,11},{10,... | collective-permute-start | bytes 98312 | tf_op jit(solution)/shard_map/ppermute | solution.py:855
  10.2 0.1 pad_add_fusion.where
  10.2 0.0 collective-permute-done.1.refs_1_
  10.2 0.0 collective-permute-done.2.refs_2_
  10.2 0.2 collective-permute-done.3.refs_3_
  10.4 0.0 copy-done.3
  10.4 4.0 %near.1 = (f32[3,512]{1,0:T(4,128)}, f32[128,128]{1,0:T(8,128)S(1)}, f32[16,1024]{1,0:T(8,128)S(1)}) custom-call(s32[2]{0:T(128)S(1)} %copy-done.3, f32[4,12]{1,0:T(4,128)S(1)} %copy-done.2, s32[3]{0:T(128)S(1)} %pad_add_fusion.where, f32[8,512]{1,0:T(8,128)S(1)} %get-tuple-element.23.own.first, f32[8,512]{1,0:T(8,128)S(1)} %collective-permute-done.other.second, ...), custom_call_target="tpu_custom_call" | custom-call | tf_op jit(solution)/shard_map/near/pallas_call | solution.py:755
  14.4 0.0 collective-permute-done.4.infos
  14.4 3.9 %far.1 = (f32[16,256]{1,0:T(8,128)S(1)}, f32[16,256]{1,0:T(8,128)S(1)}, f32[16,256]{1,0:T(8,128)S(1)}, f32[16,256]{1,0:T(8,128)S(1)}) custom-call(s32[2]{0:T(128)S(1)} %copy-done.3, s32[3]{0:T(128)S(1)} %pad_add_fusion.where, f32[128,128]{1,0:T(8,128)S(1)} %get-tuple-element.30.rows, f32[16,1024]{1,0:T(8,128)S(1)} %get-tuple-element.31.partial, ...), custom_call_target="tpu_custom_call" | custom-call | tf_op jit(solution)/shard_map/far/pallas_call | solution.py:755
  18.3 1.4 %collective-permute-start.5 = (f32[16,256]{1,0:T(8,128)S(1)}, f32[16,256]{1,0:T(8,128)S(1)}, u32[]{:S(2)}, u32[]{:S(2)}) collective-permute-start(f32[16,256]{1,0:T(8,128)S(1)} %get-tuple-element.32), channel_id=1, source_target_pairs={{0,8},{4,12},{8,0},{12,4},{1,9},{5,13},{9,1},{13,5},{2,10},{6,14},... | collective-permute-start | bytes 49160 | tf_op jit(solution)/shard_map/ppermute | solution.py:855
  19.7 0.2 collective-permute-start.6
  19.8 0.6 %collective-permute-start.7 = (f32[16,256]{1,0:T(8,128)S(1)}, f32[16,256]{1,0:T(8,128)S(1)}, u32[]{:S(2)}, u32[]{:S(2)}) collective-permute-start(f32[16,256]{1,0:T(8,128)S(1)} %get-tuple-element.35), channel_id=1, source_target_pairs={{0,4},{4,0},{8,12},{12,8},{1,5},{5,1},{9,13},{13,9},{2,6},{6,2},{1... | collective-permute-start | bytes 49160 | tf_op jit(solution)/shard_map/ppermute | solution.py:855
  20.5 0.1 pad_add_fusion.1.where
  20.5 0.8 %collective-permute-done.7.refs_1_ = f32[16,256]{1,0:T(8,128)S(1)} collective-permute-done((f32[16,256]{1,0:T(8,128)S(1)}, f32[16,256]{1,0:T(8,128)S(1)}, u32[]{:S(2)}, u32[]{:S(2)}) %collective-permute-start.7) | collective-permute-done | bytes 16416 | tf_op jit(solution)/shard_map/ppermute | solution.py:855
  21.3 0.0 copy-done.1
  21.3 0.0 copy-done
  21.3 1.6 %update.2 = (f32[59,1024]{1,0:T(8,128)}, f32[59,1024]{1,0:T(8,128)}, f32[59,1024]{1,0:T(8,128)}) custom-call(s32[2]{0:T(128)S(1)} %pad_add_fusion.2.where, f32[4,12]{1,0:T(4,128)S(1)} %copy-done.2, f32[59,1024]{1,0:T(8,128)S(1)} %get-tuple-element.24.params, f32[59,1024]{1,0:T(8,128)S(1)} %copy-done, f32[59,1024]{1,0:T(8,128)S(1)} %copy-done.1, ...), custom_call_target="tpu_custom_call" | custom-call | tf_op jit(solution)/shard_map/update/pallas_call | solution.py:829
  22.9 0.0 collective-permute-done.5.refs_0_
  22.9 0.1 collective-permute-done.6.refs_1_
  23.0 1.6 %update.3 = (f32[59,1024]{1,0:T(8,128)}, f32[59,1024]{1,0:T(8,128)}, f32[59,1024]{1,0:T(8,128)}) custom-call(s32[2]{0:T(128)S(1)} %pad_add_fusion.1.where, f32[4,12]{1,0:T(4,128)S(1)} %copy-done.2, f32[59,1024]{1,0:T(8,128)S(1)} %get-tuple-element.24.params, f32[59,1024]{1,0:T(8,128)S(1)} %copy-done, ...), custom_call_target="tpu_custom_call", output_to_operand_aliasing={{0}: (7, {}), {1}: (8, {}), {2}: (9, {})} | custom-call | tf_op jit(solution)/shard_map/update/pallas_call | solution.py:829
  (1 shorter events, 0.0 us)
Async XLA Ops:
  1.7 3.1 %copy-start.2 = (f32[4,12]{1,0:T(4,128)S(1)}, f32[4,12]{1,0:T(4,128)}, u32[]{:S(2)}) copy-start(f32[4,12]{1,0:T(4,128)} %cams.7) | copy-start | bytes 580
  1.7 5.8 %collective-permute-start = (f32[8,512]{1,0:T(8,128)S(1)}, f32[8,512]{1,0:T(8,128)S(1)}, u32[]{:S(2)}, u32[]{:S(2)}) collective-permute-start(f32[8,512]{1,0:T(8,128)S(1)} %get-tuple-element.23.own.first), channel_id=1, source_target_pairs={{0,1},{1,0},{2,3},{3,2},{4,5},{5,4},{6,7},{7,6},{8,9},{9,8},{10,11... | collective-permute-start | bytes 49160 | tf_op jit(solution)/shard_map/ppermute | solution.py:855
  4.8 5.6 %copy-start.3 = (s32[2]{0:T(128)S(1)}, s32[2]{0:T(128)}, u32[]{:S(2)}) copy-start(s32[2]{0:T(128)} %tile_ids.3) | copy-start | bytes 28
  4.8 16.5 %copy-start.1 = (f32[59,1024]{1,0:T(8,128)S(1)}, f32[59,1024]{1,0:T(8,128)}, u32[]{:S(2)}) copy-start(f32[59,1024]{1,0:T(8,128)} %adam_v.3) | copy-start | bytes 724996
  5.5 15.8 %copy-start = (f32[59,1024]{1,0:T(8,128)S(1)}, f32[59,1024]{1,0:T(8,128)}, u32[]{:S(2)}) copy-start(f32[59,1024]{1,0:T(8,128)} %adam_m.3) | copy-start | bytes 724996
  5.5 4.7 %collective-permute-start.1 = (f32[24,256]{1,0:T(8,128)S(1)}, f32[24,256]{1,0:T(8,128)S(1)}, u32[]{:S(2)}, u32[]{:S(2)}) collective-permute-start(f32[24,256]{1,0:T(8,128)S(1)} %get-tuple-element.26), channel_id=1, source_target_pairs={{0,4},{4,0},{8,12},{12,8},{1,5},{5,1},{9,13},{13,9},{2,6},{6,2},{1... | collective-permute-start | bytes 73736 | tf_op jit(solution)/shard_map/ppermute | solution.py:855
  5.6 4.6 %collective-permute-start.2 = (f32[24,256]{1,0:T(8,128)S(1)}, f32[24,256]{1,0:T(8,128)S(1)}, u32[]{:S(2)}, u32[]{:S(2)}) collective-permute-start(f32[24,256]{1,0:T(8,128)S(1)} %get-tuple-element.27), channel_id=1, source_target_pairs={{0,8},{4,12},{8,0},{12,4},{1,9},{5,13},{9,1},{13,5},{2,10},{6,14},... | collective-permute-start | bytes 73736 | tf_op jit(solution)/shard_map/ppermute | solution.py:855
  7.2 3.3 %collective-permute-start.3 = (f32[24,256]{1,0:T(8,128)S(1)}, f32[24,256]{1,0:T(8,128)S(1)}, u32[]{:S(2)}, u32[]{:S(2)}) collective-permute-start(f32[24,256]{1,0:T(8,128)S(1)} %get-tuple-element.28), channel_id=1, source_target_pairs={{0,12},{4,8},{8,4},{12,0},{1,13},{5,9},{9,5},{13,1},{2,14},{6,10},... | collective-permute-start | bytes 73736 | tf_op jit(solution)/shard_map/ppermute | solution.py:855
  7.5 6.8 %collective-permute-start.4 = (f32[16,512]{1,0:T(8,128)S(1)}, f32[16,512]{1,0:T(8,128)S(1)}, u32[]{:S(2)}, u32[]{:S(2)}) collective-permute-start(f32[16,512]{1,0:T(8,128)S(1)} %join.1), channel_id=1, source_target_pairs={{0,2},{1,3},{2,0},{3,1},{4,6},{5,7},{6,4},{7,5},{8,10},{9,11},{10,... | collective-permute-start | bytes 98312 | tf_op jit(solution)/shard_map/ppermute | solution.py:855
  18.3 4.7 %collective-permute-start.5 = (f32[16,256]{1,0:T(8,128)S(1)}, f32[16,256]{1,0:T(8,128)S(1)}, u32[]{:S(2)}, u32[]{:S(2)}) collective-permute-start(f32[16,256]{1,0:T(8,128)S(1)} %get-tuple-element.32), channel_id=1, source_target_pairs={{0,8},{4,12},{8,0},{12,4},{1,9},{5,13},{9,1},{13,5},{2,10},{6,14},... | collective-permute-start | bytes 49160 | tf_op jit(solution)/shard_map/ppermute | solution.py:855
  19.7 3.3 %collective-permute-start.6 = (f32[16,256]{1,0:T(8,128)S(1)}, f32[16,256]{1,0:T(8,128)S(1)}, u32[]{:S(2)}, u32[]{:S(2)}) collective-permute-start(f32[16,256]{1,0:T(8,128)S(1)} %get-tuple-element.33), channel_id=1, source_target_pairs={{0,12},{4,8},{8,4},{12,0},{1,13},{5,9},{9,5},{13,1},{2,14},{6,10},... | collective-permute-start | bytes 49160 | tf_op jit(solution)/shard_map/ppermute | solution.py:855
  19.8 1.5 %collective-permute-start.7 = (f32[16,256]{1,0:T(8,128)S(1)}, f32[16,256]{1,0:T(8,128)S(1)}, u32[]{:S(2)}, u32[]{:S(2)}) collective-permute-start(f32[16,256]{1,0:T(8,128)S(1)} %get-tuple-element.35), channel_id=1, source_target_pairs={{0,4},{4,0},{8,12},{12,8},{1,5},{5,1},{9,13},{13,9},{2,6},{6,2},{1... | collective-permute-start | bytes 49160 | tf_op jit(solution)/shard_map/ppermute | solution.py:855

commit v16 on v15

--- a/solution.py
+++ b/solution.py
@@ -498,7 +498,7 @@
     nought = jnp.zeros((spans, LANES), F32)
     lax.fori_loop(0, steps, forward, nought + 1.0)
 
-    errors, wrongs, moments = [], [], []
+    errors = []
     for n in range(tiles_here):
         g, t = n // tile_count, n % tile_count
         for part in range(parts):
@@ -517,17 +517,14 @@
         low = error - high
         errors += [high, high, low]
 
-        def block(values, first, total):
-            rows_in = sum(value.shape[0] for value in values)
-            return jnp.concatenate(
-                [jnp.zeros((first, pixels), F32)] * (first > 0)
-                + values
-                + [jnp.zeros((total - first - rows_in, pixels), F32)],
-                axis=0,
-            ).astype(BF16)
-
-        wrongs.append(block([high, low], 16 * n, LANES))
-        moments.append(block([basis], 16 * tiles_here + 8 * n, LANES))
+        hue = jnp.concatenate([high, low], axis=0).astype(BF16)
+        across = ((1,), (1,))
+        grads = matmul(hue, weight_2[:listed, at], across) + matmul(hue, weight_2[listed:, at], across)
+        grads = grads[0:8] + grads[8:16]
+        for h in range(halves):
+            acc_s[h, 8 * n : 8 * n + 8, :] = grads[:, h * LANES : (h + 1) * LANES]
+            row = n * halves + h
+            ninth_s[row : row + 1, :] = grads[2:3, h * LANES : (h + 1) * LANES]
     pull = matmul(colour_s[...].astype(BF16), jnp.concatenate(errors, axis=0).astype(BF16), down)
     for n in range(tiles_here):
         for part in range(parts):
@@ -554,26 +551,19 @@
 
     lax.fori_loop(0, steps, backward, nought)
 
-    across = ((1,), (1,))
-    high, low = split(jnp.concatenate([push_s[of_span(span), :] for span in range(spans)], axis=1))
-    sums = matmul(weight_2[...], jnp.concatenate(wrongs, axis=1), across)
-    sums = sums + matmul(
-        jnp.concatenate([high, low], axis=0), jnp.concatenate(moments, axis=1), across
-    )
-    sums = (sums[:listed] + sums[listed:]).T
-    for h in range(halves):
-        sums_s[h] = sums[:, h * LANES : (h + 1) * LANES]
+    basis = basis.astype(BF16)
+    for n in range(tiles_here):
+        high, low = split(
+            jnp.concatenate([push_s[of_span(n * parts + part), :] for part in range(parts)], axis=1)
+        )
+        moments = matmul(basis, high, across) + matmul(basis, low, across)
+        for h in range(halves):
+            sums_s[h, 8 * n : 8 * n + 8, :] = moments[:, h * LANES : (h + 1) * LANES]
     m_00, m_10, m_01, m_20, m_11, m_02 = [
-        of_lists(sums_s, 16 * tiles_here + m) for m in range(6)
+        of_lists(sums_s, m) for m in range(6)
     ]
     n_10 = m_10 - mean_u * m_00
     n_01 = m_01 - mean_v * m_00
-    for n in range(tiles_here):
-        for h in range(halves):
-            grads = sums_s[h, 16 * n : 16 * n + 8, :] + sums_s[h, 16 * n + 8 : 16 * n + 16, :]
-            acc_s[h, 8 * n : 8 * n + 8, :] = grads
-            row = n * halves + h
-            ninth_s[row : row + 1, :] = grads[2:3, :]
     for f, value in (
         (2, -(2.0 * quad_a * n_10 + quad_b * n_01)),
         (3, -(2.0 * quad_c * n_01 + quad_b * n_10)),
@@ -772,7 +762,7 @@
         pltpu.VMEM((listed // LANES, 8 * tiles, LANES), F32),
         pltpu.VMEM((8, tiles * listed), F32),
         pltpu.VMEM((24 * tiles, tiles * listed), F32),
-        pltpu.VMEM((listed // LANES, LANES, LANES), F32),
+        pltpu.VMEM((listed // LANES, 8 * tiles, LANES), F32),
         pltpu.VMEM((8, LANES), jnp.int32),
         pltpu.VMEM((listed // LANES, 8 * tiles, LANES), F32),
         pltpu.VMEM((8, LANES), F32),

time: 24.7 us -> 24.5 us (level)
  Pallas kernels: 12.8 us -> 12.5 us
    pallas_call x5, Pallas kernels: 9.59 us -> 9.33 us  [call(): pl.pallas_call(kernel, out_shape=out_shape, in_specs=in_specs, out_specs=...]
  transfers between devices with their start and end apart: 8 -> 8, of which waited for: 3 -> 3; matrix products, arithmetic and copies ran while one was open for 1% -> 1% of each run, Pallas kernels for 26% -> 25%
where the time goes in v16:
time: 24.5 us; the launch traced here: 24.3 us
  Pallas kernels  12.5 us (51%)
  starting transfers between devices  9.85 us (40%)
  waiting for transfers between devices  0.99 us (4%)
  between operations  0.71 us (3%)
    ppermute x8, starting transfers between devices, swap(): lax.ppermute(value, axis, [(k, k ^ d) for k in range(lax.axis_size(axis))])  9.85 us
    pallas_call x5, Pallas kernels, call(): pl.pallas_call(kernel, out_shape=out_shape, in_specs=in_specs, out_specs=...  9.33 us
    pallas_call x2, Pallas kernels, update(): pl.pallas_call(functools.partial(update_kernel, len(packets), len(before)...  3.18 us
    ppermute x8, waiting for transfers between devices, swap(): lax.ppermute(value, axis, [(k, k ^ d) for k in range(lax.axis_size(axis))])  0.99 us
  transfers between devices with their start and end apart: 8, of which 3 were waited for; matrix products, arithmetic and copies ran while one was open for 1% of the time, Pallas kernels for 25%

profile of v16, /device:TPU:0, one launch (start us, length us, event | category | flops | bytes accessed | tf_op | source)
XLA Modules:
  0.0 24.3 jit_solution(6038038678260147403)
XLA Ops:
  0.6 1.0 %pack.1 = (f32[8,512]{1,0:T(8,128)S(1)}, f32[59,1024]{1,0:T(8,128)S(1)}) custom-call(s32[1]{0:T(128)} %bitcast.2.where, s32[2,1,256]{2,1,0:T(1,128)} %bitcast.4, s32[2,256]{1,0:T(2,128)} %refs_1_.1, f32[3,512]{1,0:T(4,128)} %refs_2_.1, f32[59,1024]{1,0:T(8,128)} %refs_3_.1), custom_call_target="tpu_custom_call" | custom-call | tf_op jit(solution)/shard_map/pack/pallas_call | solution.py:745
  1.7 0.0 copy-start.2
  1.7 3.1 %collective-permute-start = (f32[8,512]{1,0:T(8,128)S(1)}, f32[8,512]{1,0:T(8,128)S(1)}, u32[]{:S(2)}, u32[]{:S(2)}) collective-permute-start(f32[8,512]{1,0:T(8,128)S(1)} %get-tuple-element.23.own.first), channel_id=1, source_target_pairs={{0,1},{1,0},{2,3},{3,2},{4,5},{5,4},{6,7},{7,6},{8,9},{9,8},{10,11... | collective-permute-start | bytes 49160 | tf_op jit(solution)/shard_map/ppermute | solution.py:845
  4.8 0.0 copy-done.2
  4.8 0.0 copy-start.3
  4.8 0.0 copy-start.1
  4.8 0.7 %cut.1 = (f32[24,256]{1,0:T(8,128)S(1)}, f32[24,256]{1,0:T(8,128)S(1)}, f32[24,256]{1,0:T(8,128)S(1)}, f32[24,256]{1,0:T(8,128)S(1)}) custom-call(s32[1]{0:T(128)} %bitcast.2.where, f32[4,12]{1,0:T(4,128)S(1)} %copy-done.2, f32[59,1024]{1,0:T(8,128)S(1)} %get-tuple-element.24.params), custom_call_target="tpu_custom_call" | custom-call | tf_op jit(solution)/shard_map/cut/pallas_call | solution.py:745
  5.5 0.0 copy-start
  5.5 0.1 collective-permute-start.1
  5.6 1.6 %collective-permute-start.2 = (f32[24,256]{1,0:T(8,128)S(1)}, f32[24,256]{1,0:T(8,128)S(1)}, u32[]{:S(2)}, u32[]{:S(2)}) collective-permute-start(f32[24,256]{1,0:T(8,128)S(1)} %get-tuple-element.27), channel_id=1, source_target_pairs={{0,8},{4,12},{8,0},{12,4},{1,9},{5,13},{9,1},{13,5},{2,10},{6,14},... | collective-permute-start | bytes 73736 | tf_op jit(solution)/shard_map/ppermute | solution.py:845
  7.2 0.3 %collective-permute-start.3 = (f32[24,256]{1,0:T(8,128)S(1)}, f32[24,256]{1,0:T(8,128)S(1)}, u32[]{:S(2)}, u32[]{:S(2)}) collective-permute-start(f32[24,256]{1,0:T(8,128)S(1)} %get-tuple-element.28), channel_id=1, source_target_pairs={{0,12},{4,8},{8,4},{12,0},{1,13},{5,9},{9,5},{13,1},{2,14},{6,10},... | collective-permute-start | bytes 73736 | tf_op jit(solution)/shard_map/ppermute | solution.py:845
  7.5 0.1 pad_add_fusion.2.where
  7.5 0.0 collective-permute-done.other.second
  7.5 2.6 %collective-permute-start.4 = (f32[16,512]{1,0:T(8,128)S(1)}, f32[16,512]{1,0:T(8,128)S(1)}, u32[]{:S(2)}, u32[]{:S(2)}) collective-permute-start(f32[16,512]{1,0:T(8,128)S(1)} %join.1), channel_id=1, source_target_pairs={{0,2},{1,3},{2,0},{3,1},{4,6},{5,7},{6,4},{7,5},{8,10},{9,11},{10,... | collective-permute-start | bytes 98312 | tf_op jit(solution)/shard_map/ppermute | solution.py:845
  10.2 0.1 pad_add_fusion.where
  10.2 0.0 collective-permute-done.1.refs_1_
  10.2 0.0 collective-permute-done.2.refs_2_
  10.2 0.2 collective-permute-done.3.refs_3_
  10.4 0.0 copy-done.3
  10.4 3.8 %near.1 = (f32[3,512]{1,0:T(4,128)}, f32[128,128]{1,0:T(8,128)S(1)}, f32[16,1024]{1,0:T(8,128)S(1)}) custom-call(s32[2]{0:T(128)S(1)} %copy-done.3, f32[4,12]{1,0:T(4,128)S(1)} %copy-done.2, s32[3]{0:T(128)S(1)} %pad_add_fusion.where, f32[8,512]{1,0:T(8,128)S(1)} %get-tuple-element.23.own.first, f32[8,512]{1,0:T(8,128)S(1)} %collective-permute-done.other.second, ...), custom_call_target="tpu_custom_call" | custom-call | tf_op jit(solution)/shard_map/near/pallas_call | solution.py:745
  14.2 0.0 collective-permute-done.4.infos
  14.2 3.7 %far.1 = (f32[16,256]{1,0:T(8,128)S(1)}, f32[16,256]{1,0:T(8,128)S(1)}, f32[16,256]{1,0:T(8,128)S(1)}, f32[16,256]{1,0:T(8,128)S(1)}) custom-call(s32[2]{0:T(128)S(1)} %copy-done.3, s32[3]{0:T(128)S(1)} %pad_add_fusion.where, f32[128,128]{1,0:T(8,128)S(1)} %get-tuple-element.30.rows, f32[16,1024]{1,0:T(8,128)S(1)} %get-tuple-element.31.partial, ...), custom_call_target="tpu_custom_call" | custom-call | tf_op jit(solution)/shard_map/far/pallas_call | solution.py:745
  18.0 1.4 %collective-permute-start.5 = (f32[16,256]{1,0:T(8,128)S(1)}, f32[16,256]{1,0:T(8,128)S(1)}, u32[]{:S(2)}, u32[]{:S(2)}) collective-permute-start(f32[16,256]{1,0:T(8,128)S(1)} %get-tuple-element.32), channel_id=1, source_target_pairs={{0,8},{4,12},{8,0},{12,4},{1,9},{5,13},{9,1},{13,5},{2,10},{6,14},... | collective-permute-start | bytes 49160 | tf_op jit(solution)/shard_map/ppermute | solution.py:845
  19.4 0.2 collective-permute-start.6
  19.6 0.6 %collective-permute-start.7 = (f32[16,256]{1,0:T(8,128)S(1)}, f32[16,256]{1,0:T(8,128)S(1)}, u32[]{:S(2)}, u32[]{:S(2)}) collective-permute-start(f32[16,256]{1,0:T(8,128)S(1)} %get-tuple-element.35), channel_id=1, source_target_pairs={{0,4},{4,0},{8,12},{12,8},{1,5},{5,1},{9,13},{13,9},{2,6},{6,2},{1... | collective-permute-start | bytes 49160 | tf_op jit(solution)/shard_map/ppermute | solution.py:845
  20.2 0.1 pad_add_fusion.1.where
  20.3 0.8 %collective-permute-done.7.refs_1_ = f32[16,256]{1,0:T(8,128)S(1)} collective-permute-done((f32[16,256]{1,0:T(8,128)S(1)}, f32[16,256]{1,0:T(8,128)S(1)}, u32[]{:S(2)}, u32[]{:S(2)}) %collective-permute-start.7) | collective-permute-done | bytes 16416 | tf_op jit(solution)/shard_map/ppermute | solution.py:845
  21.0 0.0 copy-done.1
  21.0 0.0 copy-done
  21.0 1.6 %update.2 = (f32[59,1024]{1,0:T(8,128)}, f32[59,1024]{1,0:T(8,128)}, f32[59,1024]{1,0:T(8,128)}) custom-call(s32[2]{0:T(128)S(1)} %pad_add_fusion.2.where, f32[4,12]{1,0:T(4,128)S(1)} %copy-done.2, f32[59,1024]{1,0:T(8,128)S(1)} %get-tuple-element.24.params, f32[59,1024]{1,0:T(8,128)S(1)} %copy-done, f32[59,1024]{1,0:T(8,128)S(1)} %copy-done.1, ...), custom_call_target="tpu_custom_call" | custom-call | tf_op jit(solution)/shard_map/update/pallas_call | solution.py:819
  22.6 0.0 collective-permute-done.5.refs_0_
  22.7 0.1 collective-permute-done.6.refs_1_
  22.7 1.6 %update.3 = (f32[59,1024]{1,0:T(8,128)}, f32[59,1024]{1,0:T(8,128)}, f32[59,1024]{1,0:T(8,128)}) custom-call(s32[2]{0:T(128)S(1)} %pad_add_fusion.1.where, f32[4,12]{1,0:T(4,128)S(1)} %copy-done.2, f32[59,1024]{1,0:T(8,128)S(1)} %get-tuple-element.24.params, f32[59,1024]{1,0:T(8,128)S(1)} %copy-done, ...), custom_call_target="tpu_custom_call", output_to_operand_aliasing={{0}: (7, {}), {1}: (8, {}), {2}: (9, {})} | custom-call | tf_op jit(solution)/shard_map/update/pallas_call | solution.py:819
  (1 shorter events, 0.0 us)
Async XLA Ops:
  1.7 3.1 %copy-start.2 = (f32[4,12]{1,0:T(4,128)S(1)}, f32[4,12]{1,0:T(4,128)}, u32[]{:S(2)}) copy-start(f32[4,12]{1,0:T(4,128)} %cams.7) | copy-start | bytes 580
  1.7 5.8 %collective-permute-start = (f32[8,512]{1,0:T(8,128)S(1)}, f32[8,512]{1,0:T(8,128)S(1)}, u32[]{:S(2)}, u32[]{:S(2)}) collective-permute-start(f32[8,512]{1,0:T(8,128)S(1)} %get-tuple-element.23.own.first), channel_id=1, source_target_pairs={{0,1},{1,0},{2,3},{3,2},{4,5},{5,4},{6,7},{7,6},{8,9},{9,8},{10,11... | collective-permute-start | bytes 49160 | tf_op jit(solution)/shard_map/ppermute | solution.py:845
  4.8 5.6 %copy-start.3 = (s32[2]{0:T(128)S(1)}, s32[2]{0:T(128)}, u32[]{:S(2)}) copy-start(s32[2]{0:T(128)} %tile_ids.3) | copy-start | bytes 28
  4.8 16.3 %copy-start.1 = (f32[59,1024]{1,0:T(8,128)S(1)}, f32[59,1024]{1,0:T(8,128)}, u32[]{:S(2)}) copy-start(f32[59,1024]{1,0:T(8,128)} %adam_v.3) | copy-start | bytes 724996
  5.5 15.5 %copy-start = (f32[59,1024]{1,0:T(8,128)S(1)}, f32[59,1024]{1,0:T(8,128)}, u32[]{:S(2)}) copy-start(f32[59,1024]{1,0:T(8,128)} %adam_m.3) | copy-start | bytes 724996
  5.5 4.7 %collective-permute-start.1 = (f32[24,256]{1,0:T(8,128)S(1)}, f32[24,256]{1,0:T(8,128)S(1)}, u32[]{:S(2)}, u32[]{:S(2)}) collective-permute-start(f32[24,256]{1,0:T(8,128)S(1)} %get-tuple-element.26), channel_id=1, source_target_pairs={{0,4},{4,0},{8,12},{12,8},{1,5},{5,1},{9,13},{13,9},{2,6},{6,2},{1... | collective-permute-start | bytes 73736 | tf_op jit(solution)/shard_map/ppermute | solution.py:845
  5.6 4.6 %collective-permute-start.2 = (f32[24,256]{1,0:T(8,128)S(1)}, f32[24,256]{1,0:T(8,128)S(1)}, u32[]{:S(2)}, u32[]{:S(2)}) collective-permute-start(f32[24,256]{1,0:T(8,128)S(1)} %get-tuple-element.27), channel_id=1, source_target_pairs={{0,8},{4,12},{8,0},{12,4},{1,9},{5,13},{9,1},{13,5},{2,10},{6,14},... | collective-permute-start | bytes 73736 | tf_op jit(solution)/shard_map/ppermute | solution.py:845
  7.2 3.3 %collective-permute-start.3 = (f32[24,256]{1,0:T(8,128)S(1)}, f32[24,256]{1,0:T(8,128)S(1)}, u32[]{:S(2)}, u32[]{:S(2)}) collective-permute-start(f32[24,256]{1,0:T(8,128)S(1)} %get-tuple-element.28), channel_id=1, source_target_pairs={{0,12},{4,8},{8,4},{12,0},{1,13},{5,9},{9,5},{13,1},{2,14},{6,10},... | collective-permute-start | bytes 73736 | tf_op jit(solution)/shard_map/ppermute | solution.py:845
  7.5 6.7 %collective-permute-start.4 = (f32[16,512]{1,0:T(8,128)S(1)}, f32[16,512]{1,0:T(8,128)S(1)}, u32[]{:S(2)}, u32[]{:S(2)}) collective-permute-start(f32[16,512]{1,0:T(8,128)S(1)} %join.1), channel_id=1, source_target_pairs={{0,2},{1,3},{2,0},{3,1},{4,6},{5,7},{6,4},{7,5},{8,10},{9,11},{10,... | collective-permute-start | bytes 98312 | tf_op jit(solution)/shard_map/ppermute | solution.py:845
  18.0 4.7 %collective-permute-start.5 = (f32[16,256]{1,0:T(8,128)S(1)}, f32[16,256]{1,0:T(8,128)S(1)}, u32[]{:S(2)}, u32[]{:S(2)}) collective-permute-start(f32[16,256]{1,0:T(8,128)S(1)} %get-tuple-element.32), channel_id=1, source_target_pairs={{0,8},{4,12},{8,0},{12,4},{1,9},{5,13},{9,1},{13,5},{2,10},{6,14},... | collective-permute-start | bytes 49160 | tf_op jit(solution)/shard_map/ppermute | solution.py:845
  19.4 3.3 %collective-permute-start.6 = (f32[16,256]{1,0:T(8,128)S(1)}, f32[16,256]{1,0:T(8,128)S(1)}, u32[]{:S(2)}, u32[]{:S(2)}) collective-permute-start(f32[16,256]{1,0:T(8,128)S(1)} %get-tuple-element.33), channel_id=1, source_target_pairs={{0,12},{4,8},{8,4},{12,0},{1,13},{5,9},{9,5},{13,1},{2,14},{6,10},... | collective-permute-start | bytes 49160 | tf_op jit(solution)/shard_map/ppermute | solution.py:845
  19.6 1.5 %collective-permute-start.7 = (f32[16,256]{1,0:T(8,128)S(1)}, f32[16,256]{1,0:T(8,128)S(1)}, u32[]{:S(2)}, u32[]{:S(2)}) collective-permute-start(f32[16,256]{1,0:T(8,128)S(1)} %get-tuple-element.35), channel_id=1, source_target_pairs={{0,4},{4,0},{8,12},{12,8},{1,5},{5,1},{9,13},{13,9},{2,6},{6,2},{1... | collective-permute-start | bytes 49160 | tf_op jit(solution)/shard_map/ppermute | solution.py:845

commit v17 on v16

--- a/solution.py
+++ b/solution.py
@@ -478,7 +478,7 @@
             colour_s[24 * n + at : 24 * n + at + 8, here] = value
         hues.append(jnp.concatenate([high, low], axis=0).astype(BF16))
 
-    unroll, quad = 32, 4
+    unroll, quad = 128, 4
     steps = listed // unroll
 
     def forward(step, passed):

time: 24.5 us -> 24.9 us (1.016)
  Pallas kernels: 12.5 us -> 12.9 us
    pallas_call x5, Pallas kernels: 9.33 us -> 9.71 us  [call(): pl.pallas_call(kernel, out_shape=out_shape, in_specs=in_specs, out_specs=...]
  transfers between devices with their start and end apart: 8 -> 8, of which waited for: 3 -> 3; matrix products, arithmetic and copies ran while one was open for 1% -> 1% of each run, Pallas kernels for 25% -> 26%
where the time goes in v17:
time: 24.9 us; the launch traced here: 24.7 us
  Pallas kernels  12.9 us (52%)
  starting transfers between devices  9.85 us (40%)
  waiting for transfers between devices  1 us (4%)
  between operations  0.71 us (3%)
    ppermute x8, starting transfers between devices, swap(): lax.ppermute(value, axis, [(k, k ^ d) for k in range(lax.axis_size(axis))])  9.85 us
    pallas_call x5, Pallas kernels, call(): pl.pallas_call(kernel, out_shape=out_shape, in_specs=in_specs, out_specs=...  9.71 us
    pallas_call x2, Pallas kernels, update(): pl.pallas_call(functools.partial(update_kernel, len(packets), len(before)...  3.18 us
    ppermute x8, waiting for transfers between devices, swap(): lax.ppermute(value, axis, [(k, k ^ d) for k in range(lax.axis_size(axis))])  1 us
  transfers between devices with their start and end apart: 8, of which 3 were waited for; matrix products, arithmetic and copies ran while one was open for 1% of the time, Pallas kernels for 26%

profile of v17, /device:TPU:0, one launch (start us, length us, event | category | flops | bytes accessed | tf_op | source)
XLA Modules:
  0.0 24.7 jit_solution(1783026612871403010)
XLA Ops:
  0.6 1.0 %pack.1 = (f32[8,512]{1,0:T(8,128)S(1)}, f32[59,1024]{1,0:T(8,128)S(1)}) custom-call(s32[1]{0:T(128)} %bitcast.2.where, s32[2,1,256]{2,1,0:T(1,128)} %bitcast.4, s32[2,256]{1,0:T(2,128)} %refs_1_.1, f32[3,512]{1,0:T(4,128)} %refs_2_.1, f32[59,1024]{1,0:T(8,128)} %refs_3_.1), custom_call_target="tpu_custom_call" | custom-call | tf_op jit(solution)/shard_map/pack/pallas_call | solution.py:745
  1.7 0.0 copy-start.2
  1.7 3.1 %collective-permute-start = (f32[8,512]{1,0:T(8,128)S(1)}, f32[8,512]{1,0:T(8,128)S(1)}, u32[]{:S(2)}, u32[]{:S(2)}) collective-permute-start(f32[8,512]{1,0:T(8,128)S(1)} %get-tuple-element.23.own.first), channel_id=1, source_target_pairs={{0,1},{1,0},{2,3},{3,2},{4,5},{5,4},{6,7},{7,6},{8,9},{9,8},{10,11... | collective-permute-start | bytes 49160 | tf_op jit(solution)/shard_map/ppermute | solution.py:845
  4.8 0.0 copy-done.2
  4.8 0.0 copy-start.3
  4.8 0.0 copy-start.1
  4.8 0.7 %cut.1 = (f32[24,256]{1,0:T(8,128)S(1)}, f32[24,256]{1,0:T(8,128)S(1)}, f32[24,256]{1,0:T(8,128)S(1)}, f32[24,256]{1,0:T(8,128)S(1)}) custom-call(s32[1]{0:T(128)} %bitcast.2.where, f32[4,12]{1,0:T(4,128)S(1)} %copy-done.2, f32[59,1024]{1,0:T(8,128)S(1)} %get-tuple-element.24.params), custom_call_target="tpu_custom_call" | custom-call | tf_op jit(solution)/shard_map/cut/pallas_call | solution.py:745
  5.5 0.0 copy-start
  5.5 0.1 collective-permute-start.1
  5.6 1.6 %collective-permute-start.2 = (f32[24,256]{1,0:T(8,128)S(1)}, f32[24,256]{1,0:T(8,128)S(1)}, u32[]{:S(2)}, u32[]{:S(2)}) collective-permute-start(f32[24,256]{1,0:T(8,128)S(1)} %get-tuple-element.27), channel_id=1, source_target_pairs={{0,8},{4,12},{8,0},{12,4},{1,9},{5,13},{9,1},{13,5},{2,10},{6,14},... | collective-permute-start | bytes 73736 | tf_op jit(solution)/shard_map/ppermute | solution.py:845
  7.2 0.3 %collective-permute-start.3 = (f32[24,256]{1,0:T(8,128)S(1)}, f32[24,256]{1,0:T(8,128)S(1)}, u32[]{:S(2)}, u32[]{:S(2)}) collective-permute-start(f32[24,256]{1,0:T(8,128)S(1)} %get-tuple-element.28), channel_id=1, source_target_pairs={{0,12},{4,8},{8,4},{12,0},{1,13},{5,9},{9,5},{13,1},{2,14},{6,10},... | collective-permute-start | bytes 73736 | tf_op jit(solution)/shard_map/ppermute | solution.py:845
  7.5 0.1 pad_add_fusion.2.where
  7.5 0.0 collective-permute-done.other.second
  7.5 2.6 %collective-permute-start.4 = (f32[16,512]{1,0:T(8,128)S(1)}, f32[16,512]{1,0:T(8,128)S(1)}, u32[]{:S(2)}, u32[]{:S(2)}) collective-permute-start(f32[16,512]{1,0:T(8,128)S(1)} %join.1), channel_id=1, source_target_pairs={{0,2},{1,3},{2,0},{3,1},{4,6},{5,7},{6,4},{7,5},{8,10},{9,11},{10,... | collective-permute-start | bytes 98312 | tf_op jit(solution)/shard_map/ppermute | solution.py:845
  10.2 0.1 pad_add_fusion.where
  10.2 0.0 collective-permute-done.1.refs_1_
  10.2 0.0 collective-permute-done.2.refs_2_
  10.2 0.2 collective-permute-done.3.refs_3_
  10.4 0.0 copy-done.3
  10.4 4.0 %near.1 = (f32[3,512]{1,0:T(4,128)}, f32[128,128]{1,0:T(8,128)S(1)}, f32[16,1024]{1,0:T(8,128)S(1)}) custom-call(s32[2]{0:T(128)S(1)} %copy-done.3, f32[4,12]{1,0:T(4,128)S(1)} %copy-done.2, s32[3]{0:T(128)S(1)} %pad_add_fusion.where, f32[8,512]{1,0:T(8,128)S(1)} %get-tuple-element.23.own.first, f32[8,512]{1,0:T(8,128)S(1)} %collective-permute-done.other.second, ...), custom_call_target="tpu_custom_call" | custom-call | tf_op jit(solution)/shard_map/near/pallas_call | solution.py:745
  14.4 0.0 collective-permute-done.4.infos
  14.4 3.9 %far.1 = (f32[16,256]{1,0:T(8,128)S(1)}, f32[16,256]{1,0:T(8,128)S(1)}, f32[16,256]{1,0:T(8,128)S(1)}, f32[16,256]{1,0:T(8,128)S(1)}) custom-call(s32[2]{0:T(128)S(1)} %copy-done.3, s32[3]{0:T(128)S(1)} %pad_add_fusion.where, f32[128,128]{1,0:T(8,128)S(1)} %get-tuple-element.30.rows, f32[16,1024]{1,0:T(8,128)S(1)} %get-tuple-element.31.partial, ...), custom_call_target="tpu_custom_call" | custom-call | tf_op jit(solution)/shard_map/far/pallas_call | solution.py:745
  18.4 1.4 %collective-permute-start.5 = (f32[16,256]{1,0:T(8,128)S(1)}, f32[16,256]{1,0:T(8,128)S(1)}, u32[]{:S(2)}, u32[]{:S(2)}) collective-permute-start(f32[16,256]{1,0:T(8,128)S(1)} %get-tuple-element.32), channel_id=1, source_target_pairs={{0,8},{4,12},{8,0},{12,4},{1,9},{5,13},{9,1},{13,5},{2,10},{6,14},... | collective-permute-start | bytes 49160 | tf_op jit(solution)/shard_map/ppermute | solution.py:845
  19.8 0.2 collective-permute-start.6
  20.0 0.6 %collective-permute-start.7 = (f32[16,256]{1,0:T(8,128)S(1)}, f32[16,256]{1,0:T(8,128)S(1)}, u32[]{:S(2)}, u32[]{:S(2)}) collective-permute-start(f32[16,256]{1,0:T(8,128)S(1)} %get-tuple-element.35), channel_id=1, source_target_pairs={{0,4},{4,0},{8,12},{12,8},{1,5},{5,1},{9,13},{13,9},{2,6},{6,2},{1... | collective-permute-start | bytes 49160 | tf_op jit(solution)/shard_map/ppermute | solution.py:845
  20.6 0.1 pad_add_fusion.1.where
  20.7 0.8 %collective-permute-done.7.refs_1_ = f32[16,256]{1,0:T(8,128)S(1)} collective-permute-done((f32[16,256]{1,0:T(8,128)S(1)}, f32[16,256]{1,0:T(8,128)S(1)}, u32[]{:S(2)}, u32[]{:S(2)}) %collective-permute-start.7) | collective-permute-done | bytes 16416 | tf_op jit(solution)/shard_map/ppermute | solution.py:845
  21.4 0.0 copy-done.1
  21.4 0.0 copy-done
  21.4 1.6 %update.2 = (f32[59,1024]{1,0:T(8,128)}, f32[59,1024]{1,0:T(8,128)}, f32[59,1024]{1,0:T(8,128)}) custom-call(s32[2]{0:T(128)S(1)} %pad_add_fusion.2.where, f32[4,12]{1,0:T(4,128)S(1)} %copy-done.2, f32[59,1024]{1,0:T(8,128)S(1)} %get-tuple-element.24.params, f32[59,1024]{1,0:T(8,128)S(1)} %copy-done, f32[59,1024]{1,0:T(8,128)S(1)} %copy-done.1, ...), custom_call_target="tpu_custom_call" | custom-call | tf_op jit(solution)/shard_map/update/pallas_call | solution.py:819
  23.0 0.0 collective-permute-done.5.refs_0_
  23.0 0.1 collective-permute-done.6.refs_1_
  23.1 1.6 %update.3 = (f32[59,1024]{1,0:T(8,128)}, f32[59,1024]{1,0:T(8,128)}, f32[59,1024]{1,0:T(8,128)}) custom-call(s32[2]{0:T(128)S(1)} %pad_add_fusion.1.where, f32[4,12]{1,0:T(4,128)S(1)} %copy-done.2, f32[59,1024]{1,0:T(8,128)S(1)} %get-tuple-element.24.params, f32[59,1024]{1,0:T(8,128)S(1)} %copy-done, ...), custom_call_target="tpu_custom_call", output_to_operand_aliasing={{0}: (7, {}), {1}: (8, {}), {2}: (9, {})} | custom-call | tf_op jit(solution)/shard_map/update/pallas_call | solution.py:819
  (1 shorter events, 0.0 us)
Async XLA Ops:
  1.7 3.1 %copy-start.2 = (f32[4,12]{1,0:T(4,128)S(1)}, f32[4,12]{1,0:T(4,128)}, u32[]{:S(2)}) copy-start(f32[4,12]{1,0:T(4,128)} %cams.7) | copy-start | bytes 580
  1.7 5.8 %collective-permute-start = (f32[8,512]{1,0:T(8,128)S(1)}, f32[8,512]{1,0:T(8,128)S(1)}, u32[]{:S(2)}, u32[]{:S(2)}) collective-permute-start(f32[8,512]{1,0:T(8,128)S(1)} %get-tuple-element.23.own.first), channel_id=1, source_target_pairs={{0,1},{1,0},{2,3},{3,2},{4,5},{5,4},{6,7},{7,6},{8,9},{9,8},{10,11... | collective-permute-start | bytes 49160 | tf_op jit(solution)/shard_map/ppermute | solution.py:845
  4.8 5.6 %copy-start.3 = (s32[2]{0:T(128)S(1)}, s32[2]{0:T(128)}, u32[]{:S(2)}) copy-start(s32[2]{0:T(128)} %tile_ids.3) | copy-start | bytes 28
  4.8 16.6 %copy-start.1 = (f32[59,1024]{1,0:T(8,128)S(1)}, f32[59,1024]{1,0:T(8,128)}, u32[]{:S(2)}) copy-start(f32[59,1024]{1,0:T(8,128)} %adam_v.3) | copy-start | bytes 724996
  5.5 15.9 %copy-start = (f32[59,1024]{1,0:T(8,128)S(1)}, f32[59,1024]{1,0:T(8,128)}, u32[]{:S(2)}) copy-start(f32[59,1024]{1,0:T(8,128)} %adam_m.3) | copy-start | bytes 724996
  5.5 4.7 %collective-permute-start.1 = (f32[24,256]{1,0:T(8,128)S(1)}, f32[24,256]{1,0:T(8,128)S(1)}, u32[]{:S(2)}, u32[]{:S(2)}) collective-permute-start(f32[24,256]{1,0:T(8,128)S(1)} %get-tuple-element.26), channel_id=1, source_target_pairs={{0,4},{4,0},{8,12},{12,8},{1,5},{5,1},{9,13},{13,9},{2,6},{6,2},{1... | collective-permute-start | bytes 73736 | tf_op jit(solution)/shard_map/ppermute | solution.py:845
  5.6 4.6 %collective-permute-start.2 = (f32[24,256]{1,0:T(8,128)S(1)}, f32[24,256]{1,0:T(8,128)S(1)}, u32[]{:S(2)}, u32[]{:S(2)}) collective-permute-start(f32[24,256]{1,0:T(8,128)S(1)} %get-tuple-element.27), channel_id=1, source_target_pairs={{0,8},{4,12},{8,0},{12,4},{1,9},{5,13},{9,1},{13,5},{2,10},{6,14},... | collective-permute-start | bytes 73736 | tf_op jit(solution)/shard_map/ppermute | solution.py:845
  7.2 3.3 %collective-permute-start.3 = (f32[24,256]{1,0:T(8,128)S(1)}, f32[24,256]{1,0:T(8,128)S(1)}, u32[]{:S(2)}, u32[]{:S(2)}) collective-permute-start(f32[24,256]{1,0:T(8,128)S(1)} %get-tuple-element.28), channel_id=1, source_target_pairs={{0,12},{4,8},{8,4},{12,0},{1,13},{5,9},{9,5},{13,1},{2,14},{6,10},... | collective-permute-start | bytes 73736 | tf_op jit(solution)/shard_map/ppermute | solution.py:845
  7.5 6.9 %collective-permute-start.4 = (f32[16,512]{1,0:T(8,128)S(1)}, f32[16,512]{1,0:T(8,128)S(1)}, u32[]{:S(2)}, u32[]{:S(2)}) collective-permute-start(f32[16,512]{1,0:T(8,128)S(1)} %join.1), channel_id=1, source_target_pairs={{0,2},{1,3},{2,0},{3,1},{4,6},{5,7},{6,4},{7,5},{8,10},{9,11},{10,... | collective-permute-start | bytes 98312 | tf_op jit(solution)/shard_map/ppermute | solution.py:845
  18.4 4.7 %collective-permute-start.5 = (f32[16,256]{1,0:T(8,128)S(1)}, f32[16,256]{1,0:T(8,128)S(1)}, u32[]{:S(2)}, u32[]{:S(2)}) collective-permute-start(f32[16,256]{1,0:T(8,128)S(1)} %get-tuple-element.32), channel_id=1, source_target_pairs={{0,8},{4,12},{8,0},{12,4},{1,9},{5,13},{9,1},{13,5},{2,10},{6,14},... | collective-permute-start | bytes 49160 | tf_op jit(solution)/shard_map/ppermute | solution.py:845
  19.8 3.3 %collective-permute-start.6 = (f32[16,256]{1,0:T(8,128)S(1)}, f32[16,256]{1,0:T(8,128)S(1)}, u32[]{:S(2)}, u32[]{:S(2)}) collective-permute-start(f32[16,256]{1,0:T(8,128)S(1)} %get-tuple-element.33), channel_id=1, source_target_pairs={{0,12},{4,8},{8,4},{12,0},{1,13},{5,9},{9,5},{13,1},{2,14},{6,10},... | collective-permute-start | bytes 49160 | tf_op jit(solution)/shard_map/ppermute | solution.py:845
  20.0 1.5 %collective-permute-start.7 = (f32[16,256]{1,0:T(8,128)S(1)}, f32[16,256]{1,0:T(8,128)S(1)}, u32[]{:S(2)}, u32[]{:S(2)}) collective-permute-start(f32[16,256]{1,0:T(8,128)S(1)} %get-tuple-element.35), channel_id=1, source_target_pairs={{0,4},{4,0},{8,12},{12,8},{1,5},{5,1},{9,13},{13,9},{2,6},{6,2},{1... | collective-permute-start | bytes 49160 | tf_op jit(solution)/shard_map/ppermute | solution.py:845

commit v18 on v17

--- a/solution.py
+++ b/solution.py
@@ -478,7 +478,7 @@
             colour_s[24 * n + at : 24 * n + at + 8, here] = value
         hues.append(jnp.concatenate([high, low], axis=0).astype(BF16))
 
-    unroll, quad = 128, 4
+    unroll, quad = 64, 4
     steps = listed // unroll
 
     def forward(step, passed):
@@ -662,17 +662,18 @@
     out[half:, :] = second[...]
 
 
-def update_kernel(pieces, follows, where, cams, params, adam_m, adam_v, *refs):
+def update_kernel(pieces, follows, first_piece, cams, params, adam_m, adam_v, *refs):
     packets, refs = refs[:pieces], refs[pieces + 3 * follows :]
     sinks, (feats, rows, grads, made, sems) = refs[:3], refs[3:]
     features = params.shape[0]
     chunk = packets[0].shape[1]
     width = pieces * chunk
     slabs = width // LANES
-    start = (where[0] ^ where[1]) // pieces * pieces * chunk
+    place = lax.axis_index("gs") ^ first_piece if pieces > 1 else 0
+    start = place // pieces * pieces * chunk
     for d in range(pieces):
         for h in range(chunk // LANES):
-            slab = (where[0] ^ where[1] ^ d) % pieces * (chunk // LANES) + h
+            slab = (place ^ d) % pieces * (chunk // LANES) + h
             rows[pl.ds(slab, ROWS, stride=slabs), :] = packets[d][:, h * LANES : (h + 1) * LANES]
     pulled = [rows[f * slabs : (f + 1) * slabs, :] for f in range(10)]
     view = pulled[9]
@@ -810,16 +811,16 @@
     )[0]
 
 
-def update(own, first, cameras, params, adam_m, adam_v, packets, before):
+def update(first, cameras, params, adam_m, adam_v, packets, before):
     features = params.shape[0]
     width = sum(packet.shape[1] for packet in packets)
     slabs = width // LANES
     shape = jax.ShapeDtypeStruct(params.shape, F32)
-    at = 5 + len(packets)
+    at = 4 + len(packets)
     return pl.pallas_call(
-        functools.partial(update_kernel, len(packets), len(before) > 0),
+        functools.partial(update_kernel, len(packets), len(before) > 0, first),
         out_shape=(shape, shape, shape),
-        in_specs=[smem()] * 2
+        in_specs=[smem()]
         + [vmem()] * (3 + len(packets))
         + [any_space()] * len(before),
         out_specs=(any_space(),) * 3,
@@ -834,7 +835,6 @@
         compiler_params=pltpu.CompilerParams(vmem_limit_bytes=32 * 1024 * 1024),
         name="update",
     )(
-        jnp.stack([own, jnp.int32(first)]).astype(jnp.int32),
         cameras, params, adam_m, adam_v, *packets, *before,
     )
 
@@ -878,16 +878,13 @@
     packets = [swap(packets[d], "gs", d) for d in range(shards)]
     if blocks > 1:
         packets = [block_sum(packet, along, team) for packet in packets]
-    if aligned:
-        own = group
-    else:
+    if not aligned:
         packets = [jnp.stack(packets)[jnp.arange(shards) ^ group].transpose(1, 0, 2).reshape(ROWS, -1)]
-        own = jnp.int32(0)
     made = ()
     count = max(1, len(packets) // 2)
     for first in range(0, len(packets), count):
         made = update(
-            own, first, cameras, params, adam_m, adam_v, packets[first : first + count], made
+            first, cameras, params, adam_m, adam_v, packets[first : first + count], made
         )
     new_params, new_m, new_v = made
     return (rendered, new_params, new_m, new_v)

time: 24.9 us -> 24.4 us (0.980)
  starting transfers between devices: 9.85 us -> 9.54 us
  Pallas kernels: 12.9 us -> 12.6 us
  waiting for transfers between devices: 1 us -> 1.29 us
    ppermute x8, starting transfers between devices: 9.85 us -> 9.54 us  [swap(): lax.ppermute(value, axis, [(k, k ^ d) for k in range(lax.axis_size(axis))])]
    ppermute x8, waiting for transfers between devices: 1 us -> 1.29 us  [swap(): lax.ppermute(value, axis, [(k, k ^ d) for k in range(lax.axis_size(axis))])]
    pallas_call x5, Pallas kernels: 9.71 us -> 9.43 us  [call(): pl.pallas_call(kernel, out_shape=out_shape, in_specs=in_specs, out_specs=...]
  transfers between devices with their start and end apart: 8 -> 8, of which waited for: 3 -> 3; matrix products, arithmetic and copies ran while one was open for 1% -> 0% of each run, Pallas kernels for 26% -> 26%
where the time goes in v18:
time: 24.4 us; the launch traced here: 24.2 us
  Pallas kernels  12.6 us (52%)
  starting transfers between devices  9.54 us (39%)
  waiting for transfers between devices  1.29 us (5%)
  between operations  0.7 us (3%)
    ppermute x8, starting transfers between devices, swap(): lax.ppermute(value, axis, [(k, k ^ d) for k in range(lax.axis_size(axis))])  9.54 us
    pallas_call x5, Pallas kernels, call(): pl.pallas_call(kernel, out_shape=out_shape, in_specs=in_specs, out_specs=...  9.43 us
    pallas_call x2, Pallas kernels, update(): pl.pallas_call(functools.partial(update_kernel, len(packets), len(before)...  3.2 us
    ppermute x8, waiting for transfers between devices, swap(): lax.ppermute(value, axis, [(k, k ^ d) for k in range(lax.axis_size(axis))])  1.29 us
  transfers between devices with their start and end apart: 8, of which 3 were waited for; matrix products, arithmetic and copies ran while one was open for 0% of the time, Pallas kernels for 26%

profile of v18, /device:TPU:0, one launch (start us, length us, event | category | flops | bytes accessed | tf_op | source)
XLA Modules:
  0.0 24.2 jit_solution(17519685872251502844)
XLA Ops:
  0.6 1.0 %pack.1 = (f32[8,512]{1,0:T(8,128)S(1)}, f32[59,1024]{1,0:T(8,128)S(1)}) custom-call(s32[1]{0:T(128)} %bitcast.2.where, s32[2,1,256]{2,1,0:T(1,128)} %bitcast.4, s32[2,256]{1,0:T(2,128)} %refs_1_.1, f32[3,512]{1,0:T(4,128)} %refs_2_.1, f32[59,1024]{1,0:T(8,128)} %refs_3_.1), custom_call_target="tpu_custom_call" | custom-call | tf_op jit(solution)/shard_map/pack/pallas_call | solution.py:746
  1.7 0.0 copy-start.2
  1.7 3.1 %collective-permute-start = (f32[8,512]{1,0:T(8,128)S(1)}, f32[8,512]{1,0:T(8,128)S(1)}, u32[]{:S(2)}, u32[]{:S(2)}) collective-permute-start(f32[8,512]{1,0:T(8,128)S(1)} %get-tuple-element.23.own.first), channel_id=1, source_target_pairs={{0,1},{1,0},{2,3},{3,2},{4,5},{5,4},{6,7},{7,6},{8,9},{9,8},{10,11... | collective-permute-start | bytes 49160 | tf_op jit(solution)/shard_map/ppermute | solution.py:845
  4.8 0.0 copy-done.2
  4.8 0.0 copy-start.3
  4.8 0.0 copy-start.1
  4.8 0.7 %cut.1 = (f32[24,256]{1,0:T(8,128)S(1)}, f32[24,256]{1,0:T(8,128)S(1)}, f32[24,256]{1,0:T(8,128)S(1)}, f32[24,256]{1,0:T(8,128)S(1)}) custom-call(s32[1]{0:T(128)} %bitcast.2.where, f32[4,12]{1,0:T(4,128)S(1)} %copy-done.2, f32[59,1024]{1,0:T(8,128)S(1)} %get-tuple-element.24.params), custom_call_target="tpu_custom_call" | custom-call | tf_op jit(solution)/shard_map/cut/pallas_call | solution.py:746
  5.5 0.0 copy-start
  5.5 0.1 collective-permute-start.1
  5.6 1.6 %collective-permute-start.2 = (f32[24,256]{1,0:T(8,128)S(1)}, f32[24,256]{1,0:T(8,128)S(1)}, u32[]{:S(2)}, u32[]{:S(2)}) collective-permute-start(f32[24,256]{1,0:T(8,128)S(1)} %get-tuple-element.27), channel_id=1, source_target_pairs={{0,8},{4,12},{8,0},{12,4},{1,9},{5,13},{9,1},{13,5},{2,10},{6,14},... | collective-permute-start | bytes 73736 | tf_op jit(solution)/shard_map/ppermute | solution.py:845
  7.2 0.3 %collective-permute-start.3 = (f32[24,256]{1,0:T(8,128)S(1)}, f32[24,256]{1,0:T(8,128)S(1)}, u32[]{:S(2)}, u32[]{:S(2)}) collective-permute-start(f32[24,256]{1,0:T(8,128)S(1)} %get-tuple-element.28), channel_id=1, source_target_pairs={{0,12},{4,8},{8,4},{12,0},{1,13},{5,9},{9,5},{13,1},{2,14},{6,10},... | collective-permute-start | bytes 73736 | tf_op jit(solution)/shard_map/ppermute | solution.py:845
  7.5 0.0 collective-permute-done.other.second
  7.5 2.6 %collective-permute-start.4 = (f32[16,512]{1,0:T(8,128)S(1)}, f32[16,512]{1,0:T(8,128)S(1)}, u32[]{:S(2)}, u32[]{:S(2)}) collective-permute-start(f32[16,512]{1,0:T(8,128)S(1)} %join.1), channel_id=1, source_target_pairs={{0,2},{1,3},{2,0},{3,1},{4,6},{5,7},{6,4},{7,5},{8,10},{9,11},{10,... | collective-permute-start | bytes 98312 | tf_op jit(solution)/shard_map/ppermute | solution.py:845
  10.1 0.1 pad_add_fusion.where
  10.1 0.0 collective-permute-done.1.refs_1_
  10.1 0.0 collective-permute-done.2.refs_2_
  10.1 0.3 %collective-permute-done.3.refs_3_ = f32[24,256]{1,0:T(8,128)S(1)} collective-permute-done((f32[24,256]{1,0:T(8,128)S(1)}, f32[24,256]{1,0:T(8,128)S(1)}, u32[]{:S(2)}, u32[]{:S(2)}) %collective-permute-start.3) | collective-permute-done | bytes 24608 | tf_op jit(solution)/shard_map/ppermute | solution.py:845
  10.4 0.0 copy-done.3
  10.4 3.9 %near.1 = (f32[3,512]{1,0:T(4,128)}, f32[128,128]{1,0:T(8,128)S(1)}, f32[16,1024]{1,0:T(8,128)S(1)}) custom-call(s32[2]{0:T(128)S(1)} %copy-done.3, f32[4,12]{1,0:T(4,128)S(1)} %copy-done.2, s32[3]{0:T(128)S(1)} %pad_add_fusion.where, f32[8,512]{1,0:T(8,128)S(1)} %get-tuple-element.23.own.first, f32[8,512]{1,0:T(8,128)S(1)} %collective-permute-done.other.second, ...), custom_call_target="tpu_custom_call" | custom-call | tf_op jit(solution)/shard_map/near/pallas_call | solution.py:746
  14.3 0.0 collective-permute-done.4.infos
  14.3 3.8 %far.1 = (f32[16,256]{1,0:T(8,128)S(1)}, f32[16,256]{1,0:T(8,128)S(1)}, f32[16,256]{1,0:T(8,128)S(1)}, f32[16,256]{1,0:T(8,128)S(1)}) custom-call(s32[2]{0:T(128)S(1)} %copy-done.3, s32[3]{0:T(128)S(1)} %pad_add_fusion.where, f32[128,128]{1,0:T(8,128)S(1)} %get-tuple-element.30.rows, f32[16,1024]{1,0:T(8,128)S(1)} %get-tuple-element.31.partial, ...), custom_call_target="tpu_custom_call" | custom-call | tf_op jit(solution)/shard_map/far/pallas_call | solution.py:746
  18.1 0.2 collective-permute-start.7
  18.3 1.2 %collective-permute-start.5 = (f32[16,256]{1,0:T(8,128)S(1)}, f32[16,256]{1,0:T(8,128)S(1)}, u32[]{:S(2)}, u32[]{:S(2)}) collective-permute-start(f32[16,256]{1,0:T(8,128)S(1)} %get-tuple-element.32), channel_id=1, source_target_pairs={{0,8},{4,12},{8,0},{12,4},{1,9},{5,13},{9,1},{13,5},{2,10},{6,14},... | collective-permute-start | bytes 49160 | tf_op jit(solution)/shard_map/ppermute | solution.py:845
  19.5 0.5 %collective-permute-start.6 = (f32[16,256]{1,0:T(8,128)S(1)}, f32[16,256]{1,0:T(8,128)S(1)}, u32[]{:S(2)}, u32[]{:S(2)}) collective-permute-start(f32[16,256]{1,0:T(8,128)S(1)} %get-tuple-element.33), channel_id=1, source_target_pairs={{0,12},{4,8},{8,4},{12,0},{1,13},{5,9},{9,5},{13,1},{2,14},{6,10},... | collective-permute-start | bytes 49160 | tf_op jit(solution)/shard_map/ppermute | solution.py:845
  20.0 0.0 collective-permute-done.7.refs_1_
  20.0 0.0 copy-done.1
  20.0 0.0 copy-done
  20.0 1.6 %update.2 = (f32[59,1024]{1,0:T(8,128)}, f32[59,1024]{1,0:T(8,128)}, f32[59,1024]{1,0:T(8,128)}) custom-call(f32[4,12]{1,0:T(4,128)S(1)} %copy-done.2, f32[59,1024]{1,0:T(8,128)S(1)} %get-tuple-element.24.params, f32[59,1024]{1,0:T(8,128)S(1)} %copy-done, f32[59,1024]{1,0:T(8,128)S(1)} %copy-done.1, f32[16,256]{1,0:T(8,128)S(1)} %get-tuple-element.34.refs_0_, ...), custom_call_target="tpu_custom_call" | custom-call | tf_op jit(solution)/shard_map/update/pallas_call | solution.py:820
  21.6 0.4 %collective-permute-done.5.refs_0_ = f32[16,256]{1,0:T(8,128)S(1)} collective-permute-done((f32[16,256]{1,0:T(8,128)S(1)}, f32[16,256]{1,0:T(8,128)S(1)}, u32[]{:S(2)}, u32[]{:S(2)}) %collective-permute-start.5) | collective-permute-done | bytes 16416 | tf_op jit(solution)/shard_map/ppermute | solution.py:845
  22.1 0.6 %collective-permute-done.6.refs_1_ = f32[16,256]{1,0:T(8,128)S(1)} collective-permute-done((f32[16,256]{1,0:T(8,128)S(1)}, f32[16,256]{1,0:T(8,128)S(1)}, u32[]{:S(2)}, u32[]{:S(2)}) %collective-permute-start.6) | collective-permute-done | bytes 16416 | tf_op jit(solution)/shard_map/ppermute | solution.py:845
  22.6 1.6 %update.3 = (f32[59,1024]{1,0:T(8,128)}, f32[59,1024]{1,0:T(8,128)}, f32[59,1024]{1,0:T(8,128)}) custom-call(f32[4,12]{1,0:T(4,128)S(1)} %copy-done.2, f32[59,1024]{1,0:T(8,128)S(1)} %get-tuple-element.24.params, f32[59,1024]{1,0:T(8,128)S(1)} %copy-done, f32[59,1024]{1,0:T(8,128)S(1)} %copy-done.1, ...), custom_call_target="tpu_custom_call", output_to_operand_aliasing={{0}: (6, {}), {1}: (7, {}), {2}: (8, {})} | custom-call | tf_op jit(solution)/shard_map/update/pallas_call | solution.py:820
  (1 shorter events, 0.0 us)
Async XLA Ops:
  1.7 3.1 %copy-start.2 = (f32[4,12]{1,0:T(4,128)S(1)}, f32[4,12]{1,0:T(4,128)}, u32[]{:S(2)}) copy-start(f32[4,12]{1,0:T(4,128)} %cams.7) | copy-start | bytes 580
  1.7 5.8 %collective-permute-start = (f32[8,512]{1,0:T(8,128)S(1)}, f32[8,512]{1,0:T(8,128)S(1)}, u32[]{:S(2)}, u32[]{:S(2)}) collective-permute-start(f32[8,512]{1,0:T(8,128)S(1)} %get-tuple-element.23.own.first), channel_id=1, source_target_pairs={{0,1},{1,0},{2,3},{3,2},{4,5},{5,4},{6,7},{7,6},{8,9},{9,8},{10,11... | collective-permute-start | bytes 49160 | tf_op jit(solution)/shard_map/ppermute | solution.py:845
  4.8 5.6 %copy-start.3 = (s32[2]{0:T(128)S(1)}, s32[2]{0:T(128)}, u32[]{:S(2)}) copy-start(s32[2]{0:T(128)} %tile_ids.3) | copy-start | bytes 28
  4.8 15.2 %copy-start.1 = (f32[59,1024]{1,0:T(8,128)S(1)}, f32[59,1024]{1,0:T(8,128)}, u32[]{:S(2)}) copy-start(f32[59,1024]{1,0:T(8,128)} %adam_v.3) | copy-start | bytes 724996
  5.5 14.5 %copy-start = (f32[59,1024]{1,0:T(8,128)S(1)}, f32[59,1024]{1,0:T(8,128)}, u32[]{:S(2)}) copy-start(f32[59,1024]{1,0:T(8,128)} %adam_m.3) | copy-start | bytes 724996
  5.5 4.6 %collective-permute-start.1 = (f32[24,256]{1,0:T(8,128)S(1)}, f32[24,256]{1,0:T(8,128)S(1)}, u32[]{:S(2)}, u32[]{:S(2)}) collective-permute-start(f32[24,256]{1,0:T(8,128)S(1)} %get-tuple-element.26), channel_id=1, source_target_pairs={{0,4},{4,0},{8,12},{12,8},{1,5},{5,1},{9,13},{13,9},{2,6},{6,2},{1... | collective-permute-start | bytes 73736 | tf_op jit(solution)/shard_map/ppermute | solution.py:845
  5.6 4.5 %collective-permute-start.2 = (f32[24,256]{1,0:T(8,128)S(1)}, f32[24,256]{1,0:T(8,128)S(1)}, u32[]{:S(2)}, u32[]{:S(2)}) collective-permute-start(f32[24,256]{1,0:T(8,128)S(1)} %get-tuple-element.27), channel_id=1, source_target_pairs={{0,8},{4,12},{8,0},{12,4},{1,9},{5,13},{9,1},{13,5},{2,10},{6,14},... | collective-permute-start | bytes 73736 | tf_op jit(solution)/shard_map/ppermute | solution.py:845
  7.2 3.3 %collective-permute-start.3 = (f32[24,256]{1,0:T(8,128)S(1)}, f32[24,256]{1,0:T(8,128)S(1)}, u32[]{:S(2)}, u32[]{:S(2)}) collective-permute-start(f32[24,256]{1,0:T(8,128)S(1)} %get-tuple-element.28), channel_id=1, source_target_pairs={{0,12},{4,8},{8,4},{12,0},{1,13},{5,9},{9,5},{13,1},{2,14},{6,10},... | collective-permute-start | bytes 73736 | tf_op jit(solution)/shard_map/ppermute | solution.py:845
  7.5 6.8 %collective-permute-start.4 = (f32[16,512]{1,0:T(8,128)S(1)}, f32[16,512]{1,0:T(8,128)S(1)}, u32[]{:S(2)}, u32[]{:S(2)}) collective-permute-start(f32[16,512]{1,0:T(8,128)S(1)} %join.1), channel_id=1, source_target_pairs={{0,2},{1,3},{2,0},{3,1},{4,6},{5,7},{6,4},{7,5},{8,10},{9,11},{10,... | collective-permute-start | bytes 98312 | tf_op jit(solution)/shard_map/ppermute | solution.py:845
  18.1 1.9 %collective-permute-start.7 = (f32[16,256]{1,0:T(8,128)S(1)}, f32[16,256]{1,0:T(8,128)S(1)}, u32[]{:S(2)}, u32[]{:S(2)}) collective-permute-start(f32[16,256]{1,0:T(8,128)S(1)} %get-tuple-element.35), channel_id=1, source_target_pairs={{0,4},{4,0},{8,12},{12,8},{1,5},{5,1},{9,13},{13,9},{2,6},{6,2},{1... | collective-permute-start | bytes 49160 | tf_op jit(solution)/shard_map/ppermute | solution.py:845
  18.3 3.7 %collective-permute-start.5 = (f32[16,256]{1,0:T(8,128)S(1)}, f32[16,256]{1,0:T(8,128)S(1)}, u32[]{:S(2)}, u32[]{:S(2)}) collective-permute-start(f32[16,256]{1,0:T(8,128)S(1)} %get-tuple-element.32), channel_id=1, source_target_pairs={{0,8},{4,12},{8,0},{12,4},{1,9},{5,13},{9,1},{13,5},{2,10},{6,14},... | collective-permute-start | bytes 49160 | tf_op jit(solution)/shard_map/ppermute | solution.py:845
  19.5 3.2 %collective-permute-start.6 = (f32[16,256]{1,0:T(8,128)S(1)}, f32[16,256]{1,0:T(8,128)S(1)}, u32[]{:S(2)}, u32[]{:S(2)}) collective-permute-start(f32[16,256]{1,0:T(8,128)S(1)} %get-tuple-element.33), channel_id=1, source_target_pairs={{0,12},{4,8},{8,4},{12,0},{1,13},{5,9},{9,5},{13,1},{2,14},{6,10},... | collective-permute-start | bytes 49160 | tf_op jit(solution)/shard_map/ppermute | solution.py:845

commit v19 on v17

--- a/solution.py
+++ b/solution.py
@@ -361,8 +361,8 @@
             (jax.ShapeDtypeStruct((count, columns // pieces), F32),) * pieces,
             [smem()] * 2 + [vmem()],
             [
-                pltpu.VMEM((features * slabs, LANES), F32),
-                pltpu.VMEM((count * slabs, LANES), F32),
+                pltpu.VMEM(((features + 8) * slabs, LANES), F32),
+                pltpu.VMEM((count * (slabs + 1), LANES), F32),
             ],
             (group.reshape(1), cameras, params),
         )
@@ -395,7 +395,7 @@
     halves = listed // LANES
     tiles_here = groups * tile_count
     spans = tiles_here * parts
-    slabs = rows.shape[0] // ROWS
+    slabs = rows.shape[0] // ROWS - 1
     side = TILE_SIDE
     first_col, first_row = tiles
 
@@ -478,7 +478,7 @@
             colour_s[24 * n + at : 24 * n + at + 8, here] = value
         hues.append(jnp.concatenate([high, low], axis=0).astype(BF16))
 
-    unroll, quad = 128, 4
+    unroll, quad = 16, 4
     steps = listed // unroll
 
     def forward(step, passed):
@@ -640,7 +640,7 @@
     row_of = lax.broadcasted_iota(jnp.int32, (8, LANES), 0)
     lane_of = lax.broadcasted_iota(jnp.int32, (8, LANES), 1)
     chunk = packets[0].shape[1]
-    for s in range(rows.shape[0] // ROWS):
+    for s in range(rows.shape[0] // ROWS - 1):
         total, ninth = pool_sum(s, info_s, *work[-2:])
         total = total + partial[0:8, s * LANES : (s + 1) * LANES]
         ninth = ninth + partial[8:9, s * LANES : (s + 1) * LANES]
@@ -710,10 +710,12 @@
             grad = grads[pl.ds(row * slabs + s, count, stride=slabs), :]
             moment = beta_one * adam_m[span, column(s)] + (1.0 - beta_one) * grad
             second = beta_two * adam_v[span, column(s)] + (1.0 - beta_two) * grad * grad
+            scaled = second * unbias
+            root = scaled * lax.rsqrt(scaled)
             made.at[1][here] = moment
             made.at[2][here] = second
             made.at[0][here] = params[span, column(s)] - rate * moment / (
-                jnp.sqrt(second * unbias) + adam_eps
+                root + adam_eps
             )
         if row % 16 == 8 or row + count == features:
             first = row // 16 * 16
@@ -757,14 +759,14 @@
     tiles = 2 * tile_count
     spans = tiles * pixels // LANES
     assert spans < LIST_STEP and tiles * listed // LANES == 8 and tiles == 4
-    return [pltpu.VMEM((listed * LIST_STEP, LANES), F32)] * 4 + [
+    return [pltpu.VMEM(((listed + 1) * LIST_STEP, LANES), F32)] * 4 + [
         pltpu.VMEM((2 * listed, spans * LANES), BF16),
-        pltpu.VMEM((listed // LANES, 8 * tiles, LANES), F32),
+        pltpu.VMEM((listed // LANES, 8 * tiles + 8, LANES), F32),
         pltpu.VMEM((8, tiles * listed), F32),
         pltpu.VMEM((24 * tiles, tiles * listed), F32),
-        pltpu.VMEM((listed // LANES, 8 * tiles, LANES), F32),
+        pltpu.VMEM((listed // LANES, 8 * tiles + 8, LANES), F32),
         pltpu.VMEM((8, LANES), jnp.int32),
-        pltpu.VMEM((listed // LANES, 8 * tiles, LANES), F32),
+        pltpu.VMEM((listed // LANES, 8 * tiles + 8, LANES), F32),
         pltpu.VMEM((8, LANES), F32),
     ]
 
@@ -779,11 +781,11 @@
         "near",
         (
             jax.ShapeDtypeStruct((3, own.shape[1]), F32),
-            jax.ShapeDtypeStruct((ROWS * slabs, LANES), F32),
+            jax.ShapeDtypeStruct((ROWS * (slabs + 1), LANES), F32),
             jax.ShapeDtypeStruct((ROWS, width), F32),
         ),
         [smem()] * 3 + [vmem()] * (2 + len(parts)),
-        [pltpu.VMEM((features * slabs, LANES), F32), pltpu.VMEM((2,) + own.shape, F32)]
+        [pltpu.VMEM(((features + 8) * slabs, LANES), F32), pltpu.VMEM((2,) + own.shape, F32)]
         + work_shapes(tile_count, pixels, listed),
         (tile_ids, cameras, where, own, other, *parts),
     )
@@ -824,9 +826,9 @@
         + [any_space()] * len(before),
         out_specs=(any_space(),) * 3,
         scratch_shapes=[
-            pltpu.VMEM((features * slabs, LANES), F32),
-            pltpu.VMEM((ROWS * slabs, LANES), F32),
-            pltpu.VMEM((features * slabs, LANES), F32),
+            pltpu.VMEM(((features + 8) * slabs, LANES), F32),
+            pltpu.VMEM(((ROWS + 1) * slabs, LANES), F32),
+            pltpu.VMEM(((features + 8) * slabs, LANES), F32),
             pltpu.VMEM((3, features, width), F32),
             pltpu.SemaphoreType.DMA((3, (features + 15) // 16)),
         ],

time: 24.9 us -> 24.7 us (level)
  transfers between devices with their start and end apart: 8 -> 8, of which waited for: 3 -> 3; matrix products, arithmetic and copies ran while one was open for 1% -> 1% of each run, Pallas kernels for 26% -> 25%
where the time goes in v19:
time: 24.7 us; the launch traced here: 24.6 us
  Pallas kernels  12.7 us (51%)
  starting transfers between devices  9.85 us (40%)
  waiting for transfers between devices  1 us (4%)
  between operations  0.71 us (3%)
    ppermute x8, starting transfers between devices, swap(): lax.ppermute(value, axis, [(k, k ^ d) for k in range(lax.axis_size(axis))])  9.85 us
    pallas_call x5, Pallas kernels, call(): pl.pallas_call(kernel, out_shape=out_shape, in_specs=in_specs, out_specs=...  9.58 us
    pallas_call x2, Pallas kernels, update(): pl.pallas_call(functools.partial(update_kernel, len(packets), len(before)...  3.17 us
    ppermute x8, waiting for transfers between devices, swap(): lax.ppermute(value, axis, [(k, k ^ d) for k in range(lax.axis_size(axis))])  1 us
  transfers between devices with their start and end apart: 8, of which 3 were waited for; matrix products, arithmetic and copies ran while one was open for 1% of the time, Pallas kernels for 25%

profile of v19, /device:TPU:0, one launch (start us, length us, event | category | flops | bytes accessed | tf_op | source)
XLA Modules:
  0.0 24.6 jit_solution(8774483633606387497)
XLA Ops:
  0.6 1.0 %pack.1 = (f32[8,512]{1,0:T(8,128)S(1)}, f32[59,1024]{1,0:T(8,128)S(1)}) custom-call(s32[1]{0:T(128)} %bitcast.2.where, s32[2,1,256]{2,1,0:T(1,128)} %bitcast.4, s32[2,256]{1,0:T(2,128)} %refs_1_.1, f32[3,512]{1,0:T(4,128)} %refs_2_.1, f32[59,1024]{1,0:T(8,128)} %refs_3_.1), custom_call_target="tpu_custom_call" | custom-call | tf_op jit(solution)/shard_map/pack/pallas_call | solution.py:747
  1.7 0.0 copy-start.2
  1.7 3.1 %collective-permute-start = (f32[8,512]{1,0:T(8,128)S(1)}, f32[8,512]{1,0:T(8,128)S(1)}, u32[]{:S(2)}, u32[]{:S(2)}) collective-permute-start(f32[8,512]{1,0:T(8,128)S(1)} %get-tuple-element.23.own.first), channel_id=1, source_target_pairs={{0,1},{1,0},{2,3},{3,2},{4,5},{5,4},{6,7},{7,6},{8,9},{9,8},{10,11... | collective-permute-start | bytes 49160 | tf_op jit(solution)/shard_map/ppermute | solution.py:847
  4.8 0.0 copy-done.2
  4.8 0.0 copy-start.3
  4.8 0.0 copy-start.1
  4.8 0.7 %cut.1 = (f32[24,256]{1,0:T(8,128)S(1)}, f32[24,256]{1,0:T(8,128)S(1)}, f32[24,256]{1,0:T(8,128)S(1)}, f32[24,256]{1,0:T(8,128)S(1)}) custom-call(s32[1]{0:T(128)} %bitcast.2.where, f32[4,12]{1,0:T(4,128)S(1)} %copy-done.2, f32[59,1024]{1,0:T(8,128)S(1)} %get-tuple-element.24.params), custom_call_target="tpu_custom_call" | custom-call | tf_op jit(solution)/shard_map/cut/pallas_call | solution.py:747
  5.5 0.0 copy-start
  5.5 0.1 collective-permute-start.1
  5.6 1.6 %collective-permute-start.2 = (f32[24,256]{1,0:T(8,128)S(1)}, f32[24,256]{1,0:T(8,128)S(1)}, u32[]{:S(2)}, u32[]{:S(2)}) collective-permute-start(f32[24,256]{1,0:T(8,128)S(1)} %get-tuple-element.27), channel_id=1, source_target_pairs={{0,8},{4,12},{8,0},{12,4},{1,9},{5,13},{9,1},{13,5},{2,10},{6,14},... | collective-permute-start | bytes 73736 | tf_op jit(solution)/shard_map/ppermute | solution.py:847
  7.2 0.3 %collective-permute-start.3 = (f32[24,256]{1,0:T(8,128)S(1)}, f32[24,256]{1,0:T(8,128)S(1)}, u32[]{:S(2)}, u32[]{:S(2)}) collective-permute-start(f32[24,256]{1,0:T(8,128)S(1)} %get-tuple-element.28), channel_id=1, source_target_pairs={{0,12},{4,8},{8,4},{12,0},{1,13},{5,9},{9,5},{13,1},{2,14},{6,10},... | collective-permute-start | bytes 73736 | tf_op jit(solution)/shard_map/ppermute | solution.py:847
  7.5 0.1 pad_add_fusion.2.where
  7.5 0.0 collective-permute-done.other.second
  7.5 2.6 %collective-permute-start.4 = (f32[16,512]{1,0:T(8,128)S(1)}, f32[16,512]{1,0:T(8,128)S(1)}, u32[]{:S(2)}, u32[]{:S(2)}) collective-permute-start(f32[16,512]{1,0:T(8,128)S(1)} %join.1), channel_id=1, source_target_pairs={{0,2},{1,3},{2,0},{3,1},{4,6},{5,7},{6,4},{7,5},{8,10},{9,11},{10,... | collective-permute-start | bytes 98312 | tf_op jit(solution)/shard_map/ppermute | solution.py:847
  10.2 0.1 pad_add_fusion.where
  10.2 0.0 collective-permute-done.1.refs_1_
  10.2 0.0 collective-permute-done.2.refs_2_
  10.2 0.2 collective-permute-done.3.refs_3_
  10.4 0.0 copy-done.3
  10.4 4.0 %near.1 = (f32[3,512]{1,0:T(4,128)}, f32[144,128]{1,0:T(8,128)S(1)}, f32[16,1024]{1,0:T(8,128)S(1)}) custom-call(s32[2]{0:T(128)S(1)} %copy-done.3, f32[4,12]{1,0:T(4,128)S(1)} %copy-done.2, s32[3]{0:T(128)S(1)} %pad_add_fusion.where, f32[8,512]{1,0:T(8,128)S(1)} %get-tuple-element.23.own.first, f32[8,512]{1,0:T(8,128)S(1)} %collective-permute-done.other.second, ...), custom_call_target="tpu_custom_call" | custom-call | tf_op jit(solution)/shard_map/near/pallas_call | solution.py:747
  14.4 0.0 collective-permute-done.4.infos
  14.4 3.9 %far.1 = (f32[16,256]{1,0:T(8,128)S(1)}, f32[16,256]{1,0:T(8,128)S(1)}, f32[16,256]{1,0:T(8,128)S(1)}, f32[16,256]{1,0:T(8,128)S(1)}) custom-call(s32[2]{0:T(128)S(1)} %copy-done.3, s32[3]{0:T(128)S(1)} %pad_add_fusion.where, f32[144,128]{1,0:T(8,128)S(1)} %get-tuple-element.30.rows, f32[16,1024]{1,0:T(8,128)S(1)} %get-tuple-element.31.partial, ...), custom_call_target="tpu_custom_call" | custom-call | tf_op jit(solution)/shard_map/far/pallas_call | solution.py:747
  18.2 1.4 %collective-permute-start.5 = (f32[16,256]{1,0:T(8,128)S(1)}, f32[16,256]{1,0:T(8,128)S(1)}, u32[]{:S(2)}, u32[]{:S(2)}) collective-permute-start(f32[16,256]{1,0:T(8,128)S(1)} %get-tuple-element.32), channel_id=1, source_target_pairs={{0,8},{4,12},{8,0},{12,4},{1,9},{5,13},{9,1},{13,5},{2,10},{6,14},... | collective-permute-start | bytes 49160 | tf_op jit(solution)/shard_map/ppermute | solution.py:847
  19.7 0.2 collective-permute-start.6
  19.8 0.6 %collective-permute-start.7 = (f32[16,256]{1,0:T(8,128)S(1)}, f32[16,256]{1,0:T(8,128)S(1)}, u32[]{:S(2)}, u32[]{:S(2)}) collective-permute-start(f32[16,256]{1,0:T(8,128)S(1)} %get-tuple-element.35), channel_id=1, source_target_pairs={{0,4},{4,0},{8,12},{12,8},{1,5},{5,1},{9,13},{13,9},{2,6},{6,2},{1... | collective-permute-start | bytes 49160 | tf_op jit(solution)/shard_map/ppermute | solution.py:847
  20.5 0.1 pad_add_fusion.1.where
  20.5 0.8 %collective-permute-done.7.refs_1_ = f32[16,256]{1,0:T(8,128)S(1)} collective-permute-done((f32[16,256]{1,0:T(8,128)S(1)}, f32[16,256]{1,0:T(8,128)S(1)}, u32[]{:S(2)}, u32[]{:S(2)}) %collective-permute-start.7) | collective-permute-done | bytes 16416 | tf_op jit(solution)/shard_map/ppermute | solution.py:847
  21.3 0.0 copy-done.1
  21.3 0.0 copy-done
  21.3 1.6 %update.2 = (f32[59,1024]{1,0:T(8,128)}, f32[59,1024]{1,0:T(8,128)}, f32[59,1024]{1,0:T(8,128)}) custom-call(s32[2]{0:T(128)S(1)} %pad_add_fusion.2.where, f32[4,12]{1,0:T(4,128)S(1)} %copy-done.2, f32[59,1024]{1,0:T(8,128)S(1)} %get-tuple-element.24.params, f32[59,1024]{1,0:T(8,128)S(1)} %copy-done, f32[59,1024]{1,0:T(8,128)S(1)} %copy-done.1, ...), custom_call_target="tpu_custom_call" | custom-call | tf_op jit(solution)/shard_map/update/pallas_call | solution.py:821
  22.9 0.0 collective-permute-done.5.refs_0_
  22.9 0.1 collective-permute-done.6.refs_1_
  23.0 1.6 %update.3 = (f32[59,1024]{1,0:T(8,128)}, f32[59,1024]{1,0:T(8,128)}, f32[59,1024]{1,0:T(8,128)}) custom-call(s32[2]{0:T(128)S(1)} %pad_add_fusion.1.where, f32[4,12]{1,0:T(4,128)S(1)} %copy-done.2, f32[59,1024]{1,0:T(8,128)S(1)} %get-tuple-element.24.params, f32[59,1024]{1,0:T(8,128)S(1)} %copy-done, ...), custom_call_target="tpu_custom_call", output_to_operand_aliasing={{0}: (7, {}), {1}: (8, {}), {2}: (9, {})} | custom-call | tf_op jit(solution)/shard_map/update/pallas_call | solution.py:821
  (1 shorter events, 0.0 us)
Async XLA Ops:
  1.7 3.1 %copy-start.2 = (f32[4,12]{1,0:T(4,128)S(1)}, f32[4,12]{1,0:T(4,128)}, u32[]{:S(2)}) copy-start(f32[4,12]{1,0:T(4,128)} %cams.7) | copy-start | bytes 580
  1.7 5.8 %collective-permute-start = (f32[8,512]{1,0:T(8,128)S(1)}, f32[8,512]{1,0:T(8,128)S(1)}, u32[]{:S(2)}, u32[]{:S(2)}) collective-permute-start(f32[8,512]{1,0:T(8,128)S(1)} %get-tuple-element.23.own.first), channel_id=1, source_target_pairs={{0,1},{1,0},{2,3},{3,2},{4,5},{5,4},{6,7},{7,6},{8,9},{9,8},{10,11... | collective-permute-start | bytes 49160 | tf_op jit(solution)/shard_map/ppermute | solution.py:847
  4.8 5.6 %copy-start.3 = (s32[2]{0:T(128)S(1)}, s32[2]{0:T(128)}, u32[]{:S(2)}) copy-start(s32[2]{0:T(128)} %tile_ids.3) | copy-start | bytes 28
  4.8 16.5 %copy-start.1 = (f32[59,1024]{1,0:T(8,128)S(1)}, f32[59,1024]{1,0:T(8,128)}, u32[]{:S(2)}) copy-start(f32[59,1024]{1,0:T(8,128)} %adam_v.3) | copy-start | bytes 724996
  5.5 15.8 %copy-start = (f32[59,1024]{1,0:T(8,128)S(1)}, f32[59,1024]{1,0:T(8,128)}, u32[]{:S(2)}) copy-start(f32[59,1024]{1,0:T(8,128)} %adam_m.3) | copy-start | bytes 724996
  5.5 4.7 %collective-permute-start.1 = (f32[24,256]{1,0:T(8,128)S(1)}, f32[24,256]{1,0:T(8,128)S(1)}, u32[]{:S(2)}, u32[]{:S(2)}) collective-permute-start(f32[24,256]{1,0:T(8,128)S(1)} %get-tuple-element.26), channel_id=1, source_target_pairs={{0,4},{4,0},{8,12},{12,8},{1,5},{5,1},{9,13},{13,9},{2,6},{6,2},{1... | collective-permute-start | bytes 73736 | tf_op jit(solution)/shard_map/ppermute | solution.py:847
  5.6 4.6 %collective-permute-start.2 = (f32[24,256]{1,0:T(8,128)S(1)}, f32[24,256]{1,0:T(8,128)S(1)}, u32[]{:S(2)}, u32[]{:S(2)}) collective-permute-start(f32[24,256]{1,0:T(8,128)S(1)} %get-tuple-element.27), channel_id=1, source_target_pairs={{0,8},{4,12},{8,0},{12,4},{1,9},{5,13},{9,1},{13,5},{2,10},{6,14},... | collective-permute-start | bytes 73736 | tf_op jit(solution)/shard_map/ppermute | solution.py:847
  7.2 3.3 %collective-permute-start.3 = (f32[24,256]{1,0:T(8,128)S(1)}, f32[24,256]{1,0:T(8,128)S(1)}, u32[]{:S(2)}, u32[]{:S(2)}) collective-permute-start(f32[24,256]{1,0:T(8,128)S(1)} %get-tuple-element.28), channel_id=1, source_target_pairs={{0,12},{4,8},{8,4},{12,0},{1,13},{5,9},{9,5},{13,1},{2,14},{6,10},... | collective-permute-start | bytes 73736 | tf_op jit(solution)/shard_map/ppermute | solution.py:847
  7.5 6.8 %collective-permute-start.4 = (f32[16,512]{1,0:T(8,128)S(1)}, f32[16,512]{1,0:T(8,128)S(1)}, u32[]{:S(2)}, u32[]{:S(2)}) collective-permute-start(f32[16,512]{1,0:T(8,128)S(1)} %join.1), channel_id=1, source_target_pairs={{0,2},{1,3},{2,0},{3,1},{4,6},{5,7},{6,4},{7,5},{8,10},{9,11},{10,... | collective-permute-start | bytes 98312 | tf_op jit(solution)/shard_map/ppermute | solution.py:847
  18.2 4.6 %collective-permute-start.5 = (f32[16,256]{1,0:T(8,128)S(1)}, f32[16,256]{1,0:T(8,128)S(1)}, u32[]{:S(2)}, u32[]{:S(2)}) collective-permute-start(f32[16,256]{1,0:T(8,128)S(1)} %get-tuple-element.32), channel_id=1, source_target_pairs={{0,8},{4,12},{8,0},{12,4},{1,9},{5,13},{9,1},{13,5},{2,10},{6,14},... | collective-permute-start | bytes 49160 | tf_op jit(solution)/shard_map/ppermute | solution.py:847
  19.7 3.3 %collective-permute-start.6 = (f32[16,256]{1,0:T(8,128)S(1)}, f32[16,256]{1,0:T(8,128)S(1)}, u32[]{:S(2)}, u32[]{:S(2)}) collective-permute-start(f32[16,256]{1,0:T(8,128)S(1)} %get-tuple-element.33), channel_id=1, source_target_pairs={{0,12},{4,8},{8,4},{12,0},{1,13},{5,9},{9,5},{13,1},{2,14},{6,10},... | collective-permute-start | bytes 49160 | tf_op jit(solution)/shard_map/ppermute | solution.py:847
  19.8 1.5 %collective-permute-start.7 = (f32[16,256]{1,0:T(8,128)S(1)}, f32[16,256]{1,0:T(8,128)S(1)}, u32[]{:S(2)}, u32[]{:S(2)}) collective-permute-start(f32[16,256]{1,0:T(8,128)S(1)} %get-tuple-element.35), channel_id=1, source_target_pairs={{0,4},{4,0},{8,12},{12,8},{1,5},{5,1},{9,13},{13,9},{2,6},{6,2},{1... | collective-permute-start | bytes 49160 | tf_op jit(solution)/shard_map/ppermute | solution.py:847

commit v20 on v19

--- a/solution.py
+++ b/solution.py
@@ -478,7 +478,7 @@
             colour_s[24 * n + at : 24 * n + at + 8, here] = value
         hues.append(jnp.concatenate([high, low], axis=0).astype(BF16))
 
-    unroll, quad = 16, 4
+    unroll, quad = 32, 4
     steps = listed // unroll
 
     def forward(step, passed):
@@ -710,12 +710,10 @@
             grad = grads[pl.ds(row * slabs + s, count, stride=slabs), :]
             moment = beta_one * adam_m[span, column(s)] + (1.0 - beta_one) * grad
             second = beta_two * adam_v[span, column(s)] + (1.0 - beta_two) * grad * grad
-            scaled = second * unbias
-            root = scaled * lax.rsqrt(scaled)
             made.at[1][here] = moment
             made.at[2][here] = second
             made.at[0][here] = params[span, column(s)] - rate * moment / (
-                root + adam_eps
+                jnp.sqrt(second * unbias) + adam_eps
             )
         if row % 16 == 8 or row + count == features:
             first = row // 16 * 16

time: 24.7 us -> 24.5 us (level)
    pallas_call x5, Pallas kernels: 9.58 us -> 9.32 us  [call(): pl.pallas_call(kernel, out_shape=out_shape, in_specs=in_specs, out_specs=...]
where the time goes in v20:
time: 24.5 us; the launch traced here: 24.3 us
  Pallas kernels  12.5 us (51%)
  starting transfers between devices  9.85 us (40%)
  waiting for transfers between devices  0.99 us (4%)
  between operations  0.71 us (3%)
    ppermute x8, starting transfers between devices, swap(): lax.ppermute(value, axis, [(k, k ^ d) for k in range(lax.axis_size(axis))])  9.85 us
    pallas_call x5, Pallas kernels, call(): pl.pallas_call(kernel, out_shape=out_shape, in_specs=in_specs, out_specs=...  9.32 us
    pallas_call x2, Pallas kernels, update(): pl.pallas_call(functools.partial(update_kernel, len(packets), len(before)...  3.18 us
    ppermute x8, waiting for transfers between devices, swap(): lax.ppermute(value, axis, [(k, k ^ d) for k in range(lax.axis_size(axis))])  0.99 us
  transfers between devices with their start and end apart: 8, of which 3 were waited for; matrix products, arithmetic and copies ran while one was open for 1% of the time, Pallas kernels for 25%

profile of v20, /device:TPU:0, one launch (start us, length us, event | category | flops | bytes accessed | tf_op | source)
XLA Modules:
  0.0 24.3 jit_solution(2685902632092277504)
XLA Ops:
  0.6 1.0 %pack.1 = (f32[8,512]{1,0:T(8,128)S(1)}, f32[59,1024]{1,0:T(8,128)S(1)}) custom-call(s32[1]{0:T(128)} %bitcast.2.where, s32[2,1,256]{2,1,0:T(1,128)} %bitcast.4, s32[2,256]{1,0:T(2,128)} %refs_1_.1, f32[3,512]{1,0:T(4,128)} %refs_2_.1, f32[59,1024]{1,0:T(8,128)} %refs_3_.1), custom_call_target="tpu_custom_call" | custom-call | tf_op jit(solution)/shard_map/pack/pallas_call | solution.py:745
  1.7 0.0 copy-start.2
  1.7 3.1 %collective-permute-start = (f32[8,512]{1,0:T(8,128)S(1)}, f32[8,512]{1,0:T(8,128)S(1)}, u32[]{:S(2)}, u32[]{:S(2)}) collective-permute-start(f32[8,512]{1,0:T(8,128)S(1)} %get-tuple-element.23.own.first), channel_id=1, source_target_pairs={{0,1},{1,0},{2,3},{3,2},{4,5},{5,4},{6,7},{7,6},{8,9},{9,8},{10,11... | collective-permute-start | bytes 49160 | tf_op jit(solution)/shard_map/ppermute | solution.py:845
  4.8 0.0 copy-done.2
  4.8 0.0 copy-start.3
  4.8 0.0 copy-start.1
  4.8 0.7 %cut.1 = (f32[24,256]{1,0:T(8,128)S(1)}, f32[24,256]{1,0:T(8,128)S(1)}, f32[24,256]{1,0:T(8,128)S(1)}, f32[24,256]{1,0:T(8,128)S(1)}) custom-call(s32[1]{0:T(128)} %bitcast.2.where, f32[4,12]{1,0:T(4,128)S(1)} %copy-done.2, f32[59,1024]{1,0:T(8,128)S(1)} %get-tuple-element.24.params), custom_call_target="tpu_custom_call" | custom-call | tf_op jit(solution)/shard_map/cut/pallas_call | solution.py:745
  5.5 0.0 copy-start
  5.5 0.1 collective-permute-start.1
  5.6 1.6 %collective-permute-start.2 = (f32[24,256]{1,0:T(8,128)S(1)}, f32[24,256]{1,0:T(8,128)S(1)}, u32[]{:S(2)}, u32[]{:S(2)}) collective-permute-start(f32[24,256]{1,0:T(8,128)S(1)} %get-tuple-element.27), channel_id=1, source_target_pairs={{0,8},{4,12},{8,0},{12,4},{1,9},{5,13},{9,1},{13,5},{2,10},{6,14},... | collective-permute-start | bytes 73736 | tf_op jit(solution)/shard_map/ppermute | solution.py:845
  7.2 0.3 %collective-permute-start.3 = (f32[24,256]{1,0:T(8,128)S(1)}, f32[24,256]{1,0:T(8,128)S(1)}, u32[]{:S(2)}, u32[]{:S(2)}) collective-permute-start(f32[24,256]{1,0:T(8,128)S(1)} %get-tuple-element.28), channel_id=1, source_target_pairs={{0,12},{4,8},{8,4},{12,0},{1,13},{5,9},{9,5},{13,1},{2,14},{6,10},... | collective-permute-start | bytes 73736 | tf_op jit(solution)/shard_map/ppermute | solution.py:845
  7.5 0.1 pad_add_fusion.2.where
  7.5 0.0 collective-permute-done.other.second
  7.5 2.6 %collective-permute-start.4 = (f32[16,512]{1,0:T(8,128)S(1)}, f32[16,512]{1,0:T(8,128)S(1)}, u32[]{:S(2)}, u32[]{:S(2)}) collective-permute-start(f32[16,512]{1,0:T(8,128)S(1)} %join.1), channel_id=1, source_target_pairs={{0,2},{1,3},{2,0},{3,1},{4,6},{5,7},{6,4},{7,5},{8,10},{9,11},{10,... | collective-permute-start | bytes 98312 | tf_op jit(solution)/shard_map/ppermute | solution.py:845
  10.2 0.1 pad_add_fusion.where
  10.2 0.0 collective-permute-done.1.refs_1_
  10.2 0.0 collective-permute-done.2.refs_2_
  10.2 0.2 collective-permute-done.3.refs_3_
  10.4 0.0 copy-done.3
  10.4 3.8 %near.1 = (f32[3,512]{1,0:T(4,128)}, f32[144,128]{1,0:T(8,128)S(1)}, f32[16,1024]{1,0:T(8,128)S(1)}) custom-call(s32[2]{0:T(128)S(1)} %copy-done.3, f32[4,12]{1,0:T(4,128)S(1)} %copy-done.2, s32[3]{0:T(128)S(1)} %pad_add_fusion.where, f32[8,512]{1,0:T(8,128)S(1)} %get-tuple-element.23.own.first, f32[8,512]{1,0:T(8,128)S(1)} %collective-permute-done.other.second, ...), custom_call_target="tpu_custom_call" | custom-call | tf_op jit(solution)/shard_map/near/pallas_call | solution.py:745
  14.2 0.0 collective-permute-done.4.infos
  14.2 3.7 %far.1 = (f32[16,256]{1,0:T(8,128)S(1)}, f32[16,256]{1,0:T(8,128)S(1)}, f32[16,256]{1,0:T(8,128)S(1)}, f32[16,256]{1,0:T(8,128)S(1)}) custom-call(s32[2]{0:T(128)S(1)} %copy-done.3, s32[3]{0:T(128)S(1)} %pad_add_fusion.where, f32[144,128]{1,0:T(8,128)S(1)} %get-tuple-element.30.rows, f32[16,1024]{1,0:T(8,128)S(1)} %get-tuple-element.31.partial, ...), custom_call_target="tpu_custom_call" | custom-call | tf_op jit(solution)/shard_map/far/pallas_call | solution.py:745
  18.0 1.4 %collective-permute-start.5 = (f32[16,256]{1,0:T(8,128)S(1)}, f32[16,256]{1,0:T(8,128)S(1)}, u32[]{:S(2)}, u32[]{:S(2)}) collective-permute-start(f32[16,256]{1,0:T(8,128)S(1)} %get-tuple-element.32), channel_id=1, source_target_pairs={{0,8},{4,12},{8,0},{12,4},{1,9},{5,13},{9,1},{13,5},{2,10},{6,14},... | collective-permute-start | bytes 49160 | tf_op jit(solution)/shard_map/ppermute | solution.py:845
  19.4 0.2 collective-permute-start.6
  19.6 0.6 %collective-permute-start.7 = (f32[16,256]{1,0:T(8,128)S(1)}, f32[16,256]{1,0:T(8,128)S(1)}, u32[]{:S(2)}, u32[]{:S(2)}) collective-permute-start(f32[16,256]{1,0:T(8,128)S(1)} %get-tuple-element.35), channel_id=1, source_target_pairs={{0,4},{4,0},{8,12},{12,8},{1,5},{5,1},{9,13},{13,9},{2,6},{6,2},{1... | collective-permute-start | bytes 49160 | tf_op jit(solution)/shard_map/ppermute | solution.py:845
  20.2 0.1 pad_add_fusion.1.where
  20.3 0.8 %collective-permute-done.7.refs_1_ = f32[16,256]{1,0:T(8,128)S(1)} collective-permute-done((f32[16,256]{1,0:T(8,128)S(1)}, f32[16,256]{1,0:T(8,128)S(1)}, u32[]{:S(2)}, u32[]{:S(2)}) %collective-permute-start.7) | collective-permute-done | bytes 16416 | tf_op jit(solution)/shard_map/ppermute | solution.py:845
  21.0 0.0 copy-done.1
  21.0 0.0 copy-done
  21.0 1.6 %update.2 = (f32[59,1024]{1,0:T(8,128)}, f32[59,1024]{1,0:T(8,128)}, f32[59,1024]{1,0:T(8,128)}) custom-call(s32[2]{0:T(128)S(1)} %pad_add_fusion.2.where, f32[4,12]{1,0:T(4,128)S(1)} %copy-done.2, f32[59,1024]{1,0:T(8,128)S(1)} %get-tuple-element.24.params, f32[59,1024]{1,0:T(8,128)S(1)} %copy-done, f32[59,1024]{1,0:T(8,128)S(1)} %copy-done.1, ...), custom_call_target="tpu_custom_call" | custom-call | tf_op jit(solution)/shard_map/update/pallas_call | solution.py:819
  22.6 0.0 collective-permute-done.5.refs_0_
  22.7 0.1 collective-permute-done.6.refs_1_
  22.7 1.6 %update.3 = (f32[59,1024]{1,0:T(8,128)}, f32[59,1024]{1,0:T(8,128)}, f32[59,1024]{1,0:T(8,128)}) custom-call(s32[2]{0:T(128)S(1)} %pad_add_fusion.1.where, f32[4,12]{1,0:T(4,128)S(1)} %copy-done.2, f32[59,1024]{1,0:T(8,128)S(1)} %get-tuple-element.24.params, f32[59,1024]{1,0:T(8,128)S(1)} %copy-done, ...), custom_call_target="tpu_custom_call", output_to_operand_aliasing={{0}: (7, {}), {1}: (8, {}), {2}: (9, {})} | custom-call | tf_op jit(solution)/shard_map/update/pallas_call | solution.py:819
  (1 shorter events, 0.0 us)
Async XLA Ops:
  1.7 3.1 %copy-start.2 = (f32[4,12]{1,0:T(4,128)S(1)}, f32[4,12]{1,0:T(4,128)}, u32[]{:S(2)}) copy-start(f32[4,12]{1,0:T(4,128)} %cams.7) | copy-start | bytes 580
  1.7 5.8 %collective-permute-start = (f32[8,512]{1,0:T(8,128)S(1)}, f32[8,512]{1,0:T(8,128)S(1)}, u32[]{:S(2)}, u32[]{:S(2)}) collective-permute-start(f32[8,512]{1,0:T(8,128)S(1)} %get-tuple-element.23.own.first), channel_id=1, source_target_pairs={{0,1},{1,0},{2,3},{3,2},{4,5},{5,4},{6,7},{7,6},{8,9},{9,8},{10,11... | collective-permute-start | bytes 49160 | tf_op jit(solution)/shard_map/ppermute | solution.py:845
  4.8 5.6 %copy-start.3 = (s32[2]{0:T(128)S(1)}, s32[2]{0:T(128)}, u32[]{:S(2)}) copy-start(s32[2]{0:T(128)} %tile_ids.3) | copy-start | bytes 28
  4.8 16.3 %copy-start.1 = (f32[59,1024]{1,0:T(8,128)S(1)}, f32[59,1024]{1,0:T(8,128)}, u32[]{:S(2)}) copy-start(f32[59,1024]{1,0:T(8,128)} %adam_v.3) | copy-start | bytes 724996
  5.5 15.5 %copy-start = (f32[59,1024]{1,0:T(8,128)S(1)}, f32[59,1024]{1,0:T(8,128)}, u32[]{:S(2)}) copy-start(f32[59,1024]{1,0:T(8,128)} %adam_m.3) | copy-start | bytes 724996
  5.5 4.7 %collective-permute-start.1 = (f32[24,256]{1,0:T(8,128)S(1)}, f32[24,256]{1,0:T(8,128)S(1)}, u32[]{:S(2)}, u32[]{:S(2)}) collective-permute-start(f32[24,256]{1,0:T(8,128)S(1)} %get-tuple-element.26), channel_id=1, source_target_pairs={{0,4},{4,0},{8,12},{12,8},{1,5},{5,1},{9,13},{13,9},{2,6},{6,2},{1... | collective-permute-start | bytes 73736 | tf_op jit(solution)/shard_map/ppermute | solution.py:845
  5.6 4.6 %collective-permute-start.2 = (f32[24,256]{1,0:T(8,128)S(1)}, f32[24,256]{1,0:T(8,128)S(1)}, u32[]{:S(2)}, u32[]{:S(2)}) collective-permute-start(f32[24,256]{1,0:T(8,128)S(1)} %get-tuple-element.27), channel_id=1, source_target_pairs={{0,8},{4,12},{8,0},{12,4},{1,9},{5,13},{9,1},{13,5},{2,10},{6,14},... | collective-permute-start | bytes 73736 | tf_op jit(solution)/shard_map/ppermute | solution.py:845
  7.2 3.3 %collective-permute-start.3 = (f32[24,256]{1,0:T(8,128)S(1)}, f32[24,256]{1,0:T(8,128)S(1)}, u32[]{:S(2)}, u32[]{:S(2)}) collective-permute-start(f32[24,256]{1,0:T(8,128)S(1)} %get-tuple-element.28), channel_id=1, source_target_pairs={{0,12},{4,8},{8,4},{12,0},{1,13},{5,9},{9,5},{13,1},{2,14},{6,10},... | collective-permute-start | bytes 73736 | tf_op jit(solution)/shard_map/ppermute | solution.py:845
  7.5 6.7 %collective-permute-start.4 = (f32[16,512]{1,0:T(8,128)S(1)}, f32[16,512]{1,0:T(8,128)S(1)}, u32[]{:S(2)}, u32[]{:S(2)}) collective-permute-start(f32[16,512]{1,0:T(8,128)S(1)} %join.1), channel_id=1, source_target_pairs={{0,2},{1,3},{2,0},{3,1},{4,6},{5,7},{6,4},{7,5},{8,10},{9,11},{10,... | collective-permute-start | bytes 98312 | tf_op jit(solution)/shard_map/ppermute | solution.py:845
  18.0 4.7 %collective-permute-start.5 = (f32[16,256]{1,0:T(8,128)S(1)}, f32[16,256]{1,0:T(8,128)S(1)}, u32[]{:S(2)}, u32[]{:S(2)}) collective-permute-start(f32[16,256]{1,0:T(8,128)S(1)} %get-tuple-element.32), channel_id=1, source_target_pairs={{0,8},{4,12},{8,0},{12,4},{1,9},{5,13},{9,1},{13,5},{2,10},{6,14},... | collective-permute-start | bytes 49160 | tf_op jit(solution)/shard_map/ppermute | solution.py:845
  19.4 3.3 %collective-permute-start.6 = (f32[16,256]{1,0:T(8,128)S(1)}, f32[16,256]{1,0:T(8,128)S(1)}, u32[]{:S(2)}, u32[]{:S(2)}) collective-permute-start(f32[16,256]{1,0:T(8,128)S(1)} %get-tuple-element.33), channel_id=1, source_target_pairs={{0,12},{4,8},{8,4},{12,0},{1,13},{5,9},{9,5},{13,1},{2,14},{6,10},... | collective-permute-start | bytes 49160 | tf_op jit(solution)/shard_map/ppermute | solution.py:845
  19.6 1.5 %collective-permute-start.7 = (f32[16,256]{1,0:T(8,128)S(1)}, f32[16,256]{1,0:T(8,128)S(1)}, u32[]{:S(2)}, u32[]{:S(2)}) collective-permute-start(f32[16,256]{1,0:T(8,128)S(1)} %get-tuple-element.35), channel_id=1, source_target_pairs={{0,4},{4,0},{8,12},{12,8},{1,5},{5,1},{9,13},{13,9},{2,6},{6,2},{1... | collective-permute-start | bytes 49160 | tf_op jit(solution)/shard_map/ppermute | solution.py:845

commit v21 on v20

--- a/solution.py
+++ b/solution.py
@@ -167,12 +167,40 @@
     return [mean_x, mean_y, *part["conic"], log_opacity]
 
 
-def project_pull(feat, cam, grads, put):
-    part = project_parts(feat, cam)
+def flatten(part, basis):
+    values = [value for row in part["rot"] for value in row]
+    values += [part[key] for key in ("inv", "u", "v", "finv", "rnorm", "rlen")]
+    values += list(part["rotor"]) + list(part["conic"]) + list(part["way"])
+    for key in ("turn", "screen", "axes", "wide"):
+        values += [value for row in part[key] for value in row]
+    return values + basis[1:]
+
+
+def unflatten(values):
+    values = iter(values)
+
+    def take(count):
+        return [next(values) for _ in range(count)]
+
+    def table(count):
+        return [take(3) for _ in range(count)]
+
+    part = dict(rot=table(3))
+    for key in ("inv", "u", "v", "finv", "rnorm", "rlen"):
+        part[key] = next(values)
+    part["rotor"], part["conic"], part["way"] = take(4), take(3), take(3)
+    for key, count in (("turn", 3), ("screen", 2), ("axes", 2), ("wide", 2)):
+        part[key] = table(count)
+    return part, [None] + take(15)
+
+
+READY = 9 + 6 + 4 + 3 + 3 + 9 + 6 + 6 + 6 + 15
+
+
+def project_pull(feat, part, basis, grads, put):
     g_mx, g_my, g_a, g_b, g_c, g_o = grads[:6]
     g_col = grads[6:9]
     way, rlen = part["way"], part["rlen"]
-    basis = sh_basis(*way)
     pulled = [None]
     for k in range(3):
         put(11 + 16 * k, sh_const[0] * g_col[k])
@@ -323,10 +351,10 @@
 
 
 def sent_rows(views):
-    return (11 + 3 * views + 7) // 8 * 8
-
-
-def cut_kernel(pieces, where, cams, params, *refs):
+    return (12 + 3 * views + 7) // 8 * 8
+
+
+def cut_kernel(pieces, where, tile_ids, cams, params, *refs):
     parts, (feats, rows) = refs[:pieces], refs[pieces:]
     views = cams.shape[0]
     count = sent_rows(views)
@@ -338,7 +366,8 @@
     values = [feat(f) for f in range(11)]
     for v in range(views):
         values += shade(feat, [cams[v, i] for i in range(12)])
-    values += [jnp.zeros((slabs, LANES), F32)] * (count - len(values))
+    values += [jnp.zeros((slabs, LANES), F32)] * (count - 1 - len(values))
+    values.append(jnp.full((slabs, LANES), (tile_ids[0] // (TILES_X * TILES_Y)).astype(F32), F32))
     for f, value in enumerate(values):
         rows[pl.ds(f, slabs, stride=count), :] = value
     each = slabs // pieces
@@ -350,7 +379,7 @@
             ]
 
 
-def cut(group, cameras, params, pieces):
+def cut(group, tile_ids, cameras, params, pieces):
     features, columns = params.shape
     slabs = columns // LANES
     count = sent_rows(cameras.shape[0])
@@ -359,12 +388,12 @@
             functools.partial(cut_kernel, pieces),
             "cut",
             (jax.ShapeDtypeStruct((count, columns // pieces), F32),) * pieces,
-            [smem()] * 2 + [vmem()],
+            [smem()] * 3 + [vmem()],
             [
                 pltpu.VMEM(((features + 8) * slabs, LANES), F32),
                 pltpu.VMEM((count * (slabs + 1), LANES), F32),
             ],
-            (group.reshape(1), cameras, params),
+            (group.reshape(1), tile_ids, cameras, params),
         )
     )
 
@@ -662,26 +691,23 @@
     out[half:, :] = second[...]
 
 
-def update_kernel(pieces, follows, where, cams, params, adam_m, adam_v, *refs):
-    packets, refs = refs[:pieces], refs[pieces + 3 * follows :]
-    sinks, (feats, rows, grads, made, sems) = refs[:3], refs[3:]
+def update_kernel(pieces, follows, prepares, ready, where, cams, params, adam_m, adam_v, *refs):
+    packets, refs = refs[:pieces], refs[pieces:]
+    senders, refs = refs[: pieces * prepares], refs[pieces * prepares :]
+    made_ready, refs = refs[: 2 * ready], refs[2 * ready + 3 * follows :]
+    sinks, refs = refs[:3], refs[3:]
+    next_ready, (feats, rows, grads, made, sems) = refs[: 2 * prepares], refs[2 * prepares :]
     features = params.shape[0]
     chunk = packets[0].shape[1]
     width = pieces * chunk
     slabs = width // LANES
-    start = (where[0] ^ where[1]) // pieces * pieces * chunk
+    place = where[0] ^ where[1]
+    start = place // pieces * pieces * chunk
     for d in range(pieces):
         for h in range(chunk // LANES):
-            slab = (where[0] ^ where[1] ^ d) % pieces * (chunk // LANES) + h
+            slab = (place ^ d) % pieces * (chunk // LANES) + h
             rows[pl.ds(slab, ROWS, stride=slabs), :] = packets[d][:, h * LANES : (h + 1) * LANES]
     pulled = [rows[f * slabs : (f + 1) * slabs, :] for f in range(10)]
-    view = pulled[9]
-    cam = []
-    for i in range(12):
-        value = jnp.full((slabs, LANES), cams[0, i], F32)
-        for v in range(1, cams.shape[0]):
-            value = jnp.where(view == float(v), cams[v, i], value)
-        cam.append(value)
 
     def put(f, value):
         grads[f * slabs : (f + 1) * slabs, :] = value
@@ -689,14 +715,29 @@
     def column(s):
         return pl.ds(pl.multiple_of(start + s * LANES, LANES), LANES)
 
-    for s in range(slabs):
-        for row in range(0, features, 8):
-            count = min(8, features - row)
-            feats[pl.ds(row * slabs + s, count, stride=slabs), :] = params[
-                row : row + count, column(s)
-            ]
+    def forward(first, held, view):
+        for s in range(slabs):
+            at = pl.ds(pl.multiple_of(first + s * LANES, LANES), LANES)
+            for row in range(0, features, 8):
+                count = min(8, features - row)
+                held[pl.ds(row * slabs + s, count, stride=slabs), :] = params[row : row + count, at]
+        cam = []
+        for i in range(12):
+            value = jnp.full((slabs, LANES), cams[0, i], F32)
+            for v in range(1, cams.shape[0]):
+                value = jnp.where(view == float(v), cams[v, i], value)
+            cam.append(value)
+        part = project_parts(lambda f: held[f * slabs : (f + 1) * slabs, :], cam)
+        return part, sh_basis(*part["way"])
+
+    if ready:
+        feats, saved = made_ready
+        part, basis = unflatten([saved[8 * i : 8 * i + slabs, :] for i in range(READY)])
+    else:
+        part, basis = forward(start, feats, pulled[9])
     project_pull(
-        lambda f: feats[f * slabs : (f + 1) * slabs, :], cam, pulled[2:8] + pulled[:2] + pulled[8:9], put
+        lambda f: feats[f * slabs : (f + 1) * slabs, :],
+        part, basis, pulled[2:8] + pulled[:2] + pulled[8:9], put,
     )
     rate = learn_rate / (1.0 - beta_one**adam_steps)
     unbias = 1.0 / (1.0 - beta_two**adam_steps)
@@ -725,6 +766,17 @@
                 )
                 store.start()
                 stores.append(store)
+    if prepares:
+        held, saved = next_ready
+        place = place ^ pieces
+        for d in range(pieces):
+            for h in range(chunk // LANES):
+                slab = (place ^ d) % pieces * (chunk // LANES) + h
+                last = senders[d].shape[0] - 1
+                rows[pl.ds(slab, 1), :] = senders[d][last : last + 1, h * LANES : (h + 1) * LANES]
+        part, basis = forward(place // pieces * pieces * chunk, held, rows[:slabs, :])
+        for i, value in enumerate(flatten(part, basis)):
+            saved[8 * i : 8 * i + slabs, :] = value
     for store in stores:
         store.wait()
 
@@ -810,23 +862,27 @@
     )[0]
 
 
-def update(own, first, cameras, params, adam_m, adam_v, packets, before):
+def update(own, first, cameras, params, adam_m, adam_v, packets, before, senders, ready):
     features = params.shape[0]
     width = sum(packet.shape[1] for packet in packets)
     slabs = width // LANES
     shape = jax.ShapeDtypeStruct(params.shape, F32)
-    at = 5 + len(packets)
-    return pl.pallas_call(
-        functools.partial(update_kernel, len(packets), len(before) > 0),
-        out_shape=(shape, shape, shape),
+    by_feature = ((features + 8) * slabs, LANES)
+    prepares = len(senders) > 0
+    at = 5 + len(packets) + len(senders) + len(ready)
+    out = pl.pallas_call(
+        functools.partial(update_kernel, len(packets), len(before) > 0, prepares, len(ready) > 0),
+        out_shape=(shape, shape, shape)
+        + (jax.ShapeDtypeStruct(by_feature, F32), jax.ShapeDtypeStruct((8 * READY, LANES), F32))
+        * prepares,
         in_specs=[smem()] * 2
-        + [vmem()] * (3 + len(packets))
+        + [vmem()] * (3 + len(packets) + len(senders) + len(ready))
         + [any_space()] * len(before),
-        out_specs=(any_space(),) * 3,
+        out_specs=(any_space(),) * 3 + (vmem(),) * (2 * prepares),
         scratch_shapes=[
-            pltpu.VMEM(((features + 8) * slabs, LANES), F32),
+            pltpu.VMEM(by_feature, F32),
             pltpu.VMEM(((ROWS + 1) * slabs, LANES), F32),
-            pltpu.VMEM(((features + 8) * slabs, LANES), F32),
+            pltpu.VMEM(by_feature, F32),
             pltpu.VMEM((3, features, width), F32),
             pltpu.SemaphoreType.DMA((3, (features + 15) // 16)),
         ],
@@ -835,8 +891,9 @@
         name="update",
     )(
         jnp.stack([own, jnp.int32(first)]).astype(jnp.int32),
-        cameras, params, adam_m, adam_v, *packets, *before,
-    )
+        cameras, params, adam_m, adam_v, *packets, *senders, *ready, *before,
+    )
+    return out[:3], out[3:]
 
 
 def swap(value, axis, d):
@@ -859,7 +916,7 @@
     blocks = along // team
 
     info, params = pack(group, params, target, hit_shard, hit_local, shards)
-    parts = cut(group, cameras, params, shards if aligned else 1)
+    parts = cut(group, tile_ids, cameras, params, shards if aligned else 1)
     if not aligned:
         parts = [
             lax.dynamic_slice_in_dim(parts[0], (group ^ d) * chunk, chunk, axis=1)
@@ -883,11 +940,13 @@
     else:
         packets = [jnp.stack(packets)[jnp.arange(shards) ^ group].transpose(1, 0, 2).reshape(ROWS, -1)]
         own = jnp.int32(0)
-    made = ()
+    made = ready = ()
     count = max(1, len(packets) // 2)
     for first in range(0, len(packets), count):
-        made = update(
-            own, first, cameras, params, adam_m, adam_v, packets[first : first + count], made
+        known = first == 0 and len(packets) == 2 * count and blocks == 1
+        made, ready = update(
+            own, first, cameras, params, adam_m, adam_v, packets[first : first + count], made,
+            parts[count:] if known else [], ready,
         )
     new_params, new_m, new_v = made
     return (rendered, new_params, new_m, new_v)

time: 24.5 us -> 24.4 us (level)
  no operation moved by 1% of the time
where the time goes in v21:
time: 24.4 us; the launch traced here: 24.2 us
  Pallas kernels  12.4 us (51%)
  starting transfers between devices  9.85 us (40%)
  waiting for transfers between devices  1 us (4%)
  between operations  0.72 us (3%)
    ppermute x8, starting transfers between devices, swap(): lax.ppermute(value, axis, [(k, k ^ d) for k in range(lax.axis_size(axis))])  9.85 us
    pallas_call x5, Pallas kernels, call(): pl.pallas_call(kernel, out_shape=out_shape, in_specs=in_specs, out_specs=...  9.32 us
    pallas_call x2, Pallas kernels, update(): pl.pallas_call(functools.partial(update_kernel, len(packets), len(before)...  3.1 us
    ppermute x8, waiting for transfers between devices, swap(): lax.ppermute(value, axis, [(k, k ^ d) for k in range(lax.axis_size(axis))])  1 us
  transfers between devices with their start and end apart: 8, of which 3 were waited for; matrix products, arithmetic and copies ran while one was open for 1% of the time, Pallas kernels for 25%

profile of v21, /device:TPU:0, one launch (start us, length us, event | category | flops | bytes accessed | tf_op | source)
XLA Modules:
  0.0 24.2 jit_solution(3768341482502312222)
XLA Ops:
  0.6 1.0 %pack.1 = (f32[8,512]{1,0:T(8,128)S(1)}, f32[59,1024]{1,0:T(8,128)S(1)}) custom-call(s32[1]{0:T(128)} %bitcast.2.where, s32[2,1,256]{2,1,0:T(1,128)} %bitcast.4, s32[2,256]{1,0:T(2,128)} %refs_1_.1, f32[3,512]{1,0:T(4,128)} %refs_2_.1, f32[59,1024]{1,0:T(8,128)} %refs_3_.1), custom_call_target="tpu_custom_call" | custom-call | tf_op jit(solution)/shard_map/pack/pallas_call | solution.py:797
  1.7 0.0 copy-start.2
  1.7 0.0 copy-start.3
  1.7 3.1 %collective-permute-start = (f32[8,512]{1,0:T(8,128)S(1)}, f32[8,512]{1,0:T(8,128)S(1)}, u32[]{:S(2)}, u32[]{:S(2)}) collective-permute-start(f32[8,512]{1,0:T(8,128)S(1)} %get-tuple-element.25.own.first), channel_id=1, source_target_pairs={{0,1},{1,0},{2,3},{3,2},{4,5},{5,4},{6,7},{7,6},{8,9},{9,8},{10,11... | collective-permute-start | bytes 49160 | tf_op jit(solution)/shard_map/ppermute | solution.py:902
  4.8 0.0 copy-done.2
  4.8 0.0 copy-done.3
  4.8 0.0 copy-start.1
  4.8 0.7 %cut.1 = (f32[24,256]{1,0:T(8,128)S(1)}, f32[24,256]{1,0:T(8,128)S(1)}, f32[24,256]{1,0:T(8,128)S(1)}, f32[24,256]{1,0:T(8,128)S(1)}) custom-call(s32[1]{0:T(128)} %bitcast.2.where, s32[2]{0:T(128)S(1)} %copy-done.3, f32[4,12]{1,0:T(4,128)S(1)} %copy-done.2, f32[59,1024]{1,0:T(8,128)S(1)} %get-tuple-element.26.params), custom_call_target="tpu_custom_call" | custom-call | tf_op jit(solution)/shard_map/cut/pallas_call | solution.py:797
  5.5 0.0 copy-start
  5.5 0.1 collective-permute-start.1
  5.6 1.6 %collective-permute-start.2 = (f32[24,256]{1,0:T(8,128)S(1)}, f32[24,256]{1,0:T(8,128)S(1)}, u32[]{:S(2)}, u32[]{:S(2)}) collective-permute-start(f32[24,256]{1,0:T(8,128)S(1)} %get-tuple-element.29), channel_id=1, source_target_pairs={{0,8},{4,12},{8,0},{12,4},{1,9},{5,13},{9,1},{13,5},{2,10},{6,14},... | collective-permute-start | bytes 73736 | tf_op jit(solution)/shard_map/ppermute | solution.py:902
  7.2 0.3 %collective-permute-start.3 = (f32[24,256]{1,0:T(8,128)S(1)}, f32[24,256]{1,0:T(8,128)S(1)}, u32[]{:S(2)}, u32[]{:S(2)}) collective-permute-start(f32[24,256]{1,0:T(8,128)S(1)} %get-tuple-element.30), channel_id=1, source_target_pairs={{0,12},{4,8},{8,4},{12,0},{1,13},{5,9},{9,5},{13,1},{2,14},{6,10},... | collective-permute-start | bytes 73736 | tf_op jit(solution)/shard_map/ppermute | solution.py:902
  7.5 0.1 pad_add_fusion.2.where
  7.6 0.0 collective-permute-done.other.second
  7.6 2.6 %collective-permute-start.4 = (f32[16,512]{1,0:T(8,128)S(1)}, f32[16,512]{1,0:T(8,128)S(1)}, u32[]{:S(2)}, u32[]{:S(2)}) collective-permute-start(f32[16,512]{1,0:T(8,128)S(1)} %join.1), channel_id=1, source_target_pairs={{0,2},{1,3},{2,0},{3,1},{4,6},{5,7},{6,4},{7,5},{8,10},{9,11},{10,... | collective-permute-start | bytes 98312 | tf_op jit(solution)/shard_map/ppermute | solution.py:902
  10.2 0.1 pad_add_fusion.where
  10.3 0.0 collective-permute-done.1.refs_1_
  10.3 0.0 collective-permute-done.2.refs_2_
  10.3 0.2 collective-permute-done.3.refs_3_
  10.4 3.8 %near.1 = (f32[3,512]{1,0:T(4,128)}, f32[144,128]{1,0:T(8,128)S(1)}, f32[16,1024]{1,0:T(8,128)S(1)}) custom-call(s32[2]{0:T(128)S(1)} %copy-done.3, f32[4,12]{1,0:T(4,128)S(1)} %copy-done.2, s32[3]{0:T(128)S(1)} %pad_add_fusion.where, f32[8,512]{1,0:T(8,128)S(1)} %get-tuple-element.25.own.first, f32[8,512]{1,0:T(8,128)S(1)} %collective-permute-done.other.second, ...), custom_call_target="tpu_custom_call" | custom-call | tf_op jit(solution)/shard_map/near/pallas_call | solution.py:797
  14.2 0.0 collective-permute-done.4.infos
  14.3 3.7 %far.1 = (f32[16,256]{1,0:T(8,128)S(1)}, f32[16,256]{1,0:T(8,128)S(1)}, f32[16,256]{1,0:T(8,128)S(1)}, f32[16,256]{1,0:T(8,128)S(1)}) custom-call(s32[2]{0:T(128)S(1)} %copy-done.3, s32[3]{0:T(128)S(1)} %pad_add_fusion.where, f32[144,128]{1,0:T(8,128)S(1)} %get-tuple-element.32.rows, f32[16,1024]{1,0:T(8,128)S(1)} %get-tuple-element.33.partial, ...), custom_call_target="tpu_custom_call" | custom-call | tf_op jit(solution)/shard_map/far/pallas_call | solution.py:797
  18.0 1.4 %collective-permute-start.5 = (f32[16,256]{1,0:T(8,128)S(1)}, f32[16,256]{1,0:T(8,128)S(1)}, u32[]{:S(2)}, u32[]{:S(2)}) collective-permute-start(f32[16,256]{1,0:T(8,128)S(1)} %get-tuple-element.34), channel_id=1, source_target_pairs={{0,8},{4,12},{8,0},{12,4},{1,9},{5,13},{9,1},{13,5},{2,10},{6,14},... | collective-permute-start | bytes 49160 | tf_op jit(solution)/shard_map/ppermute | solution.py:902
  19.4 0.2 collective-permute-start.6
  19.6 0.6 %collective-permute-start.7 = (f32[16,256]{1,0:T(8,128)S(1)}, f32[16,256]{1,0:T(8,128)S(1)}, u32[]{:S(2)}, u32[]{:S(2)}) collective-permute-start(f32[16,256]{1,0:T(8,128)S(1)} %get-tuple-element.37), channel_id=1, source_target_pairs={{0,4},{4,0},{8,12},{12,8},{1,5},{5,1},{9,13},{13,9},{2,6},{6,2},{1... | collective-permute-start | bytes 49160 | tf_op jit(solution)/shard_map/ppermute | solution.py:902
  20.2 0.1 pad_add_fusion.1.where
  20.3 0.8 %collective-permute-done.7.refs_1_ = f32[16,256]{1,0:T(8,128)S(1)} collective-permute-done((f32[16,256]{1,0:T(8,128)S(1)}, f32[16,256]{1,0:T(8,128)S(1)}, u32[]{:S(2)}, u32[]{:S(2)}) %collective-permute-start.7) | collective-permute-done | bytes 16416 | tf_op jit(solution)/shard_map/ppermute | solution.py:902
  21.1 0.0 copy-done.1
  21.1 0.0 copy-done
  21.1 1.6 %update.2 = (f32[59,1024]{1,0:T(8,128)}, f32[59,1024]{1,0:T(8,128)}, f32[59,1024]{1,0:T(8,128)}, f32[268,128]{1,0:T(8,128)S(1)}, f32[536,128]{1,0:T(8,128)S(1)}) custom-call(s32[2]{0:T(128)S(1)} %pad_add_fusion.2.where, f32[4,12]{1,0:T(4,128)S(1)} %copy-done.2, f32[59,1024]{1,0:T(8,128)S(1)} %get-tuple-element.26.params, f32[59,1024]{1,0:T(8,128)S(1)} %copy-done, ...), custom_call_target="tpu_custom_call" | custom-call | tf_op jit(solution)/shard_map/update/pallas_call | solution.py:873
  22.6 0.0 collective-permute-done.5.refs_0_
  22.7 0.1 collective-permute-done.6.refs_1_
  22.7 1.5 %update.3 = (f32[59,1024]{1,0:T(8,128)}, f32[59,1024]{1,0:T(8,128)}, f32[59,1024]{1,0:T(8,128)}) custom-call(s32[2]{0:T(128)S(1)} %pad_add_fusion.1.where, f32[4,12]{1,0:T(4,128)S(1)} %copy-done.2, f32[59,1024]{1,0:T(8,128)S(1)} %get-tuple-element.26.params, f32[59,1024]{1,0:T(8,128)S(1)} %copy-done, ...), custom_call_target="tpu_custom_call", output_to_operand_aliasing={{0}: (9, {}), {1}: (10, {}), {2}: (11, {})} | custom-call | tf_op jit(solution)/shard_map/update/pallas_call | solution.py:873
  (1 shorter events, 0.0 us)
Async XLA Ops:
  1.7 3.1 %copy-start.2 = (f32[4,12]{1,0:T(4,128)S(1)}, f32[4,12]{1,0:T(4,128)}, u32[]{:S(2)}) copy-start(f32[4,12]{1,0:T(4,128)} %cams.7) | copy-start | bytes 580
  1.7 3.1 %copy-start.3 = (s32[2]{0:T(128)S(1)}, s32[2]{0:T(128)}, u32[]{:S(2)}) copy-start(s32[2]{0:T(128)} %tile_ids.5) | copy-start | bytes 28
  1.7 5.9 %collective-permute-start = (f32[8,512]{1,0:T(8,128)S(1)}, f32[8,512]{1,0:T(8,128)S(1)}, u32[]{:S(2)}, u32[]{:S(2)}) collective-permute-start(f32[8,512]{1,0:T(8,128)S(1)} %get-tuple-element.25.own.first), channel_id=1, source_target_pairs={{0,1},{1,0},{2,3},{3,2},{4,5},{5,4},{6,7},{7,6},{8,9},{9,8},{10,11... | collective-permute-start | bytes 49160 | tf_op jit(solution)/shard_map/ppermute | solution.py:902
  4.8 16.3 %copy-start.1 = (f32[59,1024]{1,0:T(8,128)S(1)}, f32[59,1024]{1,0:T(8,128)}, u32[]{:S(2)}) copy-start(f32[59,1024]{1,0:T(8,128)} %adam_v.3) | copy-start | bytes 724996
  5.5 15.5 %copy-start = (f32[59,1024]{1,0:T(8,128)S(1)}, f32[59,1024]{1,0:T(8,128)}, u32[]{:S(2)}) copy-start(f32[59,1024]{1,0:T(8,128)} %adam_m.3) | copy-start | bytes 724996
  5.5 4.7 %collective-permute-start.1 = (f32[24,256]{1,0:T(8,128)S(1)}, f32[24,256]{1,0:T(8,128)S(1)}, u32[]{:S(2)}, u32[]{:S(2)}) collective-permute-start(f32[24,256]{1,0:T(8,128)S(1)} %get-tuple-element.28), channel_id=1, source_target_pairs={{0,4},{4,0},{8,12},{12,8},{1,5},{5,1},{9,13},{13,9},{2,6},{6,2},{1... | collective-permute-start | bytes 73736 | tf_op jit(solution)/shard_map/ppermute | solution.py:902
  5.6 4.6 %collective-permute-start.2 = (f32[24,256]{1,0:T(8,128)S(1)}, f32[24,256]{1,0:T(8,128)S(1)}, u32[]{:S(2)}, u32[]{:S(2)}) collective-permute-start(f32[24,256]{1,0:T(8,128)S(1)} %get-tuple-element.29), channel_id=1, source_target_pairs={{0,8},{4,12},{8,0},{12,4},{1,9},{5,13},{9,1},{13,5},{2,10},{6,14},... | collective-permute-start | bytes 73736 | tf_op jit(solution)/shard_map/ppermute | solution.py:902
  7.2 3.3 %collective-permute-start.3 = (f32[24,256]{1,0:T(8,128)S(1)}, f32[24,256]{1,0:T(8,128)S(1)}, u32[]{:S(2)}, u32[]{:S(2)}) collective-permute-start(f32[24,256]{1,0:T(8,128)S(1)} %get-tuple-element.30), channel_id=1, source_target_pairs={{0,12},{4,8},{8,4},{12,0},{1,13},{5,9},{9,5},{13,1},{2,14},{6,10},... | collective-permute-start | bytes 73736 | tf_op jit(solution)/shard_map/ppermute | solution.py:902
  7.6 6.7 %collective-permute-start.4 = (f32[16,512]{1,0:T(8,128)S(1)}, f32[16,512]{1,0:T(8,128)S(1)}, u32[]{:S(2)}, u32[]{:S(2)}) collective-permute-start(f32[16,512]{1,0:T(8,128)S(1)} %join.1), channel_id=1, source_target_pairs={{0,2},{1,3},{2,0},{3,1},{4,6},{5,7},{6,4},{7,5},{8,10},{9,11},{10,... | collective-permute-start | bytes 98312 | tf_op jit(solution)/shard_map/ppermute | solution.py:902
  18.0 4.6 %collective-permute-start.5 = (f32[16,256]{1,0:T(8,128)S(1)}, f32[16,256]{1,0:T(8,128)S(1)}, u32[]{:S(2)}, u32[]{:S(2)}) collective-permute-start(f32[16,256]{1,0:T(8,128)S(1)} %get-tuple-element.34), channel_id=1, source_target_pairs={{0,8},{4,12},{8,0},{12,4},{1,9},{5,13},{9,1},{13,5},{2,10},{6,14},... | collective-permute-start | bytes 49160 | tf_op jit(solution)/shard_map/ppermute | solution.py:902
  19.4 3.3 %collective-permute-start.6 = (f32[16,256]{1,0:T(8,128)S(1)}, f32[16,256]{1,0:T(8,128)S(1)}, u32[]{:S(2)}, u32[]{:S(2)}) collective-permute-start(f32[16,256]{1,0:T(8,128)S(1)} %get-tuple-element.35), channel_id=1, source_target_pairs={{0,12},{4,8},{8,4},{12,0},{1,13},{5,9},{9,5},{13,1},{2,14},{6,10},... | collective-permute-start | bytes 49160 | tf_op jit(solution)/shard_map/ppermute | solution.py:902
  19.6 1.5 %collective-permute-start.7 = (f32[16,256]{1,0:T(8,128)S(1)}, f32[16,256]{1,0:T(8,128)S(1)}, u32[]{:S(2)}, u32[]{:S(2)}) collective-permute-start(f32[16,256]{1,0:T(8,128)S(1)} %get-tuple-element.37), channel_id=1, source_target_pairs={{0,4},{4,0},{8,12},{12,8},{1,5},{5,1},{9,13},{13,9},{2,6},{6,2},{1... | collective-permute-start | bytes 49160 | tf_op jit(solution)/shard_map/ppermute | solution.py:902

commit v22 on v21

--- a/solution.py
+++ b/solution.py
@@ -691,18 +691,31 @@
     out[half:, :] = second[...]
 
 
-def update_kernel(pieces, follows, prepares, ready, where, cams, params, adam_m, adam_v, *refs):
+def update_kernel(pieces, final, follows, prepares, ready, where, cams, params, adam_m, adam_v, *refs):
     packets, refs = refs[:pieces], refs[pieces:]
     senders, refs = refs[: pieces * prepares], refs[pieces * prepares :]
-    made_ready, refs = refs[: 2 * ready], refs[2 * ready + 3 * follows :]
-    sinks, refs = refs[:3], refs[3:]
-    next_ready, (feats, rows, grads, made, sems) = refs[: 2 * prepares], refs[2 * prepares :]
+    made_ready, refs = refs[: 2 * ready], refs[2 * ready :]
+    earlier, refs = refs[:follows], refs[follows:]
+    if final:
+        sinks, (feats, rows, grads, made, sems) = refs[:3], refs[3:]
+    else:
+        made, refs = refs[0], refs[1:]
+        next_ready, (feats, rows, grads) = refs[: 2 * prepares], refs[2 * prepares :]
     features = params.shape[0]
     chunk = packets[0].shape[1]
     width = pieces * chunk
     slabs = width // LANES
     place = where[0] ^ where[1]
     start = place // pieces * pieces * chunk
+    stores = []
+    if follows:
+        other = pl.ds(pl.multiple_of((place ^ pieces) // pieces * pieces * chunk, LANES), width)
+        for k in range(3):
+            store = pltpu.make_async_copy(
+                earlier[0].at[k], sinks[k].at[:, other], sems.at[k, (features + 15) // 16]
+            )
+            store.start()
+            stores.append(store)
     for d in range(pieces):
         for h in range(chunk // LANES):
             slab = (place ^ d) % pieces * (chunk // LANES) + h
@@ -741,7 +754,6 @@
     )
     rate = learn_rate / (1.0 - beta_one**adam_steps)
     unbias = 1.0 / (1.0 - beta_two**adam_steps)
-    stores = []
     order = list(range(16, features, 8)) + [0, 8]
     for row in order:
         count = min(8, features - row)
@@ -756,7 +768,7 @@
             made.at[0][here] = params[span, column(s)] - rate * moment / (
                 jnp.sqrt(second * unbias) + adam_eps
             )
-        if row % 16 == 8 or row + count == features:
+        if final and (row % 16 == 8 or row + count == features):
             first = row // 16 * 16
             span = pl.ds(first, row + count - first)
             columns = pl.ds(pl.multiple_of(start, LANES), width)
@@ -862,38 +874,48 @@
     )[0]
 
 
-def update(own, first, cameras, params, adam_m, adam_v, packets, before, senders, ready):
+def update(own, first, cameras, params, adam_m, adam_v, packets, earlier, senders, ready, final):
     features = params.shape[0]
     width = sum(packet.shape[1] for packet in packets)
     slabs = width // LANES
     shape = jax.ShapeDtypeStruct(params.shape, F32)
     by_feature = ((features + 8) * slabs, LANES)
     prepares = len(senders) > 0
-    at = 5 + len(packets) + len(senders) + len(ready)
-    out = pl.pallas_call(
-        functools.partial(update_kernel, len(packets), len(before) > 0, prepares, len(ready) > 0),
-        out_shape=(shape, shape, shape)
-        + (jax.ShapeDtypeStruct(by_feature, F32), jax.ShapeDtypeStruct((8 * READY, LANES), F32))
-        * prepares,
-        in_specs=[smem()] * 2
-        + [vmem()] * (3 + len(packets) + len(senders) + len(ready))
-        + [any_space()] * len(before),
-        out_specs=(any_space(),) * 3 + (vmem(),) * (2 * prepares),
-        scratch_shapes=[
-            pltpu.VMEM(by_feature, F32),
-            pltpu.VMEM(((ROWS + 1) * slabs, LANES), F32),
-            pltpu.VMEM(by_feature, F32),
-            pltpu.VMEM((3, features, width), F32),
-            pltpu.SemaphoreType.DMA((3, (features + 15) // 16)),
-        ],
-        input_output_aliases={at + k: k for k in range(len(before))},
-        compiler_params=pltpu.CompilerParams(vmem_limit_bytes=32 * 1024 * 1024),
-        name="update",
-    )(
-        jnp.stack([own, jnp.int32(first)]).astype(jnp.int32),
-        cameras, params, adam_m, adam_v, *packets, *senders, *ready, *before,
-    )
-    return out[:3], out[3:]
+    scratch = [
+        pltpu.VMEM(by_feature, F32),
+        pltpu.VMEM(((ROWS + 1) * slabs, LANES), F32),
+        pltpu.VMEM(by_feature, F32),
+    ]
+    results = (3, features, width)
+    if final:
+        out_shape, out_specs = (shape, shape, shape), (any_space(),) * 3
+        scratch += [
+            pltpu.VMEM(results, F32),
+            pltpu.SemaphoreType.DMA((3, (features + 15) // 16 + 1)),
+        ]
+    else:
+        out_shape = (jax.ShapeDtypeStruct(results, F32),)
+        if prepares:
+            out_shape += (
+                jax.ShapeDtypeStruct(by_feature, F32),
+                jax.ShapeDtypeStruct((8 * READY, LANES), F32),
+            )
+        out_specs = (vmem(),) * len(out_shape)
+    return call(
+        functools.partial(
+            update_kernel, len(packets), final, len(earlier), prepares, len(ready) > 0
+        ),
+        "update",
+        out_shape,
+        [smem()] * 2
+        + [vmem()] * (3 + len(packets) + len(senders) + len(ready) + len(earlier)),
+        scratch,
+        (
+            jnp.stack([own, jnp.int32(first)]).astype(jnp.int32),
+            cameras, params, adam_m, adam_v, *packets, *senders, *ready, *earlier,
+        ),
+        out_specs,
+    )
 
 
 def swap(value, axis, d):
@@ -940,15 +962,17 @@
     else:
         packets = [jnp.stack(packets)[jnp.arange(shards) ^ group].transpose(1, 0, 2).reshape(ROWS, -1)]
         own = jnp.int32(0)
-    made = ready = ()
-    count = max(1, len(packets) // 2)
-    for first in range(0, len(packets), count):
-        known = first == 0 and len(packets) == 2 * count and blocks == 1
-        made, ready = update(
-            own, first, cameras, params, adam_m, adam_v, packets[first : first + count], made,
-            parts[count:] if known else [], ready,
+    earlier, ready = [], []
+    half = len(packets) // 2
+    if half > 0:
+        out = update(
+            own, 0, cameras, params, adam_m, adam_v, packets[:half], [],
+            parts[half:] if blocks == 1 else [], [], False,
         )
-    new_params, new_m, new_v = made
+        earlier, ready = list(out[:1]), list(out[1:])
+    new_params, new_m, new_v = update(
+        own, half, cameras, params, adam_m, adam_v, packets[half:], earlier, [], ready, True
+    )
     return (rendered, new_params, new_m, new_v)
 
 

time: 24.4 us -> 24.5 us (level)
  waiting for transfers between devices: 1 us -> 1.74 us
  Pallas kernels: 12.4 us -> 11.7 us
    pallas_call x2 -> x0, Pallas kernels: 3.1 us -> none  [update(): pl.pallas_call(functools.partial(update_kernel, len(packets), len(before)...]
    pallas_call x5 -> x7, Pallas kernels: 9.32 us -> 11.7 us  [call(): pl.pallas_call(kernel, out_shape=out_shape, in_specs=in_specs, out_specs=...]
    ppermute x8, waiting for transfers between devices: 1 us -> 1.74 us  [swap(): lax.ppermute(value, axis, [(k, k ^ d) for k in range(lax.axis_size(axis))])]
  transfers between devices with their start and end apart: 8 -> 8, of which waited for: 3 -> 3; matrix products, arithmetic and copies ran while one was open for 1% -> 1% of each run, Pallas kernels for 25% -> 22%
where the time goes in v22:
time: 24.5 us; the launch traced here: 24.3 us
  Pallas kernels  11.7 us (48%)
  starting transfers between devices  9.85 us (40%)
  waiting for transfers between devices  1.74 us (7%)
  between operations  0.71 us (3%)
    pallas_call x7, Pallas kernels, call(): pl.pallas_call(kernel, out_shape=out_shape, in_specs=in_specs, out_specs=...  11.7 us
    ppermute x8, starting transfers between devices, swap(): lax.ppermute(value, axis, [(k, k ^ d) for k in range(lax.axis_size(axis))])  9.85 us
    ppermute x8, waiting for transfers between devices, swap(): lax.ppermute(value, axis, [(k, k ^ d) for k in range(lax.axis_size(axis))])  1.74 us
  transfers between devices with their start and end apart: 8, of which 3 were waited for; matrix products, arithmetic and copies ran while one was open for 1% of the time, Pallas kernels for 22%

profile of v22, /device:TPU:0, one launch (start us, length us, event | category | flops | bytes accessed | tf_op | source)
XLA Modules:
  0.0 24.3 jit_solution(18092016893246535812)
XLA Ops:
  0.6 1.0 %pack.1 = (f32[8,512]{1,0:T(8,128)S(1)}, f32[59,1024]{1,0:T(8,128)S(1)}) custom-call(s32[1]{0:T(128)} %bitcast.2.where, s32[2,1,256]{2,1,0:T(1,128)} %bitcast.4, s32[2,256]{1,0:T(2,128)} %refs_1_.1, f32[3,512]{1,0:T(4,128)} %refs_2_.1, f32[59,1024]{1,0:T(8,128)} %refs_3_.1), custom_call_target="tpu_custom_call" | custom-call | tf_op jit(solution)/shard_map/pack/pallas_call | solution.py:809
  1.7 0.0 copy-start.2
  1.7 0.0 copy-start.3
  1.7 3.1 %collective-permute-start = (f32[8,512]{1,0:T(8,128)S(1)}, f32[8,512]{1,0:T(8,128)S(1)}, u32[]{:S(2)}, u32[]{:S(2)}) collective-permute-start(f32[8,512]{1,0:T(8,128)S(1)} %get-tuple-element.23.own.first), channel_id=1, source_target_pairs={{0,1},{1,0},{2,3},{3,2},{4,5},{5,4},{6,7},{7,6},{8,9},{9,8},{10,11... | collective-permute-start | bytes 49160 | tf_op jit(solution)/shard_map/ppermute | solution.py:924
  4.8 0.0 copy-done.2
  4.8 0.0 copy-done.3
  4.8 0.0 copy-start.1
  4.8 0.7 %cut.1 = (f32[24,256]{1,0:T(8,128)S(1)}, f32[24,256]{1,0:T(8,128)S(1)}, f32[24,256]{1,0:T(8,128)S(1)}, f32[24,256]{1,0:T(8,128)S(1)}) custom-call(s32[1]{0:T(128)} %bitcast.2.where, s32[2]{0:T(128)S(1)} %copy-done.3, f32[4,12]{1,0:T(4,128)S(1)} %copy-done.2, f32[59,1024]{1,0:T(8,128)S(1)} %get-tuple-element.24.params), custom_call_target="tpu_custom_call" | custom-call | tf_op jit(solution)/shard_map/cut/pallas_call | solution.py:809
  5.5 0.0 copy-start
  5.5 0.1 collective-permute-start.1
  5.6 1.6 %collective-permute-start.2 = (f32[24,256]{1,0:T(8,128)S(1)}, f32[24,256]{1,0:T(8,128)S(1)}, u32[]{:S(2)}, u32[]{:S(2)}) collective-permute-start(f32[24,256]{1,0:T(8,128)S(1)} %get-tuple-element.27), channel_id=1, source_target_pairs={{0,8},{4,12},{8,0},{12,4},{1,9},{5,13},{9,1},{13,5},{2,10},{6,14},... | collective-permute-start | bytes 73736 | tf_op jit(solution)/shard_map/ppermute | solution.py:924
  7.2 0.3 %collective-permute-start.3 = (f32[24,256]{1,0:T(8,128)S(1)}, f32[24,256]{1,0:T(8,128)S(1)}, u32[]{:S(2)}, u32[]{:S(2)}) collective-permute-start(f32[24,256]{1,0:T(8,128)S(1)} %get-tuple-element.28), channel_id=1, source_target_pairs={{0,12},{4,8},{8,4},{12,0},{1,13},{5,9},{9,5},{13,1},{2,14},{6,10},... | collective-permute-start | bytes 73736 | tf_op jit(solution)/shard_map/ppermute | solution.py:924
  7.5 0.1 pad_add_fusion.2.where
  7.6 0.0 collective-permute-done.other.second
  7.6 2.6 %collective-permute-start.4 = (f32[16,512]{1,0:T(8,128)S(1)}, f32[16,512]{1,0:T(8,128)S(1)}, u32[]{:S(2)}, u32[]{:S(2)}) collective-permute-start(f32[16,512]{1,0:T(8,128)S(1)} %join.1), channel_id=1, source_target_pairs={{0,2},{1,3},{2,0},{3,1},{4,6},{5,7},{6,4},{7,5},{8,10},{9,11},{10,... | collective-permute-start | bytes 98312 | tf_op jit(solution)/shard_map/ppermute | solution.py:924
  10.2 0.1 pad_add_fusion.where
  10.3 0.0 collective-permute-done.1.refs_1_
  10.3 0.0 collective-permute-done.2.refs_2_
  10.3 0.2 collective-permute-done.3.refs_3_
  10.4 3.8 %near.1 = (f32[3,512]{1,0:T(4,128)}, f32[144,128]{1,0:T(8,128)S(1)}, f32[16,1024]{1,0:T(8,128)S(1)}) custom-call(s32[2]{0:T(128)S(1)} %copy-done.3, f32[4,12]{1,0:T(4,128)S(1)} %copy-done.2, s32[3]{0:T(128)S(1)} %pad_add_fusion.where, f32[8,512]{1,0:T(8,128)S(1)} %get-tuple-element.23.own.first, f32[8,512]{1,0:T(8,128)S(1)} %collective-permute-done.other.second, ...), custom_call_target="tpu_custom_call" | custom-call | tf_op jit(solution)/shard_map/near/pallas_call | solution.py:809
  14.2 0.0 collective-permute-done.4.infos
  14.3 3.7 %far.1 = (f32[16,256]{1,0:T(8,128)S(1)}, f32[16,256]{1,0:T(8,128)S(1)}, f32[16,256]{1,0:T(8,128)S(1)}, f32[16,256]{1,0:T(8,128)S(1)}) custom-call(s32[2]{0:T(128)S(1)} %copy-done.3, s32[3]{0:T(128)S(1)} %pad_add_fusion.where, f32[144,128]{1,0:T(8,128)S(1)} %get-tuple-element.30.rows, f32[16,1024]{1,0:T(8,128)S(1)} %get-tuple-element.31.partial, ...), custom_call_target="tpu_custom_call" | custom-call | tf_op jit(solution)/shard_map/far/pallas_call | solution.py:809
  18.0 1.4 %collective-permute-start.5 = (f32[16,256]{1,0:T(8,128)S(1)}, f32[16,256]{1,0:T(8,128)S(1)}, u32[]{:S(2)}, u32[]{:S(2)}) collective-permute-start(f32[16,256]{1,0:T(8,128)S(1)} %get-tuple-element.32), channel_id=1, source_target_pairs={{0,8},{4,12},{8,0},{12,4},{1,9},{5,13},{9,1},{13,5},{2,10},{6,14},... | collective-permute-start | bytes 49160 | tf_op jit(solution)/shard_map/ppermute | solution.py:924
  19.4 0.2 collective-permute-start.6
  19.6 0.6 %collective-permute-start.7 = (f32[16,256]{1,0:T(8,128)S(1)}, f32[16,256]{1,0:T(8,128)S(1)}, u32[]{:S(2)}, u32[]{:S(2)}) collective-permute-start(f32[16,256]{1,0:T(8,128)S(1)} %get-tuple-element.35), channel_id=1, source_target_pairs={{0,4},{4,0},{8,12},{12,8},{1,5},{5,1},{9,13},{13,9},{2,6},{6,2},{1... | collective-permute-start | bytes 49160 | tf_op jit(solution)/shard_map/ppermute | solution.py:924
  20.2 0.1 pad_add_fusion.1.where
  20.3 0.8 %collective-permute-done.7.refs_1_ = f32[16,256]{1,0:T(8,128)S(1)} collective-permute-done((f32[16,256]{1,0:T(8,128)S(1)}, f32[16,256]{1,0:T(8,128)S(1)}, u32[]{:S(2)}, u32[]{:S(2)}) %collective-permute-start.7) | collective-permute-done | bytes 16416 | tf_op jit(solution)/shard_map/ppermute | solution.py:924
  21.1 0.0 copy-done.1
  21.1 0.0 copy-done
  21.1 0.8 %update.2 = (f32[3,59,512]{2,1,0:T(8,128)S(1)}, f32[268,128]{1,0:T(8,128)S(1)}, f32[536,128]{1,0:T(8,128)S(1)}) custom-call(s32[2]{0:T(128)S(1)} %pad_add_fusion.2.where, f32[4,12]{1,0:T(4,128)S(1)} %copy-done.2, f32[59,1024]{1,0:T(8,128)S(1)} %get-tuple-element.24.params, f32[59,1024]{1,0:T(8,128)S(1)} %copy-done, f32[59,1024]{1,0:T(8,128)S(1)} %copy-done.1, ...), custom_call_target="tpu_custom_call" | custom-call | tf_op jit(solution)/shard_map/update/pallas_call | solution.py:809
  21.9 0.0 collective-permute-done.5.refs_0_
  21.9 0.8 %collective-permute-done.6.refs_1_ = f32[16,256]{1,0:T(8,128)S(1)} collective-permute-done((f32[16,256]{1,0:T(8,128)S(1)}, f32[16,256]{1,0:T(8,128)S(1)}, u32[]{:S(2)}, u32[]{:S(2)}) %collective-permute-start.6) | collective-permute-done | bytes 16416 | tf_op jit(solution)/shard_map/ppermute | solution.py:924
  22.7 1.6 %update.3 = (f32[59,1024]{1,0:T(8,128)}, f32[59,1024]{1,0:T(8,128)}, f32[59,1024]{1,0:T(8,128)}) custom-call(s32[2]{0:T(128)S(1)} %pad_add_fusion.1.where, f32[4,12]{1,0:T(4,128)S(1)} %copy-done.2, f32[59,1024]{1,0:T(8,128)S(1)} %get-tuple-element.24.params, f32[59,1024]{1,0:T(8,128)S(1)} %copy-done, f32[59,1024]{1,0:T(8,128)S(1)} %copy-done.1, ...), custom_call_target="tpu_custom_call" | custom-call | tf_op jit(solution)/shard_map/update/pallas_call | solution.py:809
  (1 shorter events, 0.0 us)
Async XLA Ops:
  1.7 3.1 %copy-start.2 = (f32[4,12]{1,0:T(4,128)S(1)}, f32[4,12]{1,0:T(4,128)}, u32[]{:S(2)}) copy-start(f32[4,12]{1,0:T(4,128)} %cams.7) | copy-start | bytes 580
  1.7 3.1 %copy-start.3 = (s32[2]{0:T(128)S(1)}, s32[2]{0:T(128)}, u32[]{:S(2)}) copy-start(s32[2]{0:T(128)} %tile_ids.5) | copy-start | bytes 28
  1.7 5.9 %collective-permute-start = (f32[8,512]{1,0:T(8,128)S(1)}, f32[8,512]{1,0:T(8,128)S(1)}, u32[]{:S(2)}, u32[]{:S(2)}) collective-permute-start(f32[8,512]{1,0:T(8,128)S(1)} %get-tuple-element.23.own.first), channel_id=1, source_target_pairs={{0,1},{1,0},{2,3},{3,2},{4,5},{5,4},{6,7},{7,6},{8,9},{9,8},{10,11... | collective-permute-start | bytes 49160 | tf_op jit(solution)/shard_map/ppermute | solution.py:924
  4.8 16.3 %copy-start.1 = (f32[59,1024]{1,0:T(8,128)S(1)}, f32[59,1024]{1,0:T(8,128)}, u32[]{:S(2)}) copy-start(f32[59,1024]{1,0:T(8,128)} %adam_v.3) | copy-start | bytes 724996
  5.5 15.5 %copy-start = (f32[59,1024]{1,0:T(8,128)S(1)}, f32[59,1024]{1,0:T(8,128)}, u32[]{:S(2)}) copy-start(f32[59,1024]{1,0:T(8,128)} %adam_m.3) | copy-start | bytes 724996
  5.5 4.7 %collective-permute-start.1 = (f32[24,256]{1,0:T(8,128)S(1)}, f32[24,256]{1,0:T(8,128)S(1)}, u32[]{:S(2)}, u32[]{:S(2)}) collective-permute-start(f32[24,256]{1,0:T(8,128)S(1)} %get-tuple-element.26), channel_id=1, source_target_pairs={{0,4},{4,0},{8,12},{12,8},{1,5},{5,1},{9,13},{13,9},{2,6},{6,2},{1... | collective-permute-start | bytes 73736 | tf_op jit(solution)/shard_map/ppermute | solution.py:924
  5.6 4.6 %collective-permute-start.2 = (f32[24,256]{1,0:T(8,128)S(1)}, f32[24,256]{1,0:T(8,128)S(1)}, u32[]{:S(2)}, u32[]{:S(2)}) collective-permute-start(f32[24,256]{1,0:T(8,128)S(1)} %get-tuple-element.27), channel_id=1, source_target_pairs={{0,8},{4,12},{8,0},{12,4},{1,9},{5,13},{9,1},{13,5},{2,10},{6,14},... | collective-permute-start | bytes 73736 | tf_op jit(solution)/shard_map/ppermute | solution.py:924
  7.2 3.3 %collective-permute-start.3 = (f32[24,256]{1,0:T(8,128)S(1)}, f32[24,256]{1,0:T(8,128)S(1)}, u32[]{:S(2)}, u32[]{:S(2)}) collective-permute-start(f32[24,256]{1,0:T(8,128)S(1)} %get-tuple-element.28), channel_id=1, source_target_pairs={{0,12},{4,8},{8,4},{12,0},{1,13},{5,9},{9,5},{13,1},{2,14},{6,10},... | collective-permute-start | bytes 73736 | tf_op jit(solution)/shard_map/ppermute | solution.py:924
  7.6 6.7 %collective-permute-start.4 = (f32[16,512]{1,0:T(8,128)S(1)}, f32[16,512]{1,0:T(8,128)S(1)}, u32[]{:S(2)}, u32[]{:S(2)}) collective-permute-start(f32[16,512]{1,0:T(8,128)S(1)} %join.1), channel_id=1, source_target_pairs={{0,2},{1,3},{2,0},{3,1},{4,6},{5,7},{6,4},{7,5},{8,10},{9,11},{10,... | collective-permute-start | bytes 98312 | tf_op jit(solution)/shard_map/ppermute | solution.py:924
  18.0 3.9 %collective-permute-start.5 = (f32[16,256]{1,0:T(8,128)S(1)}, f32[16,256]{1,0:T(8,128)S(1)}, u32[]{:S(2)}, u32[]{:S(2)}) collective-permute-start(f32[16,256]{1,0:T(8,128)S(1)} %get-tuple-element.32), channel_id=1, source_target_pairs={{0,8},{4,12},{8,0},{12,4},{1,9},{5,13},{9,1},{13,5},{2,10},{6,14},... | collective-permute-start | bytes 49160 | tf_op jit(solution)/shard_map/ppermute | solution.py:924
  19.4 3.3 %collective-permute-start.6 = (f32[16,256]{1,0:T(8,128)S(1)}, f32[16,256]{1,0:T(8,128)S(1)}, u32[]{:S(2)}, u32[]{:S(2)}) collective-permute-start(f32[16,256]{1,0:T(8,128)S(1)} %get-tuple-element.33), channel_id=1, source_target_pairs={{0,12},{4,8},{8,4},{12,0},{1,13},{5,9},{9,5},{13,1},{2,14},{6,10},... | collective-permute-start | bytes 49160 | tf_op jit(solution)/shard_map/ppermute | solution.py:924
  19.6 1.5 %collective-permute-start.7 = (f32[16,256]{1,0:T(8,128)S(1)}, f32[16,256]{1,0:T(8,128)S(1)}, u32[]{:S(2)}, u32[]{:S(2)}) collective-permute-start(f32[16,256]{1,0:T(8,128)S(1)} %get-tuple-element.35), channel_id=1, source_target_pairs={{0,4},{4,0},{8,12},{12,8},{1,5},{5,1},{9,13},{13,9},{2,6},{6,2},{1... | collective-permute-start | bytes 49160 | tf_op jit(solution)/shard_map/ppermute | solution.py:924

commit v23 on v22

--- a/solution.py
+++ b/solution.py
@@ -658,6 +658,10 @@
         partial[0:8, at], partial[8:9, at] = pool_sum(s, info_s, *work[-2:])
 
 
+def packet_width(packet):
+    return packet.shape[1] - (LANES if packet.shape[0] == 8 else 0)
+
+
 def far_kernel(blocks, tile_ids, where, rows, partial, infos, *refs):
     *packets, info_s = refs[: len(refs) - 12]
     work = refs[len(refs) - 12 :]
@@ -668,7 +672,11 @@
     share = (tile_ids[0] // (TILES_X * TILES_Y)).astype(F32)
     row_of = lax.broadcasted_iota(jnp.int32, (8, LANES), 0)
     lane_of = lax.broadcasted_iota(jnp.int32, (8, LANES), 1)
-    chunk = packets[0].shape[1]
+    chunk = packet_width(packets[0])
+    compact = packets[0].shape[0] == 8
+    if compact:
+        for packet in packets:
+            packet[:, chunk:] = jnp.zeros((8, LANES), F32)
     for s in range(rows.shape[0] // ROWS - 1):
         total, ninth = pool_sum(s, info_s, *work[-2:])
         total = total + partial[0:8, s * LANES : (s + 1) * LANES]
@@ -680,9 +688,15 @@
             mine = jnp.where(column % where[2] // (where[2] // blocks) == where[1], share, 0.0)
         at = slice(s * LANES % chunk, s * LANES % chunk + LANES)
         packets[s * LANES // chunk][0:8, at] = total
-        packets[s * LANES // chunk][8:16, at] = jnp.where(
-            row_of == 0, jnp.broadcast_to(ninth, (8, LANES)), mine
-        )
+        if compact:
+            each, h = chunk // LANES, s % (chunk // LANES)
+            mine = jnp.broadcast_to(mine, (8, LANES))[0:1]
+            packets[s * LANES // chunk][h : h + 1, chunk:] = ninth
+            packets[s * LANES // chunk][each + h : each + h + 1, chunk:] = mine
+        else:
+            packets[s * LANES // chunk][8:16, at] = jnp.where(
+                row_of == 0, jnp.broadcast_to(ninth, (8, LANES)), mine
+            )
 
 
 def join_kernel(first, second, out):
@@ -702,7 +716,7 @@
         made, refs = refs[0], refs[1:]
         next_ready, (feats, rows, grads) = refs[: 2 * prepares], refs[2 * prepares :]
     features = params.shape[0]
-    chunk = packets[0].shape[1]
+    chunk = packet_width(packets[0])
     width = pieces * chunk
     slabs = width // LANES
     place = where[0] ^ where[1]
@@ -719,7 +733,12 @@
     for d in range(pieces):
         for h in range(chunk // LANES):
             slab = (place ^ d) % pieces * (chunk // LANES) + h
-            rows[pl.ds(slab, ROWS, stride=slabs), :] = packets[d][:, h * LANES : (h + 1) * LANES]
+            packet, each = packets[d], chunk // LANES
+            count = packet.shape[0]
+            rows[pl.ds(slab, count, stride=slabs), :] = packet[:, h * LANES : (h + 1) * LANES]
+            if count == 8:
+                rows[pl.ds(8 * slabs + slab, 1), :] = packet[h : h + 1, chunk:]
+                rows[pl.ds(9 * slabs + slab, 1), :] = packet[each + h : each + h + 1, chunk:]
     pulled = [rows[f * slabs : (f + 1) * slabs, :] for f in range(10)]
 
     def put(f, value):
@@ -857,10 +876,14 @@
     width = partial.shape[1]
     pixels = listed = infos.shape[1] // tile_count
     info = (infos.shape[0] // 2, infos.shape[1])
+    shape = (ROWS, width)
+    if pieces > 1:
+        assert width // pieces // LANES <= 4
+        shape = (8, width // pieces + LANES)
     return call(
         functools.partial(far_kernel, blocks),
         "far",
-        (jax.ShapeDtypeStruct((ROWS, width // pieces), F32),) * pieces,
+        (jax.ShapeDtypeStruct(shape, F32),) * pieces,
         [smem()] * 2 + [vmem()] * 3,
         [pltpu.VMEM((2,) + info, F32)] + work_shapes(tile_count, pixels, listed),
         (tile_ids, where, rows, partial, infos),
@@ -876,7 +899,7 @@
 
 def update(own, first, cameras, params, adam_m, adam_v, packets, earlier, senders, ready, final):
     features = params.shape[0]
-    width = sum(packet.shape[1] for packet in packets)
+    width = sum(packet_width(packet) for packet in packets)
     slabs = width // LANES
     shape = jax.ShapeDtypeStruct(params.shape, F32)
     by_feature = ((features + 8) * slabs, LANES)

time: 24.5 us -> 24.4 us (level)
  no operation moved by 1% of the time
where the time goes in v23:
time: 24.4 us; the launch traced here: 24.2 us
  Pallas kernels  11.7 us (48%)
  starting transfers between devices  9.85 us (40%)
  waiting for transfers between devices  1.65 us (7%)
  between operations  0.71 us (3%)
    pallas_call x7, Pallas kernels, call(): pl.pallas_call(kernel, out_shape=out_shape, in_specs=in_specs, out_specs=...  11.7 us
    ppermute x8, starting transfers between devices, swap(): lax.ppermute(value, axis, [(k, k ^ d) for k in range(lax.axis_size(axis))])  9.85 us
    ppermute x8, waiting for transfers between devices, swap(): lax.ppermute(value, axis, [(k, k ^ d) for k in range(lax.axis_size(axis))])  1.65 us
  transfers between devices with their start and end apart: 8, of which 3 were waited for; matrix products, arithmetic and copies ran while one was open for 1% of the time, Pallas kernels for 22%

profile of v23, /device:TPU:0, one launch (start us, length us, event | category | flops | bytes accessed | tf_op | source)
XLA Modules:
  0.0 24.2 jit_solution(8829396631948217886)
XLA Ops:
  0.6 1.0 %pack.1 = (f32[8,512]{1,0:T(8,128)S(1)}, f32[59,1024]{1,0:T(8,128)S(1)}) custom-call(s32[1]{0:T(128)} %bitcast.2.where, s32[2,1,256]{2,1,0:T(1,128)} %bitcast.4, s32[2,256]{1,0:T(2,128)} %refs_1_.1, f32[3,512]{1,0:T(4,128)} %refs_2_.1, f32[59,1024]{1,0:T(8,128)} %refs_3_.1), custom_call_target="tpu_custom_call" | custom-call | tf_op jit(solution)/shard_map/pack/pallas_call | solution.py:828
  1.7 0.0 copy-start.2
  1.7 0.0 copy-start.3
  1.7 3.1 %collective-permute-start = (f32[8,512]{1,0:T(8,128)S(1)}, f32[8,512]{1,0:T(8,128)S(1)}, u32[]{:S(2)}, u32[]{:S(2)}) collective-permute-start(f32[8,512]{1,0:T(8,128)S(1)} %get-tuple-element.23.own.first), channel_id=1, source_target_pairs={{0,1},{1,0},{2,3},{3,2},{4,5},{5,4},{6,7},{7,6},{8,9},{9,8},{10,11... | collective-permute-start | bytes 49160 | tf_op jit(solution)/shard_map/ppermute | solution.py:947
  4.8 0.0 copy-done.2
  4.8 0.0 copy-done.3
  4.8 0.0 copy-start.1
  4.8 0.7 %cut.1 = (f32[24,256]{1,0:T(8,128)S(1)}, f32[24,256]{1,0:T(8,128)S(1)}, f32[24,256]{1,0:T(8,128)S(1)}, f32[24,256]{1,0:T(8,128)S(1)}) custom-call(s32[1]{0:T(128)} %bitcast.2.where, s32[2]{0:T(128)S(1)} %copy-done.3, f32[4,12]{1,0:T(4,128)S(1)} %copy-done.2, f32[59,1024]{1,0:T(8,128)S(1)} %get-tuple-element.24.params), custom_call_target="tpu_custom_call" | custom-call | tf_op jit(solution)/shard_map/cut/pallas_call | solution.py:828
  5.5 0.0 copy-start
  5.5 0.1 collective-permute-start.1
  5.6 1.6 %collective-permute-start.2 = (f32[24,256]{1,0:T(8,128)S(1)}, f32[24,256]{1,0:T(8,128)S(1)}, u32[]{:S(2)}, u32[]{:S(2)}) collective-permute-start(f32[24,256]{1,0:T(8,128)S(1)} %get-tuple-element.27), channel_id=1, source_target_pairs={{0,8},{4,12},{8,0},{12,4},{1,9},{5,13},{9,1},{13,5},{2,10},{6,14},... | collective-permute-start | bytes 73736 | tf_op jit(solution)/shard_map/ppermute | solution.py:947
  7.2 0.3 %collective-permute-start.3 = (f32[24,256]{1,0:T(8,128)S(1)}, f32[24,256]{1,0:T(8,128)S(1)}, u32[]{:S(2)}, u32[]{:S(2)}) collective-permute-start(f32[24,256]{1,0:T(8,128)S(1)} %get-tuple-element.28), channel_id=1, source_target_pairs={{0,12},{4,8},{8,4},{12,0},{1,13},{5,9},{9,5},{13,1},{2,14},{6,10},... | collective-permute-start | bytes 73736 | tf_op jit(solution)/shard_map/ppermute | solution.py:947
  7.5 0.1 pad_add_fusion.2.where
  7.6 0.0 collective-permute-done.other.second
  7.6 2.6 %collective-permute-start.4 = (f32[16,512]{1,0:T(8,128)S(1)}, f32[16,512]{1,0:T(8,128)S(1)}, u32[]{:S(2)}, u32[]{:S(2)}) collective-permute-start(f32[16,512]{1,0:T(8,128)S(1)} %join.1), channel_id=1, source_target_pairs={{0,2},{1,3},{2,0},{3,1},{4,6},{5,7},{6,4},{7,5},{8,10},{9,11},{10,... | collective-permute-start | bytes 98312 | tf_op jit(solution)/shard_map/ppermute | solution.py:947
  10.2 0.1 pad_add_fusion.where
  10.3 0.0 collective-permute-done.1.refs_1_
  10.3 0.0 collective-permute-done.2.refs_2_
  10.3 0.2 collective-permute-done.3.refs_3_
  10.4 3.8 %near.1 = (f32[3,512]{1,0:T(4,128)}, f32[144,128]{1,0:T(8,128)S(1)}, f32[16,1024]{1,0:T(8,128)S(1)}) custom-call(s32[2]{0:T(128)S(1)} %copy-done.3, f32[4,12]{1,0:T(4,128)S(1)} %copy-done.2, s32[3]{0:T(128)S(1)} %pad_add_fusion.where, f32[8,512]{1,0:T(8,128)S(1)} %get-tuple-element.23.own.first, f32[8,512]{1,0:T(8,128)S(1)} %collective-permute-done.other.second, ...), custom_call_target="tpu_custom_call" | custom-call | tf_op jit(solution)/shard_map/near/pallas_call | solution.py:828
  14.2 0.0 collective-permute-done.4.infos
  14.3 3.7 %far.1 = (f32[8,384]{1,0:T(8,128)S(1)}, f32[8,384]{1,0:T(8,128)S(1)}, f32[8,384]{1,0:T(8,128)S(1)}, f32[8,384]{1,0:T(8,128)S(1)}) custom-call(s32[2]{0:T(128)S(1)} %copy-done.3, s32[3]{0:T(128)S(1)} %pad_add_fusion.where, f32[144,128]{1,0:T(8,128)S(1)} %get-tuple-element.30.rows, f32[16,1024]{1,0:T(8,128)S(1)} %get-tuple-element.31.partial, ...), custom_call_target="tpu_custom_call" | custom-call | tf_op jit(solution)/shard_map/far/pallas_call | solution.py:828
  18.0 1.4 %collective-permute-start.5 = (f32[8,384]{1,0:T(8,128)S(1)}, f32[8,384]{1,0:T(8,128)S(1)}, u32[]{:S(2)}, u32[]{:S(2)}) collective-permute-start(f32[8,384]{1,0:T(8,128)S(1)} %get-tuple-element.32), channel_id=1, source_target_pairs={{0,8},{4,12},{8,0},{12,4},{1,9},{5,13},{9,1},{13,5},{2,10},{6,14},... | collective-permute-start | bytes 36872 | tf_op jit(solution)/shard_map/ppermute | solution.py:947
  19.4 0.2 collective-permute-start.6
  19.6 0.6 %collective-permute-start.7 = (f32[8,384]{1,0:T(8,128)S(1)}, f32[8,384]{1,0:T(8,128)S(1)}, u32[]{:S(2)}, u32[]{:S(2)}) collective-permute-start(f32[8,384]{1,0:T(8,128)S(1)} %get-tuple-element.35), channel_id=1, source_target_pairs={{0,4},{4,0},{8,12},{12,8},{1,5},{5,1},{9,13},{13,9},{2,6},{6,2},{1... | collective-permute-start | bytes 36872 | tf_op jit(solution)/shard_map/ppermute | solution.py:947
  20.2 0.1 pad_add_fusion.1.where
  20.3 0.8 %collective-permute-done.7.refs_1_ = f32[8,384]{1,0:T(8,128)S(1)} collective-permute-done((f32[8,384]{1,0:T(8,128)S(1)}, f32[8,384]{1,0:T(8,128)S(1)}, u32[]{:S(2)}, u32[]{:S(2)}) %collective-permute-start.7) | collective-permute-done | bytes 12320 | tf_op jit(solution)/shard_map/ppermute | solution.py:947
  21.0 0.0 copy-done.1
  21.0 0.0 copy-done
  21.1 0.8 %update.2 = (f32[3,59,512]{2,1,0:T(8,128)S(1)}, f32[268,128]{1,0:T(8,128)S(1)}, f32[536,128]{1,0:T(8,128)S(1)}) custom-call(s32[2]{0:T(128)S(1)} %pad_add_fusion.2.where, f32[4,12]{1,0:T(4,128)S(1)} %copy-done.2, f32[59,1024]{1,0:T(8,128)S(1)} %get-tuple-element.24.params, f32[59,1024]{1,0:T(8,128)S(1)} %copy-done, f32[59,1024]{1,0:T(8,128)S(1)} %copy-done.1, ...), custom_call_target="tpu_custom_call" | custom-call | tf_op jit(solution)/shard_map/update/pallas_call | solution.py:828
  21.9 0.0 collective-permute-done.5.refs_0_
  21.9 0.7 %collective-permute-done.6.refs_1_ = f32[8,384]{1,0:T(8,128)S(1)} collective-permute-done((f32[8,384]{1,0:T(8,128)S(1)}, f32[8,384]{1,0:T(8,128)S(1)}, u32[]{:S(2)}, u32[]{:S(2)}) %collective-permute-start.6) | collective-permute-done | bytes 12320 | tf_op jit(solution)/shard_map/ppermute | solution.py:947
  22.6 1.6 %update.3 = (f32[59,1024]{1,0:T(8,128)}, f32[59,1024]{1,0:T(8,128)}, f32[59,1024]{1,0:T(8,128)}) custom-call(s32[2]{0:T(128)S(1)} %pad_add_fusion.1.where, f32[4,12]{1,0:T(4,128)S(1)} %copy-done.2, f32[59,1024]{1,0:T(8,128)S(1)} %get-tuple-element.24.params, f32[59,1024]{1,0:T(8,128)S(1)} %copy-done, f32[59,1024]{1,0:T(8,128)S(1)} %copy-done.1, ...), custom_call_target="tpu_custom_call" | custom-call | tf_op jit(solution)/shard_map/update/pallas_call | solution.py:828
  (1 shorter events, 0.0 us)
Async XLA Ops:
  1.7 3.1 %copy-start.2 = (f32[4,12]{1,0:T(4,128)S(1)}, f32[4,12]{1,0:T(4,128)}, u32[]{:S(2)}) copy-start(f32[4,12]{1,0:T(4,128)} %cams.7) | copy-start | bytes 580
  1.7 3.1 %copy-start.3 = (s32[2]{0:T(128)S(1)}, s32[2]{0:T(128)}, u32[]{:S(2)}) copy-start(s32[2]{0:T(128)} %tile_ids.5) | copy-start | bytes 28
  1.7 5.9 %collective-permute-start = (f32[8,512]{1,0:T(8,128)S(1)}, f32[8,512]{1,0:T(8,128)S(1)}, u32[]{:S(2)}, u32[]{:S(2)}) collective-permute-start(f32[8,512]{1,0:T(8,128)S(1)} %get-tuple-element.23.own.first), channel_id=1, source_target_pairs={{0,1},{1,0},{2,3},{3,2},{4,5},{5,4},{6,7},{7,6},{8,9},{9,8},{10,11... | collective-permute-start | bytes 49160 | tf_op jit(solution)/shard_map/ppermute | solution.py:947
  4.8 16.2 %copy-start.1 = (f32[59,1024]{1,0:T(8,128)S(1)}, f32[59,1024]{1,0:T(8,128)}, u32[]{:S(2)}) copy-start(f32[59,1024]{1,0:T(8,128)} %adam_v.3) | copy-start | bytes 724996
  5.5 15.5 %copy-start = (f32[59,1024]{1,0:T(8,128)S(1)}, f32[59,1024]{1,0:T(8,128)}, u32[]{:S(2)}) copy-start(f32[59,1024]{1,0:T(8,128)} %adam_m.3) | copy-start | bytes 724996
  5.5 4.7 %collective-permute-start.1 = (f32[24,256]{1,0:T(8,128)S(1)}, f32[24,256]{1,0:T(8,128)S(1)}, u32[]{:S(2)}, u32[]{:S(2)}) collective-permute-start(f32[24,256]{1,0:T(8,128)S(1)} %get-tuple-element.26), channel_id=1, source_target_pairs={{0,4},{4,0},{8,12},{12,8},{1,5},{5,1},{9,13},{13,9},{2,6},{6,2},{1... | collective-permute-start | bytes 73736 | tf_op jit(solution)/shard_map/ppermute | solution.py:947
  5.6 4.6 %collective-permute-start.2 = (f32[24,256]{1,0:T(8,128)S(1)}, f32[24,256]{1,0:T(8,128)S(1)}, u32[]{:S(2)}, u32[]{:S(2)}) collective-permute-start(f32[24,256]{1,0:T(8,128)S(1)} %get-tuple-element.27), channel_id=1, source_target_pairs={{0,8},{4,12},{8,0},{12,4},{1,9},{5,13},{9,1},{13,5},{2,10},{6,14},... | collective-permute-start | bytes 73736 | tf_op jit(solution)/shard_map/ppermute | solution.py:947
  7.2 3.3 %collective-permute-start.3 = (f32[24,256]{1,0:T(8,128)S(1)}, f32[24,256]{1,0:T(8,128)S(1)}, u32[]{:S(2)}, u32[]{:S(2)}) collective-permute-start(f32[24,256]{1,0:T(8,128)S(1)} %get-tuple-element.28), channel_id=1, source_target_pairs={{0,12},{4,8},{8,4},{12,0},{1,13},{5,9},{9,5},{13,1},{2,14},{6,10},... | collective-permute-start | bytes 73736 | tf_op jit(solution)/shard_map/ppermute | solution.py:947
  7.6 6.7 %collective-permute-start.4 = (f32[16,512]{1,0:T(8,128)S(1)}, f32[16,512]{1,0:T(8,128)S(1)}, u32[]{:S(2)}, u32[]{:S(2)}) collective-permute-start(f32[16,512]{1,0:T(8,128)S(1)} %join.1), channel_id=1, source_target_pairs={{0,2},{1,3},{2,0},{3,1},{4,6},{5,7},{6,4},{7,5},{8,10},{9,11},{10,... | collective-permute-start | bytes 98312 | tf_op jit(solution)/shard_map/ppermute | solution.py:947
  18.0 3.9 %collective-permute-start.5 = (f32[8,384]{1,0:T(8,128)S(1)}, f32[8,384]{1,0:T(8,128)S(1)}, u32[]{:S(2)}, u32[]{:S(2)}) collective-permute-start(f32[8,384]{1,0:T(8,128)S(1)} %get-tuple-element.32), channel_id=1, source_target_pairs={{0,8},{4,12},{8,0},{12,4},{1,9},{5,13},{9,1},{13,5},{2,10},{6,14},... | collective-permute-start | bytes 36872 | tf_op jit(solution)/shard_map/ppermute | solution.py:947
  19.4 3.2 %collective-permute-start.6 = (f32[8,384]{1,0:T(8,128)S(1)}, f32[8,384]{1,0:T(8,128)S(1)}, u32[]{:S(2)}, u32[]{:S(2)}) collective-permute-start(f32[8,384]{1,0:T(8,128)S(1)} %get-tuple-element.33), channel_id=1, source_target_pairs={{0,12},{4,8},{8,4},{12,0},{1,13},{5,9},{9,5},{13,1},{2,14},{6,10},... | collective-permute-start | bytes 36872 | tf_op jit(solution)/shard_map/ppermute | solution.py:947
  19.6 1.5 %collective-permute-start.7 = (f32[8,384]{1,0:T(8,128)S(1)}, f32[8,384]{1,0:T(8,128)S(1)}, u32[]{:S(2)}, u32[]{:S(2)}) collective-permute-start(f32[8,384]{1,0:T(8,128)S(1)} %get-tuple-element.35), channel_id=1, source_target_pairs={{0,4},{4,0},{8,12},{12,8},{1,5},{5,1},{9,13},{13,9},{2,6},{6,2},{1... | collective-permute-start | bytes 36872 | tf_op jit(solution)/shard_map/ppermute | solution.py:947

commit v24 on v23

--- a/solution.py
+++ b/solution.py
@@ -705,7 +705,7 @@
     out[half:, :] = second[...]
 
 
-def update_kernel(pieces, final, follows, prepares, ready, where, cams, params, adam_m, adam_v, *refs):
+def update_kernel(pieces, first_piece, final, follows, prepares, ready, where, cams, params, adam_m, adam_v, *refs):
     packets, refs = refs[:pieces], refs[pieces:]
     senders, refs = refs[: pieces * prepares], refs[pieces * prepares :]
     made_ready, refs = refs[: 2 * ready], refs[2 * ready :]
@@ -719,7 +719,7 @@
     chunk = packet_width(packets[0])
     width = pieces * chunk
     slabs = width // LANES
-    place = where[0] ^ where[1]
+    place = where[3] ^ first_piece
     start = place // pieces * pieces * chunk
     stores = []
     if follows:
@@ -897,7 +897,7 @@
     )[0]
 
 
-def update(own, first, cameras, params, adam_m, adam_v, packets, earlier, senders, ready, final):
+def update(where, first, cameras, params, adam_m, adam_v, packets, earlier, senders, ready, final):
     features = params.shape[0]
     width = sum(packet_width(packet) for packet in packets)
     slabs = width // LANES
@@ -926,7 +926,7 @@
         out_specs = (vmem(),) * len(out_shape)
     return call(
         functools.partial(
-            update_kernel, len(packets), final, len(earlier), prepares, len(ready) > 0
+            update_kernel, len(packets), first, final, len(earlier), prepares, len(ready) > 0
         ),
         "update",
         out_shape,
@@ -934,8 +934,7 @@
         + [vmem()] * (3 + len(packets) + len(senders) + len(ready) + len(earlier)),
         scratch,
         (
-            jnp.stack([own, jnp.int32(first)]).astype(jnp.int32),
-            cameras, params, adam_m, adam_v, *packets, *senders, *ready, *earlier,
+            where, cameras, params, adam_m, adam_v, *packets, *senders, *ready, *earlier,
         ),
         out_specs,
     )
@@ -972,7 +971,8 @@
     beyond = swap(join(info, beside), "tile", 2)
     if not aligned:
         parts = [jnp.concatenate(parts, axis=1)]
-    where = jnp.stack([seat % team, seat // team, jnp.int32(chunk)]).astype(jnp.int32)
+    own = group if aligned else jnp.int32(0)
+    where = jnp.stack([seat % team, seat // team, jnp.int32(chunk), own]).astype(jnp.int32)
     rendered, rows, partial = near(tile_ids, cameras, where, info, beside, parts, tile_count)
     packets = far(tile_ids, where, rows, partial, beyond, len(parts), tile_count, blocks)
     if not aligned:
@@ -980,21 +980,18 @@
     packets = [swap(packets[d], "gs", d) for d in range(shards)]
     if blocks > 1:
         packets = [block_sum(packet, along, team) for packet in packets]
-    if aligned:
-        own = group
-    else:
+    if not aligned:
         packets = [jnp.stack(packets)[jnp.arange(shards) ^ group].transpose(1, 0, 2).reshape(ROWS, -1)]
-        own = jnp.int32(0)
     earlier, ready = [], []
     half = len(packets) // 2
     if half > 0:
         out = update(
-            own, 0, cameras, params, adam_m, adam_v, packets[:half], [],
+            where, 0, cameras, params, adam_m, adam_v, packets[:half], [],
             parts[half:] if blocks == 1 else [], [], False,
         )
         earlier, ready = list(out[:1]), list(out[1:])
     new_params, new_m, new_v = update(
-        own, half, cameras, params, adam_m, adam_v, packets[half:], earlier, [], ready, True
+        where, half, cameras, params, adam_m, adam_v, packets[half:], earlier, [], ready, True
     )
     return (rendered, new_params, new_m, new_v)
 

time: 24.4 us -> 24.2 us (level)
  waiting for transfers between devices: 1.65 us -> 1.99 us
  starting transfers between devices: 9.85 us -> 9.54 us
    ppermute x8, waiting for transfers between devices: 1.65 us -> 1.99 us  [swap(): lax.ppermute(value, axis, [(k, k ^ d) for k in range(lax.axis_size(axis))])]
    ppermute x8, starting transfers between devices: 9.85 us -> 9.54 us  [swap(): lax.ppermute(value, axis, [(k, k ^ d) for k in range(lax.axis_size(axis))])]
  transfers between devices with their start and end apart: 8 -> 8, of which waited for: 3 -> 3; matrix products, arithmetic and copies ran while one was open for 1% -> 0% of each run, Pallas kernels for 22% -> 22%
where the time goes in v24:
time: 24.2 us; the launch traced here: 24.1 us
  Pallas kernels  11.7 us (48%)
  starting transfers between devices  9.54 us (39%)
  waiting for transfers between devices  1.99 us (8%)
  between operations  0.71 us (3%)
    pallas_call x7, Pallas kernels, call(): pl.pallas_call(kernel, out_shape=out_shape, in_specs=in_specs, out_specs=...  11.7 us
    ppermute x8, starting transfers between devices, swap(): lax.ppermute(value, axis, [(k, k ^ d) for k in range(lax.axis_size(axis))])  9.54 us
    ppermute x8, waiting for transfers between devices, swap(): lax.ppermute(value, axis, [(k, k ^ d) for k in range(lax.axis_size(axis))])  1.99 us
  transfers between devices with their start and end apart: 8, of which 3 were waited for; matrix products, arithmetic and copies ran while one was open for 0% of the time, Pallas kernels for 22%

profile of v24, /device:TPU:0, one launch (start us, length us, event | category | flops | bytes accessed | tf_op | source)
XLA Modules:
  0.0 24.1 jit_solution(8007895739867544212)
XLA Ops:
  0.6 1.0 %pack.1 = (f32[8,512]{1,0:T(8,128)S(1)}, f32[59,1024]{1,0:T(8,128)S(1)}) custom-call(s32[1]{0:T(128)} %bitcast.2.where, s32[2,1,256]{2,1,0:T(1,128)} %bitcast.4, s32[2,256]{1,0:T(2,128)} %refs_1_.1, f32[3,512]{1,0:T(4,128)} %refs_2_.1, f32[59,1024]{1,0:T(8,128)} %refs_3_.1), custom_call_target="tpu_custom_call" | custom-call | tf_op jit(solution)/shard_map/pack/pallas_call | solution.py:828
  1.7 0.0 copy-start.2
  1.7 0.0 copy-start.3
  1.7 3.1 %collective-permute-start = (f32[8,512]{1,0:T(8,128)S(1)}, f32[8,512]{1,0:T(8,128)S(1)}, u32[]{:S(2)}, u32[]{:S(2)}) collective-permute-start(f32[8,512]{1,0:T(8,128)S(1)} %get-tuple-element.23.own.first), channel_id=1, source_target_pairs={{0,1},{1,0},{2,3},{3,2},{4,5},{5,4},{6,7},{7,6},{8,9},{9,8},{10,11... | collective-permute-start | bytes 49160 | tf_op jit(solution)/shard_map/ppermute | solution.py:946
  4.8 0.0 copy-done.2
  4.8 0.0 copy-done.3
  4.8 0.0 copy-start.1
  4.8 0.7 %cut.1 = (f32[24,256]{1,0:T(8,128)S(1)}, f32[24,256]{1,0:T(8,128)S(1)}, f32[24,256]{1,0:T(8,128)S(1)}, f32[24,256]{1,0:T(8,128)S(1)}) custom-call(s32[1]{0:T(128)} %bitcast.2.where, s32[2]{0:T(128)S(1)} %copy-done.3, f32[4,12]{1,0:T(4,128)S(1)} %copy-done.2, f32[59,1024]{1,0:T(8,128)S(1)} %get-tuple-element.24.params), custom_call_target="tpu_custom_call" | custom-call | tf_op jit(solution)/shard_map/cut/pallas_call | solution.py:828
  5.5 0.0 copy-start
  5.5 0.1 collective-permute-start.1
  5.6 1.6 %collective-permute-start.2 = (f32[24,256]{1,0:T(8,128)S(1)}, f32[24,256]{1,0:T(8,128)S(1)}, u32[]{:S(2)}, u32[]{:S(2)}) collective-permute-start(f32[24,256]{1,0:T(8,128)S(1)} %get-tuple-element.27), channel_id=1, source_target_pairs={{0,8},{4,12},{8,0},{12,4},{1,9},{5,13},{9,1},{13,5},{2,10},{6,14},... | collective-permute-start | bytes 73736 | tf_op jit(solution)/shard_map/ppermute | solution.py:946
  7.2 0.3 %collective-permute-start.3 = (f32[24,256]{1,0:T(8,128)S(1)}, f32[24,256]{1,0:T(8,128)S(1)}, u32[]{:S(2)}, u32[]{:S(2)}) collective-permute-start(f32[24,256]{1,0:T(8,128)S(1)} %get-tuple-element.28), channel_id=1, source_target_pairs={{0,12},{4,8},{8,4},{12,0},{1,13},{5,9},{9,5},{13,1},{2,14},{6,10},... | collective-permute-start | bytes 73736 | tf_op jit(solution)/shard_map/ppermute | solution.py:946
  7.5 0.0 collective-permute-done.other.second
  7.5 2.6 %collective-permute-start.4 = (f32[16,512]{1,0:T(8,128)S(1)}, f32[16,512]{1,0:T(8,128)S(1)}, u32[]{:S(2)}, u32[]{:S(2)}) collective-permute-start(f32[16,512]{1,0:T(8,128)S(1)} %join.1), channel_id=1, source_target_pairs={{0,2},{1,3},{2,0},{3,1},{4,6},{5,7},{6,4},{7,5},{8,10},{9,11},{10,... | collective-permute-start | bytes 98312 | tf_op jit(solution)/shard_map/ppermute | solution.py:946
  10.1 0.1 pad_add_fusion.where
  10.2 0.0 collective-permute-done.1.refs_1_
  10.2 0.0 collective-permute-done.2.refs_2_
  10.2 0.3 %collective-permute-done.3.refs_3_ = f32[24,256]{1,0:T(8,128)S(1)} collective-permute-done((f32[24,256]{1,0:T(8,128)S(1)}, f32[24,256]{1,0:T(8,128)S(1)}, u32[]{:S(2)}, u32[]{:S(2)}) %collective-permute-start.3) | collective-permute-done | bytes 24608 | tf_op jit(solution)/shard_map/ppermute | solution.py:946
  10.4 3.8 %near.1 = (f32[3,512]{1,0:T(4,128)}, f32[144,128]{1,0:T(8,128)S(1)}, f32[16,1024]{1,0:T(8,128)S(1)}) custom-call(s32[2]{0:T(128)S(1)} %copy-done.3, f32[4,12]{1,0:T(4,128)S(1)} %copy-done.2, s32[4]{0:T(128)S(1)} %pad_add_fusion.where, f32[8,512]{1,0:T(8,128)S(1)} %get-tuple-element.23.own.first, f32[8,512]{1,0:T(8,128)S(1)} %collective-permute-done.other.second, ...), custom_call_target="tpu_custom_call" | custom-call | tf_op jit(solution)/shard_map/near/pallas_call | solution.py:828
  14.2 0.0 collective-permute-done.4.infos
  14.3 3.7 %far.1 = (f32[8,384]{1,0:T(8,128)S(1)}, f32[8,384]{1,0:T(8,128)S(1)}, f32[8,384]{1,0:T(8,128)S(1)}, f32[8,384]{1,0:T(8,128)S(1)}) custom-call(s32[2]{0:T(128)S(1)} %copy-done.3, s32[4]{0:T(128)S(1)} %pad_add_fusion.where, f32[144,128]{1,0:T(8,128)S(1)} %get-tuple-element.30.rows, f32[16,1024]{1,0:T(8,128)S(1)} %get-tuple-element.31.partial, ...), custom_call_target="tpu_custom_call" | custom-call | tf_op jit(solution)/shard_map/far/pallas_call | solution.py:828
  18.0 0.2 collective-permute-start.7
  18.2 1.1 %collective-permute-start.5 = (f32[8,384]{1,0:T(8,128)S(1)}, f32[8,384]{1,0:T(8,128)S(1)}, u32[]{:S(2)}, u32[]{:S(2)}) collective-permute-start(f32[8,384]{1,0:T(8,128)S(1)} %get-tuple-element.32), channel_id=1, source_target_pairs={{0,8},{4,12},{8,0},{12,4},{1,9},{5,13},{9,1},{13,5},{2,10},{6,14},... | collective-permute-start | bytes 36872 | tf_op jit(solution)/shard_map/ppermute | solution.py:946
  19.4 0.5 %collective-permute-start.6 = (f32[8,384]{1,0:T(8,128)S(1)}, f32[8,384]{1,0:T(8,128)S(1)}, u32[]{:S(2)}, u32[]{:S(2)}) collective-permute-start(f32[8,384]{1,0:T(8,128)S(1)} %get-tuple-element.33), channel_id=1, source_target_pairs={{0,12},{4,8},{8,4},{12,0},{1,13},{5,9},{9,5},{13,1},{2,14},{6,10},... | collective-permute-start | bytes 36872 | tf_op jit(solution)/shard_map/ppermute | solution.py:946
  19.9 0.0 collective-permute-done.7.refs_1_
  19.9 0.0 copy-done.1
  19.9 0.0 copy-done
  19.9 0.8 %update.2 = (f32[3,59,512]{2,1,0:T(8,128)S(1)}, f32[268,128]{1,0:T(8,128)S(1)}, f32[536,128]{1,0:T(8,128)S(1)}) custom-call(s32[4]{0:T(128)S(1)} %pad_add_fusion.where, f32[4,12]{1,0:T(4,128)S(1)} %copy-done.2, f32[59,1024]{1,0:T(8,128)S(1)} %get-tuple-element.24.params, f32[59,1024]{1,0:T(8,128)S(1)} %copy-done, f32[59,1024]{1,0:T(8,128)S(1)} %copy-done.1, ...), custom_call_target="tpu_custom_call" | custom-call | tf_op jit(solution)/shard_map/update/pallas_call | solution.py:828
  20.8 1.1 %collective-permute-done.5.refs_0_ = f32[8,384]{1,0:T(8,128)S(1)} collective-permute-done((f32[8,384]{1,0:T(8,128)S(1)}, f32[8,384]{1,0:T(8,128)S(1)}, u32[]{:S(2)}, u32[]{:S(2)}) %collective-permute-start.5) | collective-permute-done | bytes 12320 | tf_op jit(solution)/shard_map/ppermute | solution.py:946
  21.9 0.6 %collective-permute-done.6.refs_1_ = f32[8,384]{1,0:T(8,128)S(1)} collective-permute-done((f32[8,384]{1,0:T(8,128)S(1)}, f32[8,384]{1,0:T(8,128)S(1)}, u32[]{:S(2)}, u32[]{:S(2)}) %collective-permute-start.6) | collective-permute-done | bytes 12320 | tf_op jit(solution)/shard_map/ppermute | solution.py:946
  22.5 1.6 %update.3 = (f32[59,1024]{1,0:T(8,128)}, f32[59,1024]{1,0:T(8,128)}, f32[59,1024]{1,0:T(8,128)}) custom-call(s32[4]{0:T(128)S(1)} %pad_add_fusion.where, f32[4,12]{1,0:T(4,128)S(1)} %copy-done.2, f32[59,1024]{1,0:T(8,128)S(1)} %get-tuple-element.24.params, f32[59,1024]{1,0:T(8,128)S(1)} %copy-done, f32[59,1024]{1,0:T(8,128)S(1)} %copy-done.1, ...), custom_call_target="tpu_custom_call" | custom-call | tf_op jit(solution)/shard_map/update/pallas_call | solution.py:828
  (1 shorter events, 0.0 us)
Async XLA Ops:
  1.7 3.1 %copy-start.2 = (f32[4,12]{1,0:T(4,128)S(1)}, f32[4,12]{1,0:T(4,128)}, u32[]{:S(2)}) copy-start(f32[4,12]{1,0:T(4,128)} %cams.7) | copy-start | bytes 580
  1.7 3.1 %copy-start.3 = (s32[2]{0:T(128)S(1)}, s32[2]{0:T(128)}, u32[]{:S(2)}) copy-start(s32[2]{0:T(128)} %tile_ids.5) | copy-start | bytes 28
  1.7 5.8 %collective-permute-start = (f32[8,512]{1,0:T(8,128)S(1)}, f32[8,512]{1,0:T(8,128)S(1)}, u32[]{:S(2)}, u32[]{:S(2)}) collective-permute-start(f32[8,512]{1,0:T(8,128)S(1)} %get-tuple-element.23.own.first), channel_id=1, source_target_pairs={{0,1},{1,0},{2,3},{3,2},{4,5},{5,4},{6,7},{7,6},{8,9},{9,8},{10,11... | collective-permute-start | bytes 49160 | tf_op jit(solution)/shard_map/ppermute | solution.py:946
  4.8 15.1 %copy-start.1 = (f32[59,1024]{1,0:T(8,128)S(1)}, f32[59,1024]{1,0:T(8,128)}, u32[]{:S(2)}) copy-start(f32[59,1024]{1,0:T(8,128)} %adam_v.3) | copy-start | bytes 724996
  5.5 14.4 %copy-start = (f32[59,1024]{1,0:T(8,128)S(1)}, f32[59,1024]{1,0:T(8,128)}, u32[]{:S(2)}) copy-start(f32[59,1024]{1,0:T(8,128)} %adam_m.3) | copy-start | bytes 724996
  5.5 4.6 %collective-permute-start.1 = (f32[24,256]{1,0:T(8,128)S(1)}, f32[24,256]{1,0:T(8,128)S(1)}, u32[]{:S(2)}, u32[]{:S(2)}) collective-permute-start(f32[24,256]{1,0:T(8,128)S(1)} %get-tuple-element.26), channel_id=1, source_target_pairs={{0,4},{4,0},{8,12},{12,8},{1,5},{5,1},{9,13},{13,9},{2,6},{6,2},{1... | collective-permute-start | bytes 73736 | tf_op jit(solution)/shard_map/ppermute | solution.py:946
  5.6 4.5 %collective-permute-start.2 = (f32[24,256]{1,0:T(8,128)S(1)}, f32[24,256]{1,0:T(8,128)S(1)}, u32[]{:S(2)}, u32[]{:S(2)}) collective-permute-start(f32[24,256]{1,0:T(8,128)S(1)} %get-tuple-element.27), channel_id=1, source_target_pairs={{0,8},{4,12},{8,0},{12,4},{1,9},{5,13},{9,1},{13,5},{2,10},{6,14},... | collective-permute-start | bytes 73736 | tf_op jit(solution)/shard_map/ppermute | solution.py:946
  7.2 3.3 %collective-permute-start.3 = (f32[24,256]{1,0:T(8,128)S(1)}, f32[24,256]{1,0:T(8,128)S(1)}, u32[]{:S(2)}, u32[]{:S(2)}) collective-permute-start(f32[24,256]{1,0:T(8,128)S(1)} %get-tuple-element.28), channel_id=1, source_target_pairs={{0,12},{4,8},{8,4},{12,0},{1,13},{5,9},{9,5},{13,1},{2,14},{6,10},... | collective-permute-start | bytes 73736 | tf_op jit(solution)/shard_map/ppermute | solution.py:946
  7.5 6.8 %collective-permute-start.4 = (f32[16,512]{1,0:T(8,128)S(1)}, f32[16,512]{1,0:T(8,128)S(1)}, u32[]{:S(2)}, u32[]{:S(2)}) collective-permute-start(f32[16,512]{1,0:T(8,128)S(1)} %join.1), channel_id=1, source_target_pairs={{0,2},{1,3},{2,0},{3,1},{4,6},{5,7},{6,4},{7,5},{8,10},{9,11},{10,... | collective-permute-start | bytes 98312 | tf_op jit(solution)/shard_map/ppermute | solution.py:946
  18.0 1.9 %collective-permute-start.7 = (f32[8,384]{1,0:T(8,128)S(1)}, f32[8,384]{1,0:T(8,128)S(1)}, u32[]{:S(2)}, u32[]{:S(2)}) collective-permute-start(f32[8,384]{1,0:T(8,128)S(1)} %get-tuple-element.35), channel_id=1, source_target_pairs={{0,4},{4,0},{8,12},{12,8},{1,5},{5,1},{9,13},{13,9},{2,6},{6,2},{1... | collective-permute-start | bytes 36872 | tf_op jit(solution)/shard_map/ppermute | solution.py:946
  18.2 3.7 %collective-permute-start.5 = (f32[8,384]{1,0:T(8,128)S(1)}, f32[8,384]{1,0:T(8,128)S(1)}, u32[]{:S(2)}, u32[]{:S(2)}) collective-permute-start(f32[8,384]{1,0:T(8,128)S(1)} %get-tuple-element.32), channel_id=1, source_target_pairs={{0,8},{4,12},{8,0},{12,4},{1,9},{5,13},{9,1},{13,5},{2,10},{6,14},... | collective-permute-start | bytes 36872 | tf_op jit(solution)/shard_map/ppermute | solution.py:946
  19.4 3.1 %collective-permute-start.6 = (f32[8,384]{1,0:T(8,128)S(1)}, f32[8,384]{1,0:T(8,128)S(1)}, u32[]{:S(2)}, u32[]{:S(2)}) collective-permute-start(f32[8,384]{1,0:T(8,128)S(1)} %get-tuple-element.33), channel_id=1, source_target_pairs={{0,12},{4,8},{8,4},{12,0},{1,13},{5,9},{9,5},{13,1},{2,14},{6,10},... | collective-permute-start | bytes 36872 | tf_op jit(solution)/shard_map/ppermute | solution.py:946
